TPU v7x, 32 devices: a whole 2x2x4 slice. The times are simulated.
32 devices in a mesh: grp: 2 (over y), feat: 4 (over z), pos: 2 (over x), rep: 2 (over core).
Axes of the slice: x: 2, y: 2, z: 4, core: 2. Of those that a mesh axis runs over, the one named last changes fastest.
Arguments:
- active_ids: int32 [4, 16, 28], P(('grp', 'pos'), 'feat'), parts along dimension 0, may hold values from 0 to 4095, as said below
- active_vals: float32 [4, 16, 28], P(('grp', 'pos'), 'feat'), parts along dimension 0, may hold values from 0.1 to 10
- block_pattern: int32 [4, 4, 4], P(('grp', 'pos')), parts along dimension 0, may hold values from 0 to 1, as said below
- target_slots: int32 [4, 128], P(('grp', 'pos')), parts along dimension 0, may hold values from 0 to 447
- encoder: bfloat16 [4096, 2304], P(('feat', 'pos'), 'rep'), may hold values from -0.125 to 0.125
- decoder: bfloat16 [4096, 3, 2304], P(('feat', 'pos'), None, 'rep'), may hold values from -6 to 6
Outputs:
- edges: bfloat16 [4, 448, 448], P(('grp', 'pos'), ('feat', 'rep')), parts along dimension 0
- influence: float32 [4, 448, 128], P(('grp', 'pos'), ('feat', 'rep')), parts along dimension 0
There are 2 independent parts, one for each index of `grp`. A program takes and returns all parts, laid end to end along the dimension named above; an argument that names none is the same for every part. Nothing has to cross between parts.
Inputs may be any that keep to these rules, and one draw needn't show every extreme that they name: `active_ids`: feature f is held by index f // 512 of feat+pos. In each prompt's aligned blocks of 4 positions (112 slots), at most 20 features belong to one holder, and in each prompt one holder has exactly 20 in every block. `block_pattern`: for each prompt: 1 on the diagonal, 0 above it, 0 or 1 below it.
All inputs are finite; a program needn't handle non-finite values.
Results may differ from a plain program's by a relative error of at most 0.006.
Values may be sent and summed in bfloat16 or wider, within the bound.
No kernel may reach another device: no remote copies, remote signals or barrier semaphores. Data moves between devices by JAX's collectives and lax.ppermute only.
A program may use at most 64 MiB of HBM per device.

v0:
```python
import jax
import jax.numpy as jnp
from jax import lax
from jax.sharding import PartitionSpec as P

ITERS = 3


def tile_mask(pattern, tgt_start, tgt_count, src_count, kslots, block_rows):
    blocks = jnp.arange(pattern.shape[0])
    tgt_slot = tgt_start + jnp.arange(tgt_count)
    src_slot = jnp.arange(src_count)
    causal = src_slot[None, :] // kslots <= tgt_slot[:, None] // kslots
    tgt_onehot = (tgt_slot[:, None] // block_rows == blocks[None, :]).astype(jnp.float32)
    src_onehot = (src_slot[:, None] // block_rows == blocks[None, :]).astype(jnp.float32)
    allowed = jnp.dot(jnp.dot(tgt_onehot, pattern.astype(jnp.float32)), src_onehot.T)
    return jnp.where(causal, allowed, 0.0)


def per_device(active_ids, active_vals, block_pattern, target_slots, encoder, decoder):
    feat_count = lax.axis_size("feat")
    feat_index = lax.axis_index("feat")
    holder_count = lax.axis_size(("feat", "pos"))
    width_parts = lax.axis_size("rep")
    width_index = lax.axis_index("rep")
    table_rows = encoder.shape[0]
    half_width = encoder.shape[1]
    depth_count = decoder.shape[1]
    kslots = active_ids.shape[2]
    block_rows = active_ids.shape[1] * kslots
    prompt_slots = block_rows * feat_count
    result_rows = block_rows // width_parts
    capacity = max(2, (10 * block_rows + 7 * holder_count - 1) // (7 * holder_count))
    entry_ids = active_ids.reshape(block_rows)
    entry_vals = active_vals.reshape(block_rows)
    owners = entry_ids // table_rows
    local_rows = entry_ids % table_rows
    owner_hits = (owners[:, None] == jnp.arange(holder_count)[None, :]).astype(jnp.int32)
    earlier = jnp.sum((jnp.cumsum(owner_hits, axis=0) - owner_hits) * owner_hits, axis=1)
    buffer_slot = owners * capacity + earlier
    requests = jnp.full((holder_count * capacity,), -1, jnp.int32).at[buffer_slot].set(local_rows)
    requests = requests.reshape(holder_count, capacity)
    safe_rows = jnp.maximum(
        lax.all_to_all(requests, ("feat", "pos"), split_axis=0, concat_axis=0, tiled=True), 0
    )
    found = jnp.concatenate([encoder[safe_rows][:, :, None, :], decoder[safe_rows]], axis=2)
    fetched = lax.all_to_all(found, ("feat", "pos"), split_axis=0, concat_axis=0, tiled=True)
    looked_up = fetched.reshape(holder_count * capacity, depth_count + 1, half_width)[buffer_slot]
    layer = entry_ids % (depth_count + 1)
    depth = jnp.arange(depth_count)
    keep = (layer[:, None] <= depth[None, :]).astype(jnp.float32) * entry_vals[:, None]
    scaled = (looked_up[:, 1:, :].astype(jnp.float32) * keep[:, :, None]).astype(jnp.bfloat16)
    scaled = scaled.reshape(block_rows, depth_count * half_width)
    own_enc = looked_up[:, 0, :]
    pattern = block_pattern[0]
    first_row = feat_index * block_rows
    contract = (((1,), (1,)), ((), ()))
    chosen = (layer[:, None] == depth[None, :] + 1).astype(jnp.bfloat16)
    placed = (own_enc[:, None, :] * chosen[:, :, None]).reshape(
        own_enc.shape[0], depth_count * half_width
    )
    piece = lax.all_gather(scaled, "feat", axis=0, tiled=True)
    add_term = lax.dot_general(placed, piece, contract, preferred_element_type=jnp.float32)
    add_term = add_term * tile_mask(
        pattern, first_row, block_rows, piece.shape[0], kslots, block_rows
    )
    edges = lax.psum_scatter(add_term, "rep", scatter_dimension=0, tiled=True).astype(jnp.bfloat16)
    magnitude = jnp.abs(edges.astype(jnp.float32))
    weights = magnitude / jnp.maximum(jnp.sum(magnitude, axis=1, keepdims=True), 1.0)
    row_start = first_row + width_index * result_rows
    current = ((row_start + jnp.arange(result_rows))[:, None] == target_slots[0][None, :]).astype(
        jnp.float32
    )
    accum = jnp.zeros_like(current)
    over_rows = (((0,), (0,)), ((), ()))
    for sweep in range(ITERS):
        term = lax.dot_general(
            weights,
            current,
            over_rows,
            precision=lax.Precision.HIGHEST,
            preferred_element_type=jnp.float32,
        )
        current = lax.psum_scatter(
            term.astype(jnp.bfloat16), ("feat", "rep"), scatter_dimension=0, tiled=True
        ).astype(jnp.float32)
        accum = accum + current
    influence = accum * float(prompt_slots)
    return (edges[None], influence[None])


def solution(mesh):
    return jax.shard_map(
        per_device,
        mesh=mesh,
        in_specs=(
            P(("grp", "pos"), "feat", None),
            P(("grp", "pos"), "feat", None),
            P(("grp", "pos"), None, None),
            P(("grp", "pos"), None),
            P(("feat", "pos"), "rep"),
            P(("feat", "pos"), None, "rep"),
        ),
        out_specs=(
            P(("grp", "pos"), ("feat", "rep"), None),
            P(("grp", "pos"), ("feat", "rep"), None),
        ),
        check_vma=False,
    )
```

profile of v0, /device:TPU:0, one launch (start us, length us, event | category | flops | bytes accessed | tf_op | source)
XLA Modules:
  0.0 271.0 jit_solution(4975857788142258606)
XLA Ops:
  14.5 13.5 %all_to_all.14 = s32[8,1,20]{2,1,0:T(1,128)S(1)} all-to-all(s32[8,1,20]{2,1,0:T(1,128)S(1)} %all_to_all.9), channel_id=1, replica_groups=mesh['grp'=2,'feat'=4,'pos'=2,'rep'=2] {'feat','pos'}, dimensions={0} | all-to-all | bytes 1280 | tf_op jit(solution)/shard_map/all_to_all | solution.py:44
  28.1 3.4 %gather_fusion = bf16[160,1152]{1,0:T(8,128)(2,1)} fusion(bf16[512,1152]{1,0:T(8,128)(2,1)} %param.10, s32[1024]{0:T(1024)S(1)} %pad_clamp_fusion.1), kind=kCustom, calls=%fused_computation | custom fusion | bytes 737920 | tf_op jit(solution)/shard_map/gather | solution.py:46
  31.5 1.8 broadcast_in_dim.12
  33.4 7.0 %gather_fusion.1 = bf16[160,3,1152]{2,0,1:T(8,128)(2,1)} fusion(bf16[512,3,1152]{2,0,1:T(8,128)(2,1)S(1)} %copy-done, s32[1024]{0:T(1024)S(1)} %pad_clamp_fusion.1), kind=kCustom, calls=%fused_computation.1 | custom fusion | bytes 2212480 | tf_op jit(solution)/shard_map/gather | solution.py:46
  40.3 2.2 reshape.329
  44.2 2.3 copy.22
  46.5 4.4 %all-to-all-start.1 = ((bf16[8,20,4,1152]{3,2,1,0:T(4,128)(2,1)}), bf16[8,20,4,1152]{3,2,1,0:T(4,128)(2,1)}, u32[]{:S(2)}, u32[]{:S(2)}) async-start(bf16[8,20,4,1152]{3,2,1,0:T(4,128)(2,1)} %copy.22), calls=%async_computation.1 | async-start | bytes 2949120 | tf_op jit(solution)/shard_map/all_to_all | solution.py:47
  51.7 33.1 %all-to-all-done.1 = bf16[8,20,4,1152]{3,2,1,0:T(4,128)(2,1)} async-done(((bf16[8,20,4,1152]{3,2,1,0:T(4,128)(2,1)}), bf16[8,20,4,1152]{3,2,1,0:T(4,128)(2,1)}, u32[]{:S(2)}, u32[]{:S(2)}) %all-to-all-start.1) | async-done | bytes 1474592 | tf_op jit(solution)/shard_map/all_to_all | solution.py:47
  84.9 3.8 %gather_fusion.2 = bf16[112,4,1152]{2,1,0:T(4,128)(2,1)} fusion(bf16[160,4,1152]{2,1,0:T(4,128)(2,1)} %bitcast.2, s32[1024]{0:T(1024)S(1)} %pad_clamp_fusion), kind=kCustom, calls=%fused_computation.2 | custom fusion | bytes 2064832 | tf_op jit(solution)/shard_map/gather | solution.py:48
  91.6 2.2 copy.25
  93.8 2.2 copy.26
  96.9 1.8 convolution_select_fusion
  98.7 2.4 slice.14
  101.0 2.0 copy.27
  103.0 1.9 broadcast_multiply_fusion
  105.0 52.7 %all-gather.2.cloned.1.call-done = bf16[448,3456]{1,0:T(8,128)(2,1)} async-done(((bf16[112,3456]{1,0:T(8,128)(2,1)}), bf16[448,3456]{1,0:T(8,128)(2,1)}) %all-gather.2.cloned.1.call-update) | async-done | bytes 3096592 | tf_op jit(solution)/shard_map/all_gather | solution.py:62
  157.7 3.9 %convolution_multiply_fusion = f32[112,448]{1,0:T(8,128)} fusion(f32[112,448]{1,0:T(8,128)} %convolution_select_fusion, bf16[112,3456]{0,1:T(8,128)(2,1)} %bitcast.28, bf16[448,3456]{1,0:T(8,128)(2,1)} %all-gather.2.cloned.1.call-done), kind=kOutput, calls=%fused_computation.6 | convolution fusion | flops 346866688 | bytes 4272128 | tf_op jit(solution)/shard_map/dot_general | solution.py:63
  161.6 6.3 %reduce-scatter.11.cloned.1.call-done = f32[56,448]{1,0:T(8,128)} async-done(((f32[112,448]{1,0:T(8,128)}), f32[56,448]{1,0:T(8,128)}) %reduce-scatter.11.cloned.1.call-update) | async-done | bytes 100368 | tf_op jit(solution)/shard_map/reduce_scatter | solution.py:67
  169.6 2.0 convolution_convert_fusion.2
  171.7 31.1 %reduce-scatter.13.cloned.1.call-done = bf16[56,128]{1,0:T(8,128)(2,1)} async-done(((bf16[448,128]{1,0:T(8,128)(2,1)}), bf16[56,128]{1,0:T(8,128)(2,1)}) %reduce-scatter.13.cloned.1.call-update) | async-done | bytes 14352
  202.8 2.0 convolution_convert_fusion.1
  204.8 28.1 %reduce-scatter.15.cloned.1.call-done = bf16[56,128]{1,0:T(8,128)(2,1)} async-done(((bf16[448,128]{1,0:T(8,128)(2,1)}), bf16[56,128]{1,0:T(8,128)(2,1)}) %reduce-scatter.15.cloned.1.call-update) | async-done | bytes 14352
  232.9 2.0 convolution_convert_fusion
  235.0 28.1 %reduce-scatter.17.cloned.1.call-done = bf16[56,128]{1,0:T(8,128)(2,1)} async-done(((bf16[448,128]{1,0:T(8,128)(2,1)}), bf16[56,128]{1,0:T(8,128)(2,1)}) %reduce-scatter.17.cloned.1.call-update) | async-done | bytes 14352
  (44 shorter events, 16.8 us)
Async XLA Ops:
  7.2 26.2 %copy-start = (bf16[512,3,1152]{2,0,1:T(8,128)(2,1)S(1)}, bf16[512,3,1152]{2,0,1:T(8,128)(2,1)}, u32[]{:S(2)}) copy-start(bf16[512,3,1152]{2,0,1:T(8,128)(2,1)} %param.11) | copy-start | bytes 10616836
  12.8 0.5 copy-start.2
  46.5 4.5 %copy-start.1 = (f32[1,4,28]{2,1,0:T(4,128)S(1)}, f32[1,4,28]{2,1,0:T(4,128)}, u32[]{:S(2)}) copy-start(f32[1,4,28]{2,1,0:T(4,128)} %param.7) | copy-start | bytes 1348
  46.5 38.4 %all-to-all-start.1 = ((bf16[8,20,4,1152]{3,2,1,0:T(4,128)(2,1)}), bf16[8,20,4,1152]{3,2,1,0:T(4,128)(2,1)}, u32[]{:S(2)}, u32[]{:S(2)}) async-start(bf16[8,20,4,1152]{3,2,1,0:T(4,128)(2,1)} %copy.22), calls=%async_computation.1 | async-start | bytes 2949120 | tf_op jit(solution)/shard_map/all_to_all | solution.py:47
  50.9 106.7 %all-gather.2.cloned.1.call-start = ((), (), s32[]{:S(2)}) async-start(), calls=%async_computation.6 | async-start | bytes 3870720 | tf_op jit(solution)/shard_map/all_gather | solution.py:62
  96.0 72.0 %reduce-scatter.11.cloned.1.call-start = ((), (), s32[]{:S(2)}) async-start(), calls=%async_computation.7 | async-start | bytes 344064 | tf_op jit(solution)/shard_map/reduce_scatter | solution.py:67
  157.7 12.0 %copy-start.3 = (s32[1,128]{1,0:T(1,128)S(1)}, s32[1,128]{1,0:T(1,128)}, u32[]{:S(2)}) copy-start(s32[1,128]{1,0:T(1,128)} %param.9) | copy-start | bytes 1540
  161.6 41.2 %reduce-scatter.13.cloned.1.call-start = ((), (), s32[]{:S(2)}) async-start(), calls=%async_computation.8 | async-start | bytes 129024
  171.6 61.3 %reduce-scatter.15.cloned.1.call-start = ((), (), s32[]{:S(2)}) async-start(), calls=%async_computation.9 | async-start | bytes 129024
  204.8 58.3 %reduce-scatter.17.cloned.1.call-start = ((), (), s32[]{:S(2)}) async-start(), calls=%async_computation.10 | async-start | bytes 129024
Sparse Core Ops, SparseCore 0:
  96.1 61.4 all-gather.1
  161.7 6.2 reduce-scatter.10
  171.8 30.9 reduce-scatter.12
  205.0 27.9 reduce-scatter.14
  235.1 27.9 reduce-scatter.16
where the time goes:
time: 272 us; the launch traced here: 271 us
  waiting for transfers between devices  180 us (66%)
  local copies, waits for them, and re-layouts  34.7 us (13%)
  between operations  13.9 us (5%)
  blocking collectives  13.5 us (5%)
  other arithmetic  12.8 us (5%)
  matrix products  11.7 us (4%)
  starting transfers between devices  4.8 us (2%)
    unnamed x8, waiting for transfers between devices  87.4 us
    all_gather x1, waiting for transfers between devices, per_device(): piece = lax.all_gather(scaled, 'feat', axis=0, tiled=True)  52.7 us
    all_to_all x1, waiting for transfers between devices, per_device(): lax.all_to_all(found, ('feat', 'pos'), split_axis=0, concat_axis=0, tiled...  33.1 us
    all_to_all x1, blocking collectives, per_device(): lax.all_to_all(requests, ('feat', 'pos'), split_axis=0, concat_axis=0, ti...  13.5 us
    gather x2, local copies, waits for them, and re-layouts, per_device(): decoder[safe_rows]  9.2 us
    reduce_scatter x1, waiting for transfers between devices, per_device(): lax.psum_scatter(add_term, 'rep', scatter_dimension=0, tiled=True)  6.34 us
    dot_general x3, matrix products, per_device(): lax.dot_general(weights, current, over_rows, precision=lax.Precision.HIGH...  5.97 us
  transfers between devices with their start and end apart: 6, of which 6 were waited for; matrix products, arithmetic and copies ran while one was open for 3% of the time, Pallas kernels for 0%

commit v1 on v0

v1 whole, which is shorter than its diff:
```python
import jax
import jax.numpy as jnp
from jax import lax
from jax.experimental import pallas as pl
from jax.experimental.pallas import tpu as pltpu
from jax.sharding import PartitionSpec as P

ITERS = 3
F32 = jnp.float32
BF16 = jnp.bfloat16
NN = (((1,), (0,)), ((), ()))
NT = (((1,), (1,)), ((), ()))
TILE = 8
KERNEL_SLOTS = 1024
DIRECT = 16


def dot(a, b, dims=NN):
    return lax.dot_general(a, b, dims, preferred_element_type=F32)


def dot_exact(a, b):
    return lax.dot_general(a, b, NN, precision=lax.Precision.HIGHEST, preferred_element_type=F32)


def iota(shape, dim):
    return lax.broadcasted_iota(jnp.int32, shape, dim).astype(F32)


def floor_div(x, n):
    return jnp.floor((x + 0.5) * (1.0 / n))


def on_core(fn, scalars, args, outs, kernel=True):
    if not kernel:
        return fn(scalars, *args)
    count = len(args)

    def body(scalar_ref, *refs):
        values = [ref[...] for ref in refs[:count]]
        results = fn([scalar_ref[i] for i in range(len(scalars))], *values)
        for ref, value in zip(refs[count:], results):
            ref[...] = value

    return pl.pallas_call(
        body,
        out_shape=outs,
        in_specs=[pl.BlockSpec(memory_space=pltpu.SMEM)]
        + [pl.BlockSpec(memory_space=pltpu.VMEM)] * count,
        out_specs=[pl.BlockSpec(memory_space=pltpu.VMEM)] * len(outs),
        compiler_params=pltpu.CompilerParams(vmem_limit_bytes=56 * 1024 * 1024),
    )(jnp.stack(scalars).astype(jnp.int32), *args)


def rotate(x, axis, step):
    count = lax.axis_size(axis)
    return lax.ppermute(x, axis, [(i, (i + step) % count) for i in range(count)])


def shape(*dims, dtype=F32):
    return jax.ShapeDtypeStruct(dims, dtype)


def per_device(active_ids, active_vals, block_pattern, target_slots, encoder, decoder):
    feats = lax.axis_size("feat")
    poses = lax.axis_size("pos")
    reps = lax.axis_size("rep")
    holders = feats * poses
    feat = lax.axis_index("feat")
    pos = lax.axis_index("pos")
    rep = lax.axis_index("rep")
    scalars = [feat, pos, rep]
    table_rows, width = encoder.shape
    depth = decoder.shape[1]
    layers = depth + 1
    positions, kslots = active_ids.shape[1:]
    block_rows = positions * kslots
    slots = block_rows * feats
    capacity = max(2, (10 * block_rows + 7 * holders - 1) // (7 * holders))
    listed = capacity * feats
    column = poses * listed
    half = column // reps
    result_rows = block_rows // reps
    panel = target_slots.shape[1]
    tiles = -(-positions // TILE) * TILE
    small = slots <= KERNEL_SLOTS

    def pack(_, ids, vals):
        pad = jnp.zeros((tiles - positions, kslots), F32)
        return (jnp.concatenate([ids[0].astype(F32), pad, vals[0], pad], axis=0)[None],)

    (packed,) = on_core(pack, scalars, [active_ids, active_vals], [shape(1, 2 * tiles, kslots)])
    if holders <= DIRECT:
        pieces = [packed] + [rotate(packed, ("feat", "pos"), m) for m in range(1, holders)]
    else:
        pieces = [lax.all_gather(packed, ("feat", "pos"), axis=0, tiled=True)]

    def block_of(values, own, feat_of, pos_of):
        wanted = feat_of * poses + pos_of
        if len(values) == 1:
            return lax.dynamic_index_in_dim(values[0], wanted, 0, keepdims=False)
        shift = lax.rem(own - wanted + holders, holders)
        picked = values[0][0]
        for m in range(1, holders):
            picked = jnp.where(shift == m, values[m][0], picked)
        return picked

    def list_row(slot):
        place = floor_div(slot, kslots)
        block = floor_div(place, positions)
        return block * tiles + place - block * positions

    def slot_entry(slot):
        return slot - floor_div(slot, kslots) * kslots

    def as_row(table):
        spread = (iota((kslots, slots), 0) == slot_entry(iota((kslots, slots), 1))).astype(F32)
        mine = iota((table.shape[0], slots), 0) == list_row(iota((table.shape[0], slots), 1))
        return jnp.sum(jnp.where(mine, dot_exact(table, spread), 0.0), axis=0, keepdims=True)

    def as_col(table):
        spread = (list_row(iota((slots, table.shape[0]), 0)) == iota((slots, table.shape[0]), 1))
        mine = slot_entry(iota((slots, kslots), 0)) == iota((slots, kslots), 1)
        return jnp.sum(
            jnp.where(mine, dot_exact(spread.astype(F32), table), 0.0), axis=1, keepdims=True
        )

    def gather(scalars, *values):
        feat, pos, _ = scalars
        enc, dec = values[-2:]
        own = feat * poses + pos
        rows = []
        lists = []
        for k in range(poses):
            prompt = lax.rem(pos + k, poses)
            blocks = [block_of(values[:-2], own, a, prompt) for a in range(feats)]
            lists.append(
                (
                    jnp.concatenate([b[:tiles] for b in blocks], axis=0),
                    jnp.concatenate([b[tiles:] for b in blocks], axis=0),
                )
            )
            rows.append((as_row(lists[k][0]), as_row(lists[k][1])))
        hits = [floor_div(ids, table_rows) == own.astype(F32) for ids, _ in rows]
        earlier = (iota((slots, slots), 0) < iota((slots, slots), 1)).astype(BF16)
        ranks = dot(jnp.concatenate([h.astype(BF16) for h in hits], axis=0), earlier)
        picks, gains, ids_of = [], [], []
        for k in range(poses):
            chosen = jnp.where(
                hits[k] & (ranks[k : k + 1] == iota((listed, slots), 0)), 1.0, 0.0
            )
            ids = jnp.sum(chosen * rows[k][0], axis=1, keepdims=True)
            ids_of.append(ids)
            gains.append(jnp.sum(chosen * rows[k][1], axis=1, keepdims=True))
            live = jnp.sum(chosen, axis=1, keepdims=True) > 0.0
            local = jnp.where(live, ids - own.astype(F32) * table_rows, -1.0)
            picks.append((local == iota((listed, table_rows), 1)).astype(BF16))
        picks = jnp.concatenate(picks, axis=0)
        gains = jnp.concatenate(gains, axis=0)
        ids_of = jnp.concatenate(ids_of, axis=0)
        layer = ids_of - floor_div(ids_of, layers) * layers
        enc_rows = dot(picks, enc).astype(BF16)
        dec_rows = []
        for l in range(depth):
            gain = jnp.where(layer <= l, gains, 0.0)
            dec_rows.append((dot(picks, dec[l]) * gain).astype(BF16))
        out = [enc_rows[k * listed : (k + 1) * listed] for k in range(poses)]
        out += [
            jnp.stack([d[k * listed : (k + 1) * listed] for d in dec_rows], axis=0)
            for k in range(poses)
        ]
        return out + [lists[0][0]]

    outs = [shape(listed, width, dtype=BF16)] * poses
    outs += [shape(depth, listed, width, dtype=BF16)] * poses + [shape(feats * tiles, kslots)]
    gathered = on_core(
        gather,
        scalars,
        list(pieces) + [encoder, jnp.transpose(decoder, (1, 0, 2))],
        outs,
        kernel=holders <= DIRECT,
    )
    enc_rows, dec_rows, my_list = gathered[:poses], gathered[poses : 2 * poses], gathered[-1]

    enc_rows = [enc_rows[0]] + [rotate(enc_rows[k], "pos", k) for k in range(1, poses)]
    dec_rows = [dec_rows[0]] + [rotate(dec_rows[k], "pos", k) for k in range(1, poses)]
    ring = [enc_rows]
    for _ in range(1, feats):
        ring.append([rotate(rows, "feat", 1) for rows in ring[-1]])
    enc_shards = [rows for step in ring for rows in step]

    def places(scalars, ids_list, pattern):
        feat, pos, rep = scalars
        ids_row = as_row(ids_list)
        owner_row = floor_div(ids_row, table_rows)
        owner = floor_div(as_col(ids_list), table_rows)
        same = (owner == owner_row) & (iota((slots, slots), 1) < iota((slots, slots), 0))
        rank = jnp.sum(jnp.where(same, 1.0, 0.0), axis=1, keepdims=True)
        feat_of = floor_div(owner, poses)
        step = feat.astype(F32) - feat_of
        step = jnp.where(step < 0.0, step + feats, step)
        turn = pos.astype(F32) - (owner - feat_of * poses)
        turn = jnp.where(turn < 0.0, turn + poses, turn)
        place = (step * poses + turn) * listed + rank
        placing = (place == iota((slots, holders * listed), 1)).astype(BF16)
        layer_row = ids_row - floor_div(ids_row, layers) * layers
        allowed = jnp.where(pattern[0] == 1, 1.0, 0.0).astype(BF16)

        def in_block(slot, dim, extent):
            wide = (extent, feats) if dim == 0 else (feats, extent)
            return (floor_div(slot, block_rows) == iota(wide, 1 - dim)).astype(BF16)

        sources = in_block(iota((slots, 1), 0), 0, slots)
        across = dot(sources, allowed, NT).astype(BF16)
        mask = dot(across, in_block(iota((1, slots), 1), 1, slots))
        causal = floor_div(iota((slots, slots), 0), kslots) <= floor_div(
            iota((slots, slots), 1), kslots
        )
        mask = jnp.where(causal, mask, 0.0).astype(BF16)
        first = (feat * reps + rep).astype(F32) * result_rows
        own_slot = first + iota((result_rows, 1), 0)
        own_mask = dot(in_block(own_slot, 0, result_rows), allowed).astype(BF16)
        own_mask = dot(own_mask, in_block(iota((1, slots), 1), 1, slots))
        own_causal = floor_div(iota((result_rows, slots), 1), kslots) <= floor_div(
            first + iota((result_rows, slots), 0), kslots
        )
        own_mask = jnp.where(own_causal, own_mask, 0.0)
        return placing, layer_row, mask, own_mask

    placing, layer_row, mask, own_mask = on_core(
        places,
        scalars,
        [my_list, block_pattern],
        [
            shape(slots, holders * listed, dtype=BF16),
            shape(1, slots),
            shape(slots, slots, dtype=BF16),
            shape(result_rows, slots),
        ],
        kernel=small,
    )

    def products(scalars, placing, layer_row, *values):
        rep = scalars[2]
        enc = jnp.concatenate(values[: feats * poses], axis=0)
        targets = dot(placing, enc).astype(BF16)
        dec = values[feats * poses :]
        raw = jnp.zeros((column, slots), F32)
        for l in range(depth):
            rows = jnp.concatenate([d[l] for d in dec], axis=0)
            raw = raw + jnp.where(layer_row == l + 1.0, dot(rows, targets, NT), 0.0)
        first = rep == 0
        return (
            jnp.where(first, raw[:half], raw[half:]),
            jnp.where(first, raw[half:], raw[:half]),
        )

    keep, send = on_core(
        products,
        scalars,
        [placing, layer_row] + enc_shards + list(dec_rows),
        [shape(half, slots)] * 2,
        kernel=small,
    )
    own_edges = (keep + rotate(send, "rep", 1)).astype(BF16)
    shards = [own_edges] + [rotate(own_edges, "feat", k) for k in range(1, feats)]
    others = [rotate(shard, "rep", 1) for shard in shards]

    def finish(scalars, placing, mask, own_mask, targets, *values):
        feat, _, rep = scalars
        first = rep == 0
        parts = []
        for mine, other in zip(values[:feats], values[feats:]):
            parts += [jnp.where(first, mine, other), jnp.where(first, other, mine)]
        padded = jnp.concatenate(parts, axis=0)
        magnitude = jnp.abs(dot(placing, padded) * mask.astype(F32))
        total = jnp.maximum(jnp.sum(magnitude, axis=0, keepdims=True), 1.0)
        magnitude = magnitude.astype(BF16)
        diagonal = iota((slots, slots), 0) == iota((slots, slots), 1)
        scale = 1.0 / jnp.sum(jnp.where(diagonal, total, 0.0), axis=1, keepdims=True)
        current = (iota((slots, panel), 0) == targets.astype(F32)).astype(F32)
        accum = jnp.zeros((slots, panel), F32)
        for _ in range(ITERS):
            scaled = current * scale
            high = scaled.astype(BF16)
            low = (scaled - high.astype(F32)).astype(BF16)
            both = dot(magnitude, jnp.concatenate([high, low], axis=1))
            current = both[:, :panel] + both[:, panel:]
            accum = accum + current
        index = feat * reps + rep
        influence = accum[:result_rows]
        for w in range(1, feats * reps):
            influence = jnp.where(
                index == w, accum[w * result_rows : (w + 1) * result_rows], influence
            )
        start = (index * result_rows).astype(F32)
        own = start + iota((result_rows, slots), 0) == iota((result_rows, slots), 1)
        rows = dot(own.astype(BF16), padded, NT).astype(BF16)
        edges = (dot(rows, placing, NT) * own_mask).astype(BF16)
        return edges[None], (influence * float(slots))[None]

    edges, influence = on_core(
        finish,
        scalars,
        [placing, mask, own_mask, target_slots] + shards + others,
        [shape(1, result_rows, slots, dtype=BF16), shape(1, result_rows, panel)],
        kernel=small,
    )
    return edges, influence


def solution(mesh):
    return jax.shard_map(
        per_device,
        mesh=mesh,
        in_specs=(
            P(("grp", "pos"), "feat", None),
            P(("grp", "pos"), "feat", None),
            P(("grp", "pos"), None, None),
            P(("grp", "pos"), None),
            P(("feat", "pos"), "rep"),
            P(("feat", "pos"), None, "rep"),
        ),
        out_specs=(
            P(("grp", "pos"), ("feat", "rep"), None),
            P(("grp", "pos"), ("feat", "rep"), None),
        ),
        check_vma=False,
    )
```

time: 272 us -> 79.3 us (0.29)
  waiting for transfers between devices: 180 us -> 41.5 us
  local copies, waits for them, and re-layouts: 34.7 us -> 1.83 us
  Pallas kernels: 0 us -> 17.6 us
  blocking collectives: 13.5 us -> 0 us
  between operations: 13.9 us -> 0.83 us
  matrix products: 11.7 us -> 0 us
  other arithmetic: 12.8 us -> 1.59 us
  starting transfers between devices: 4.8 us -> 15.6 us
    unnamed x8 -> x0, waiting for transfers between devices: 87.4 us -> none
    all_gather x1 -> x0, waiting for transfers between devices: 52.7 us -> none  [per_device(): piece = lax.all_gather(scaled, 'feat', axis=0, tiled=True)]
    ppermute x0 -> x23, waiting for transfers between devices: none -> 41.5 us  [rotate(): lax.ppermute(x, axis, [(i, (i + step) % count) for i in range(count)])]
    all_to_all x1 -> x0, waiting for transfers between devices: 33.1 us -> none  [per_device(): lax.all_to_all(found, ('feat', 'pos'), split_axis=0, concat_axis=0, tiled...]
    pallas_call x0 -> x5, Pallas kernels: none -> 17.6 us  [on_core(): pl.pallas_call(body, out_shape=outs, in_specs=[pl.BlockSpec(memory_space=...]
    gather x4 -> x0, local copies, waits for them, and re-layouts: 16.4 us -> none  [the longest x2 9.2 us: per_device(): decoder[safe_rows]]
    ppermute x0 -> x23, starting transfers between devices: none -> 15.6 us  [rotate(): lax.ppermute(x, axis, [(i, (i + step) % count) for i in range(count)])]
    all_to_all x1 -> x0, blocking collectives: 13.5 us -> none  [per_device(): lax.all_to_all(requests, ('feat', 'pos'), split_axis=0, concat_axis=0, ti...]
  transfers between devices with their start and end apart: 6 -> 23, of which waited for: 6 -> 15; matrix products, arithmetic and copies ran while one was open for 3% -> 0% of each run, Pallas kernels for 0% -> 3%
where the time goes in v1:
time: 79.3 us; the launch traced here: 79 us
  waiting for transfers between devices  41.5 us (52%)
  Pallas kernels  17.6 us (22%)
  starting transfers between devices  15.6 us (20%)
  local copies, waits for them, and re-layouts  1.83 us (2%)
  other arithmetic  1.59 us (2%)
  between operations  0.83 us (1%)
    ppermute x23, waiting for transfers between devices, rotate(): lax.ppermute(x, axis, [(i, (i + step) % count) for i in range(count)])  41.5 us
    pallas_call x5, Pallas kernels, on_core(): pl.pallas_call(body, out_shape=outs, in_specs=[pl.BlockSpec(memory_space=...  17.6 us
    ppermute x23, starting transfers between devices, rotate(): lax.ppermute(x, axis, [(i, (i + step) % count) for i in range(count)])  15.6 us
    unnamed x46, local copies, waits for them, and re-layouts  1.83 us
  transfers between devices with their start and end apart: 23, of which 15 were waited for; matrix products, arithmetic and copies ran while one was open for 0% of the time, Pallas kernels for 3%

profile of v1, /device:TPU:0, one launch (start us, length us, event | category | flops | bytes accessed | tf_op | source)
XLA Modules:
  0.0 79.0 jit_solution(16753285153228993989)
XLA Ops:
  1.3 1.3 %shard_map.77.refs_0_ = f32[1,16,28]{2,1,0:T(8,128)} custom-call(s32[3]{0:T(128)} %pad_add_fusion.scalar_ref, s32[1,4,28]{2,1,0:T(4,128)} %refs_0_.1, f32[1,4,28]{2,1,0:T(4,128)} %refs_1_.2), custom_call_target="tpu_custom_call" | custom-call | tf_op jit(solution)/shard_map/pallas_call | solution.py:45
  2.6 6.0 %collective-permute-start.6 = (f32[1,16,28]{2,1,0:T(8,128)}, f32[1,16,28]{2,1,0:T(8,128)S(1)}, u32[]{:S(2)}, u32[]{:S(2)}) collective-permute-start(f32[1,16,28]{2,1,0:T(8,128)} %shard_map.77.refs_0_), channel_id=1, source_target_pairs={{0,14},{2,0},{4,2},{6,4},{8,6},{10,8},{12,10},{14,12},{1,15},{3,1}... | collective-permute-start | bytes 5384 | tf_op jit(solution)/shard_map/ppermute | solution.py:57
  9.0 3.0 %collective-permute-start.3 = (f32[1,16,28]{2,1,0:T(8,128)}, f32[1,16,28]{2,1,0:T(8,128)S(1)}, u32[]{:S(2)}, u32[]{:S(2)}) collective-permute-start(f32[1,16,28]{2,1,0:T(8,128)} %shard_map.77.refs_0_), channel_id=1, source_target_pairs={{0,8},{2,10},{4,12},{6,14},{8,0},{10,2},{12,4},{14,6},{1,9},{3,11}... | collective-permute-start | bytes 5384 | tf_op jit(solution)/shard_map/ppermute | solution.py:57
  12.0 1.8 %collective-permute-start.1 = (f32[1,16,28]{2,1,0:T(8,128)}, f32[1,16,28]{2,1,0:T(8,128)S(1)}, u32[]{:S(2)}, u32[]{:S(2)}) collective-permute-start(f32[1,16,28]{2,1,0:T(8,128)} %shard_map.77.refs_0_), channel_id=1, source_target_pairs={{0,4},{2,6},{4,8},{6,10},{8,12},{10,14},{12,0},{14,2},{1,5},{3,7},... | collective-permute-start | bytes 5384 | tf_op jit(solution)/shard_map/ppermute | solution.py:57
  13.9 1.1 %collective-permute-start = (f32[1,16,28]{2,1,0:T(8,128)}, f32[1,16,28]{2,1,0:T(8,128)S(1)}, u32[]{:S(2)}, u32[]{:S(2)}) collective-permute-start(f32[1,16,28]{2,1,0:T(8,128)} %shard_map.77.refs_0_), channel_id=1, source_target_pairs={{0,2},{2,4},{4,6},{6,8},{8,10},{10,12},{12,14},{14,0},{1,3},{3,5},... | collective-permute-start | bytes 5384 | tf_op jit(solution)/shard_map/ppermute | solution.py:57
  15.0 2.7 %collective-permute-done.2.refs_3_ = f32[1,16,28]{2,1,0:T(8,128)S(1)} collective-permute-done((f32[1,16,28]{2,1,0:T(8,128)}, f32[1,16,28]{2,1,0:T(8,128)S(1)}, u32[]{:S(2)}, u32[]{:S(2)}) %collective-permute-start.2) | collective-permute-done | bytes 1824 | tf_op jit(solution)/shard_map/ppermute | solution.py:57
  17.7 1.0 %collective-permute-done.1.refs_2_ = f32[1,16,28]{2,1,0:T(8,128)S(1)} collective-permute-done((f32[1,16,28]{2,1,0:T(8,128)}, f32[1,16,28]{2,1,0:T(8,128)S(1)}, u32[]{:S(2)}, u32[]{:S(2)}) %collective-permute-start.1) | collective-permute-done | bytes 1824 | tf_op jit(solution)/shard_map/ppermute | solution.py:57
  18.7 1.7 %collective-permute-done.refs_1_ = f32[1,16,28]{2,1,0:T(8,128)S(1)} collective-permute-done((f32[1,16,28]{2,1,0:T(8,128)}, f32[1,16,28]{2,1,0:T(8,128)S(1)}, u32[]{:S(2)}, u32[]{:S(2)}) %collective-permute-start) | collective-permute-done | bytes 1824 | tf_op jit(solution)/shard_map/ppermute | solution.py:57
  21.0 5.1 %shard_map.78 = (bf16[80,1152]{1,0:T(8,128)(2,1)}, bf16[80,1152]{1,0:T(8,128)(2,1)}, bf16[3,80,1152]{2,1,0:T(8,128)(2,1)}, bf16[3,80,1152]{2,1,0:T(8,128)(2,1)}, f32[32,28]{1,0:T(8,128)}) custom-call(s32[3]{0:T(128)} %pad_add_fusion.scalar_ref, f32[1,16,28]{2,1,0:T(8,128)} %shard_map.77.refs_0_, f32[1,16,28]{2,1,0:T(8,128)} %copy-done.22, ...), custom_call_target="tpu_custom_call" | custom-call | tf_op jit(solution)/shard_map/pallas_call | solution.py:45
  26.6 6.6 %collective-permute-done.7.refs_3_ = bf16[80,1152]{1,0:T(8,128)(2,1)S(1)} collective-permute-done((bf16[80,1152]{1,0:T(8,128)(2,1)}, bf16[80,1152]{1,0:T(8,128)(2,1)S(1)}, u32[]{:S(2)}, u32[]{:S(2)}) %collective-permute-start.7) | collective-permute-done | bytes 184352 | tf_op jit(solution)/shard_map/ppermute | solution.py:57
  33.2 2.1 %collective-permute-done.8.refs_4_ = bf16[80,1152]{1,0:T(8,128)(2,1)S(1)} collective-permute-done((bf16[80,1152]{1,0:T(8,128)(2,1)}, bf16[80,1152]{1,0:T(8,128)(2,1)S(1)}, u32[]{:S(2)}, u32[]{:S(2)}) %collective-permute-start.8) | collective-permute-done | bytes 184352 | tf_op jit(solution)/shard_map/ppermute | solution.py:57
  35.4 5.8 %collective-permute-done.9.refs_5_ = bf16[80,1152]{1,0:T(8,128)(2,1)S(1)} collective-permute-done((bf16[80,1152]{1,0:T(8,128)(2,1)S(1)}, bf16[80,1152]{1,0:T(8,128)(2,1)S(1)}, u32[]{:S(2)}, u32[]{:S(2)}) %collective-permute-start.9) | collective-permute-done | bytes 184352 | tf_op jit(solution)/shard_map/ppermute | solution.py:57
  41.2 3.9 %collective-permute-done.10.refs_6_ = bf16[80,1152]{1,0:T(8,128)(2,1)S(1)} collective-permute-done((bf16[80,1152]{1,0:T(8,128)(2,1)S(1)}, bf16[80,1152]{1,0:T(8,128)(2,1)S(1)}, u32[]{:S(2)}, u32[]{:S(2)}) %collective-permute-start.10) | collective-permute-done | bytes 184352 | tf_op jit(solution)/shard_map/ppermute | solution.py:57
  45.2 3.5 %collective-permute-done.11.refs_7_ = bf16[80,1152]{1,0:T(8,128)(2,1)S(1)} collective-permute-done((bf16[80,1152]{1,0:T(8,128)(2,1)S(1)}, bf16[80,1152]{1,0:T(8,128)(2,1)S(1)}, u32[]{:S(2)}, u32[]{:S(2)}) %collective-permute-start.11) | collective-permute-done | bytes 184352 | tf_op jit(solution)/shard_map/ppermute | solution.py:57
  48.6 2.6 %shard_map.79 = (bf16[448,640]{1,0:T(8,128)(2,1)}, f32[1,448]{1,0:T(1,128)}, bf16[448,448]{1,0:T(8,128)(2,1)}, f32[56,448]{1,0:T(8,128)}) custom-call(s32[3]{0:T(128)} %pad_add_fusion.scalar_ref, f32[32,28]{1,0:T(8,128)} %get-tuple-element.13.refs_0_, s32[1,4,4]{2,1,0:T(4,128)} %refs_1_.3), custom_call_target="tpu_custom_call" | custom-call | tf_op jit(solution)/shard_map/pallas_call | solution.py:45
  51.3 1.2 %collective-permute-done.12.refs_8_ = bf16[80,1152]{1,0:T(8,128)(2,1)S(1)} collective-permute-done((bf16[80,1152]{1,0:T(8,128)(2,1)S(1)}, bf16[80,1152]{1,0:T(8,128)(2,1)S(1)}, u32[]{:S(2)}, u32[]{:S(2)}) %collective-permute-start.12) | collective-permute-done | bytes 184352 | tf_op jit(solution)/shard_map/ppermute | solution.py:57
  52.5 3.5 %collective-permute-done.13.refs_9_ = bf16[80,1152]{1,0:T(8,128)(2,1)S(1)} collective-permute-done((bf16[80,1152]{1,0:T(8,128)(2,1)S(1)}, bf16[80,1152]{1,0:T(8,128)(2,1)S(1)}, u32[]{:S(2)}, u32[]{:S(2)}) %collective-permute-start.13) | collective-permute-done | bytes 184352 | tf_op jit(solution)/shard_map/ppermute | solution.py:57
  56.7 4.6 %shard_map.80 = (f32[80,448]{1,0:T(8,128)}, f32[80,448]{1,0:T(8,128)}) custom-call(s32[3]{0:T(128)} %pad_add_fusion.scalar_ref, bf16[448,640]{1,0:T(8,128)(2,1)} %get-tuple-element.14.refs_0_, f32[1,448]{1,0:T(1,128)} %get-tuple-element.17.refs_1_, bf16[80,1152]{1,0:T(8,128)(2,1)} %get-tuple-element.18.refs_2_, bf16[80,1152]{1,0:T(8,128)(2,1)} %copy-done.2, ...), custom_call_target="tpu_custom_call" | custom-call | tf_op jit(solution)/shard_map/pallas_call | solution.py:45
  61.3 1.6 %collective-permute-done.15 = f32[80,448]{1,0:T(8,128)S(1)} collective-permute-done((f32[80,448]{1,0:T(8,128)}, f32[80,448]{1,0:T(8,128)S(1)}, u32[]{:S(2)}, u32[]{:S(2)}) %collective-permute-start.15) | collective-permute-done | bytes 143392 | tf_op jit(solution)/shard_map/ppermute | solution.py:57
  62.9 0.9 %add_convert_fusion.refs_4_ = bf16[80,448]{1,0:T(8,128)(2,1)S(1)} fusion(f32[80,448]{1,0:T(8,128)} %get-tuple-element.22, f32[80,448]{1,0:T(8,128)S(1)} %collective-permute-done.15), kind=kLoop, calls=%fused_computation | loop fusion | flops 71680 | bytes 358400 | tf_op jit(solution)/shard_map/convert_element_type | solution.py:265
  64.0 1.9 %collective-permute-start.16 = (bf16[80,448]{1,0:T(8,128)(2,1)S(1)}, bf16[80,448]{1,0:T(8,128)(2,1)S(1)}, u32[]{:S(2)}, u32[]{:S(2)}) collective-permute-start(bf16[80,448]{1,0:T(8,128)(2,1)S(1)} %add_convert_fusion.refs_4_), channel_id=1, source_target_pairs={{0,4},{4,8},{8,12},{12,0},{1,5},{5,9},{9,13},{13,1},{2,6},{6,10},{... | collective-permute-start | bytes 215048 | tf_op jit(solution)/shard_map/ppermute | solution.py:57
  65.9 3.6 %collective-permute-done.18.refs_7_ = bf16[80,448]{1,0:T(8,128)(2,1)S(1)} collective-permute-done((bf16[80,448]{1,0:T(8,128)(2,1)S(1)}, bf16[80,448]{1,0:T(8,128)(2,1)S(1)}, u32[]{:S(2)}, u32[]{:S(2)}) %collective-permute-start.18) | collective-permute-done | bytes 71712 | tf_op jit(solution)/shard_map/ppermute | solution.py:57
  69.6 3.4 %collective-permute-done.17.refs_6_ = bf16[80,448]{1,0:T(8,128)(2,1)S(1)} collective-permute-done((bf16[80,448]{1,0:T(8,128)(2,1)S(1)}, bf16[80,448]{1,0:T(8,128)(2,1)S(1)}, u32[]{:S(2)}, u32[]{:S(2)}) %collective-permute-start.17) | collective-permute-done | bytes 71712 | tf_op jit(solution)/shard_map/ppermute | solution.py:57
  75.0 4.0 %shard_map.81 = (bf16[1,56,448]{2,1,0:T(8,128)(2,1)}, f32[1,56,128]{2,1,0:T(8,128)}) custom-call(s32[3]{0:T(128)} %pad_add_fusion.scalar_ref, bf16[448,640]{1,0:T(8,128)(2,1)} %get-tuple-element.14.refs_0_, bf16[448,448]{1,0:T(8,128)(2,1)} %get-tuple-element.15.refs_1_, f32[56,448]{1,0:T(8,128)} %get-tuple-element.16.refs_2_, s32[1,128]{1,0:T(1,128)} %refs_3_.1, ...), custom_call_target="tpu_custom_call" | custom-call | tf_op jit(solution)/shard_map/pallas_call | solution.py:45
  (75 shorter events, 5.1 us)
Async XLA Ops:
  2.6 9.4 %collective-permute-start.6 = (f32[1,16,28]{2,1,0:T(8,128)}, f32[1,16,28]{2,1,0:T(8,128)S(1)}, u32[]{:S(2)}, u32[]{:S(2)}) collective-permute-start(f32[1,16,28]{2,1,0:T(8,128)} %shard_map.77.refs_0_), channel_id=1, source_target_pairs={{0,14},{2,0},{4,2},{6,4},{8,6},{10,8},{12,10},{14,12},{1,15},{3,1}... | collective-permute-start | bytes 5384 | tf_op jit(solution)/shard_map/ppermute | solution.py:57
  8.6 5.3 %collective-permute-start.5 = (f32[1,16,28]{2,1,0:T(8,128)}, f32[1,16,28]{2,1,0:T(8,128)S(1)}, u32[]{:S(2)}, u32[]{:S(2)}) collective-permute-start(f32[1,16,28]{2,1,0:T(8,128)} %shard_map.77.refs_0_), channel_id=1, source_target_pairs={{0,12},{2,14},{4,0},{6,2},{8,4},{10,6},{12,8},{14,10},{1,13},{3,15... | collective-permute-start | bytes 5384 | tf_op jit(solution)/shard_map/ppermute | solution.py:57
  9.0 6.0 %collective-permute-start.4 = (f32[1,16,28]{2,1,0:T(8,128)}, f32[1,16,28]{2,1,0:T(8,128)S(1)}, u32[]{:S(2)}, u32[]{:S(2)}) collective-permute-start(f32[1,16,28]{2,1,0:T(8,128)} %shard_map.77.refs_0_), channel_id=1, source_target_pairs={{0,10},{2,12},{4,14},{6,0},{8,2},{10,4},{12,6},{14,8},{1,11},{3,13... | collective-permute-start | bytes 5384 | tf_op jit(solution)/shard_map/ppermute | solution.py:57
  9.0 6.0 %collective-permute-start.3 = (f32[1,16,28]{2,1,0:T(8,128)}, f32[1,16,28]{2,1,0:T(8,128)S(1)}, u32[]{:S(2)}, u32[]{:S(2)}) collective-permute-start(f32[1,16,28]{2,1,0:T(8,128)} %shard_map.77.refs_0_), channel_id=1, source_target_pairs={{0,8},{2,10},{4,12},{6,14},{8,0},{10,2},{12,4},{14,6},{1,9},{3,11}... | collective-permute-start | bytes 5384 | tf_op jit(solution)/shard_map/ppermute | solution.py:57
  12.0 5.7 %collective-permute-start.2 = (f32[1,16,28]{2,1,0:T(8,128)}, f32[1,16,28]{2,1,0:T(8,128)S(1)}, u32[]{:S(2)}, u32[]{:S(2)}) collective-permute-start(f32[1,16,28]{2,1,0:T(8,128)} %shard_map.77.refs_0_), channel_id=1, source_target_pairs={{0,6},{2,8},{4,10},{6,12},{8,14},{10,0},{12,2},{14,4},{1,7},{3,9},... | collective-permute-start | bytes 5384 | tf_op jit(solution)/shard_map/ppermute | solution.py:57
  12.0 6.7 %collective-permute-start.1 = (f32[1,16,28]{2,1,0:T(8,128)}, f32[1,16,28]{2,1,0:T(8,128)S(1)}, u32[]{:S(2)}, u32[]{:S(2)}) collective-permute-start(f32[1,16,28]{2,1,0:T(8,128)} %shard_map.77.refs_0_), channel_id=1, source_target_pairs={{0,4},{2,6},{4,8},{6,10},{8,12},{10,14},{12,0},{14,2},{1,5},{3,7},... | collective-permute-start | bytes 5384 | tf_op jit(solution)/shard_map/ppermute | solution.py:57
  13.9 6.6 %collective-permute-start = (f32[1,16,28]{2,1,0:T(8,128)}, f32[1,16,28]{2,1,0:T(8,128)S(1)}, u32[]{:S(2)}, u32[]{:S(2)}) collective-permute-start(f32[1,16,28]{2,1,0:T(8,128)} %shard_map.77.refs_0_), channel_id=1, source_target_pairs={{0,2},{2,4},{4,6},{6,8},{8,10},{10,12},{12,14},{14,0},{1,3},{3,5},... | collective-permute-start | bytes 5384 | tf_op jit(solution)/shard_map/ppermute | solution.py:57
  26.1 7.1 %collective-permute-start.7 = (bf16[80,1152]{1,0:T(8,128)(2,1)}, bf16[80,1152]{1,0:T(8,128)(2,1)S(1)}, u32[]{:S(2)}, u32[]{:S(2)}) collective-permute-start(bf16[80,1152]{1,0:T(8,128)(2,1)} %get-tuple-element.19), channel_id=1, source_target_pairs={{0,2},{2,0},{1,3},{3,1},{4,6},{6,4},{5,7},{7,5},{8,10},{10,8},{9,1... | collective-permute-start | bytes 552968 | tf_op jit(solution)/shard_map/ppermute | solution.py:57
  26.1 9.3 %collective-permute-start.8 = (bf16[80,1152]{1,0:T(8,128)(2,1)}, bf16[80,1152]{1,0:T(8,128)(2,1)S(1)}, u32[]{:S(2)}, u32[]{:S(2)}) collective-permute-start(bf16[80,1152]{1,0:T(8,128)(2,1)} %get-tuple-element.18.refs_2_), channel_id=1, source_target_pairs={{0,4},{4,8},{8,12},{12,0},{1,5},{5,9},{9,13},{13,1},{2,6},{6,10},{... | collective-permute-start | bytes 552968 | tf_op jit(solution)/shard_map/ppermute | solution.py:57
  33.2 22.8 %copy-start.2 = (bf16[80,1152]{1,0:T(8,128)(2,1)}, bf16[80,1152]{1,0:T(8,128)(2,1)S(1)}, u32[]{:S(2)}) copy-start(bf16[80,1152]{1,0:T(8,128)(2,1)S(1)} %collective-permute-done.7.refs_3_) | copy-start | bytes 552964
  33.2 8.0 %collective-permute-start.9 = (bf16[80,1152]{1,0:T(8,128)(2,1)S(1)}, bf16[80,1152]{1,0:T(8,128)(2,1)S(1)}, u32[]{:S(2)}, u32[]{:S(2)}) collective-permute-start(bf16[80,1152]{1,0:T(8,128)(2,1)S(1)} %collective-permute-done.7.refs_3_), channel_id=1, source_target_pairs={{0,4},{4,8},{8,12},{12,0},{1,5},{5,9},{9,13},{13,1},{2,6},{6,10},{... | collective-permute-start | bytes 552968 | tf_op jit(solution)/shard_map/ppermute | solution.py:57
  33.2 18.0 %collective-permute-start.14 = (bf16[3,80,1152]{2,1,0:T(8,128)(2,1)}, bf16[3,80,1152]{2,1,0:T(8,128)(2,1)S(1)}, u32[]{:S(2)}, u32[]{:S(2)}) collective-permute-start(bf16[3,80,1152]{2,1,0:T(8,128)(2,1)} %get-tuple-element.21), channel_id=1, source_target_pairs={{0,2},{2,0},{1,3},{3,1},{4,6},{6,4},{5,7},{7,5},{8,10},{10,8},{9,1... | collective-permute-start | bytes 1658888 | tf_op jit(solution)/shard_map/ppermute | solution.py:57
  35.4 9.8 %collective-permute-start.10 = (bf16[80,1152]{1,0:T(8,128)(2,1)S(1)}, bf16[80,1152]{1,0:T(8,128)(2,1)S(1)}, u32[]{:S(2)}, u32[]{:S(2)}) collective-permute-start(bf16[80,1152]{1,0:T(8,128)(2,1)S(1)} %collective-permute-done.8.refs_4_), channel_id=1, source_target_pairs={{0,4},{4,8},{8,12},{12,0},{1,5},{5,9},{9,13},{13,1},{2,6},{6,10},{... | collective-permute-start | bytes 552968 | tf_op jit(solution)/shard_map/ppermute | solution.py:57
  41.2 7.4 %collective-permute-start.11 = (bf16[80,1152]{1,0:T(8,128)(2,1)S(1)}, bf16[80,1152]{1,0:T(8,128)(2,1)S(1)}, u32[]{:S(2)}, u32[]{:S(2)}) collective-permute-start(bf16[80,1152]{1,0:T(8,128)(2,1)S(1)} %collective-permute-done.9.refs_5_), channel_id=1, source_target_pairs={{0,4},{4,8},{8,12},{12,0},{1,5},{5,9},{9,13},{13,1},{2,6},{6,10},{... | collective-permute-start | bytes 552968 | tf_op jit(solution)/shard_map/ppermute | solution.py:57
  45.2 7.3 %collective-permute-start.12 = (bf16[80,1152]{1,0:T(8,128)(2,1)S(1)}, bf16[80,1152]{1,0:T(8,128)(2,1)S(1)}, u32[]{:S(2)}, u32[]{:S(2)}) collective-permute-start(bf16[80,1152]{1,0:T(8,128)(2,1)S(1)} %collective-permute-done.10.refs_6_), channel_id=1, source_target_pairs={{0,4},{4,8},{8,12},{12,0},{1,5},{5,9},{9,13},{13,1},{2,6},{6,10},{... | collective-permute-start | bytes 552968 | tf_op jit(solution)/shard_map/ppermute | solution.py:57
  48.6 7.3 %collective-permute-start.13 = (bf16[80,1152]{1,0:T(8,128)(2,1)S(1)}, bf16[80,1152]{1,0:T(8,128)(2,1)S(1)}, u32[]{:S(2)}, u32[]{:S(2)}) collective-permute-start(bf16[80,1152]{1,0:T(8,128)(2,1)S(1)} %collective-permute-done.11.refs_7_), channel_id=1, source_target_pairs={{0,4},{4,8},{8,12},{12,0},{1,5},{5,9},{9,13},{13,1},{2,6},{6,10},{... | collective-permute-start | bytes 552968 | tf_op jit(solution)/shard_map/ppermute | solution.py:57
  61.3 1.6 %collective-permute-start.15 = (f32[80,448]{1,0:T(8,128)}, f32[80,448]{1,0:T(8,128)S(1)}, u32[]{:S(2)}, u32[]{:S(2)}) collective-permute-start(f32[80,448]{1,0:T(8,128)} %get-tuple-element.23), channel_id=1, source_target_pairs={{0,1},{1,0},{2,3},{3,2},{4,5},{5,4},{6,7},{7,6},{8,9},{9,8},{10,11... | collective-permute-start | bytes 430088 | tf_op jit(solution)/shard_map/ppermute | solution.py:57
  63.9 5.7 %collective-permute-start.18 = (bf16[80,448]{1,0:T(8,128)(2,1)S(1)}, bf16[80,448]{1,0:T(8,128)(2,1)S(1)}, u32[]{:S(2)}, u32[]{:S(2)}) collective-permute-start(bf16[80,448]{1,0:T(8,128)(2,1)S(1)} %add_convert_fusion.refs_4_), channel_id=1, source_target_pairs={{0,12},{4,0},{8,4},{12,8},{1,13},{5,1},{9,5},{13,9},{2,14},{6,2},{... | collective-permute-start | bytes 215048 | tf_op jit(solution)/shard_map/ppermute | solution.py:57
  63.9 9.0 %collective-permute-start.17 = (bf16[80,448]{1,0:T(8,128)(2,1)S(1)}, bf16[80,448]{1,0:T(8,128)(2,1)S(1)}, u32[]{:S(2)}, u32[]{:S(2)}) collective-permute-start(bf16[80,448]{1,0:T(8,128)(2,1)S(1)} %add_convert_fusion.refs_4_), channel_id=1, source_target_pairs={{0,8},{4,12},{8,0},{12,4},{1,9},{5,13},{9,1},{13,5},{2,10},{6,14},... | collective-permute-start | bytes 215048 | tf_op jit(solution)/shard_map/ppermute | solution.py:57
  64.0 8.9 %collective-permute-start.16 = (bf16[80,448]{1,0:T(8,128)(2,1)S(1)}, bf16[80,448]{1,0:T(8,128)(2,1)S(1)}, u32[]{:S(2)}, u32[]{:S(2)}) collective-permute-start(bf16[80,448]{1,0:T(8,128)(2,1)S(1)} %add_convert_fusion.refs_4_), channel_id=1, source_target_pairs={{0,4},{4,8},{8,12},{12,0},{1,5},{5,9},{9,13},{13,1},{2,6},{6,10},{... | collective-permute-start | bytes 215048 | tf_op jit(solution)/shard_map/ppermute | solution.py:57
  65.9 7.5 %collective-permute-start.19 = (bf16[80,448]{1,0:T(8,128)(2,1)S(1)}, bf16[80,448]{1,0:T(8,128)(2,1)S(1)}, u32[]{:S(2)}, u32[]{:S(2)}) collective-permute-start(bf16[80,448]{1,0:T(8,128)(2,1)S(1)} %add_convert_fusion.refs_4_), channel_id=1, source_target_pairs={{0,1},{1,0},{2,3},{3,2},{4,5},{5,4},{6,7},{7,6},{8,9},{9,8},{10,11... | collective-permute-start | bytes 215048 | tf_op jit(solution)/shard_map/ppermute | solution.py:57
  69.6 3.9 %collective-permute-start.22 = (bf16[80,448]{1,0:T(8,128)(2,1)S(1)}, bf16[80,448]{1,0:T(8,128)(2,1)S(1)}, u32[]{:S(2)}, u32[]{:S(2)}) collective-permute-start(bf16[80,448]{1,0:T(8,128)(2,1)S(1)} %collective-permute-done.18.refs_7_), channel_id=1, source_target_pairs={{0,1},{1,0},{2,3},{3,2},{4,5},{5,4},{6,7},{7,6},{8,9},{9,8},{10,11... | collective-permute-start | bytes 215048 | tf_op jit(solution)/shard_map/ppermute | solution.py:57
  72.9 1.3 %collective-permute-start.21 = (bf16[80,448]{1,0:T(8,128)(2,1)S(1)}, bf16[80,448]{1,0:T(8,128)(2,1)S(1)}, u32[]{:S(2)}, u32[]{:S(2)}) collective-permute-start(bf16[80,448]{1,0:T(8,128)(2,1)S(1)} %collective-permute-done.17.refs_6_), channel_id=1, source_target_pairs={{0,1},{1,0},{2,3},{3,2},{4,5},{5,4},{6,7},{7,6},{8,9},{9,8},{10,11... | collective-permute-start | bytes 215048 | tf_op jit(solution)/shard_map/ppermute | solution.py:57
  73.0 1.4 %collective-permute-start.20 = (bf16[80,448]{1,0:T(8,128)(2,1)S(1)}, bf16[80,448]{1,0:T(8,128)(2,1)S(1)}, u32[]{:S(2)}, u32[]{:S(2)}) collective-permute-start(bf16[80,448]{1,0:T(8,128)(2,1)S(1)} %collective-permute-done.16.refs_5_), channel_id=1, source_target_pairs={{0,1},{1,0},{2,3},{3,2},{4,5},{5,4},{6,7},{7,6},{8,9},{9,8},{10,11... | collective-permute-start | bytes 215048 | tf_op jit(solution)/shard_map/ppermute | solution.py:57
  (22 other events, 114.9 us)

commit v2 on v1

v2 whole, which is shorter than its diff:
```python
import jax
import jax.numpy as jnp
from jax import lax
from jax.experimental import pallas as pl
from jax.experimental.pallas import tpu as pltpu
from jax.sharding import PartitionSpec as P

ITERS = 3
F32 = jnp.float32
BF16 = jnp.bfloat16
NN = (((1,), (0,)), ((), ()))
NT = (((1,), (1,)), ((), ()))
LANES = 128
KERNEL_SLOTS = 1024


def dot(a, b, dims=NN):
    return lax.dot_general(a, b, dims, preferred_element_type=F32)


def dot_exact(a, b):
    return lax.dot_general(a, b, NN, precision=lax.Precision.HIGHEST, preferred_element_type=F32)


def iota(shape, dim):
    return lax.broadcasted_iota(jnp.int32, shape, dim).astype(F32)


def floor_div(x, n):
    return jnp.floor((x + 0.5) * (1.0 / n))


def on_core(fn, args, outs, kernel=True, after=(), cost=None):
    if not kernel:
        return fn(*args)
    count = len(args)

    def body(*refs):
        results = fn(*[ref[...] for ref in refs[:count]])
        for ref, value in zip(refs[count + len(after) :], results):
            ref[...] = value

    estimate = None
    if cost is not None:
        estimate = pl.CostEstimate(flops=cost[0], bytes_accessed=cost[1], transcendentals=0)
    return pl.pallas_call(
        body,
        out_shape=outs,
        in_specs=[pl.BlockSpec(memory_space=pltpu.VMEM)] * count
        + [pl.BlockSpec(memory_space=pl.ANY)] * len(after),
        out_specs=[pl.BlockSpec(memory_space=pltpu.VMEM)] * len(outs),
        compiler_params=pltpu.CompilerParams(vmem_limit_bytes=56 * 1024 * 1024),
        cost_estimate=estimate,
    )(*args, *after)


def rotate(x, axis, step):
    count = lax.axis_size(axis)
    return lax.ppermute(x, axis, [(i, (i + step) % count) for i in range(count)])


def ring_place(index, count):
    low = floor_div(index, 2)
    return jnp.where(index > 2 * low, count - 1 - low, low)


def ring_next(x, axis):
    count = lax.axis_size(axis)
    order = list(range(0, count, 2)) + list(range(1, count, 2))[::-1]
    return lax.ppermute(x, axis, [(order[i], order[(i + 1) % count]) for i in range(count)])


def ring_spread(x, axis):
    count = lax.axis_size(axis)
    order = list(range(0, count, 2)) + list(range(1, count, 2))[::-1]
    return [x] + [
        lax.ppermute(x, axis, [(order[i], order[(i + k) % count]) for i in range(count)])
        for k in range(1, count)
    ]


def part(x, kernel):
    return x.astype(BF16) if kernel else lax.reduce_precision(x, 8, 7).astype(BF16)


def shape(*dims, dtype=F32):
    return jax.ShapeDtypeStruct(dims, dtype)


def per_device(active_ids, active_vals, block_pattern, target_slots, encoder, decoder):
    feats = lax.axis_size("feat")
    poses = lax.axis_size("pos")
    reps = lax.axis_size("rep")
    holders = feats * poses
    table_rows, width = encoder.shape
    depth = decoder.shape[1]
    layers = depth + 1
    positions, kslots = active_ids.shape[1:]
    block_rows = positions * kslots
    slots = block_rows * feats
    capacity = max(2, (10 * block_rows + 7 * holders - 1) // (7 * holders))
    listed = capacity * feats
    column = poses * listed
    half = column // reps
    result_rows = block_rows // reps
    panel = target_slots.shape[1]
    small = slots <= KERNEL_SLOTS

    def place():
        feat, pos = lax.axis_index("feat"), lax.axis_index("pos")
        return feat.astype(F32), pos.astype(F32), lax.axis_index("rep").astype(F32)

    def pack(ids, vals):
        one = jnp.concatenate([ids[0].astype(F32), vals[0]], axis=0)
        one = jnp.concatenate([one, jnp.zeros((2 * positions, LANES - kslots), F32)], axis=1)
        return (jnp.broadcast_to(one, (holders,) + one.shape),)

    (packed,) = on_core(
        pack, [active_ids, active_vals], [shape(holders, 2 * positions, LANES)]
    )
    lists = lax.all_to_all(packed, ("feat", "pos"), split_axis=0, concat_axis=0, tiled=True)

    def list_of(values, prompt):
        blocks = []
        for a in range(feats):
            block = values[a * poses]
            for q in range(1, poses):
                block = jnp.where(prompt == q, values[a * poses + q], block)
            blocks.append(block)
        return jnp.concatenate(blocks, axis=0)[:, :kslots]

    def list_row(slot):
        place = floor_div(slot, kslots)
        return place + floor_div(place, positions) * positions

    def slot_entry(slot):
        return slot - floor_div(slot, kslots) * kslots

    def as_rows(table):
        spread = (iota((kslots, slots), 0) == slot_entry(iota((kslots, slots), 1))).astype(F32)
        wide = dot_exact(table, spread)
        row = iota(wide.shape, 0) - list_row(iota(wide.shape, 1))
        ids = jnp.sum(jnp.where(row == 0, wide, 0.0), axis=0, keepdims=True)
        return ids, jnp.sum(jnp.where(row == positions, wide, 0.0), axis=0, keepdims=True)

    def as_col(table):
        wide = (slots, table.shape[0])
        spread = (list_row(iota(wide, 0)) == iota(wide, 1)).astype(F32)
        mine = slot_entry(iota((slots, kslots), 0)) == iota((slots, kslots), 1)
        return jnp.sum(jnp.where(mine, dot_exact(spread, table), 0.0), axis=1, keepdims=True)

    def choose(values, enc):
        feat, pos, _ = place()
        own = feat * poses + pos
        tables = []
        rows = []
        for k in range(poses):
            prompt = jnp.where(pos + k >= poses, pos + k - poses, pos + k)
            tables.append(list_of(values, prompt))
            rows.append(as_rows(tables[k]))
        hits = [floor_div(ids, table_rows) == own for ids, _ in rows]
        earlier = (iota((slots, slots), 0) < iota((slots, slots), 1)).astype(BF16)
        ranks = dot(jnp.concatenate([h.astype(BF16) for h in hits], axis=0), earlier)
        picks, gains, ids_of = [], [], []
        for k in range(poses):
            chosen = jnp.where(
                hits[k] & (ranks[k : k + 1] == iota((listed, slots), 0)), 1.0, 0.0
            )
            ids = jnp.sum(chosen * rows[k][0], axis=1, keepdims=True)
            ids_of.append(ids)
            gains.append(jnp.sum(chosen * rows[k][1], axis=1, keepdims=True))
            live = jnp.sum(chosen, axis=1, keepdims=True) > 0.0
            local = jnp.where(live, ids - own * table_rows, -1.0)
            picks.append((local == iota((listed, table_rows), 1)).astype(BF16))
        picks = jnp.concatenate(picks, axis=0)
        gains = jnp.concatenate(gains, axis=0)
        ids_of = jnp.concatenate(ids_of, axis=0)
        layer = ids_of - floor_div(ids_of, layers) * layers
        gains = jnp.concatenate([jnp.where(layer <= l, gains, 0.0) for l in range(depth)], axis=1)
        enc_rows = dot(picks, enc).astype(BF16)
        enc_rows = [enc_rows[k * listed : (k + 1) * listed] for k in range(poses)]
        return enc_rows + [picks, gains, tables[0]]

    outs = [shape(listed, width, dtype=BF16)] * poses
    outs += [shape(column, table_rows, dtype=BF16), shape(column, depth)]
    outs += [shape(2 * positions * feats, kslots)]
    chosen = on_core(choose, [lists, encoder], outs, small)
    enc_rows, (picks, gains, my_list) = chosen[:poses], chosen[poses:]

    enc_rows = [enc_rows[0]] + [rotate(enc_rows[k], "pos", k) for k in range(1, poses)]
    ring = [enc_rows]
    for _ in range(1, feats):
        ring.append([ring_next(rows, "feat") for rows in ring[-1]])

    def decode(picks, gains, dec):
        rows = [(dot(picks, dec[l]) * gains[:, l : l + 1]).astype(BF16) for l in range(depth)]
        return [
            jnp.stack([row[k * listed : (k + 1) * listed] for row in rows], axis=0)
            for k in range(poses)
        ]

    dec_rows = on_core(
        decode,
        [picks, gains, jnp.transpose(decoder, (1, 0, 2))],
        [shape(depth, listed, width, dtype=BF16)] * poses,
        small,
        after=enc_rows[1:],
        cost=(2 * column * table_rows * depth * width, 2 * table_rows * depth * width),
    )
    dec_rows = [dec_rows[0]] + [rotate(dec_rows[k], "pos", k) for k in range(1, poses)]

    def places(table, pattern):
        feat, pos, rep = place()

        def padded(owner, rank):
            feat_of = floor_div(owner, poses)
            step = ring_place(feat, feats) - ring_place(feat_of, feats)
            step = jnp.where(step < 0.0, step + feats, step)
            turn = pos - (owner - feat_of * poses)
            turn = jnp.where(turn < 0.0, turn + poses, turn)
            return (step * poses + turn) * listed + rank

        ids_row = as_rows(table)[0]
        ids_col = as_col(table)
        owner_row = floor_div(ids_row, table_rows)
        owner_col = floor_div(ids_col, table_rows)
        same = owner_col == owner_row
        down, across = iota((slots, slots), 0), iota((slots, slots), 1)
        rank_col = jnp.sum(jnp.where(same & (across < down), 1.0, 0.0), axis=1, keepdims=True)
        rank_row = jnp.sum(jnp.where(same & (down < across), 1.0, 0.0), axis=0, keepdims=True)
        total = holders * listed
        placing = padded(owner_col, rank_col) == iota((slots, total), 1)
        placing_t = padded(owner_row, rank_row) == iota((total, slots), 0)
        layer = ids_col - floor_div(ids_col, layers) * layers
        layer_row = jnp.sum(jnp.where(placing, layer, 0.0), axis=0, keepdims=True)
        allowed = jnp.where(pattern[0] == 1, 1.0, 0.0).astype(BF16)

        def in_block(slot, dim, extent):
            wide = (extent, feats) if dim == 0 else (feats, extent)
            return (floor_div(slot, block_rows) == iota(wide, 1 - dim)).astype(BF16)

        sources = in_block(iota((slots, 1), 0), 0, slots)
        targets = in_block(iota((1, slots), 1), 1, slots)
        mask = dot(dot(sources, allowed, NT).astype(BF16), targets)
        mask = jnp.where(floor_div(down, kslots) <= floor_div(across, kslots), mask, 0.0)
        first = (feat * reps + rep) * result_rows
        own_slot = first + iota((result_rows, 1), 0)
        own_mask = dot(in_block(own_slot, 0, result_rows), allowed).astype(BF16)
        own_mask = dot(own_mask, targets)
        own_causal = floor_div(iota((result_rows, slots), 1), kslots) <= floor_div(
            first + iota((result_rows, slots), 0), kslots
        )
        own_mask = jnp.where(own_causal, own_mask, 0.0)
        return placing.astype(BF16), placing_t.astype(BF16), layer_row, mask.astype(BF16), own_mask

    placing, placing_t, layer_row, mask, own_mask = on_core(
        places,
        [my_list, block_pattern],
        [
            shape(slots, holders * listed, dtype=BF16),
            shape(holders * listed, slots, dtype=BF16),
            shape(1, holders * listed),
            shape(slots, slots, dtype=BF16),
            shape(result_rows, slots),
        ],
        small,
        cost=(4 * slots * slots * slots, 4 * slots * slots),
    )

    def products(first, count, layer_row, placing_t, *values):
        enc = jnp.concatenate(values[: count * poses], axis=0)
        dec = values[count * poses : count * poses + poses]
        dec = jnp.concatenate([d[l] for l in range(depth) for d in dec], axis=0)
        every = dot(dec, enc, NT)
        lanes = slice(first * column, (first + count) * column)
        raw = jnp.zeros((column, count * column), F32)
        for l in range(depth):
            rows = every[l * column : (l + 1) * column]
            raw = raw + jnp.where(layer_row[:, lanes] == l + 1.0, rows, 0.0)
        high = part(raw, small)
        rest = raw - high.astype(F32)
        middle = part(rest, small)
        low = part(rest - middle.astype(F32), small)
        split = dot(jnp.concatenate([high, middle, low], axis=0), placing_t[lanes])
        return split[:column] + split[column : 2 * column] + split[2 * column :]

    def early(*values):
        return (products(0, feats - 1, *values),)

    def late(so_far, *values):
        raw = so_far + products(feats - 1, 1, *values)
        first = place()[2] == 0.0
        return (
            jnp.where(first, raw[:half], raw[half:]),
            jnp.where(first, raw[half:], raw[:half]),
        )

    early_enc = [rows for step in ring[:-1] for rows in step]
    (so_far,) = on_core(
        early,
        [layer_row, placing_t] + early_enc + list(dec_rows),
        [shape(column, slots)],
        small,
        cost=(8 * column * slots * width, 8 * column * width),
    )
    keep, send = on_core(
        late,
        [so_far, layer_row, placing_t] + list(ring[-1]) + list(dec_rows),
        [shape(half, slots)] * 2,
        small,
    )
    own_edges = (keep + rotate(send, "rep", 1)).astype(BF16)
    shards = ring_spread(own_edges, "feat")
    others = [rotate(shard, "rep", 1) for shard in shards]

    def finish(placing, mask, own_mask, targets, *values):
        feat, _, rep = place()
        first = rep == 0.0
        parts = []
        for mine, other in zip(values[:feats], values[feats:]):
            parts += [jnp.where(first, mine, other), jnp.where(first, other, mine)]
        padded = jnp.concatenate(parts, axis=0)
        magnitude = jnp.abs(dot(placing, padded) * mask.astype(F32))
        total = jnp.maximum(jnp.sum(magnitude, axis=0, keepdims=True), 1.0)
        magnitude = magnitude.astype(BF16)
        diagonal = iota((slots, slots), 0) == iota((slots, slots), 1)
        scale = 1.0 / jnp.sum(jnp.where(diagonal, total, 0.0), axis=1, keepdims=True)
        current = (iota((slots, panel), 0) == targets.astype(F32)).astype(F32)
        accum = jnp.zeros((slots, panel), F32)
        for _ in range(ITERS):
            scaled = current * scale
            high = part(scaled, small)
            low = part(scaled - high.astype(F32), small)
            both = dot(magnitude, jnp.concatenate([high, low], axis=1))
            current = both[:, :panel] + both[:, panel:]
            accum = accum + current
        index = feat * reps + rep
        influence = accum[:result_rows]
        for w in range(1, feats * reps):
            influence = jnp.where(
                index == w, accum[w * result_rows : (w + 1) * result_rows], influence
            )
        start = index * result_rows
        own = start + iota((result_rows, slots), 0) == iota((result_rows, slots), 1)
        rows = dot(own.astype(BF16), padded, NT).astype(BF16)
        edges = (dot(rows, placing, NT) * own_mask).astype(BF16)
        return edges[None], (influence * float(slots))[None]

    edges, influence = on_core(
        finish,
        [placing, mask, own_mask, target_slots] + shards + others,
        [shape(1, result_rows, slots, dtype=BF16), shape(1, result_rows, panel)],
        small,
    )
    return edges, influence


def solution(mesh):
    return jax.shard_map(
        per_device,
        mesh=mesh,
        in_specs=(
            P(("grp", "pos"), "feat", None),
            P(("grp", "pos"), "feat", None),
            P(("grp", "pos"), None, None),
            P(("grp", "pos"), None),
            P(("feat", "pos"), "rep"),
            P(("feat", "pos"), None, "rep"),
        ),
        out_specs=(
            P(("grp", "pos"), ("feat", "rep"), None),
            P(("grp", "pos"), ("feat", "rep"), None),
        ),
        check_vma=False,
    )
```

time: 79.3 us -> 82.2 us (1.037)
  blocking collectives: 0 us -> 14 us
  waiting for transfers between devices: 41.5 us -> 31.3 us
  starting transfers between devices: 15.6 us -> 8.99 us
  Pallas kernels: 17.6 us -> 22.4 us
  local copies, waits for them, and re-layouts: 1.83 us -> 3.42 us
    ppermute x23 -> x7, waiting for transfers between devices: 41.5 us -> 8.1 us  [rotate(): lax.ppermute(x, axis, [(i, (i + step) % count) for i in range(count)])]
    ppermute x0 -> x9, waiting for transfers between devices: none -> 23.1 us  [the longest x6 15.7 us: ring_next(): lax.ppermute(x, axis, [(order[i], order[(i + 1) % count]) for i in range(...]
    ppermute x23 -> x7, starting transfers between devices: 15.6 us -> 0.97 us  [rotate(): lax.ppermute(x, axis, [(i, (i + step) % count) for i in range(count)])]
    all_to_all x0 -> x1, blocking collectives: none -> 14 us  [per_device(): lax.all_to_all(packed, ('feat', 'pos'), split_axis=0, concat_axis=0, tile...]
    ppermute x0 -> x9, starting transfers between devices: none -> 8.02 us  [the longest x6 4.48 us: ring_next(): lax.ppermute(x, axis, [(order[i], order[(i + 1) % count]) for i in range(...]
    pallas_call x5 -> x7, Pallas kernels: 17.6 us -> 22.4 us  [on_core(): pl.pallas_call(body, out_shape=outs, in_specs=[pl.BlockSpec(memory_space=...]
    unnamed x46 -> x34, local copies, waits for them, and re-layouts: 1.83 us -> 3.42 us
  transfers between devices with their start and end apart: 23 -> 16, of which waited for: 15 -> 10; matrix products, arithmetic and copies ran while one was open for 0% -> 0% of each run, Pallas kernels for 3% -> 8%
where the time goes in v2:
time: 82.2 us; the launch traced here: 81.8 us
  waiting for transfers between devices  31.3 us (38%)
  Pallas kernels  22.4 us (27%)
  blocking collectives  14 us (17%)
  starting transfers between devices  8.99 us (11%)
  local copies, waits for them, and re-layouts  3.42 us (4%)
  other arithmetic  0.94 us (1%)
    pallas_call x7, Pallas kernels, on_core(): pl.pallas_call(body, out_shape=outs, in_specs=[pl.BlockSpec(memory_space=...  22.4 us
    ppermute x6, waiting for transfers between devices, ring_next(): lax.ppermute(x, axis, [(order[i], order[(i + 1) % count]) for i in range(...  15.7 us
    all_to_all x1, blocking collectives, per_device(): lax.all_to_all(packed, ('feat', 'pos'), split_axis=0, concat_axis=0, tile...  14 us
    ppermute x7, waiting for transfers between devices, rotate(): lax.ppermute(x, axis, [(i, (i + step) % count) for i in range(count)])  8.1 us
    ppermute x3, waiting for transfers between devices, ring_spread(): lax.ppermute(x, axis, [(order[i], order[(i + k) % count]) for i in range(...  7.44 us
    ppermute x6, starting transfers between devices, ring_next(): lax.ppermute(x, axis, [(order[i], order[(i + 1) % count]) for i in range(...  4.48 us
    ppermute x3, starting transfers between devices, ring_spread(): lax.ppermute(x, axis, [(order[i], order[(i + k) % count]) for i in range(...  3.54 us
    unnamed x34, local copies, waits for them, and re-layouts  3.42 us
  transfers between devices with their start and end apart: 16, of which 10 were waited for; matrix products, arithmetic and copies ran while one was open for 0% of the time, Pallas kernels for 8%

profile of v2, /device:TPU:0, one launch (start us, length us, event | category | flops | bytes accessed | tf_op | source)
XLA Modules:
  0.0 81.8 jit_solution(10814863320413788728)
XLA Ops:
  0.6 1.3 %shard_map.77 = f32[8,8,128]{2,1,0:T(8,128)} custom-call(s32[1,4,28]{2,1,0:T(4,128)} %refs_0_.1, f32[1,4,28]{2,1,0:T(4,128)} %refs_1_.3), custom_call_target="tpu_custom_call" | custom-call | tf_op jit(solution)/shard_map/pallas_call | solution.py:46
  1.9 14.0 %all_to_all.5.refs_0_ = f32[8,8,128]{2,1,0:T(8,128)} all-to-all(f32[8,8,128]{2,1,0:T(8,128)} %shard_map.77), channel_id=1, replica_groups=mesh['grp'=2,'feat'=4,'pos'=2,'rep'=2] {'feat','pos'}, dimensions={0} | all-to-all | bytes 65536 | tf_op jit(solution)/shard_map/all_to_all | solution.py:121
  16.0 2.9 %shard_map.78 = (bf16[80,1152]{1,0:T(8,128)(2,1)}, bf16[80,1152]{1,0:T(8,128)(2,1)}, bf16[160,512]{1,0:T(8,128)(2,1)}, f32[160,3]{1,0:T(8,128)}, f32[32,28]{1,0:T(8,128)}) custom-call(f32[8,8,128]{2,1,0:T(8,128)} %all_to_all.5.refs_0_, bf16[512,1152]{1,0:T(8,128)(2,1)} %refs_1_.4), custom_call_target="tpu_custom_call" | custom-call | tf_op jit(solution)/shard_map/pallas_call | solution.py:46
  19.4 5.3 %collective-permute-done.refs_3_ = bf16[80,1152]{1,0:T(8,128)(2,1)S(1)} collective-permute-done((bf16[80,1152]{1,0:T(8,128)(2,1)}, bf16[80,1152]{1,0:T(8,128)(2,1)S(1)}, u32[]{:S(2)}, u32[]{:S(2)}) %collective-permute-start) | collective-permute-done | bytes 184352 | tf_op jit(solution)/shard_map/ppermute | solution.py:59
  25.4 3.9 %shard_map.80 = (bf16[3,80,1152]{2,1,0:T(8,128)(2,1)}, bf16[3,80,1152]{2,1,0:T(8,128)(2,1)}) custom-call(bf16[160,512]{1,0:T(8,128)(2,1)} %get-tuple-element.24.refs_0_, f32[160,3]{1,0:T(8,128)} %get-tuple-element.25.refs_1_, bf16[3,512,1152]{2,1,0:T(8,128)(2,1)} %bitcast.1, bf16[80,1152]{1,0:T(8,128)(2,1)} %copy-done.1), custom_call_target="tpu_custom_call" | custom-call | flops 566231040 | bytes 3538944 | tf_op jit(solution)/shard_map/pallas_call | solution.py:46
  30.3 0.8 %collective-permute-start.2 = (bf16[80,1152]{1,0:T(8,128)(2,1)}, bf16[80,1152]{1,0:T(8,128)(2,1)S(1)}, u32[]{:S(2)}, u32[]{:S(2)}) collective-permute-start(bf16[80,1152]{1,0:T(8,128)(2,1)} %copy-done.1), channel_id=1, source_target_pairs={{0,8},{8,12},{12,4},{4,0},{1,9},{9,13},{13,5},{5,1},{2,10},{10,14}... | collective-permute-start | bytes 552968 | tf_op jit(solution)/shard_map/ppermute | solution.py:70
  31.1 5.9 %collective-permute-done.1.refs_4_ = bf16[80,1152]{1,0:T(8,128)(2,1)S(1)} collective-permute-done((bf16[80,1152]{1,0:T(8,128)(2,1)S(1)}, bf16[80,1152]{1,0:T(8,128)(2,1)S(1)}, u32[]{:S(2)}, u32[]{:S(2)}) %collective-permute-start.1) | collective-permute-done | bytes 184352 | tf_op jit(solution)/shard_map/ppermute | solution.py:70
  37.5 3.4 %collective-permute-done.2.refs_5_ = bf16[80,1152]{1,0:T(8,128)(2,1)S(1)} collective-permute-done((bf16[80,1152]{1,0:T(8,128)(2,1)}, bf16[80,1152]{1,0:T(8,128)(2,1)S(1)}, u32[]{:S(2)}, u32[]{:S(2)}) %collective-permute-start.2) | collective-permute-done | bytes 184352 | tf_op jit(solution)/shard_map/ppermute | solution.py:70
  41.5 3.4 %collective-permute-done.3.refs_6_ = bf16[80,1152]{1,0:T(8,128)(2,1)S(1)} collective-permute-done((bf16[80,1152]{1,0:T(8,128)(2,1)S(1)}, bf16[80,1152]{1,0:T(8,128)(2,1)S(1)}, u32[]{:S(2)}, u32[]{:S(2)}) %collective-permute-start.3) | collective-permute-done | bytes 184352 | tf_op jit(solution)/shard_map/ppermute | solution.py:70
  44.9 0.8 %collective-permute-start.6 = (bf16[80,1152]{1,0:T(8,128)(2,1)S(1)}, bf16[80,1152]{1,0:T(8,128)(2,1)S(1)}, u32[]{:S(2)}, u32[]{:S(2)}) collective-permute-start(bf16[80,1152]{1,0:T(8,128)(2,1)S(1)} %collective-permute-done.3.refs_6_), channel_id=1, source_target_pairs={{0,8},{8,12},{12,4},{4,0},{1,9},{9,13},{13,5},{5,1},{2,10},{10,14}... | collective-permute-start | bytes 552968 | tf_op jit(solution)/shard_map/ppermute | solution.py:70
  45.7 3.1 %collective-permute-done.4.refs_7_ = bf16[80,1152]{1,0:T(8,128)(2,1)S(1)} collective-permute-done((bf16[80,1152]{1,0:T(8,128)(2,1)S(1)}, bf16[80,1152]{1,0:T(8,128)(2,1)S(1)}, u32[]{:S(2)}, u32[]{:S(2)}) %collective-permute-start.4) | collective-permute-done | bytes 184352 | tf_op jit(solution)/shard_map/ppermute | solution.py:70
  48.8 1.1 %collective-permute-start.7 = (bf16[80,1152]{1,0:T(8,128)(2,1)S(1)}, bf16[80,1152]{1,0:T(8,128)(2,1)S(1)}, u32[]{:S(2)}, u32[]{:S(2)}) collective-permute-start(bf16[80,1152]{1,0:T(8,128)(2,1)S(1)} %collective-permute-done.4.refs_7_), channel_id=1, source_target_pairs={{0,8},{8,12},{12,4},{4,0},{1,9},{9,13},{13,5},{5,1},{2,10},{10,14}... | collective-permute-start | bytes 552968 | tf_op jit(solution)/shard_map/ppermute | solution.py:70
  50.0 3.2 %shard_map.79 = (bf16[448,640]{1,0:T(8,128)(2,1)}, bf16[640,448]{1,0:T(8,128)(2,1)}, f32[1,640]{1,0:T(1,128)}, bf16[448,448]{1,0:T(8,128)(2,1)}, f32[56,448]{1,0:T(8,128)}) custom-call(f32[32,28]{1,0:T(8,128)} %get-tuple-element.16.refs_0_, s32[1,4,4]{2,1,0:T(4,128)} %refs_1_.5), custom_call_target="tpu_custom_call" | custom-call | flops 359661568 | bytes 802816 | tf_op jit(solution)/shard_map/pallas_call | solution.py:46
  53.2 0.8 copy-done
  54.0 3.7 %shard_map.81.refs_0_ = f32[160,448]{1,0:T(8,128)} custom-call(f32[1,640]{1,0:T(1,128)} %get-tuple-element.20.refs_0_.refs_1_, bf16[640,448]{1,0:T(8,128)(2,1)} %get-tuple-element.21.refs_1_.refs_2_, bf16[80,1152]{1,0:T(8,128)(2,1)} %get-tuple-element.22.refs_2_, bf16[80,1152]{1,0:T(8,128)(2,1)} %copy-done.1, bf16[80,1152]{1,0:T(8,128)(2,1)} %copy-done.4, ...), custom_call_target="tpu_custom_call" | custom-call | flops 660602880 | bytes 1474560 | tf_op jit(solution)/shard_map/pallas_call | solution.py:46
  59.0 3.3 %shard_map.82 = (f32[80,448]{1,0:T(8,128)}, f32[80,448]{1,0:T(8,128)}) custom-call(f32[160,448]{1,0:T(8,128)} %shard_map.81.refs_0_, f32[1,640]{1,0:T(1,128)} %get-tuple-element.20.refs_0_.refs_1_, bf16[640,448]{1,0:T(8,128)(2,1)} %get-tuple-element.21.refs_1_.refs_2_, bf16[80,1152]{1,0:T(8,128)(2,1)} %copy-done.7, bf16[80,1152]{1,0:T(8,128)(2,1)} %copy-done.9, ...), custom_call_target="tpu_custom_call" | custom-call | tf_op jit(solution)/shard_map/pallas_call | solution.py:46
  62.4 1.6 %collective-permute-done.8 = f32[80,448]{1,0:T(8,128)S(1)} collective-permute-done((f32[80,448]{1,0:T(8,128)}, f32[80,448]{1,0:T(8,128)S(1)}, u32[]{:S(2)}, u32[]{:S(2)}) %collective-permute-start.8) | collective-permute-done | bytes 143392 | tf_op jit(solution)/shard_map/ppermute | solution.py:59
  64.0 0.9 %add_convert_fusion.refs_4_ = bf16[80,448]{1,0:T(8,128)(2,1)S(1)} fusion(f32[80,448]{1,0:T(8,128)} %get-tuple-element.28, f32[80,448]{1,0:T(8,128)S(1)} %collective-permute-done.8), kind=kLoop, calls=%fused_computation | loop fusion | flops 71680 | bytes 358400 | tf_op jit(solution)/shard_map/convert_element_type | solution.py:312
  65.0 3.2 %collective-permute-start.10 = (bf16[80,448]{1,0:T(8,128)(2,1)S(1)}, bf16[80,448]{1,0:T(8,128)(2,1)S(1)}, u32[]{:S(2)}, u32[]{:S(2)}) collective-permute-start(bf16[80,448]{1,0:T(8,128)(2,1)S(1)} %add_convert_fusion.refs_4_), channel_id=1, source_target_pairs={{0,12},{8,4},{12,0},{4,8},{1,13},{9,5},{13,1},{5,9},{2,14},{10,6},... | collective-permute-start | bytes 215048 | tf_op jit(solution)/shard_map/ppermute | solution.py:77
  68.5 1.0 %collective-permute-done.9.refs_5_ = bf16[80,448]{1,0:T(8,128)(2,1)S(1)} collective-permute-done((bf16[80,448]{1,0:T(8,128)(2,1)S(1)}, bf16[80,448]{1,0:T(8,128)(2,1)S(1)}, u32[]{:S(2)}, u32[]{:S(2)}) %collective-permute-start.9) | collective-permute-done | bytes 71712 | tf_op jit(solution)/shard_map/ppermute | solution.py:77
  69.5 3.8 %collective-permute-done.10.refs_6_ = bf16[80,448]{1,0:T(8,128)(2,1)S(1)} collective-permute-done((bf16[80,448]{1,0:T(8,128)(2,1)S(1)}, bf16[80,448]{1,0:T(8,128)(2,1)S(1)}, u32[]{:S(2)}, u32[]{:S(2)}) %collective-permute-start.10) | collective-permute-done | bytes 71712 | tf_op jit(solution)/shard_map/ppermute | solution.py:77
  73.3 2.6 %collective-permute-done.11.refs_7_ = bf16[80,448]{1,0:T(8,128)(2,1)S(1)} collective-permute-done((bf16[80,448]{1,0:T(8,128)(2,1)S(1)}, bf16[80,448]{1,0:T(8,128)(2,1)S(1)}, u32[]{:S(2)}, u32[]{:S(2)}) %collective-permute-start.11) | collective-permute-done | bytes 71712 | tf_op jit(solution)/shard_map/ppermute | solution.py:77
  76.0 1.2 %collective-permute-done.15.refs_11_ = bf16[80,448]{1,0:T(8,128)(2,1)S(1)} collective-permute-done((bf16[80,448]{1,0:T(8,128)(2,1)S(1)}, bf16[80,448]{1,0:T(8,128)(2,1)S(1)}, u32[]{:S(2)}, u32[]{:S(2)}) %collective-permute-start.15) | collective-permute-done | bytes 71712 | tf_op jit(solution)/shard_map/ppermute | solution.py:59
  77.8 4.0 %shard_map.83 = (bf16[1,56,448]{2,1,0:T(8,128)(2,1)}, f32[1,56,128]{2,1,0:T(8,128)}) custom-call(bf16[448,640]{1,0:T(8,128)(2,1)} %get-tuple-element.17.refs_0_, bf16[448,448]{1,0:T(8,128)(2,1)} %get-tuple-element.18.refs_1_, f32[56,448]{1,0:T(8,128)} %get-tuple-element.19.refs_2_, s32[1,128]{1,0:T(1,128)} %refs_3_.1, bf16[80,448]{1,0:T(8,128)(2,1)} %copy-done.2, ...), custom_call_target="tpu_custom_call" | custom-call | tf_op jit(solution)/shard_map/pallas_call | solution.py:46
  (51 shorter events, 5.6 us)
Async XLA Ops:
  18.9 10.8 %copy-start.3 = (bf16[80,1152]{1,0:T(8,128)(2,1)S(1)}, bf16[80,1152]{1,0:T(8,128)(2,1)}, u32[]{:S(2)}) copy-start(bf16[80,1152]{1,0:T(8,128)(2,1)} %get-tuple-element.22.refs_2_) | copy-start | bytes 552964
  18.9 5.7 %collective-permute-start = (bf16[80,1152]{1,0:T(8,128)(2,1)}, bf16[80,1152]{1,0:T(8,128)(2,1)S(1)}, u32[]{:S(2)}, u32[]{:S(2)}) collective-permute-start(bf16[80,1152]{1,0:T(8,128)(2,1)} %get-tuple-element.23), channel_id=1, source_target_pairs={{0,2},{2,0},{1,3},{3,1},{4,6},{6,4},{5,7},{7,5},{8,10},{10,8},{9,1... | collective-permute-start | bytes 552968 | tf_op jit(solution)/shard_map/ppermute | solution.py:59
  29.3 23.9 %collective-permute-start.5 = (bf16[3,80,1152]{2,1,0:T(8,128)(2,1)}, bf16[3,80,1152]{2,1,0:T(8,128)(2,1)S(1)}, u32[]{:S(2)}, u32[]{:S(2)}) collective-permute-start(bf16[3,80,1152]{2,1,0:T(8,128)(2,1)} %get-tuple-element.27), channel_id=1, source_target_pairs={{0,2},{2,0},{1,3},{3,1},{4,6},{6,4},{5,7},{7,5},{8,10},{10,8},{9,1... | collective-permute-start | bytes 1658888 | tf_op jit(solution)/shard_map/ppermute | solution.py:59
  29.8 7.2 %collective-permute-start.1 = (bf16[80,1152]{1,0:T(8,128)(2,1)S(1)}, bf16[80,1152]{1,0:T(8,128)(2,1)S(1)}, u32[]{:S(2)}, u32[]{:S(2)}) collective-permute-start(bf16[80,1152]{1,0:T(8,128)(2,1)S(1)} %copy-done.3), channel_id=1, source_target_pairs={{0,8},{8,12},{12,4},{4,0},{1,9},{9,13},{13,5},{5,1},{2,10},{10,14}... | collective-permute-start | bytes 552968 | tf_op jit(solution)/shard_map/ppermute | solution.py:70
  30.3 10.6 %collective-permute-start.2 = (bf16[80,1152]{1,0:T(8,128)(2,1)}, bf16[80,1152]{1,0:T(8,128)(2,1)S(1)}, u32[]{:S(2)}, u32[]{:S(2)}) collective-permute-start(bf16[80,1152]{1,0:T(8,128)(2,1)} %copy-done.1), channel_id=1, source_target_pairs={{0,8},{8,12},{12,4},{4,0},{1,9},{9,13},{13,5},{5,1},{2,10},{10,14}... | collective-permute-start | bytes 552968 | tf_op jit(solution)/shard_map/ppermute | solution.py:70
  37.0 16.2 %copy-start.4 = (bf16[80,1152]{1,0:T(8,128)(2,1)}, bf16[80,1152]{1,0:T(8,128)(2,1)S(1)}, u32[]{:S(2)}) copy-start(bf16[80,1152]{1,0:T(8,128)(2,1)S(1)} %collective-permute-done.1.refs_4_) | copy-start | bytes 552964
  37.0 7.9 %collective-permute-start.3 = (bf16[80,1152]{1,0:T(8,128)(2,1)S(1)}, bf16[80,1152]{1,0:T(8,128)(2,1)S(1)}, u32[]{:S(2)}, u32[]{:S(2)}) collective-permute-start(bf16[80,1152]{1,0:T(8,128)(2,1)S(1)} %collective-permute-done.1.refs_4_), channel_id=1, source_target_pairs={{0,8},{8,12},{12,4},{4,0},{1,9},{9,13},{13,5},{5,1},{2,10},{10,14}... | collective-permute-start | bytes 552968 | tf_op jit(solution)/shard_map/ppermute | solution.py:70
  40.9 12.3 %copy-start.5 = (bf16[80,1152]{1,0:T(8,128)(2,1)}, bf16[80,1152]{1,0:T(8,128)(2,1)S(1)}, u32[]{:S(2)}) copy-start(bf16[80,1152]{1,0:T(8,128)(2,1)S(1)} %collective-permute-done.2.refs_5_) | copy-start | bytes 552964
  40.9 7.9 %collective-permute-start.4 = (bf16[80,1152]{1,0:T(8,128)(2,1)S(1)}, bf16[80,1152]{1,0:T(8,128)(2,1)S(1)}, u32[]{:S(2)}, u32[]{:S(2)}) collective-permute-start(bf16[80,1152]{1,0:T(8,128)(2,1)S(1)} %collective-permute-done.2.refs_5_), channel_id=1, source_target_pairs={{0,8},{8,12},{12,4},{4,0},{1,9},{9,13},{13,5},{5,1},{2,10},{10,14}... | collective-permute-start | bytes 552968 | tf_op jit(solution)/shard_map/ppermute | solution.py:70
  44.9 8.3 %copy-start.6 = (bf16[80,1152]{1,0:T(8,128)(2,1)}, bf16[80,1152]{1,0:T(8,128)(2,1)S(1)}, u32[]{:S(2)}) copy-start(bf16[80,1152]{1,0:T(8,128)(2,1)S(1)} %collective-permute-done.3.refs_6_) | copy-start | bytes 552964
  44.9 12.8 %collective-permute-start.6 = (bf16[80,1152]{1,0:T(8,128)(2,1)S(1)}, bf16[80,1152]{1,0:T(8,128)(2,1)S(1)}, u32[]{:S(2)}, u32[]{:S(2)}) collective-permute-start(bf16[80,1152]{1,0:T(8,128)(2,1)S(1)} %collective-permute-done.3.refs_6_), channel_id=1, source_target_pairs={{0,8},{8,12},{12,4},{4,0},{1,9},{9,13},{13,5},{5,1},{2,10},{10,14}... | collective-permute-start | bytes 552968 | tf_op jit(solution)/shard_map/ppermute | solution.py:70
  48.8 4.4 %copy-start.8 = (bf16[80,1152]{1,0:T(8,128)(2,1)}, bf16[80,1152]{1,0:T(8,128)(2,1)S(1)}, u32[]{:S(2)}) copy-start(bf16[80,1152]{1,0:T(8,128)(2,1)S(1)} %collective-permute-done.4.refs_7_) | copy-start | bytes 552964
  48.8 8.9 %collective-permute-start.7 = (bf16[80,1152]{1,0:T(8,128)(2,1)S(1)}, bf16[80,1152]{1,0:T(8,128)(2,1)S(1)}, u32[]{:S(2)}, u32[]{:S(2)}) collective-permute-start(bf16[80,1152]{1,0:T(8,128)(2,1)S(1)} %collective-permute-done.4.refs_7_), channel_id=1, source_target_pairs={{0,8},{8,12},{12,4},{4,0},{1,9},{9,13},{13,5},{5,1},{2,10},{10,14}... | collective-permute-start | bytes 552968 | tf_op jit(solution)/shard_map/ppermute | solution.py:70
  62.4 1.6 %collective-permute-start.8 = (f32[80,448]{1,0:T(8,128)}, f32[80,448]{1,0:T(8,128)S(1)}, u32[]{:S(2)}, u32[]{:S(2)}) collective-permute-start(f32[80,448]{1,0:T(8,128)} %get-tuple-element.29), channel_id=1, source_target_pairs={{0,1},{1,0},{2,3},{3,2},{4,5},{5,4},{6,7},{7,6},{8,9},{9,8},{10,11... | collective-permute-start | bytes 430088 | tf_op jit(solution)/shard_map/ppermute | solution.py:59
  64.9 12.3 %copy-start.2 = (bf16[80,448]{1,0:T(8,128)(2,1)}, bf16[80,448]{1,0:T(8,128)(2,1)S(1)}, u32[]{:S(2)}) copy-start(bf16[80,448]{1,0:T(8,128)(2,1)S(1)} %add_convert_fusion.refs_4_) | copy-start | bytes 215044
  64.9 4.5 %collective-permute-start.9 = (bf16[80,448]{1,0:T(8,128)(2,1)S(1)}, bf16[80,448]{1,0:T(8,128)(2,1)S(1)}, u32[]{:S(2)}, u32[]{:S(2)}) collective-permute-start(bf16[80,448]{1,0:T(8,128)(2,1)S(1)} %add_convert_fusion.refs_4_), channel_id=1, source_target_pairs={{0,8},{8,12},{12,4},{4,0},{1,9},{9,13},{13,5},{5,1},{2,10},{10,14}... | collective-permute-start | bytes 215048 | tf_op jit(solution)/shard_map/ppermute | solution.py:77
  65.0 8.3 %collective-permute-start.10 = (bf16[80,448]{1,0:T(8,128)(2,1)S(1)}, bf16[80,448]{1,0:T(8,128)(2,1)S(1)}, u32[]{:S(2)}, u32[]{:S(2)}) collective-permute-start(bf16[80,448]{1,0:T(8,128)(2,1)S(1)} %add_convert_fusion.refs_4_), channel_id=1, source_target_pairs={{0,12},{8,4},{12,0},{4,8},{1,13},{9,5},{13,1},{5,9},{2,14},{10,6},... | collective-permute-start | bytes 215048 | tf_op jit(solution)/shard_map/ppermute | solution.py:77
  68.2 7.7 %collective-permute-start.11 = (bf16[80,448]{1,0:T(8,128)(2,1)S(1)}, bf16[80,448]{1,0:T(8,128)(2,1)S(1)}, u32[]{:S(2)}, u32[]{:S(2)}) collective-permute-start(bf16[80,448]{1,0:T(8,128)(2,1)S(1)} %add_convert_fusion.refs_4_), channel_id=1, source_target_pairs={{0,4},{8,0},{12,8},{4,12},{1,5},{9,1},{13,9},{5,13},{2,6},{10,2},{... | collective-permute-start | bytes 215048 | tf_op jit(solution)/shard_map/ppermute | solution.py:77
  68.5 7.5 %collective-permute-start.12 = (bf16[80,448]{1,0:T(8,128)(2,1)S(1)}, bf16[80,448]{1,0:T(8,128)(2,1)S(1)}, u32[]{:S(2)}, u32[]{:S(2)}) collective-permute-start(bf16[80,448]{1,0:T(8,128)(2,1)S(1)} %add_convert_fusion.refs_4_), channel_id=1, source_target_pairs={{0,1},{1,0},{2,3},{3,2},{4,5},{5,4},{6,7},{7,6},{8,9},{9,8},{10,11... | collective-permute-start | bytes 215048 | tf_op jit(solution)/shard_map/ppermute | solution.py:59
  69.5 7.7 %copy-start.10 = (bf16[80,448]{1,0:T(8,128)(2,1)}, bf16[80,448]{1,0:T(8,128)(2,1)S(1)}, u32[]{:S(2)}) copy-start(bf16[80,448]{1,0:T(8,128)(2,1)S(1)} %collective-permute-done.9.refs_5_) | copy-start | bytes 215044
  69.5 6.5 %collective-permute-start.13 = (bf16[80,448]{1,0:T(8,128)(2,1)S(1)}, bf16[80,448]{1,0:T(8,128)(2,1)S(1)}, u32[]{:S(2)}, u32[]{:S(2)}) collective-permute-start(bf16[80,448]{1,0:T(8,128)(2,1)S(1)} %collective-permute-done.9.refs_5_), channel_id=1, source_target_pairs={{0,1},{1,0},{2,3},{3,2},{4,5},{5,4},{6,7},{7,6},{8,9},{9,8},{10,11... | collective-permute-start | bytes 215048 | tf_op jit(solution)/shard_map/ppermute | solution.py:59
  73.3 3.9 %copy-start.11 = (bf16[80,448]{1,0:T(8,128)(2,1)}, bf16[80,448]{1,0:T(8,128)(2,1)S(1)}, u32[]{:S(2)}) copy-start(bf16[80,448]{1,0:T(8,128)(2,1)S(1)} %collective-permute-done.10.refs_6_) | copy-start | bytes 215044
  73.3 2.7 %collective-permute-start.14 = (bf16[80,448]{1,0:T(8,128)(2,1)S(1)}, bf16[80,448]{1,0:T(8,128)(2,1)S(1)}, u32[]{:S(2)}, u32[]{:S(2)}) collective-permute-start(bf16[80,448]{1,0:T(8,128)(2,1)S(1)} %collective-permute-done.10.refs_6_), channel_id=1, source_target_pairs={{0,1},{1,0},{2,3},{3,2},{4,5},{5,4},{6,7},{7,6},{8,9},{9,8},{10,11... | collective-permute-start | bytes 215048 | tf_op jit(solution)/shard_map/ppermute | solution.py:59
  75.9 1.3 %collective-permute-start.15 = (bf16[80,448]{1,0:T(8,128)(2,1)S(1)}, bf16[80,448]{1,0:T(8,128)(2,1)S(1)}, u32[]{:S(2)}, u32[]{:S(2)}) collective-permute-start(bf16[80,448]{1,0:T(8,128)(2,1)S(1)} %collective-permute-done.11.refs_7_), channel_id=1, source_target_pairs={{0,1},{1,0},{2,3},{3,2},{4,5},{5,4},{6,7},{7,6},{8,9},{9,8},{10,11... | collective-permute-start | bytes 215048 | tf_op jit(solution)/shard_map/ppermute | solution.py:59
  (9 other events, 8.6 us)

commit v3 on v2

--- a/solution.py
+++ b/solution.py
@@ -30,28 +30,59 @@
     return jnp.floor((x + 0.5) * (1.0 / n))
 
 
-def on_core(fn, args, outs, kernel=True, after=(), cost=None):
+def on_core(fn, args, outs, kernel=True, through=(), streams=(), cost=None):
     if not kernel:
-        return fn(*args)
-    count = len(args)
+        loads = [lambda i, x=x: x[i] for x in streams]
+        return list(fn(*args, *loads)) + list(through)
+    count, passed, streamed = len(args), len(through), len(streams)
 
     def body(*refs):
-        results = fn(*[ref[...] for ref in refs[:count]])
-        for ref, value in zip(refs[count + len(after) :], results):
+        sources = refs[count : count + streamed]
+        results = refs[count + streamed + passed :][: len(outs)]
+        scratch = refs[len(refs) - 2 * streamed :]
+        copies = []
+        for n in range(streamed):
+            copies.append(
+                [
+                    pltpu.make_async_copy(
+                        sources[n].at[i], scratch[2 * n].at[i], scratch[2 * n + 1].at[i]
+                    )
+                    for i in range(streams[n].shape[0])
+                ]
+            )
+            for copy in copies[-1]:
+                copy.start()
+
+        def load(n):
+            def wait(i):
+                copies[n][i].wait()
+                return scratch[2 * n][i]
+
+            return wait
+
+        values = fn(*[ref[...] for ref in refs[:count]], *[load(n) for n in range(streamed)])
+        for ref, value in zip(results, values):
             ref[...] = value
 
     estimate = None
     if cost is not None:
         estimate = pl.CostEstimate(flops=cost[0], bytes_accessed=cost[1], transcendentals=0)
-    return pl.pallas_call(
+    in_vmem = pl.BlockSpec(memory_space=pltpu.VMEM)
+    anywhere = pl.BlockSpec(memory_space=pl.ANY)
+    scratch = []
+    for x in streams:
+        scratch += [pltpu.VMEM(x.shape, x.dtype), pltpu.SemaphoreType.DMA((x.shape[0],))]
+    call = pl.pallas_call(
         body,
-        out_shape=outs,
-        in_specs=[pl.BlockSpec(memory_space=pltpu.VMEM)] * count
-        + [pl.BlockSpec(memory_space=pl.ANY)] * len(after),
-        out_specs=[pl.BlockSpec(memory_space=pltpu.VMEM)] * len(outs),
+        out_shape=list(outs) + [jax.ShapeDtypeStruct(x.shape, x.dtype) for x in through],
+        in_specs=[in_vmem] * count + [anywhere] * (streamed + passed),
+        out_specs=[in_vmem] * len(outs) + [anywhere] * passed,
+        scratch_shapes=scratch,
+        input_output_aliases={count + streamed + i: len(outs) + i for i in range(passed)},
         compiler_params=pltpu.CompilerParams(vmem_limit_bytes=56 * 1024 * 1024),
         cost_estimate=estimate,
-    )(*args, *after)
+    )
+    return list(call(*args, *streams, *through))
 
 
 def rotate(x, axis, step):
@@ -64,10 +95,15 @@
     return jnp.where(index > 2 * low, count - 1 - low, low)
 
 
-def ring_next(x, axis):
+def ring_next(x, axis, across=None, turn=0):
     count = lax.axis_size(axis)
     order = list(range(0, count, 2)) + list(range(1, count, 2))[::-1]
-    return lax.ppermute(x, axis, [(order[i], order[(i + 1) % count]) for i in range(count)])
+    steps = [(order[i], order[(i + 1) % count]) for i in range(count)]
+    if across is None:
+        return lax.ppermute(x, axis, steps)
+    wide = lax.axis_size(across)
+    pairs = [(a * wide + i, b * wide + (i + turn) % wide) for a, b in steps for i in range(wide)]
+    return lax.ppermute(x, (axis, across), pairs)
 
 
 def ring_spread(x, axis):
@@ -149,7 +185,7 @@
         mine = slot_entry(iota((slots, kslots), 0)) == iota((slots, kslots), 1)
         return jnp.sum(jnp.where(mine, dot_exact(spread, table), 0.0), axis=1, keepdims=True)
 
-    def choose(values, enc):
+    def choose(values, enc, dec):
         feat, pos, _ = place()
         own = feat * poses + pos
         tables = []
@@ -176,37 +212,29 @@
         gains = jnp.concatenate(gains, axis=0)
         ids_of = jnp.concatenate(ids_of, axis=0)
         layer = ids_of - floor_div(ids_of, layers) * layers
-        gains = jnp.concatenate([jnp.where(layer <= l, gains, 0.0) for l in range(depth)], axis=1)
-        enc_rows = dot(picks, enc).astype(BF16)
-        enc_rows = [enc_rows[k * listed : (k + 1) * listed] for k in range(poses)]
-        return enc_rows + [picks, gains, tables[0]]
-
-    outs = [shape(listed, width, dtype=BF16)] * poses
-    outs += [shape(column, table_rows, dtype=BF16), shape(column, depth)]
-    outs += [shape(2 * positions * feats, kslots)]
-    chosen = on_core(choose, [lists, encoder], outs, small)
-    enc_rows, (picks, gains, my_list) = chosen[:poses], chosen[poses:]
-
-    enc_rows = [enc_rows[0]] + [rotate(enc_rows[k], "pos", k) for k in range(1, poses)]
-    ring = [enc_rows]
-    for _ in range(1, feats):
-        ring.append([ring_next(rows, "feat") for rows in ring[-1]])
-
-    def decode(picks, gains, dec):
-        rows = [(dot(picks, dec[l]) * gains[:, l : l + 1]).astype(BF16) for l in range(depth)]
-        return [
-            jnp.stack([row[k * listed : (k + 1) * listed] for row in rows], axis=0)
-            for k in range(poses)
+        enc_rows = dot(picks, enc(0)).astype(BF16)
+        dec_rows = [
+            (dot(picks, dec(l)) * jnp.where(layer <= l, gains, 0.0)).astype(BF16)
+            for l in range(depth)
         ]
-
-    dec_rows = on_core(
-        decode,
-        [picks, gains, jnp.transpose(decoder, (1, 0, 2))],
-        [shape(depth, listed, width, dtype=BF16)] * poses,
+        out = []
+        for k in range(poses):
+            rows = slice(k * listed, (k + 1) * listed)
+            out += [enc_rows[rows], jnp.stack([d[rows] for d in dec_rows], axis=0)]
+        return out + [tables[0]]
+
+    outs = [shape(listed, width, dtype=BF16), shape(depth, listed, width, dtype=BF16)] * poses
+    *chosen, my_list = on_core(
+        choose,
+        [lists],
+        outs + [shape(2 * positions * feats, kslots)],
         small,
-        after=enc_rows[1:],
-        cost=(2 * column * table_rows * depth * width, 2 * table_rows * depth * width),
-    )
+        streams=[encoder[None], jnp.transpose(decoder, (1, 0, 2))],
+    )
+    enc_rows, dec_rows = chosen[::2], chosen[1::2]
+
+    ring = [[enc_rows[0]] + [rotate(enc_rows[k], "pos", k) for k in range(1, poses)]]
+    ring.append([ring_next(enc_rows[k], "feat", "pos", k) for k in range(poses)])
     dec_rows = [dec_rows[0]] + [rotate(dec_rows[k], "pos", k) for k in range(1, poses)]
 
     def places(table, pattern):
@@ -253,7 +281,7 @@
         own_mask = jnp.where(own_causal, own_mask, 0.0)
         return placing.astype(BF16), placing_t.astype(BF16), layer_row, mask.astype(BF16), own_mask
 
-    placing, placing_t, layer_row, mask, own_mask = on_core(
+    placing, placing_t, layer_row, mask, own_mask, *ring[1][-1:] = on_core(
         places,
         [my_list, block_pattern],
         [
@@ -264,8 +292,11 @@
             shape(result_rows, slots),
         ],
         small,
+        through=ring[1][-1:],
         cost=(4 * slots * slots * slots, 4 * slots * slots),
     )
+    for _ in range(2, feats):
+        ring.append([ring_next(rows, "feat") for rows in ring[-1]])
 
     def products(first, count, layer_row, placing_t, *values):
         enc = jnp.concatenate(values[: count * poses], axis=0)

time: 82.2 us -> 76.1 us (0.926)
  waiting for transfers between devices: 31.3 us -> 21.4 us
  starting transfers between devices: 8.99 us -> 14 us
  Pallas kernels: 22.4 us -> 21 us
    ppermute x7, waiting for transfers between devices: 8.1 us -> 2.79 us  [rotate(): lax.ppermute(x, axis, [(i, (i + step) % count) for i in range(count)])]
    ppermute x6, starting transfers between devices: 4.48 us -> 8.67 us  [the longest x4 6.56 us: ring_next(): return lax.ppermute(x, axis, steps)]
    ppermute x6, waiting for transfers between devices: 15.7 us -> 12.5 us  [the longest x2 8.46 us: ring_next(): return lax.ppermute(x, (axis, across), pairs)]
    ppermute x3, waiting for transfers between devices: 7.44 us -> 6.03 us  [ring_spread(): lax.ppermute(x, axis, [(order[i], order[(i + k) % count]) for i in range(...]
    pallas_call x7 -> x6, Pallas kernels: 22.4 us -> 21 us  [on_core(): return list(call(*args, *streams, *through))]
    unnamed x34 -> x32, local copies, waits for them, and re-layouts: 3.42 us -> 3.51 us
  transfers between devices with their start and end apart: 16 -> 16, of which waited for: 10 -> 8; matrix products, arithmetic and copies ran while one was open for 0% -> 0% of each run, Pallas kernels for 8% -> 9%
where the time goes in v3:
time: 76.1 us; the launch traced here: 75.6 us
  waiting for transfers between devices  21.4 us (28%)
  Pallas kernels  21 us (28%)
  blocking collectives  14 us (18%)
  starting transfers between devices  14 us (18%)
  local copies, waits for them, and re-layouts  3.51 us (5%)
  other arithmetic  0.94 us (1%)
    pallas_call x6, Pallas kernels, on_core(): return list(call(*args, *streams, *through))  21 us
    all_to_all x1, blocking collectives, per_device(): lax.all_to_all(packed, ('feat', 'pos'), split_axis=0, concat_axis=0, tile...  14 us
    ppermute x2, waiting for transfers between devices, ring_next(): return lax.ppermute(x, (axis, across), pairs)  8.46 us
    ppermute x4, starting transfers between devices, ring_next(): return lax.ppermute(x, axis, steps)  6.56 us
    ppermute x3, waiting for transfers between devices, ring_spread(): lax.ppermute(x, axis, [(order[i], order[(i + k) % count]) for i in range(...  6.03 us
    ppermute x4, waiting for transfers between devices, ring_next(): return lax.ppermute(x, axis, steps)  4.08 us
    ppermute x3, starting transfers between devices, ring_spread(): lax.ppermute(x, axis, [(order[i], order[(i + k) % count]) for i in range(...  3.72 us
    unnamed x32, local copies, waits for them, and re-layouts  3.51 us
  transfers between devices with their start and end apart: 16, of which 8 were waited for; matrix products, arithmetic and copies ran while one was open for 0% of the time, Pallas kernels for 9%

profile of v3, /device:TPU:0, one launch (start us, length us, event | category | flops | bytes accessed | tf_op | source)
XLA Modules:
  0.0 75.6 jit_solution(12665755040565823819)
XLA Ops:
  0.6 1.3 %shard_map.77 = f32[8,8,128]{2,1,0:T(8,128)} custom-call(s32[1,4,28]{2,1,0:T(4,128)} %refs_0_.1, f32[1,4,28]{2,1,0:T(4,128)} %refs_1_.2), custom_call_target="tpu_custom_call" | custom-call | tf_op jit(solution)/shard_map/pallas_call | solution.py:85
  1.9 14.0 %all_to_all.5.refs_0_ = f32[8,8,128]{2,1,0:T(8,128)} all-to-all(f32[8,8,128]{2,1,0:T(8,128)} %shard_map.77), channel_id=1, replica_groups=mesh['grp'=2,'feat'=4,'pos'=2,'rep'=2] {'feat','pos'}, dimensions={0} | all-to-all | bytes 65536 | tf_op jit(solution)/shard_map/all_to_all | solution.py:157
  16.0 5.5 %shard_map.78 = (bf16[80,1152]{1,0:T(8,128)(2,1)}, bf16[3,80,1152]{2,1,0:T(8,128)(2,1)}, bf16[80,1152]{1,0:T(8,128)(2,1)}, bf16[3,80,1152]{2,1,0:T(8,128)(2,1)}, f32[32,28]{1,0:T(8,128)}) custom-call(f32[8,8,128]{2,1,0:T(8,128)} %all_to_all.5.refs_0_, bf16[1,512,1152]{2,1,0:T(8,128)(2,1)} %bitcast.3, bf16[3,512,1152]{2,1,0:T(8,128)(2,1)} %bitcast.2), custom_call_target="tpu_custom_call" | custom-call | tf_op jit(solution)/shard_map/pallas_call | solution.py:85
  22.5 1.6 %collective-permute-start = (bf16[80,1152]{1,0:T(8,128)(2,1)}, bf16[80,1152]{1,0:T(8,128)(2,1)S(1)}, u32[]{:S(2)}, u32[]{:S(2)}) collective-permute-start(bf16[80,1152]{1,0:T(8,128)(2,1)} %get-tuple-element.16), channel_id=1, source_target_pairs={{0,10},{2,8},{8,14},{10,12},{12,6},{14,4},{4,2},{6,0},{1,11},{3,9}... | collective-permute-start | bytes 552968 | tf_op jit(solution)/shard_map/ppermute | solution.py:106
  24.1 5.7 %collective-permute-done.2.refs_4_ = bf16[80,1152]{1,0:T(8,128)(2,1)S(1)} collective-permute-done((bf16[80,1152]{1,0:T(8,128)(2,1)}, bf16[80,1152]{1,0:T(8,128)(2,1)S(1)}, u32[]{:S(2)}, u32[]{:S(2)}) %collective-permute-start.2) | collective-permute-done | bytes 184352 | tf_op jit(solution)/shard_map/ppermute | solution.py:106
  29.8 1.3 %collective-permute-start.3 = (bf16[80,1152]{1,0:T(8,128)(2,1)S(1)}, bf16[80,1152]{1,0:T(8,128)(2,1)S(1)}, u32[]{:S(2)}, u32[]{:S(2)}) collective-permute-start(bf16[80,1152]{1,0:T(8,128)(2,1)S(1)} %collective-permute-done.2.refs_4_), channel_id=1, source_target_pairs={{0,8},{8,12},{12,4},{4,0},{1,9},{9,13},{13,5},{5,1},{2,10},{10,14}... | collective-permute-start | bytes 552968 | tf_op jit(solution)/shard_map/ppermute | solution.py:103
  31.2 2.8 %collective-permute-done.refs_2_ = bf16[80,1152]{1,0:T(8,128)(2,1)S(1)} collective-permute-done((bf16[80,1152]{1,0:T(8,128)(2,1)}, bf16[80,1152]{1,0:T(8,128)(2,1)S(1)}, u32[]{:S(2)}, u32[]{:S(2)}) %collective-permute-start) | collective-permute-done | bytes 184352 | tf_op jit(solution)/shard_map/ppermute | solution.py:106
  33.9 0.7 copy-done.8
  34.6 3.2 %shard_map.79 = (bf16[448,640]{1,0:T(8,128)(2,1)}, bf16[640,448]{1,0:T(8,128)(2,1)}, f32[1,640]{1,0:T(1,128)}, bf16[448,448]{1,0:T(8,128)(2,1)}, f32[56,448]{1,0:T(8,128)}, /*index=5*/bf16[80,1152]{1,0:T(8,128)(2,1)}) custom-call(f32[32,28]{1,0:T(8,128)} %get-tuple-element.15.refs_0_, s32[1,4,4]{2,1,0:T(4,128)} %refs_1_.3, ...), custom_call_target="tpu_custom_call", output_to_operand_aliasing={{5}: (2, {})} | custom-call | flops 359661568 | bytes 802816 | tf_op jit(solution)/shard_map/pallas_call | solution.py:85
  37.8 1.7 %collective-permute-start.4 = (bf16[80,1152]{1,0:T(8,128)(2,1)}, bf16[80,1152]{1,0:T(8,128)(2,1)S(1)}, u32[]{:S(2)}, u32[]{:S(2)}) collective-permute-start(bf16[80,1152]{1,0:T(8,128)(2,1)} %get-tuple-element.23.refs_5_), channel_id=1, source_target_pairs={{0,8},{8,12},{12,4},{4,0},{1,9},{9,13},{13,5},{5,1},{2,10},{10,14}... | collective-permute-start | bytes 552968 | tf_op jit(solution)/shard_map/ppermute | solution.py:103
  40.3 4.1 %collective-permute-done.4.refs_7_ = bf16[80,1152]{1,0:T(8,128)(2,1)S(1)} collective-permute-done((bf16[80,1152]{1,0:T(8,128)(2,1)}, bf16[80,1152]{1,0:T(8,128)(2,1)S(1)}, u32[]{:S(2)}, u32[]{:S(2)}) %collective-permute-start.4) | collective-permute-done | bytes 184352 | tf_op jit(solution)/shard_map/ppermute | solution.py:103
  44.4 3.3 %collective-permute-start.7 = (bf16[80,1152]{1,0:T(8,128)(2,1)S(1)}, bf16[80,1152]{1,0:T(8,128)(2,1)S(1)}, u32[]{:S(2)}, u32[]{:S(2)}) collective-permute-start(bf16[80,1152]{1,0:T(8,128)(2,1)S(1)} %collective-permute-done.4.refs_7_), channel_id=1, source_target_pairs={{0,8},{8,12},{12,4},{4,0},{1,9},{9,13},{13,5},{5,1},{2,10},{10,14}... | collective-permute-start | bytes 552968 | tf_op jit(solution)/shard_map/ppermute | solution.py:103
  47.7 0.6 copy-done.7
  48.5 3.7 %shard_map.80.refs_0_ = f32[160,448]{1,0:T(8,128)} custom-call(f32[1,640]{1,0:T(1,128)} %get-tuple-element.20.refs_0_.refs_1_, bf16[640,448]{1,0:T(8,128)(2,1)} %get-tuple-element.21.refs_1_.refs_2_, bf16[80,1152]{1,0:T(8,128)(2,1)} %get-tuple-element.22.refs_2_, bf16[80,1152]{1,0:T(8,128)(2,1)} %copy-done.7, bf16[80,1152]{1,0:T(8,128)(2,1)} %copy-done.2, ...), custom_call_target="tpu_custom_call" | custom-call | flops 660602880 | bytes 1474560 | tf_op jit(solution)/shard_map/pallas_call | solution.py:85
  52.2 0.7 copy-done.5
  52.9 0.7 copy-done.6
  53.6 3.4 %shard_map.81 = (f32[80,448]{1,0:T(8,128)}, f32[80,448]{1,0:T(8,128)}) custom-call(f32[160,448]{1,0:T(8,128)} %shard_map.80.refs_0_, f32[1,640]{1,0:T(1,128)} %get-tuple-element.20.refs_0_.refs_1_, bf16[640,448]{1,0:T(8,128)(2,1)} %get-tuple-element.21.refs_1_.refs_2_, bf16[80,1152]{1,0:T(8,128)(2,1)} %copy-done.5, bf16[80,1152]{1,0:T(8,128)(2,1)} %copy-done.6, ...), custom_call_target="tpu_custom_call" | custom-call | tf_op jit(solution)/shard_map/pallas_call | solution.py:85
  56.9 1.6 %collective-permute-done.8 = f32[80,448]{1,0:T(8,128)S(1)} collective-permute-done((f32[80,448]{1,0:T(8,128)}, f32[80,448]{1,0:T(8,128)S(1)}, u32[]{:S(2)}, u32[]{:S(2)}) %collective-permute-start.8) | collective-permute-done | bytes 143392 | tf_op jit(solution)/shard_map/ppermute | solution.py:90
  58.5 0.9 %add_convert_fusion.refs_4_ = bf16[80,448]{1,0:T(8,128)(2,1)S(1)} fusion(f32[80,448]{1,0:T(8,128)} %get-tuple-element.26, f32[80,448]{1,0:T(8,128)S(1)} %collective-permute-done.8), kind=kLoop, calls=%fused_computation | loop fusion | flops 71680 | bytes 358400 | tf_op jit(solution)/shard_map/convert_element_type | solution.py:343
  60.0 2.2 %collective-permute-start.10 = (bf16[80,448]{1,0:T(8,128)(2,1)S(1)}, bf16[80,448]{1,0:T(8,128)(2,1)S(1)}, u32[]{:S(2)}, u32[]{:S(2)}) collective-permute-start(bf16[80,448]{1,0:T(8,128)(2,1)S(1)} %add_convert_fusion.refs_4_), channel_id=1, source_target_pairs={{0,12},{8,4},{12,0},{4,8},{1,13},{9,5},{13,1},{5,9},{2,14},{10,6},... | collective-permute-start | bytes 215048 | tf_op jit(solution)/shard_map/ppermute | solution.py:113
  62.2 1.0 %collective-permute-start.9 = (bf16[80,448]{1,0:T(8,128)(2,1)S(1)}, bf16[80,448]{1,0:T(8,128)(2,1)S(1)}, u32[]{:S(2)}, u32[]{:S(2)}) collective-permute-start(bf16[80,448]{1,0:T(8,128)(2,1)S(1)} %add_convert_fusion.refs_4_), channel_id=1, source_target_pairs={{0,8},{8,12},{12,4},{4,0},{1,9},{9,13},{13,5},{5,1},{2,10},{10,14}... | collective-permute-start | bytes 215048 | tf_op jit(solution)/shard_map/ppermute | solution.py:113
  63.2 6.0 %collective-permute-done.11.refs_7_ = bf16[80,448]{1,0:T(8,128)(2,1)S(1)} collective-permute-done((bf16[80,448]{1,0:T(8,128)(2,1)S(1)}, bf16[80,448]{1,0:T(8,128)(2,1)S(1)}, u32[]{:S(2)}, u32[]{:S(2)}) %collective-permute-start.11) | collective-permute-done | bytes 71712 | tf_op jit(solution)/shard_map/ppermute | solution.py:113
  69.8 0.7 collective-permute-done.15.refs_11_
  71.7 4.0 %shard_map.82 = (bf16[1,56,448]{2,1,0:T(8,128)(2,1)}, f32[1,56,128]{2,1,0:T(8,128)}) custom-call(bf16[448,640]{1,0:T(8,128)(2,1)} %get-tuple-element.17.refs_0_, bf16[448,448]{1,0:T(8,128)(2,1)} %get-tuple-element.18.refs_1_, f32[56,448]{1,0:T(8,128)} %get-tuple-element.19.refs_2_, s32[1,128]{1,0:T(1,128)} %refs_3_.1, bf16[80,448]{1,0:T(8,128)(2,1)} %copy-done.1, ...), custom_call_target="tpu_custom_call" | custom-call | tf_op jit(solution)/shard_map/pallas_call | solution.py:85
  (48 shorter events, 4.3 us)
Async XLA Ops:
  21.5 26.2 %collective-permute-start.5 = (bf16[3,80,1152]{2,1,0:T(8,128)(2,1)}, bf16[3,80,1152]{2,1,0:T(8,128)(2,1)S(1)}, u32[]{:S(2)}, u32[]{:S(2)}) collective-permute-start(bf16[3,80,1152]{2,1,0:T(8,128)(2,1)} %get-tuple-element.25), channel_id=1, source_target_pairs={{0,2},{2,0},{1,3},{3,1},{4,6},{6,4},{5,7},{7,5},{8,10},{10,8},{9,1... | collective-permute-start | bytes 1658888 | tf_op jit(solution)/shard_map/ppermute | solution.py:90
  22.0 7.8 %collective-permute-start.2 = (bf16[80,1152]{1,0:T(8,128)(2,1)}, bf16[80,1152]{1,0:T(8,128)(2,1)S(1)}, u32[]{:S(2)}, u32[]{:S(2)}) collective-permute-start(bf16[80,1152]{1,0:T(8,128)(2,1)} %get-tuple-element.22.refs_2_), channel_id=1, source_target_pairs={{0,8},{2,10},{8,12},{10,14},{12,4},{14,6},{4,0},{6,2},{1,9},{3,11}... | collective-permute-start | bytes 552968 | tf_op jit(solution)/shard_map/ppermute | solution.py:106
  22.5 11.4 %collective-permute-start = (bf16[80,1152]{1,0:T(8,128)(2,1)}, bf16[80,1152]{1,0:T(8,128)(2,1)S(1)}, u32[]{:S(2)}, u32[]{:S(2)}) collective-permute-start(bf16[80,1152]{1,0:T(8,128)(2,1)} %get-tuple-element.16), channel_id=1, source_target_pairs={{0,10},{2,8},{8,14},{10,12},{12,6},{14,4},{4,2},{6,0},{1,11},{3,9}... | collective-permute-start | bytes 552968 | tf_op jit(solution)/shard_map/ppermute | solution.py:106
  29.8 17.8 %copy-start.2 = (bf16[80,1152]{1,0:T(8,128)(2,1)}, bf16[80,1152]{1,0:T(8,128)(2,1)S(1)}, u32[]{:S(2)}) copy-start(bf16[80,1152]{1,0:T(8,128)(2,1)S(1)} %collective-permute-done.2.refs_4_) | copy-start | bytes 552964
  29.8 10.2 %collective-permute-start.3 = (bf16[80,1152]{1,0:T(8,128)(2,1)S(1)}, bf16[80,1152]{1,0:T(8,128)(2,1)S(1)}, u32[]{:S(2)}, u32[]{:S(2)}) collective-permute-start(bf16[80,1152]{1,0:T(8,128)(2,1)S(1)} %collective-permute-done.2.refs_4_), channel_id=1, source_target_pairs={{0,8},{8,12},{12,4},{4,0},{1,9},{9,13},{13,5},{5,1},{2,10},{10,14}... | collective-permute-start | bytes 552968 | tf_op jit(solution)/shard_map/ppermute | solution.py:103
  37.8 6.5 %collective-permute-start.4 = (bf16[80,1152]{1,0:T(8,128)(2,1)}, bf16[80,1152]{1,0:T(8,128)(2,1)S(1)}, u32[]{:S(2)}, u32[]{:S(2)}) collective-permute-start(bf16[80,1152]{1,0:T(8,128)(2,1)} %get-tuple-element.23.refs_5_), channel_id=1, source_target_pairs={{0,8},{8,12},{12,4},{4,0},{1,9},{9,13},{13,5},{5,1},{2,10},{10,14}... | collective-permute-start | bytes 552968 | tf_op jit(solution)/shard_map/ppermute | solution.py:103
  39.6 8.1 %collective-permute-start.1 = (bf16[80,1152]{1,0:T(8,128)(2,1)}, bf16[80,1152]{1,0:T(8,128)(2,1)S(1)}, u32[]{:S(2)}, u32[]{:S(2)}) collective-permute-start(bf16[80,1152]{1,0:T(8,128)(2,1)} %get-tuple-element.16), channel_id=1, source_target_pairs={{0,2},{2,0},{1,3},{3,1},{4,6},{6,4},{5,7},{7,5},{8,10},{10,8},{9,1... | collective-permute-start | bytes 552968 | tf_op jit(solution)/shard_map/ppermute | solution.py:90
  40.0 7.6 %copy-start.3 = (bf16[80,1152]{1,0:T(8,128)(2,1)}, bf16[80,1152]{1,0:T(8,128)(2,1)S(1)}, u32[]{:S(2)}) copy-start(bf16[80,1152]{1,0:T(8,128)(2,1)S(1)} %collective-permute-done.3.refs_6_) | copy-start | bytes 552964
  40.0 12.2 %collective-permute-start.6 = (bf16[80,1152]{1,0:T(8,128)(2,1)S(1)}, bf16[80,1152]{1,0:T(8,128)(2,1)S(1)}, u32[]{:S(2)}, u32[]{:S(2)}) collective-permute-start(bf16[80,1152]{1,0:T(8,128)(2,1)S(1)} %collective-permute-done.3.refs_6_), channel_id=1, source_target_pairs={{0,8},{8,12},{12,4},{4,0},{1,9},{9,13},{13,5},{5,1},{2,10},{10,14}... | collective-permute-start | bytes 552968 | tf_op jit(solution)/shard_map/ppermute | solution.py:103
  44.3 3.3 %copy-start.4 = (bf16[80,1152]{1,0:T(8,128)(2,1)}, bf16[80,1152]{1,0:T(8,128)(2,1)S(1)}, u32[]{:S(2)}) copy-start(bf16[80,1152]{1,0:T(8,128)(2,1)S(1)} %collective-permute-done.4.refs_7_) | copy-start | bytes 552964
  44.4 7.8 %collective-permute-start.7 = (bf16[80,1152]{1,0:T(8,128)(2,1)S(1)}, bf16[80,1152]{1,0:T(8,128)(2,1)S(1)}, u32[]{:S(2)}, u32[]{:S(2)}) collective-permute-start(bf16[80,1152]{1,0:T(8,128)(2,1)S(1)} %collective-permute-done.4.refs_7_), channel_id=1, source_target_pairs={{0,8},{8,12},{12,4},{4,0},{1,9},{9,13},{13,5},{5,1},{2,10},{10,14}... | collective-permute-start | bytes 552968 | tf_op jit(solution)/shard_map/ppermute | solution.py:103
  56.9 1.6 %collective-permute-start.8 = (f32[80,448]{1,0:T(8,128)}, f32[80,448]{1,0:T(8,128)S(1)}, u32[]{:S(2)}, u32[]{:S(2)}) collective-permute-start(f32[80,448]{1,0:T(8,128)} %get-tuple-element.27), channel_id=1, source_target_pairs={{0,1},{1,0},{2,3},{3,2},{4,5},{5,4},{6,7},{7,6},{8,9},{9,8},{10,11... | collective-permute-start | bytes 430088 | tf_op jit(solution)/shard_map/ppermute | solution.py:90
  59.5 11.6 %copy-start.1 = (bf16[80,448]{1,0:T(8,128)(2,1)}, bf16[80,448]{1,0:T(8,128)(2,1)S(1)}, u32[]{:S(2)}) copy-start(bf16[80,448]{1,0:T(8,128)(2,1)S(1)} %add_convert_fusion.refs_4_) | copy-start | bytes 215044
  59.5 9.8 %collective-permute-start.11 = (bf16[80,448]{1,0:T(8,128)(2,1)S(1)}, bf16[80,448]{1,0:T(8,128)(2,1)S(1)}, u32[]{:S(2)}, u32[]{:S(2)}) collective-permute-start(bf16[80,448]{1,0:T(8,128)(2,1)S(1)} %add_convert_fusion.refs_4_), channel_id=1, source_target_pairs={{0,4},{8,0},{12,8},{4,12},{1,5},{9,1},{13,9},{5,13},{2,6},{10,2},{... | collective-permute-start | bytes 215048 | tf_op jit(solution)/shard_map/ppermute | solution.py:113
  60.0 9.2 %collective-permute-start.10 = (bf16[80,448]{1,0:T(8,128)(2,1)S(1)}, bf16[80,448]{1,0:T(8,128)(2,1)S(1)}, u32[]{:S(2)}, u32[]{:S(2)}) collective-permute-start(bf16[80,448]{1,0:T(8,128)(2,1)S(1)} %add_convert_fusion.refs_4_), channel_id=1, source_target_pairs={{0,12},{8,4},{12,0},{4,8},{1,13},{9,5},{13,1},{5,9},{2,14},{10,6},... | collective-permute-start | bytes 215048 | tf_op jit(solution)/shard_map/ppermute | solution.py:113
  62.2 7.6 %collective-permute-start.9 = (bf16[80,448]{1,0:T(8,128)(2,1)S(1)}, bf16[80,448]{1,0:T(8,128)(2,1)S(1)}, u32[]{:S(2)}, u32[]{:S(2)}) collective-permute-start(bf16[80,448]{1,0:T(8,128)(2,1)S(1)} %add_convert_fusion.refs_4_), channel_id=1, source_target_pairs={{0,8},{8,12},{12,4},{4,0},{1,9},{9,13},{13,5},{5,1},{2,10},{10,14}... | collective-permute-start | bytes 215048 | tf_op jit(solution)/shard_map/ppermute | solution.py:113
  63.2 6.6 %collective-permute-start.12 = (bf16[80,448]{1,0:T(8,128)(2,1)S(1)}, bf16[80,448]{1,0:T(8,128)(2,1)S(1)}, u32[]{:S(2)}, u32[]{:S(2)}) collective-permute-start(bf16[80,448]{1,0:T(8,128)(2,1)S(1)} %add_convert_fusion.refs_4_), channel_id=1, source_target_pairs={{0,1},{1,0},{2,3},{3,2},{4,5},{5,4},{6,7},{7,6},{8,9},{9,8},{10,11... | collective-permute-start | bytes 215048 | tf_op jit(solution)/shard_map/ppermute | solution.py:90
  69.2 1.8 %copy-start.9 = (bf16[80,448]{1,0:T(8,128)(2,1)}, bf16[80,448]{1,0:T(8,128)(2,1)S(1)}, u32[]{:S(2)}) copy-start(bf16[80,448]{1,0:T(8,128)(2,1)S(1)} %collective-permute-done.11.refs_7_) | copy-start | bytes 215044
  69.2 1.3 %collective-permute-start.15 = (bf16[80,448]{1,0:T(8,128)(2,1)S(1)}, bf16[80,448]{1,0:T(8,128)(2,1)S(1)}, u32[]{:S(2)}, u32[]{:S(2)}) collective-permute-start(bf16[80,448]{1,0:T(8,128)(2,1)S(1)} %collective-permute-done.11.refs_7_), channel_id=1, source_target_pairs={{0,1},{1,0},{2,3},{3,2},{4,5},{5,4},{6,7},{7,6},{8,9},{9,8},{10,11... | collective-permute-start | bytes 215048 | tf_op jit(solution)/shard_map/ppermute | solution.py:90
  69.2 1.8 %copy-start.10 = (bf16[80,448]{1,0:T(8,128)(2,1)}, bf16[80,448]{1,0:T(8,128)(2,1)S(1)}, u32[]{:S(2)}) copy-start(bf16[80,448]{1,0:T(8,128)(2,1)S(1)} %collective-permute-done.10.refs_6_) | copy-start | bytes 215044
  69.2 1.4 %collective-permute-start.14 = (bf16[80,448]{1,0:T(8,128)(2,1)S(1)}, bf16[80,448]{1,0:T(8,128)(2,1)S(1)}, u32[]{:S(2)}, u32[]{:S(2)}) collective-permute-start(bf16[80,448]{1,0:T(8,128)(2,1)S(1)} %collective-permute-done.10.refs_6_), channel_id=1, source_target_pairs={{0,1},{1,0},{2,3},{3,2},{4,5},{5,4},{6,7},{7,6},{8,9},{9,8},{10,11... | collective-permute-start | bytes 215048 | tf_op jit(solution)/shard_map/ppermute | solution.py:90
  69.7 1.3 %copy-start.11 = (bf16[80,448]{1,0:T(8,128)(2,1)}, bf16[80,448]{1,0:T(8,128)(2,1)S(1)}, u32[]{:S(2)}) copy-start(bf16[80,448]{1,0:T(8,128)(2,1)S(1)} %collective-permute-done.9.refs_5_) | copy-start | bytes 215044
  69.8 1.3 %collective-permute-start.13 = (bf16[80,448]{1,0:T(8,128)(2,1)S(1)}, bf16[80,448]{1,0:T(8,128)(2,1)S(1)}, u32[]{:S(2)}, u32[]{:S(2)}) collective-permute-start(bf16[80,448]{1,0:T(8,128)(2,1)S(1)} %collective-permute-done.9.refs_5_), channel_id=1, source_target_pairs={{0,1},{1,0},{2,3},{3,2},{4,5},{5,4},{6,7},{7,6},{8,9},{9,8},{10,11... | collective-permute-start | bytes 215048 | tf_op jit(solution)/shard_map/ppermute | solution.py:90
  69.8 1.2 %copy-start.12 = (bf16[80,448]{1,0:T(8,128)(2,1)}, bf16[80,448]{1,0:T(8,128)(2,1)S(1)}, u32[]{:S(2)}) copy-start(bf16[80,448]{1,0:T(8,128)(2,1)S(1)} %collective-permute-done.12.refs_8_) | copy-start | bytes 215044
  (8 other events, 5.5 us)

commit v4 on v3

--- a/solution.py
+++ b/solution.py
@@ -18,10 +18,6 @@
     return lax.dot_general(a, b, dims, preferred_element_type=F32)
 
 
-def dot_exact(a, b):
-    return lax.dot_general(a, b, NN, precision=lax.Precision.HIGHEST, preferred_element_type=F32)
-
-
 def iota(shape, dim):
     return lax.broadcasted_iota(jnp.int32, shape, dim).astype(F32)
 
@@ -30,7 +26,7 @@
     return jnp.floor((x + 0.5) * (1.0 / n))
 
 
-def on_core(fn, args, outs, kernel=True, through=(), streams=(), cost=None):
+def on_core(fn, args, outs, kernel=True, through=(), streams=(), cost=None, room=24):
     if not kernel:
         loads = [lambda i, x=x: x[i] for x in streams]
         return list(fn(*args, *loads)) + list(through)
@@ -75,11 +71,13 @@
     call = pl.pallas_call(
         body,
         out_shape=list(outs) + [jax.ShapeDtypeStruct(x.shape, x.dtype) for x in through],
-        in_specs=[in_vmem] * count + [anywhere] * (streamed + passed),
+        in_specs=[in_vmem] * count
+        + [pl.BlockSpec(memory_space=pltpu.HBM)] * streamed
+        + [anywhere] * passed,
         out_specs=[in_vmem] * len(outs) + [anywhere] * passed,
         scratch_shapes=scratch,
         input_output_aliases={count + streamed + i: len(outs) + i for i in range(passed)},
-        compiler_params=pltpu.CompilerParams(vmem_limit_bytes=56 * 1024 * 1024),
+        compiler_params=pltpu.CompilerParams(vmem_limit_bytes=room * 1024 * 1024),
         cost_estimate=estimate,
     )
     return list(call(*args, *streams, *through))
@@ -147,12 +145,16 @@
         return feat.astype(F32), pos.astype(F32), lax.axis_index("rep").astype(F32)
 
     def pack(ids, vals):
-        one = jnp.concatenate([ids[0].astype(F32), vals[0]], axis=0)
+        one = jnp.concatenate([ids(0).astype(F32), vals(0)], axis=0)
         one = jnp.concatenate([one, jnp.zeros((2 * positions, LANES - kslots), F32)], axis=1)
         return (jnp.broadcast_to(one, (holders,) + one.shape),)
 
     (packed,) = on_core(
-        pack, [active_ids, active_vals], [shape(holders, 2 * positions, LANES)]
+        pack,
+        [],
+        [shape(holders, 2 * positions, LANES)],
+        streams=[active_ids, active_vals],
+        room=60,
     )
     lists = lax.all_to_all(packed, ("feat", "pos"), split_axis=0, concat_axis=0, tiled=True)
 
@@ -172,18 +174,28 @@
     def slot_entry(slot):
         return slot - floor_div(slot, kslots) * kslots
 
+    def pieces(table):
+        high = part(table, small)
+        rest = table - high.astype(F32)
+        middle = part(rest, small)
+        return [high, middle, part(rest - middle.astype(F32), small)]
+
     def as_rows(table):
-        spread = (iota((kslots, slots), 0) == slot_entry(iota((kslots, slots), 1))).astype(F32)
-        wide = dot_exact(table, spread)
+        spread = (iota((kslots, slots), 0) == slot_entry(iota((kslots, slots), 1))).astype(BF16)
+        wide = dot(jnp.concatenate(pieces(table), axis=0), spread)
+        count = table.shape[0]
+        wide = wide[:count] + (wide[count : 2 * count] + wide[2 * count :])
         row = iota(wide.shape, 0) - list_row(iota(wide.shape, 1))
         ids = jnp.sum(jnp.where(row == 0, wide, 0.0), axis=0, keepdims=True)
         return ids, jnp.sum(jnp.where(row == positions, wide, 0.0), axis=0, keepdims=True)
 
     def as_col(table):
         wide = (slots, table.shape[0])
-        spread = (list_row(iota(wide, 0)) == iota(wide, 1)).astype(F32)
+        spread = (list_row(iota(wide, 0)) == iota(wide, 1)).astype(BF16)
+        every = dot(spread, jnp.concatenate(pieces(table), axis=1))
+        every = every[:, :kslots] + (every[:, kslots : 2 * kslots] + every[:, 2 * kslots :])
         mine = slot_entry(iota((slots, kslots), 0)) == iota((slots, kslots), 1)
-        return jnp.sum(jnp.where(mine, dot_exact(spread, table), 0.0), axis=1, keepdims=True)
+        return jnp.sum(jnp.where(mine, every, 0.0), axis=1, keepdims=True)
 
     def choose(values, enc, dec):
         feat, pos, _ = place()
@@ -230,6 +242,7 @@
         outs + [shape(2 * positions * feats, kslots)],
         small,
         streams=[encoder[None], jnp.transpose(decoder, (1, 0, 2))],
+        room=60,
     )
     enc_rows, dec_rows = chosen[::2], chosen[1::2]
 
@@ -281,7 +294,7 @@
         own_mask = jnp.where(own_causal, own_mask, 0.0)
         return placing.astype(BF16), placing_t.astype(BF16), layer_row, mask.astype(BF16), own_mask
 
-    placing, placing_t, layer_row, mask, own_mask, *ring[1][-1:] = on_core(
+    placing, placing_t, layer_row, mask, own_mask, *ring[1][:1] = on_core(
         places,
         [my_list, block_pattern],
         [
@@ -292,7 +305,7 @@
             shape(result_rows, slots),
         ],
         small,
-        through=ring[1][-1:],
+        through=ring[1][:1],
         cost=(4 * slots * slots * slots, 4 * slots * slots),
     )
     for _ in range(2, feats):
@@ -308,12 +321,8 @@
         for l in range(depth):
             rows = every[l * column : (l + 1) * column]
             raw = raw + jnp.where(layer_row[:, lanes] == l + 1.0, rows, 0.0)
-        high = part(raw, small)
-        rest = raw - high.astype(F32)
-        middle = part(rest, small)
-        low = part(rest - middle.astype(F32), small)
-        split = dot(jnp.concatenate([high, middle, low], axis=0), placing_t[lanes])
-        return split[:column] + split[column : 2 * column] + split[2 * column :]
+        split = dot(jnp.concatenate(pieces(raw), axis=0), placing_t[lanes])
+        return split[:column] + (split[column : 2 * column] + split[2 * column :])
 
     def early(*values):
         return (products(0, feats - 1, *values),)

time: 76.1 us -> 65.3 us (0.86)
  Pallas kernels: 21 us -> 12.9 us
  waiting for transfers between devices: 21.4 us -> 19.8 us
  other arithmetic: 0.94 us -> 0.02 us
  local copies, waits for them, and re-layouts: 3.51 us -> 2.7 us
    pallas_call x6, Pallas kernels: 21 us -> 12.9 us  [on_core(): return list(call(*args, *streams, *through))]
    ppermute x7, starting transfers between devices: 1.61 us -> 0.63 us  [rotate(): lax.ppermute(x, axis, [(i, (i + step) % count) for i in range(count)])]
    ppermute x3, starting transfers between devices: 3.72 us -> 4.7 us  [ring_spread(): lax.ppermute(x, axis, [(order[i], order[(i + k) % count]) for i in range(...]
    ppermute x4, waiting for transfers between devices: 4.08 us -> 3.16 us  [ring_next(): return lax.ppermute(x, axis, steps)]
    convert_element_type x1, other arithmetic: 0.94 us -> 0.02 us  [per_device(): own_edges = (keep + rotate(send, 'rep', 1)).astype(BF16)]
    unnamed x32 -> x10, local copies, waits for them, and re-layouts: 3.51 us -> 2.7 us
  transfers between devices with their start and end apart: 16 -> 16, of which waited for: 8 -> 10; matrix products, arithmetic and copies ran while one was open for 0% -> 0% of each run, Pallas kernels for 9% -> 4%
where the time goes in v4:
time: 65.3 us; the launch traced here: 64.9 us
  waiting for transfers between devices  19.8 us (30%)
  starting transfers between devices  14.7 us (23%)
  blocking collectives  14.1 us (22%)
  Pallas kernels  12.9 us (20%)
  local copies, waits for them, and re-layouts  2.7 us (4%)
  between operations  0.72 us (1%)
    all_to_all x1, blocking collectives, per_device(): lax.all_to_all(packed, ('feat', 'pos'), split_axis=0, concat_axis=0, tile...  14.1 us
    pallas_call x6, Pallas kernels, on_core(): return list(call(*args, *streams, *through))  12.9 us
    ppermute x2, waiting for transfers between devices, ring_next(): return lax.ppermute(x, (axis, across), pairs)  8.33 us
    ppermute x4, starting transfers between devices, ring_next(): return lax.ppermute(x, axis, steps)  7.25 us
    ppermute x3, waiting for transfers between devices, ring_spread(): lax.ppermute(x, axis, [(order[i], order[(i + k) % count]) for i in range(...  5.65 us
    ppermute x3, starting transfers between devices, ring_spread(): lax.ppermute(x, axis, [(order[i], order[(i + k) % count]) for i in range(...  4.7 us
    ppermute x4, waiting for transfers between devices, ring_next(): return lax.ppermute(x, axis, steps)  3.16 us
    unnamed x10, local copies, waits for them, and re-layouts  2.7 us
  transfers between devices with their start and end apart: 16, of which 10 were waited for; matrix products, arithmetic and copies ran while one was open for 0% of the time, Pallas kernels for 4%

profile of v4, /device:TPU:0, one launch (start us, length us, event | category | flops | bytes accessed | tf_op | source)
XLA Modules:
  0.0 64.9 jit_solution(7771525129907927561)
XLA Ops:
  0.6 1.3 %shard_map.77 = f32[8,8,128]{2,1,0:T(8,128)} custom-call(s32[1,4,28]{2,1,0:T(4,128)} %refs_0_.1, f32[1,4,28]{2,1,0:T(4,128)} %refs_1_.2), custom_call_target="tpu_custom_call" | custom-call | tf_op jit(solution)/shard_map/pallas_call | solution.py:83
  2.0 14.1 %all_to_all.5.refs_0_ = f32[8,8,128]{2,1,0:T(8,128)} all-to-all(f32[8,8,128]{2,1,0:T(8,128)} %shard_map.77), channel_id=1, replica_groups=mesh['grp'=2,'feat'=4,'pos'=2,'rep'=2] {'feat','pos'}, dimensions={0} | all-to-all | bytes 65536 | tf_op jit(solution)/shard_map/all_to_all | solution.py:159
  16.0 5.5 %shard_map.78 = (bf16[80,1152]{1,0:T(8,128)(2,1)}, bf16[3,80,1152]{2,1,0:T(8,128)(2,1)}, bf16[80,1152]{1,0:T(8,128)(2,1)}, bf16[3,80,1152]{2,1,0:T(8,128)(2,1)}, f32[32,28]{1,0:T(8,128)}) custom-call(f32[8,8,128]{2,1,0:T(8,128)} %all_to_all.5.refs_0_, bf16[1,512,1152]{2,1,0:T(8,128)(2,1)} %bitcast.3, bf16[3,512,1152]{2,1,0:T(8,128)(2,1)} %bitcast.2), custom_call_target="tpu_custom_call" | custom-call | tf_op jit(solution)/shard_map/pallas_call | solution.py:83
  22.1 1.5 %collective-permute-start.2 = (bf16[80,1152]{1,0:T(8,128)(2,1)}, bf16[80,1152]{1,0:T(8,128)(2,1)S(1)}, u32[]{:S(2)}, u32[]{:S(2)}) collective-permute-start(bf16[80,1152]{1,0:T(8,128)(2,1)} %get-tuple-element.22), channel_id=1, source_target_pairs={{0,10},{2,8},{8,14},{10,12},{12,6},{14,4},{4,2},{6,0},{1,11},{3,9}... | collective-permute-start | bytes 552968 | tf_op jit(solution)/shard_map/ppermute | solution.py:104
  24.2 6.1 %collective-permute-done.2.refs_5_ = bf16[80,1152]{1,0:T(8,128)(2,1)S(1)} collective-permute-done((bf16[80,1152]{1,0:T(8,128)(2,1)}, bf16[80,1152]{1,0:T(8,128)(2,1)S(1)}, u32[]{:S(2)}, u32[]{:S(2)}) %collective-permute-start.2) | collective-permute-done | bytes 184352 | tf_op jit(solution)/shard_map/ppermute | solution.py:104
  30.3 1.4 %collective-permute-start.4 = (bf16[80,1152]{1,0:T(8,128)(2,1)S(1)}, bf16[80,1152]{1,0:T(8,128)(2,1)S(1)}, u32[]{:S(2)}, u32[]{:S(2)}) collective-permute-start(bf16[80,1152]{1,0:T(8,128)(2,1)S(1)} %collective-permute-done.2.refs_5_), channel_id=1, source_target_pairs={{0,8},{8,12},{12,4},{4,0},{1,9},{9,13},{13,5},{5,1},{2,10},{10,14}... | collective-permute-start | bytes 552968 | tf_op jit(solution)/shard_map/ppermute | solution.py:101
  31.7 2.2 %collective-permute-done.refs_2_ = bf16[80,1152]{1,0:T(8,128)(2,1)S(1)} collective-permute-done((bf16[80,1152]{1,0:T(8,128)(2,1)}, bf16[80,1152]{1,0:T(8,128)(2,1)S(1)}, u32[]{:S(2)}, u32[]{:S(2)}) %collective-permute-start) | collective-permute-done | bytes 184352 | tf_op jit(solution)/shard_map/ppermute | solution.py:104
  34.0 0.7 %copy-done.3 = f32[32,28]{1,0:T(8,128)S(1)} copy-done((f32[32,28]{1,0:T(8,128)S(1)}, f32[32,28]{1,0:T(8,128)}, u32[]{:S(2)}) %copy-start.3) | copy-done | bytes 3608
  34.7 1.4 %shard_map.79 = (bf16[448,640]{1,0:T(8,128)(2,1)S(1)}, bf16[640,448]{1,0:T(8,128)(2,1)S(1)}, f32[1,640]{1,0:T(1,128)S(1)}, bf16[448,448]{1,0:T(8,128)(2,1)S(1)},...) custom-call(f32[32,28]{1,0:T(8,128)S(1)} %copy-done.3, ...), custom_call_target="tpu_custom_call", output_to_operand_aliasing={{5}: (2, {})} | custom-call | flops 359661568 | bytes 802816 | tf_op jit(solution)/shard_map/pallas_call | solution.py:83
  36.0 1.8 %collective-permute-start.3 = (bf16[80,1152]{1,0:T(8,128)(2,1)S(1)}, bf16[80,1152]{1,0:T(8,128)(2,1)S(1)}, u32[]{:S(2)}, u32[]{:S(2)}) collective-permute-start(bf16[80,1152]{1,0:T(8,128)(2,1)S(1)} %get-tuple-element.23.refs_4_), channel_id=1, source_target_pairs={{0,8},{8,12},{12,4},{4,0},{1,9},{9,13},{13,5},{5,1},{2,10},{10,14}... | collective-permute-start | bytes 552968 | tf_op jit(solution)/shard_map/ppermute | solution.py:101
  37.8 1.8 %collective-permute-start.7 = (bf16[80,1152]{1,0:T(8,128)(2,1)S(1)}, bf16[80,1152]{1,0:T(8,128)(2,1)S(1)}, u32[]{:S(2)}, u32[]{:S(2)}) collective-permute-start(bf16[80,1152]{1,0:T(8,128)(2,1)S(1)} %collective-permute-done.4.refs_7_), channel_id=1, source_target_pairs={{0,8},{8,12},{12,4},{4,0},{1,9},{9,13},{13,5},{5,1},{2,10},{10,14}... | collective-permute-start | bytes 552968 | tf_op jit(solution)/shard_map/ppermute | solution.py:101
  39.6 3.1 %collective-permute-done.3.refs_6_ = bf16[80,1152]{1,0:T(8,128)(2,1)S(1)} collective-permute-done((bf16[80,1152]{1,0:T(8,128)(2,1)S(1)}, bf16[80,1152]{1,0:T(8,128)(2,1)S(1)}, u32[]{:S(2)}, u32[]{:S(2)}) %collective-permute-start.3) | collective-permute-done | bytes 184352 | tf_op jit(solution)/shard_map/ppermute | solution.py:101
  42.7 2.3 %collective-permute-start.6 = (bf16[80,1152]{1,0:T(8,128)(2,1)S(1)}, bf16[80,1152]{1,0:T(8,128)(2,1)S(1)}, u32[]{:S(2)}, u32[]{:S(2)}) collective-permute-start(bf16[80,1152]{1,0:T(8,128)(2,1)S(1)} %collective-permute-done.3.refs_6_), channel_id=1, source_target_pairs={{0,8},{8,12},{12,4},{4,0},{1,9},{9,13},{13,5},{5,1},{2,10},{10,14}... | collective-permute-start | bytes 552968 | tf_op jit(solution)/shard_map/ppermute | solution.py:101
  45.0 1.0 %copy-done = bf16[3,80,1152]{2,1,0:T(8,128)(2,1)S(1)} copy-done((bf16[3,80,1152]{2,1,0:T(8,128)(2,1)S(1)}, bf16[3,80,1152]{2,1,0:T(8,128)(2,1)}, u32[]{:S(2)}) %copy-start) | copy-done | bytes 552984
  46.1 0.9 %copy-done.1 = bf16[80,1152]{1,0:T(8,128)(2,1)S(1)} copy-done((bf16[80,1152]{1,0:T(8,128)(2,1)S(1)}, bf16[80,1152]{1,0:T(8,128)(2,1)}, u32[]{:S(2)}) %copy-start.1) | copy-done | bytes 184344
  47.0 1.2 %shard_map.80.refs_0_ = f32[160,448]{1,0:T(8,128)S(1)} custom-call(f32[1,640]{1,0:T(1,128)S(1)} %get-tuple-element.20.refs_0_.refs_1_, bf16[640,448]{1,0:T(8,128)(2,1)S(1)} %get-tuple-element.21.refs_1_.refs_2_, bf16[80,1152]{1,0:T(8,128)(2,1)S(1)} %copy-done.1, bf16[80,1152]{1,0:T(8,128)(2,1)S(1)} %collective-permute-done.1.refs_3_, ...), custom_call_target="tpu_custom_call" | custom-call | flops 660602880 | bytes 1474560 | tf_op jit(solution)/shard_map/pallas_call | solution.py:83
  48.3 0.9 %shard_map.81 = (f32[80,448]{1,0:T(8,128)S(1)}, f32[80,448]{1,0:T(8,128)S(1)}) custom-call(f32[160,448]{1,0:T(8,128)S(1)} %shard_map.80.refs_0_, f32[1,640]{1,0:T(1,128)S(1)} %get-tuple-element.20.refs_0_.refs_1_, bf16[640,448]{1,0:T(8,128)(2,1)S(1)} %get-tuple-element.21.refs_1_.refs_2_, bf16[80,1152]{1,0:T(8,128)(2,1)S(1)} %collective-permute-done.6.refs_3_, ...), custom_call_target="tpu_custom_call" | custom-call | tf_op jit(solution)/shard_map/pallas_call | solution.py:83
  49.3 1.4 %collective-permute-done.8 = f32[80,448]{1,0:T(8,128)S(1)} collective-permute-done((f32[80,448]{1,0:T(8,128)S(1)}, f32[80,448]{1,0:T(8,128)S(1)}, u32[]{:S(2)}, u32[]{:S(2)}) %collective-permute-start.8) | collective-permute-done | bytes 143392 | tf_op jit(solution)/shard_map/ppermute | solution.py:88
  50.7 2.5 %collective-permute-start.11 = (bf16[80,448]{1,0:T(8,128)(2,1)S(1)}, bf16[80,448]{1,0:T(8,128)(2,1)S(1)}, u32[]{:S(2)}, u32[]{:S(2)}) collective-permute-start(bf16[80,448]{1,0:T(8,128)(2,1)S(1)} %add_convert_fusion.refs_4_), channel_id=1, source_target_pairs={{0,4},{8,0},{12,8},{4,12},{1,5},{9,1},{13,9},{5,13},{2,6},{10,2},{... | collective-permute-start | bytes 215048 | tf_op jit(solution)/shard_map/ppermute | solution.py:111
  53.2 2.2 %collective-permute-start.10 = (bf16[80,448]{1,0:T(8,128)(2,1)S(1)}, bf16[80,448]{1,0:T(8,128)(2,1)S(1)}, u32[]{:S(2)}, u32[]{:S(2)}) collective-permute-start(bf16[80,448]{1,0:T(8,128)(2,1)S(1)} %add_convert_fusion.refs_4_), channel_id=1, source_target_pairs={{0,12},{8,4},{12,0},{4,8},{1,13},{9,5},{13,1},{5,9},{2,14},{10,6},... | collective-permute-start | bytes 215048 | tf_op jit(solution)/shard_map/ppermute | solution.py:111
  55.4 1.8 %collective-permute-done.11.refs_7_ = bf16[80,448]{1,0:T(8,128)(2,1)S(1)} collective-permute-done((bf16[80,448]{1,0:T(8,128)(2,1)S(1)}, bf16[80,448]{1,0:T(8,128)(2,1)S(1)}, u32[]{:S(2)}, u32[]{:S(2)}) %collective-permute-start.11) | collective-permute-done | bytes 71712 | tf_op jit(solution)/shard_map/ppermute | solution.py:111
  57.2 3.2 %collective-permute-done.10.refs_6_ = bf16[80,448]{1,0:T(8,128)(2,1)S(1)} collective-permute-done((bf16[80,448]{1,0:T(8,128)(2,1)S(1)}, bf16[80,448]{1,0:T(8,128)(2,1)S(1)}, u32[]{:S(2)}, u32[]{:S(2)}) %collective-permute-start.10) | collective-permute-done | bytes 71712 | tf_op jit(solution)/shard_map/ppermute | solution.py:111
  61.6 0.7 %collective-permute-done.13.refs_9_ = bf16[80,448]{1,0:T(8,128)(2,1)S(1)} collective-permute-done((bf16[80,448]{1,0:T(8,128)(2,1)S(1)}, bf16[80,448]{1,0:T(8,128)(2,1)S(1)}, u32[]{:S(2)}, u32[]{:S(2)}) %collective-permute-start.13) | collective-permute-done | bytes 71712 | tf_op jit(solution)/shard_map/ppermute | solution.py:88
  62.3 2.5 %shard_map.82 = (bf16[1,56,448]{2,1,0:T(8,128)(2,1)}, f32[1,56,128]{2,1,0:T(8,128)}) custom-call(bf16[448,640]{1,0:T(8,128)(2,1)S(1)} %get-tuple-element.17.refs_0_, bf16[448,448]{1,0:T(8,128)(2,1)S(1)} %get-tuple-element.18.refs_1_, f32[56,448]{1,0:T(8,128)S(1)} %get-tuple-element.19.refs_2_, s32[1,128]{1,0:T(1,128)S(1)} %copy-done.2, ...), custom_call_target="tpu_custom_call" | custom-call | tf_op jit(solution)/shard_map/pallas_call | solution.py:83
  (26 shorter events, 2.6 us)
Async XLA Ops:
  0.6 33.3 %copy-start.4 = (s32[1,4,4]{2,1,0:T(4,128)S(1)}, s32[1,4,4]{2,1,0:T(4,128)}, u32[]{:S(2)}) copy-start(s32[1,4,4]{2,1,0:T(4,128)} %refs_1_.3) | copy-start | bytes 196
  21.6 23.4 %collective-permute-start.5 = (bf16[3,80,1152]{2,1,0:T(8,128)(2,1)}, bf16[3,80,1152]{2,1,0:T(8,128)(2,1)S(1)}, u32[]{:S(2)}, u32[]{:S(2)}) collective-permute-start(bf16[3,80,1152]{2,1,0:T(8,128)(2,1)} %get-tuple-element.25), channel_id=1, source_target_pairs={{0,2},{2,0},{1,3},{3,1},{4,6},{6,4},{5,7},{7,5},{8,10},{10,8},{9,1... | collective-permute-start | bytes 1658888 | tf_op jit(solution)/shard_map/ppermute | solution.py:88
  22.1 8.2 %collective-permute-start.2 = (bf16[80,1152]{1,0:T(8,128)(2,1)}, bf16[80,1152]{1,0:T(8,128)(2,1)S(1)}, u32[]{:S(2)}, u32[]{:S(2)}) collective-permute-start(bf16[80,1152]{1,0:T(8,128)(2,1)} %get-tuple-element.22), channel_id=1, source_target_pairs={{0,10},{2,8},{8,14},{10,12},{12,6},{14,4},{4,2},{6,0},{1,11},{3,9}... | collective-permute-start | bytes 552968 | tf_op jit(solution)/shard_map/ppermute | solution.py:104
  23.6 10.3 %collective-permute-start = (bf16[80,1152]{1,0:T(8,128)(2,1)}, bf16[80,1152]{1,0:T(8,128)(2,1)S(1)}, u32[]{:S(2)}, u32[]{:S(2)}) collective-permute-start(bf16[80,1152]{1,0:T(8,128)(2,1)} %get-tuple-element.16.refs_2_), channel_id=1, source_target_pairs={{0,8},{2,10},{8,12},{10,14},{12,4},{14,6},{4,0},{6,2},{1,9},{3,11}... | collective-permute-start | bytes 552968 | tf_op jit(solution)/shard_map/ppermute | solution.py:104
  30.3 7.5 %collective-permute-start.4 = (bf16[80,1152]{1,0:T(8,128)(2,1)S(1)}, bf16[80,1152]{1,0:T(8,128)(2,1)S(1)}, u32[]{:S(2)}, u32[]{:S(2)}) collective-permute-start(bf16[80,1152]{1,0:T(8,128)(2,1)S(1)} %collective-permute-done.2.refs_5_), channel_id=1, source_target_pairs={{0,8},{8,12},{12,4},{4,0},{1,9},{9,13},{13,5},{5,1},{2,10},{10,14}... | collective-permute-start | bytes 552968 | tf_op jit(solution)/shard_map/ppermute | solution.py:101
  34.0 0.7 %copy-start.3 = (f32[32,28]{1,0:T(8,128)S(1)}, f32[32,28]{1,0:T(8,128)}, u32[]{:S(2)}) copy-start(f32[32,28]{1,0:T(8,128)} %get-tuple-element.15.refs_0_) | copy-start | bytes 10756
  34.7 27.7 %copy-start.2 = (s32[1,128]{1,0:T(1,128)S(1)}, s32[1,128]{1,0:T(1,128)}, u32[]{:S(2)}) copy-start(s32[1,128]{1,0:T(1,128)} %refs_3_.1) | copy-start | bytes 1540
  36.0 6.7 %collective-permute-start.3 = (bf16[80,1152]{1,0:T(8,128)(2,1)S(1)}, bf16[80,1152]{1,0:T(8,128)(2,1)S(1)}, u32[]{:S(2)}, u32[]{:S(2)}) collective-permute-start(bf16[80,1152]{1,0:T(8,128)(2,1)S(1)} %get-tuple-element.23.refs_4_), channel_id=1, source_target_pairs={{0,8},{8,12},{12,4},{4,0},{1,9},{9,13},{13,5},{5,1},{2,10},{10,14}... | collective-permute-start | bytes 552968 | tf_op jit(solution)/shard_map/ppermute | solution.py:101
  37.8 7.2 %collective-permute-start.1 = (bf16[80,1152]{1,0:T(8,128)(2,1)}, bf16[80,1152]{1,0:T(8,128)(2,1)S(1)}, u32[]{:S(2)}, u32[]{:S(2)}) collective-permute-start(bf16[80,1152]{1,0:T(8,128)(2,1)} %get-tuple-element.22), channel_id=1, source_target_pairs={{0,2},{2,0},{1,3},{3,1},{4,6},{6,4},{5,7},{7,5},{8,10},{10,8},{9,1... | collective-permute-start | bytes 552968 | tf_op jit(solution)/shard_map/ppermute | solution.py:88
  37.8 10.4 %collective-permute-start.7 = (bf16[80,1152]{1,0:T(8,128)(2,1)S(1)}, bf16[80,1152]{1,0:T(8,128)(2,1)S(1)}, u32[]{:S(2)}, u32[]{:S(2)}) collective-permute-start(bf16[80,1152]{1,0:T(8,128)(2,1)S(1)} %collective-permute-done.4.refs_7_), channel_id=1, source_target_pairs={{0,8},{8,12},{12,4},{4,0},{1,9},{9,13},{13,5},{5,1},{2,10},{10,14}... | collective-permute-start | bytes 552968 | tf_op jit(solution)/shard_map/ppermute | solution.py:101
  42.7 5.5 %collective-permute-start.6 = (bf16[80,1152]{1,0:T(8,128)(2,1)S(1)}, bf16[80,1152]{1,0:T(8,128)(2,1)S(1)}, u32[]{:S(2)}, u32[]{:S(2)}) collective-permute-start(bf16[80,1152]{1,0:T(8,128)(2,1)S(1)} %collective-permute-done.3.refs_6_), channel_id=1, source_target_pairs={{0,8},{8,12},{12,4},{4,0},{1,9},{9,13},{13,5},{5,1},{2,10},{10,14}... | collective-permute-start | bytes 552968 | tf_op jit(solution)/shard_map/ppermute | solution.py:101
  45.0 1.1 %copy-start = (bf16[3,80,1152]{2,1,0:T(8,128)(2,1)S(1)}, bf16[3,80,1152]{2,1,0:T(8,128)(2,1)}, u32[]{:S(2)}) copy-start(bf16[3,80,1152]{2,1,0:T(8,128)(2,1)} %get-tuple-element.24.refs_8_.refs_5_) | copy-start | bytes 1658884
  46.1 0.9 %copy-start.1 = (bf16[80,1152]{1,0:T(8,128)(2,1)S(1)}, bf16[80,1152]{1,0:T(8,128)(2,1)}, u32[]{:S(2)}) copy-start(bf16[80,1152]{1,0:T(8,128)(2,1)} %get-tuple-element.16.refs_2_) | copy-start | bytes 552964
  49.2 1.5 %collective-permute-start.8 = (f32[80,448]{1,0:T(8,128)S(1)}, f32[80,448]{1,0:T(8,128)S(1)}, u32[]{:S(2)}, u32[]{:S(2)}) collective-permute-start(f32[80,448]{1,0:T(8,128)S(1)} %get-tuple-element.27), channel_id=1, source_target_pairs={{0,1},{1,0},{2,3},{3,2},{4,5},{5,4},{6,7},{7,6},{8,9},{9,8},{10,11... | collective-permute-start | bytes 430088 | tf_op jit(solution)/shard_map/ppermute | solution.py:88
  50.7 6.5 %collective-permute-start.11 = (bf16[80,448]{1,0:T(8,128)(2,1)S(1)}, bf16[80,448]{1,0:T(8,128)(2,1)S(1)}, u32[]{:S(2)}, u32[]{:S(2)}) collective-permute-start(bf16[80,448]{1,0:T(8,128)(2,1)S(1)} %add_convert_fusion.refs_4_), channel_id=1, source_target_pairs={{0,4},{8,0},{12,8},{4,12},{1,5},{9,1},{13,9},{5,13},{2,6},{10,2},{... | collective-permute-start | bytes 215048 | tf_op jit(solution)/shard_map/ppermute | solution.py:111
  53.2 7.2 %collective-permute-start.10 = (bf16[80,448]{1,0:T(8,128)(2,1)S(1)}, bf16[80,448]{1,0:T(8,128)(2,1)S(1)}, u32[]{:S(2)}, u32[]{:S(2)}) collective-permute-start(bf16[80,448]{1,0:T(8,128)(2,1)S(1)} %add_convert_fusion.refs_4_), channel_id=1, source_target_pairs={{0,12},{8,4},{12,0},{4,8},{1,13},{9,5},{13,1},{5,9},{2,14},{10,6},... | collective-permute-start | bytes 215048 | tf_op jit(solution)/shard_map/ppermute | solution.py:111
  55.4 5.7 %collective-permute-start.9 = (bf16[80,448]{1,0:T(8,128)(2,1)S(1)}, bf16[80,448]{1,0:T(8,128)(2,1)S(1)}, u32[]{:S(2)}, u32[]{:S(2)}) collective-permute-start(bf16[80,448]{1,0:T(8,128)(2,1)S(1)} %add_convert_fusion.refs_4_), channel_id=1, source_target_pairs={{0,8},{8,12},{12,4},{4,0},{1,9},{9,13},{13,5},{5,1},{2,10},{10,14}... | collective-permute-start | bytes 215048 | tf_op jit(solution)/shard_map/ppermute | solution.py:111
  55.4 5.7 %collective-permute-start.12 = (bf16[80,448]{1,0:T(8,128)(2,1)S(1)}, bf16[80,448]{1,0:T(8,128)(2,1)S(1)}, u32[]{:S(2)}, u32[]{:S(2)}) collective-permute-start(bf16[80,448]{1,0:T(8,128)(2,1)S(1)} %add_convert_fusion.refs_4_), channel_id=1, source_target_pairs={{0,1},{1,0},{2,3},{3,2},{4,5},{5,4},{6,7},{7,6},{8,9},{9,8},{10,11... | collective-permute-start | bytes 215048 | tf_op jit(solution)/shard_map/ppermute | solution.py:88
  57.2 3.9 %collective-permute-start.15 = (bf16[80,448]{1,0:T(8,128)(2,1)S(1)}, bf16[80,448]{1,0:T(8,128)(2,1)S(1)}, u32[]{:S(2)}, u32[]{:S(2)}) collective-permute-start(bf16[80,448]{1,0:T(8,128)(2,1)S(1)} %collective-permute-done.11.refs_7_), channel_id=1, source_target_pairs={{0,1},{1,0},{2,3},{3,2},{4,5},{5,4},{6,7},{7,6},{8,9},{9,8},{10,11... | collective-permute-start | bytes 215048 | tf_op jit(solution)/shard_map/ppermute | solution.py:88
  60.4 1.3 %collective-permute-start.14 = (bf16[80,448]{1,0:T(8,128)(2,1)S(1)}, bf16[80,448]{1,0:T(8,128)(2,1)S(1)}, u32[]{:S(2)}, u32[]{:S(2)}) collective-permute-start(bf16[80,448]{1,0:T(8,128)(2,1)S(1)} %collective-permute-done.10.refs_6_), channel_id=1, source_target_pairs={{0,1},{1,0},{2,3},{3,2},{4,5},{5,4},{6,7},{7,6},{8,9},{9,8},{10,11... | collective-permute-start | bytes 215048 | tf_op jit(solution)/shard_map/ppermute | solution.py:88
  61.1 1.3 %collective-permute-start.13 = (bf16[80,448]{1,0:T(8,128)(2,1)S(1)}, bf16[80,448]{1,0:T(8,128)(2,1)S(1)}, u32[]{:S(2)}, u32[]{:S(2)}) collective-permute-start(bf16[80,448]{1,0:T(8,128)(2,1)S(1)} %collective-permute-done.9.refs_5_), channel_id=1, source_target_pairs={{0,1},{1,0},{2,3},{3,2},{4,5},{5,4},{6,7},{7,6},{8,9},{9,8},{10,11... | collective-permute-start | bytes 215048 | tf_op jit(solution)/shard_map/ppermute | solution.py:88

commit v5 on v4

--- a/solution.py
+++ b/solution.py
@@ -197,7 +197,7 @@
         mine = slot_entry(iota((slots, kslots), 0)) == iota((slots, kslots), 1)
         return jnp.sum(jnp.where(mine, every, 0.0), axis=1, keepdims=True)
 
-    def choose(values, enc, dec):
+    def choose(values):
         feat, pos, _ = place()
         own = feat * poses + pos
         tables = []
@@ -224,30 +224,45 @@
         gains = jnp.concatenate(gains, axis=0)
         ids_of = jnp.concatenate(ids_of, axis=0)
         layer = ids_of - floor_div(ids_of, layers) * layers
-        enc_rows = dot(picks, enc(0)).astype(BF16)
-        dec_rows = [
-            (dot(picks, dec(l)) * jnp.where(layer <= l, gains, 0.0)).astype(BF16)
-            for l in range(depth)
-        ]
-        out = []
-        for k in range(poses):
-            rows = slice(k * listed, (k + 1) * listed)
-            out += [enc_rows[rows], jnp.stack([d[rows] for d in dec_rows], axis=0)]
-        return out + [tables[0]]
-
-    outs = [shape(listed, width, dtype=BF16), shape(depth, listed, width, dtype=BF16)] * poses
-    *chosen, my_list = on_core(
+        gains = jnp.concatenate([jnp.where(layer <= l, gains, 0.0) for l in range(depth)], axis=1)
+        return picks, gains, tables[0]
+
+    picks, gains, my_list = on_core(
         choose,
         [lists],
-        outs + [shape(2 * positions * feats, kslots)],
-        small,
-        streams=[encoder[None], jnp.transpose(decoder, (1, 0, 2))],
-        room=60,
-    )
-    enc_rows, dec_rows = chosen[::2], chosen[1::2]
+        [
+            shape(column, table_rows, dtype=BF16),
+            shape(column, depth),
+            shape(2 * positions * feats, kslots),
+        ],
+        small,
+    )
+
+    def encode(picks, enc):
+        rows = dot(picks, enc).astype(BF16)
+        return [rows[k * listed : (k + 1) * listed] for k in range(poses)]
+
+    enc_rows = on_core(
+        encode, [picks, encoder], [shape(listed, width, dtype=BF16)] * poses, small
+    )
 
     ring = [[enc_rows[0]] + [rotate(enc_rows[k], "pos", k) for k in range(1, poses)]]
     ring.append([ring_next(enc_rows[k], "feat", "pos", k) for k in range(poses)])
+
+    def decode(picks, gains, dec):
+        rows = [(dot(picks, dec[l]) * gains[:, l : l + 1]).astype(BF16) for l in range(depth)]
+        return [
+            jnp.stack([row[k * listed : (k + 1) * listed] for row in rows], axis=0)
+            for k in range(poses)
+        ]
+
+    dec_rows = on_core(
+        decode,
+        [picks, gains, jnp.transpose(decoder, (1, 0, 2))],
+        [shape(depth, listed, width, dtype=BF16)] * poses,
+        small,
+        cost=(1, 1),
+    )
     dec_rows = [dec_rows[0]] + [rotate(dec_rows[k], "pos", k) for k in range(1, poses)]
 
     def places(table, pattern):
@@ -294,7 +309,7 @@
         own_mask = jnp.where(own_causal, own_mask, 0.0)
         return placing.astype(BF16), placing_t.astype(BF16), layer_row, mask.astype(BF16), own_mask
 
-    placing, placing_t, layer_row, mask, own_mask, *ring[1][:1] = on_core(
+    placing, placing_t, layer_row, mask, own_mask, ring[1][-1] = on_core(
         places,
         [my_list, block_pattern],
         [
@@ -305,8 +320,8 @@
             shape(result_rows, slots),
         ],
         small,
-        through=ring[1][:1],
-        cost=(4 * slots * slots * slots, 4 * slots * slots),
+        through=ring[1][-1:],
+        cost=(1, 1),
     )
     for _ in range(2, feats):
         ring.append([ring_next(rows, "feat") for rows in ring[-1]])
@@ -341,7 +356,7 @@
         [layer_row, placing_t] + early_enc + list(dec_rows),
         [shape(column, slots)],
         small,
-        cost=(8 * column * slots * width, 8 * column * width),
+        cost=(1, 1),
     )
     keep, send = on_core(
         late,

time: 65.3 us -> 63.4 us (0.971)
  Pallas kernels: 12.9 us -> 9.23 us
  waiting for transfers between devices: 19.8 us -> 20.9 us
    ppermute x2, waiting for transfers between devices: 8.33 us -> 4.46 us  [ring_next(): return lax.ppermute(x, (axis, across), pairs)]
    ppermute x4, waiting for transfers between devices: 3.16 us -> 7 us  [ring_next(): return lax.ppermute(x, axis, steps)]
    pallas_call x6 -> x8, Pallas kernels: 12.9 us -> 9.23 us  [on_core(): return list(call(*args, *streams, *through))]
    ppermute x7, starting transfers between devices: 0.63 us -> 2.55 us  [rotate(): lax.ppermute(x, axis, [(i, (i + step) % count) for i in range(count)])]
    ppermute x4, starting transfers between devices: 7.25 us -> 6.02 us  [ring_next(): return lax.ppermute(x, axis, steps)]
    ppermute x3, waiting for transfers between devices: 5.65 us -> 6.77 us  [ring_spread(): lax.ppermute(x, axis, [(order[i], order[(i + k) % count]) for i in range(...]
    ppermute x2, starting transfers between devices: 2.11 us -> 1.09 us  [ring_next(): return lax.ppermute(x, (axis, across), pairs)]
    unnamed x10 -> x8, local copies, waits for them, and re-layouts: 2.7 us -> 3.28 us
  transfers between devices with their start and end apart: 16 -> 16, of which waited for: 10 -> 10; matrix products, arithmetic and copies ran while one was open for 0% -> 0% of each run, Pallas kernels for 4% -> 5%
where the time goes in v5:
time: 63.4 us; the launch traced here: 63.1 us
  waiting for transfers between devices  20.9 us (33%)
  starting transfers between devices  15 us (24%)
  blocking collectives  13.9 us (22%)
  Pallas kernels  9.23 us (15%)
  local copies, waits for them, and re-layouts  3.28 us (5%)
  between operations  0.75 us (1%)
    all_to_all x1, blocking collectives, per_device(): lax.all_to_all(packed, ('feat', 'pos'), split_axis=0, concat_axis=0, tile...  13.9 us
    pallas_call x8, Pallas kernels, on_core(): return list(call(*args, *streams, *through))  9.23 us
    ppermute x4, waiting for transfers between devices, ring_next(): return lax.ppermute(x, axis, steps)  7 us
    ppermute x3, waiting for transfers between devices, ring_spread(): lax.ppermute(x, axis, [(order[i], order[(i + k) % count]) for i in range(...  6.77 us
    ppermute x4, starting transfers between devices, ring_next(): return lax.ppermute(x, axis, steps)  6.02 us
    ppermute x3, starting transfers between devices, ring_spread(): lax.ppermute(x, axis, [(order[i], order[(i + k) % count]) for i in range(...  5.34 us
    ppermute x2, waiting for transfers between devices, ring_next(): return lax.ppermute(x, (axis, across), pairs)  4.46 us
    unnamed x8, local copies, waits for them, and re-layouts  3.28 us
  transfers between devices with their start and end apart: 16, of which 10 were waited for; matrix products, arithmetic and copies ran while one was open for 0% of the time, Pallas kernels for 5%

profile of v5, /device:TPU:0, one launch (start us, length us, event | category | flops | bytes accessed | tf_op | source)
XLA Modules:
  0.0 63.1 jit_solution(7084675155975444780)
XLA Ops:
  0.6 1.3 %shard_map.77 = f32[8,8,128]{2,1,0:T(8,128)} custom-call(s32[1,4,28]{2,1,0:T(4,128)} %refs_0_.1, f32[1,4,28]{2,1,0:T(4,128)} %refs_1_.3), custom_call_target="tpu_custom_call" | custom-call | tf_op jit(solution)/shard_map/pallas_call | solution.py:83
  2.0 13.9 %all_to_all.5.refs_0_ = f32[8,8,128]{2,1,0:T(8,128)S(1)} all-to-all(f32[8,8,128]{2,1,0:T(8,128)} %shard_map.77), channel_id=1, replica_groups=mesh['grp'=2,'feat'=4,'pos'=2,'rep'=2] {'feat','pos'}, dimensions={0} | all-to-all | bytes 65536 | tf_op jit(solution)/shard_map/all_to_all | solution.py:159
  16.6 1.3 %copy-done.1 = bf16[512,1152]{1,0:T(8,128)(2,1)S(1)} copy-done((bf16[512,1152]{1,0:T(8,128)(2,1)S(1)}, bf16[512,1152]{1,0:T(8,128)(2,1)}, u32[]{:S(2)}) %copy-start.1) | copy-done | bytes 1179672
  18.7 2.0 %copy-done = bf16[512,3,1152]{2,0,1:T(8,128)(2,1)S(1)} copy-done((bf16[512,3,1152]{2,0,1:T(8,128)(2,1)S(1)}, bf16[512,3,1152]{2,0,1:T(8,128)(2,1)}, u32[]{:S(2)}) %copy-start) | copy-done | bytes 3538968
  21.5 1.6 %collective-permute-start.5 = (bf16[3,80,1152]{2,1,0:T(8,128)(2,1)S(1)}, bf16[3,80,1152]{2,1,0:T(8,128)(2,1)S(1)}, u32[]{:S(2)}, u32[]{:S(2)}) collective-permute-start(bf16[3,80,1152]{2,1,0:T(8,128)(2,1)S(1)} %get-tuple-element.29), channel_id=1, source_target_pairs={{0,2},{2,0},{1,3},{3,1},{4,6},{6,4},{5,7},{7,5},{8,10},{10,8},{9,1... | collective-permute-start | bytes 1658888 | tf_op jit(solution)/shard_map/ppermute | solution.py:88
  23.8 1.9 %collective-permute-done.refs_2_ = bf16[80,1152]{1,0:T(8,128)(2,1)S(1)} collective-permute-done((bf16[80,1152]{1,0:T(8,128)(2,1)S(1)}, bf16[80,1152]{1,0:T(8,128)(2,1)S(1)}, u32[]{:S(2)}, u32[]{:S(2)}) %collective-permute-start) | collective-permute-done | bytes 184352 | tf_op jit(solution)/shard_map/ppermute | solution.py:104
  25.7 1.4 %shard_map.80 = (bf16[448,640]{1,0:T(8,128)(2,1)S(1)}, bf16[640,448]{1,0:T(8,128)(2,1)S(1)}, f32[1,640]{1,0:T(1,128)S(1)}, bf16[448,448]{1,0:T(8,128)(2,1)S(1)},...) custom-call(f32[32,28]{1,0:T(8,128)S(1)} %get-tuple-element.17.refs_0_, ...), custom_call_target="tpu_custom_call", output_to_operand_aliasing={{5}: (2, {})} | custom-call | flops 1 | bytes 1 | tf_op jit(solution)/shard_map/pallas_call | solution.py:83
  27.1 1.0 %collective-permute-start.4 = (bf16[80,1152]{1,0:T(8,128)(2,1)S(1)}, bf16[80,1152]{1,0:T(8,128)(2,1)S(1)}, u32[]{:S(2)}, u32[]{:S(2)}) collective-permute-start(bf16[80,1152]{1,0:T(8,128)(2,1)S(1)} %get-tuple-element.26.refs_5_), channel_id=1, source_target_pairs={{0,8},{8,12},{12,4},{4,0},{1,9},{9,13},{13,5},{5,1},{2,10},{10,14}... | collective-permute-start | bytes 552968 | tf_op jit(solution)/shard_map/ppermute | solution.py:101
  28.1 2.5 %collective-permute-done.2.refs_4_ = bf16[80,1152]{1,0:T(8,128)(2,1)S(1)} collective-permute-done((bf16[80,1152]{1,0:T(8,128)(2,1)S(1)}, bf16[80,1152]{1,0:T(8,128)(2,1)S(1)}, u32[]{:S(2)}, u32[]{:S(2)}) %collective-permute-start.2) | collective-permute-done | bytes 184352 | tf_op jit(solution)/shard_map/ppermute | solution.py:104
  30.6 1.2 %collective-permute-start.3 = (bf16[80,1152]{1,0:T(8,128)(2,1)S(1)}, bf16[80,1152]{1,0:T(8,128)(2,1)S(1)}, u32[]{:S(2)}, u32[]{:S(2)}) collective-permute-start(bf16[80,1152]{1,0:T(8,128)(2,1)S(1)} %collective-permute-done.2.refs_4_), channel_id=1, source_target_pairs={{0,8},{8,12},{12,4},{4,0},{1,9},{9,13},{13,5},{5,1},{2,10},{10,14}... | collective-permute-start | bytes 552968 | tf_op jit(solution)/shard_map/ppermute | solution.py:101
  32.6 2.1 %collective-permute-done.4.refs_7_ = bf16[80,1152]{1,0:T(8,128)(2,1)S(1)} collective-permute-done((bf16[80,1152]{1,0:T(8,128)(2,1)S(1)}, bf16[80,1152]{1,0:T(8,128)(2,1)S(1)}, u32[]{:S(2)}, u32[]{:S(2)}) %collective-permute-start.4) | collective-permute-done | bytes 184352 | tf_op jit(solution)/shard_map/ppermute | solution.py:101
  34.7 1.9 %collective-permute-start.7 = (bf16[80,1152]{1,0:T(8,128)(2,1)S(1)}, bf16[80,1152]{1,0:T(8,128)(2,1)S(1)}, u32[]{:S(2)}, u32[]{:S(2)}) collective-permute-start(bf16[80,1152]{1,0:T(8,128)(2,1)S(1)} %collective-permute-done.4.refs_7_), channel_id=1, source_target_pairs={{0,8},{8,12},{12,4},{4,0},{1,9},{9,13},{13,5},{5,1},{2,10},{10,14}... | collective-permute-start | bytes 552968 | tf_op jit(solution)/shard_map/ppermute | solution.py:101
  36.6 2.1 %collective-permute-done.3.refs_6_ = bf16[80,1152]{1,0:T(8,128)(2,1)S(1)} collective-permute-done((bf16[80,1152]{1,0:T(8,128)(2,1)S(1)}, bf16[80,1152]{1,0:T(8,128)(2,1)S(1)}, u32[]{:S(2)}, u32[]{:S(2)}) %collective-permute-start.3) | collective-permute-done | bytes 184352 | tf_op jit(solution)/shard_map/ppermute | solution.py:101
  38.7 1.9 %collective-permute-start.6 = (bf16[80,1152]{1,0:T(8,128)(2,1)S(1)}, bf16[80,1152]{1,0:T(8,128)(2,1)S(1)}, u32[]{:S(2)}, u32[]{:S(2)}) collective-permute-start(bf16[80,1152]{1,0:T(8,128)(2,1)S(1)} %collective-permute-done.3.refs_6_), channel_id=1, source_target_pairs={{0,8},{8,12},{12,4},{4,0},{1,9},{9,13},{13,5},{5,1},{2,10},{10,14}... | collective-permute-start | bytes 552968 | tf_op jit(solution)/shard_map/ppermute | solution.py:101
  40.6 1.2 %shard_map.82.refs_0_ = f32[160,448]{1,0:T(8,128)S(1)} custom-call(f32[1,640]{1,0:T(1,128)S(1)} %get-tuple-element.23.refs_0_.refs_1_, bf16[640,448]{1,0:T(8,128)(2,1)S(1)} %get-tuple-element.24.refs_1_.refs_2_, bf16[80,1152]{1,0:T(8,128)(2,1)S(1)} %get-tuple-element.25.refs_2_, bf16[80,1152]{1,0:T(8,128)(2,1)S(1)} %collective-permute-done.1.refs_3_, ...), custom_call_target="tpu_custom_call" | custom-call | flops 1 | bytes 1 | tf_op jit(solution)/shard_map/pallas_call | solution.py:83
  41.8 2.8 %collective-permute-done.6.refs_3_ = bf16[80,1152]{1,0:T(8,128)(2,1)S(1)} collective-permute-done((bf16[80,1152]{1,0:T(8,128)(2,1)S(1)}, bf16[80,1152]{1,0:T(8,128)(2,1)S(1)}, u32[]{:S(2)}, u32[]{:S(2)}) %collective-permute-start.6) | collective-permute-done | bytes 184352 | tf_op jit(solution)/shard_map/ppermute | solution.py:101
  44.6 0.9 %shard_map.83 = (f32[80,448]{1,0:T(8,128)S(1)}, f32[80,448]{1,0:T(8,128)S(1)}) custom-call(f32[160,448]{1,0:T(8,128)S(1)} %shard_map.82.refs_0_, f32[1,640]{1,0:T(1,128)S(1)} %get-tuple-element.23.refs_0_.refs_1_, bf16[640,448]{1,0:T(8,128)(2,1)S(1)} %get-tuple-element.24.refs_1_.refs_2_, bf16[80,1152]{1,0:T(8,128)(2,1)S(1)} %collective-permute-done.6.refs_3_, ...), custom_call_target="tpu_custom_call" | custom-call | tf_op jit(solution)/shard_map/pallas_call | solution.py:83
  45.6 1.4 %collective-permute-done.8 = f32[80,448]{1,0:T(8,128)S(1)} collective-permute-done((f32[80,448]{1,0:T(8,128)S(1)}, f32[80,448]{1,0:T(8,128)S(1)}, u32[]{:S(2)}, u32[]{:S(2)}) %collective-permute-start.8) | collective-permute-done | bytes 143392 | tf_op jit(solution)/shard_map/ppermute | solution.py:88
  47.0 2.4 %collective-permute-start.9 = (bf16[80,448]{1,0:T(8,128)(2,1)S(1)}, bf16[80,448]{1,0:T(8,128)(2,1)S(1)}, u32[]{:S(2)}, u32[]{:S(2)}) collective-permute-start(bf16[80,448]{1,0:T(8,128)(2,1)S(1)} %add_convert_fusion.refs_4_), channel_id=1, source_target_pairs={{0,8},{8,12},{12,4},{4,0},{1,9},{9,13},{13,5},{5,1},{2,10},{10,14}... | collective-permute-start | bytes 215048 | tf_op jit(solution)/shard_map/ppermute | solution.py:111
  49.5 2.9 %collective-permute-start.10 = (bf16[80,448]{1,0:T(8,128)(2,1)S(1)}, bf16[80,448]{1,0:T(8,128)(2,1)S(1)}, u32[]{:S(2)}, u32[]{:S(2)}) collective-permute-start(bf16[80,448]{1,0:T(8,128)(2,1)S(1)} %add_convert_fusion.refs_4_), channel_id=1, source_target_pairs={{0,12},{8,4},{12,0},{4,8},{1,13},{9,5},{13,1},{5,9},{2,14},{10,6},... | collective-permute-start | bytes 215048 | tf_op jit(solution)/shard_map/ppermute | solution.py:111
  52.9 4.5 %collective-permute-done.10.refs_6_ = bf16[80,448]{1,0:T(8,128)(2,1)S(1)} collective-permute-done((bf16[80,448]{1,0:T(8,128)(2,1)S(1)}, bf16[80,448]{1,0:T(8,128)(2,1)S(1)}, u32[]{:S(2)}, u32[]{:S(2)}) %collective-permute-start.10) | collective-permute-done | bytes 71712 | tf_op jit(solution)/shard_map/ppermute | solution.py:111
  57.4 1.8 %collective-permute-done.11.refs_7_ = bf16[80,448]{1,0:T(8,128)(2,1)S(1)} collective-permute-done((bf16[80,448]{1,0:T(8,128)(2,1)S(1)}, bf16[80,448]{1,0:T(8,128)(2,1)S(1)}, u32[]{:S(2)}, u32[]{:S(2)}) %collective-permute-start.11) | collective-permute-done | bytes 71712 | tf_op jit(solution)/shard_map/ppermute | solution.py:111
  59.3 1.3 %collective-permute-done.15.refs_11_ = bf16[80,448]{1,0:T(8,128)(2,1)S(1)} collective-permute-done((bf16[80,448]{1,0:T(8,128)(2,1)S(1)}, bf16[80,448]{1,0:T(8,128)(2,1)S(1)}, u32[]{:S(2)}, u32[]{:S(2)}) %collective-permute-start.15) | collective-permute-done | bytes 71712 | tf_op jit(solution)/shard_map/ppermute | solution.py:88
  60.6 2.5 %shard_map.84 = (bf16[1,56,448]{2,1,0:T(8,128)(2,1)}, f32[1,56,128]{2,1,0:T(8,128)}) custom-call(bf16[448,640]{1,0:T(8,128)(2,1)S(1)} %get-tuple-element.20.refs_0_, bf16[448,448]{1,0:T(8,128)(2,1)S(1)} %get-tuple-element.21.refs_1_, f32[56,448]{1,0:T(8,128)S(1)} %get-tuple-element.22.refs_2_, s32[1,128]{1,0:T(1,128)S(1)} %copy-done.3, ...), custom_call_target="tpu_custom_call" | custom-call | tf_op jit(solution)/shard_map/pallas_call | solution.py:83
  (26 shorter events, 4.3 us)
Async XLA Ops:
  0.6 25.1 %copy-start.2 = (s32[1,4,4]{2,1,0:T(4,128)S(1)}, s32[1,4,4]{2,1,0:T(4,128)}, u32[]{:S(2)}) copy-start(s32[1,4,4]{2,1,0:T(4,128)} %refs_1_.5) | copy-start | bytes 196
  16.6 1.3 %copy-start.1 = (bf16[512,1152]{1,0:T(8,128)(2,1)S(1)}, bf16[512,1152]{1,0:T(8,128)(2,1)}, u32[]{:S(2)}) copy-start(bf16[512,1152]{1,0:T(8,128)(2,1)} %refs_1_.4) | copy-start | bytes 3538948
  18.2 7.5 %collective-permute-start = (bf16[80,1152]{1,0:T(8,128)(2,1)S(1)}, bf16[80,1152]{1,0:T(8,128)(2,1)S(1)}, u32[]{:S(2)}, u32[]{:S(2)}) collective-permute-start(bf16[80,1152]{1,0:T(8,128)(2,1)S(1)} %get-tuple-element.19), channel_id=1, source_target_pairs={{0,10},{2,8},{8,14},{10,12},{12,6},{14,4},{4,2},{6,0},{1,11},{3,9}... | collective-permute-start | bytes 552968 | tf_op jit(solution)/shard_map/ppermute | solution.py:104
  18.7 2.0 %copy-start = (bf16[512,3,1152]{2,0,1:T(8,128)(2,1)S(1)}, bf16[512,3,1152]{2,0,1:T(8,128)(2,1)}, u32[]{:S(2)}) copy-start(bf16[512,3,1152]{2,0,1:T(8,128)(2,1)} %param.11) | copy-start | bytes 10616836
  21.5 39.0 %copy-start.3 = (s32[1,128]{1,0:T(1,128)S(1)}, s32[1,128]{1,0:T(1,128)}, u32[]{:S(2)}) copy-start(s32[1,128]{1,0:T(1,128)} %refs_3_.1) | copy-start | bytes 1540
  21.5 19.0 %collective-permute-start.5 = (bf16[3,80,1152]{2,1,0:T(8,128)(2,1)S(1)}, bf16[3,80,1152]{2,1,0:T(8,128)(2,1)S(1)}, u32[]{:S(2)}, u32[]{:S(2)}) collective-permute-start(bf16[3,80,1152]{2,1,0:T(8,128)(2,1)S(1)} %get-tuple-element.29), channel_id=1, source_target_pairs={{0,2},{2,0},{1,3},{3,1},{4,6},{6,4},{5,7},{7,5},{8,10},{10,8},{9,1... | collective-permute-start | bytes 1658888 | tf_op jit(solution)/shard_map/ppermute | solution.py:88
  23.2 7.5 %collective-permute-start.2 = (bf16[80,1152]{1,0:T(8,128)(2,1)S(1)}, bf16[80,1152]{1,0:T(8,128)(2,1)S(1)}, u32[]{:S(2)}, u32[]{:S(2)}) collective-permute-start(bf16[80,1152]{1,0:T(8,128)(2,1)S(1)} %get-tuple-element.25.refs_2_), channel_id=1, source_target_pairs={{0,8},{2,10},{8,12},{10,14},{12,4},{14,6},{4,0},{6,2},{1,9},{3,11}... | collective-permute-start | bytes 552968 | tf_op jit(solution)/shard_map/ppermute | solution.py:104
  27.1 7.6 %collective-permute-start.4 = (bf16[80,1152]{1,0:T(8,128)(2,1)S(1)}, bf16[80,1152]{1,0:T(8,128)(2,1)S(1)}, u32[]{:S(2)}, u32[]{:S(2)}) collective-permute-start(bf16[80,1152]{1,0:T(8,128)(2,1)S(1)} %get-tuple-element.26.refs_5_), channel_id=1, source_target_pairs={{0,8},{8,12},{12,4},{4,0},{1,9},{9,13},{13,5},{5,1},{2,10},{10,14}... | collective-permute-start | bytes 552968 | tf_op jit(solution)/shard_map/ppermute | solution.py:101
  30.6 8.0 %collective-permute-start.3 = (bf16[80,1152]{1,0:T(8,128)(2,1)S(1)}, bf16[80,1152]{1,0:T(8,128)(2,1)S(1)}, u32[]{:S(2)}, u32[]{:S(2)}) collective-permute-start(bf16[80,1152]{1,0:T(8,128)(2,1)S(1)} %collective-permute-done.2.refs_4_), channel_id=1, source_target_pairs={{0,8},{8,12},{12,4},{4,0},{1,9},{9,13},{13,5},{5,1},{2,10},{10,14}... | collective-permute-start | bytes 552968 | tf_op jit(solution)/shard_map/ppermute | solution.py:101
  31.8 8.7 %collective-permute-start.1 = (bf16[80,1152]{1,0:T(8,128)(2,1)S(1)}, bf16[80,1152]{1,0:T(8,128)(2,1)S(1)}, u32[]{:S(2)}, u32[]{:S(2)}) collective-permute-start(bf16[80,1152]{1,0:T(8,128)(2,1)S(1)} %get-tuple-element.19), channel_id=1, source_target_pairs={{0,2},{2,0},{1,3},{3,1},{4,6},{6,4},{5,7},{7,5},{8,10},{10,8},{9,1... | collective-permute-start | bytes 552968 | tf_op jit(solution)/shard_map/ppermute | solution.py:88
  34.7 7.1 %collective-permute-start.7 = (bf16[80,1152]{1,0:T(8,128)(2,1)S(1)}, bf16[80,1152]{1,0:T(8,128)(2,1)S(1)}, u32[]{:S(2)}, u32[]{:S(2)}) collective-permute-start(bf16[80,1152]{1,0:T(8,128)(2,1)S(1)} %collective-permute-done.4.refs_7_), channel_id=1, source_target_pairs={{0,8},{8,12},{12,4},{4,0},{1,9},{9,13},{13,5},{5,1},{2,10},{10,14}... | collective-permute-start | bytes 552968 | tf_op jit(solution)/shard_map/ppermute | solution.py:101
  38.7 5.9 %collective-permute-start.6 = (bf16[80,1152]{1,0:T(8,128)(2,1)S(1)}, bf16[80,1152]{1,0:T(8,128)(2,1)S(1)}, u32[]{:S(2)}, u32[]{:S(2)}) collective-permute-start(bf16[80,1152]{1,0:T(8,128)(2,1)S(1)} %collective-permute-done.3.refs_6_), channel_id=1, source_target_pairs={{0,8},{8,12},{12,4},{4,0},{1,9},{9,13},{13,5},{5,1},{2,10},{10,14}... | collective-permute-start | bytes 552968 | tf_op jit(solution)/shard_map/ppermute | solution.py:101
  45.5 1.5 %collective-permute-start.8 = (f32[80,448]{1,0:T(8,128)S(1)}, f32[80,448]{1,0:T(8,128)S(1)}, u32[]{:S(2)}, u32[]{:S(2)}) collective-permute-start(f32[80,448]{1,0:T(8,128)S(1)} %get-tuple-element.31), channel_id=1, source_target_pairs={{0,1},{1,0},{2,3},{3,2},{4,5},{5,4},{6,7},{7,6},{8,9},{9,8},{10,11... | collective-permute-start | bytes 430088 | tf_op jit(solution)/shard_map/ppermute | solution.py:88
  47.0 5.7 %collective-permute-start.9 = (bf16[80,448]{1,0:T(8,128)(2,1)S(1)}, bf16[80,448]{1,0:T(8,128)(2,1)S(1)}, u32[]{:S(2)}, u32[]{:S(2)}) collective-permute-start(bf16[80,448]{1,0:T(8,128)(2,1)S(1)} %add_convert_fusion.refs_4_), channel_id=1, source_target_pairs={{0,8},{8,12},{12,4},{4,0},{1,9},{9,13},{13,5},{5,1},{2,10},{10,14}... | collective-permute-start | bytes 215048 | tf_op jit(solution)/shard_map/ppermute | solution.py:111
  49.5 8.0 %collective-permute-start.10 = (bf16[80,448]{1,0:T(8,128)(2,1)S(1)}, bf16[80,448]{1,0:T(8,128)(2,1)S(1)}, u32[]{:S(2)}, u32[]{:S(2)}) collective-permute-start(bf16[80,448]{1,0:T(8,128)(2,1)S(1)} %add_convert_fusion.refs_4_), channel_id=1, source_target_pairs={{0,12},{8,4},{12,0},{4,8},{1,13},{9,5},{13,1},{5,9},{2,14},{10,6},... | collective-permute-start | bytes 215048 | tf_op jit(solution)/shard_map/ppermute | solution.py:111
  52.4 6.9 %collective-permute-start.11 = (bf16[80,448]{1,0:T(8,128)(2,1)S(1)}, bf16[80,448]{1,0:T(8,128)(2,1)S(1)}, u32[]{:S(2)}, u32[]{:S(2)}) collective-permute-start(bf16[80,448]{1,0:T(8,128)(2,1)S(1)} %add_convert_fusion.refs_4_), channel_id=1, source_target_pairs={{0,4},{8,0},{12,8},{4,12},{1,5},{9,1},{13,9},{5,13},{2,6},{10,2},{... | collective-permute-start | bytes 215048 | tf_op jit(solution)/shard_map/ppermute | solution.py:111
  52.4 6.9 %collective-permute-start.12 = (bf16[80,448]{1,0:T(8,128)(2,1)S(1)}, bf16[80,448]{1,0:T(8,128)(2,1)S(1)}, u32[]{:S(2)}, u32[]{:S(2)}) collective-permute-start(bf16[80,448]{1,0:T(8,128)(2,1)S(1)} %add_convert_fusion.refs_4_), channel_id=1, source_target_pairs={{0,1},{1,0},{2,3},{3,2},{4,5},{5,4},{6,7},{7,6},{8,9},{9,8},{10,11... | collective-permute-start | bytes 215048 | tf_op jit(solution)/shard_map/ppermute | solution.py:88
  52.8 6.5 %collective-permute-start.13 = (bf16[80,448]{1,0:T(8,128)(2,1)S(1)}, bf16[80,448]{1,0:T(8,128)(2,1)S(1)}, u32[]{:S(2)}, u32[]{:S(2)}) collective-permute-start(bf16[80,448]{1,0:T(8,128)(2,1)S(1)} %collective-permute-done.9.refs_5_), channel_id=1, source_target_pairs={{0,1},{1,0},{2,3},{3,2},{4,5},{5,4},{6,7},{7,6},{8,9},{9,8},{10,11... | collective-permute-start | bytes 215048 | tf_op jit(solution)/shard_map/ppermute | solution.py:88
  57.4 1.9 %collective-permute-start.14 = (bf16[80,448]{1,0:T(8,128)(2,1)S(1)}, bf16[80,448]{1,0:T(8,128)(2,1)S(1)}, u32[]{:S(2)}, u32[]{:S(2)}) collective-permute-start(bf16[80,448]{1,0:T(8,128)(2,1)S(1)} %collective-permute-done.10.refs_6_), channel_id=1, source_target_pairs={{0,1},{1,0},{2,3},{3,2},{4,5},{5,4},{6,7},{7,6},{8,9},{9,8},{10,11... | collective-permute-start | bytes 215048 | tf_op jit(solution)/shard_map/ppermute | solution.py:88
  59.3 1.3 %collective-permute-start.15 = (bf16[80,448]{1,0:T(8,128)(2,1)S(1)}, bf16[80,448]{1,0:T(8,128)(2,1)S(1)}, u32[]{:S(2)}, u32[]{:S(2)}) collective-permute-start(bf16[80,448]{1,0:T(8,128)(2,1)S(1)} %collective-permute-done.11.refs_7_), channel_id=1, source_target_pairs={{0,1},{1,0},{2,3},{3,2},{4,5},{5,4},{6,7},{7,6},{8,9},{9,8},{10,11... | collective-permute-start | bytes 215048 | tf_op jit(solution)/shard_map/ppermute | solution.py:88

commit v6 on v5

--- a/solution.py
+++ b/solution.py
@@ -88,6 +88,10 @@
     return lax.ppermute(x, axis, [(i, (i + step) % count) for i in range(count)])
 
 
+def swap(x, axis, bit):
+    return lax.ppermute(x, axis, [(i, i ^ bit) for i in range(lax.axis_size(axis))])
+
+
 def ring_place(index, count):
     low = floor_div(index, 2)
     return jnp.where(index > 2 * low, count - 1 - low, low)
@@ -145,18 +149,33 @@
         return feat.astype(F32), pos.astype(F32), lax.axis_index("rep").astype(F32)
 
     def pack(ids, vals):
-        one = jnp.concatenate([ids(0).astype(F32), vals(0)], axis=0)
-        one = jnp.concatenate([one, jnp.zeros((2 * positions, LANES - kslots), F32)], axis=1)
-        return (jnp.broadcast_to(one, (holders,) + one.shape),)
-
-    (packed,) = on_core(
-        pack,
-        [],
-        [shape(holders, 2 * positions, LANES)],
-        streams=[active_ids, active_vals],
-        room=60,
-    )
-    lists = lax.all_to_all(packed, ("feat", "pos"), split_axis=0, concat_axis=0, tiled=True)
+        one = jnp.concatenate([ids[0].astype(F32), vals[0]], axis=0)
+        return jnp.concatenate([one, jnp.zeros((2 * positions, LANES - kslots), F32)], axis=1)[None]
+
+    def joined(mine, other, upper):
+        first = jnp.where(upper, other, mine)
+        return jnp.concatenate([first, jnp.where(upper, mine, other)], axis=0)
+
+    def upper(axis, bit):
+        return lax.rem(lax.axis_index(axis) // bit, 2) == 1
+
+    steps = [("pos", 1 << i) for i in range(poses.bit_length() - 1)]
+    steps += [("feat", 1 << i) for i in range(feats.bit_length() - 1)]
+    axis, bit = steps[0]
+    arrived = [swap(x, axis, bit) for x in (active_ids, active_vals)]
+    lists = on_core(
+        lambda a, b, c, d: (joined(pack(a, b), pack(c, d), upper("pos", 1)),),
+        [active_ids, active_vals] + arrived,
+        [shape(2, 2 * positions, LANES)],
+    )[0]
+    for axis, bit in steps[1:-1]:
+        lists = on_core(
+            lambda a, b: (joined(a, b, upper(axis, bit)),),
+            [lists, swap(lists, axis, bit)],
+            [shape(2 * lists.shape[0], 2 * positions, LANES)],
+        )[0]
+    last = steps[-1]
+    lists = [lists, swap(lists, *last)]
 
     def list_of(values, prompt):
         blocks = []
@@ -197,7 +216,8 @@
         mine = slot_entry(iota((slots, kslots), 0)) == iota((slots, kslots), 1)
         return jnp.sum(jnp.where(mine, every, 0.0), axis=1, keepdims=True)
 
-    def choose(values):
+    def choose(mine, other):
+        values = joined(mine, other, upper(*last))
         feat, pos, _ = place()
         own = feat * poses + pos
         tables = []
@@ -229,7 +249,7 @@
 
     picks, gains, my_list = on_core(
         choose,
-        [lists],
+        lists,
         [
             shape(column, table_rows, dtype=BF16),
             shape(column, depth),
@@ -309,7 +329,7 @@
         own_mask = jnp.where(own_causal, own_mask, 0.0)
         return placing.astype(BF16), placing_t.astype(BF16), layer_row, mask.astype(BF16), own_mask
 
-    placing, placing_t, layer_row, mask, own_mask, ring[1][-1] = on_core(
+    placing, placing_t, layer_row, mask, own_mask, ring[1][0] = on_core(
         places,
         [my_list, block_pattern],
         [
@@ -320,7 +340,7 @@
             shape(result_rows, slots),
         ],
         small,
-        through=ring[1][-1:],
+        through=ring[1][:1],
         cost=(1, 1),
     )
     for _ in range(2, feats):

time: 63.4 us -> 65 us (1.025)
  blocking collectives: 13.9 us -> 0 us
  starting transfers between devices: 15 us -> 27 us
  waiting for transfers between devices: 20.9 us -> 24.4 us
  Pallas kernels: 9.23 us -> 7.87 us
  local copies, waits for them, and re-layouts: 3.28 us -> 4.64 us
    all_to_all x1 -> x0, blocking collectives: 13.9 us -> none  [per_device(): lax.all_to_all(packed, ('feat', 'pos'), split_axis=0, concat_axis=0, tile...]
    ppermute x0 -> x4, waiting for transfers between devices: none -> 7.8 us  [swap(): lax.ppermute(x, axis, [(i, i ^ bit) for i in range(lax.axis_size(axis))])]
    ppermute x0 -> x4, starting transfers between devices: none -> 7.35 us  [swap(): lax.ppermute(x, axis, [(i, i ^ bit) for i in range(lax.axis_size(axis))])]
    ppermute x2, starting transfers between devices: 1.09 us -> 5.28 us  [ring_next(): return lax.ppermute(x, (axis, across), pairs)]
    ppermute x4, waiting for transfers between devices: 7 us -> 4.76 us  [ring_next(): return lax.ppermute(x, axis, steps)]
    ppermute x2, waiting for transfers between devices: 4.46 us -> 2.32 us  [ring_next(): return lax.ppermute(x, (axis, across), pairs)]
    unnamed x8 -> x12, local copies, waits for them, and re-layouts: 3.28 us -> 4.64 us
    pallas_call x8 -> x9, Pallas kernels: 9.23 us -> 7.87 us  [on_core(): return list(call(*args, *streams, *through))]
  transfers between devices with their start and end apart: 16 -> 20, of which waited for: 10 -> 13; matrix products, arithmetic and copies ran while one was open for 0% -> 0% of each run, Pallas kernels for 5% -> 5%
where the time goes in v6:
time: 65 us; the launch traced here: 64.8 us
  starting transfers between devices  27 us (42%)
  waiting for transfers between devices  24.4 us (38%)
  Pallas kernels  7.87 us (12%)
  local copies, waits for them, and re-layouts  4.64 us (7%)
  between operations  0.75 us (1%)
    pallas_call x9, Pallas kernels, on_core(): return list(call(*args, *streams, *through))  7.87 us
    ppermute x4, waiting for transfers between devices, swap(): lax.ppermute(x, axis, [(i, i ^ bit) for i in range(lax.axis_size(axis))])  7.8 us
    ppermute x4, starting transfers between devices, swap(): lax.ppermute(x, axis, [(i, i ^ bit) for i in range(lax.axis_size(axis))])  7.35 us
    ppermute x4, starting transfers between devices, ring_next(): return lax.ppermute(x, axis, steps)  7.14 us
    ppermute x3, waiting for transfers between devices, ring_spread(): lax.ppermute(x, axis, [(order[i], order[(i + k) % count]) for i in range(...  6.9 us
    ppermute x2, starting transfers between devices, ring_next(): return lax.ppermute(x, (axis, across), pairs)  5.28 us
    ppermute x4, waiting for transfers between devices, ring_next(): return lax.ppermute(x, axis, steps)  4.76 us
    unnamed x12, local copies, waits for them, and re-layouts  4.64 us
  transfers between devices with their start and end apart: 20, of which 13 were waited for; matrix products, arithmetic and copies ran while one was open for 0% of the time, Pallas kernels for 5%

profile of v6, /device:TPU:0, one launch (start us, length us, event | category | flops | bytes accessed | tf_op | source)
XLA Modules:
  0.0 64.8 jit_solution(10609187400176703361)
XLA Ops:
  0.6 3.0 %collective-permute-start = (s32[1,4,28]{2,1,0:T(4,128)}, s32[1,4,28]{2,1,0:T(4,128)S(1)}, u32[]{:S(2)}, u32[]{:S(2)}) collective-permute-start(s32[1,4,28]{2,1,0:T(4,128)} %refs_0_.1), channel_id=1, source_target_pairs={{0,2},{2,0},{1,3},{3,1},{4,6},{6,4},{5,7},{7,5},{8,10},{10,8},{9,1... | collective-permute-start | bytes 1352 | tf_op jit(solution)/shard_map/ppermute | solution.py:92
  3.7 1.7 %collective-permute-done.refs_2_ = s32[1,4,28]{2,1,0:T(4,128)S(1)} collective-permute-done((s32[1,4,28]{2,1,0:T(4,128)}, s32[1,4,28]{2,1,0:T(4,128)S(1)}, u32[]{:S(2)}, u32[]{:S(2)}) %collective-permute-start) | collective-permute-done | bytes 480 | tf_op jit(solution)/shard_map/ppermute | solution.py:92
  5.4 2.0 %collective-permute-done.1.refs_3_ = f32[1,4,28]{2,1,0:T(4,128)S(1)} collective-permute-done((f32[1,4,28]{2,1,0:T(4,128)}, f32[1,4,28]{2,1,0:T(4,128)S(1)}, u32[]{:S(2)}, u32[]{:S(2)}) %collective-permute-start.1) | collective-permute-done | bytes 480 | tf_op jit(solution)/shard_map/ppermute | solution.py:92
  8.8 1.6 %collective-permute-start.2 = (f32[2,8,128]{2,1,0:T(8,128)S(1)}, f32[2,8,128]{2,1,0:T(8,128)S(1)}, u32[]{:S(2)}, u32[]{:S(2)}) collective-permute-start(f32[2,8,128]{2,1,0:T(8,128)S(1)} %shard_map.77.refs_0_), channel_id=1, source_target_pairs={{0,4},{4,0},{8,12},{12,8},{1,5},{5,1},{9,13},{13,9},{2,6},{6,2},{1... | collective-permute-start | bytes 24584 | tf_op jit(solution)/shard_map/ppermute | solution.py:92
  10.4 2.1 %collective-permute-done.2.refs_1_ = f32[2,8,128]{2,1,0:T(8,128)S(1)} collective-permute-done((f32[2,8,128]{2,1,0:T(8,128)S(1)}, f32[2,8,128]{2,1,0:T(8,128)S(1)}, u32[]{:S(2)}, u32[]{:S(2)}) %collective-permute-start.2) | collective-permute-done | bytes 8224 | tf_op jit(solution)/shard_map/ppermute | solution.py:92
  12.5 2.6 %collective-permute-start.3 = (f32[4,8,128]{2,1,0:T(8,128)S(1)}, f32[4,8,128]{2,1,0:T(8,128)S(1)}, u32[]{:S(2)}, u32[]{:S(2)}) collective-permute-start(f32[4,8,128]{2,1,0:T(8,128)S(1)} %shard_map.78.refs_0_), channel_id=1, source_target_pairs={{0,8},{4,12},{8,0},{12,4},{1,9},{5,13},{9,1},{13,5},{2,10},{6,14},... | collective-permute-start | bytes 49160 | tf_op jit(solution)/shard_map/ppermute | solution.py:92
  15.2 2.0 %collective-permute-done.3.refs_1_ = f32[4,8,128]{2,1,0:T(8,128)S(1)} collective-permute-done((f32[4,8,128]{2,1,0:T(8,128)S(1)}, f32[4,8,128]{2,1,0:T(8,128)S(1)}, u32[]{:S(2)}, u32[]{:S(2)}) %collective-permute-start.3) | collective-permute-done | bytes 16416 | tf_op jit(solution)/shard_map/ppermute | solution.py:92
  19.5 2.7 %collective-permute-start.4 = (bf16[80,1152]{1,0:T(8,128)(2,1)S(1)}, bf16[80,1152]{1,0:T(8,128)(2,1)S(1)}, u32[]{:S(2)}, u32[]{:S(2)}) collective-permute-start(bf16[80,1152]{1,0:T(8,128)(2,1)S(1)} %get-tuple-element.19.refs_2_), channel_id=1, source_target_pairs={{0,8},{2,10},{8,12},{10,14},{12,4},{14,6},{4,0},{6,2},{1,9},{3,11}... | collective-permute-start | bytes 552968 | tf_op jit(solution)/shard_map/ppermute | solution.py:108
  22.2 2.0 %copy-done = bf16[512,3,1152]{2,0,1:T(8,128)(2,1)S(1)} copy-done((bf16[512,3,1152]{2,0,1:T(8,128)(2,1)S(1)}, bf16[512,3,1152]{2,0,1:T(8,128)(2,1)}, u32[]{:S(2)}) %copy-start) | copy-done | bytes 3538968
  25.5 2.6 %collective-permute-start.6 = (bf16[80,1152]{1,0:T(8,128)(2,1)S(1)}, bf16[80,1152]{1,0:T(8,128)(2,1)S(1)}, u32[]{:S(2)}, u32[]{:S(2)}) collective-permute-start(bf16[80,1152]{1,0:T(8,128)(2,1)S(1)} %get-tuple-element.25), channel_id=1, source_target_pairs={{0,10},{2,8},{8,14},{10,12},{12,6},{14,4},{4,2},{6,0},{1,11},{3,9}... | collective-permute-start | bytes 552968 | tf_op jit(solution)/shard_map/ppermute | solution.py:108
  28.1 1.4 %shard_map.81 = (bf16[448,640]{1,0:T(8,128)(2,1)S(1)}, bf16[640,448]{1,0:T(8,128)(2,1)S(1)}, f32[1,640]{1,0:T(1,128)S(1)}, bf16[448,448]{1,0:T(8,128)(2,1)S(1)},...) custom-call(f32[32,28]{1,0:T(8,128)S(1)} %get-tuple-element.17.refs_0_, ...), custom_call_target="tpu_custom_call", output_to_operand_aliasing={{5}: (2, {})} | custom-call | flops 1 | bytes 1 | tf_op jit(solution)/shard_map/pallas_call | solution.py:83
  29.5 1.8 %collective-permute-start.7 = (bf16[80,1152]{1,0:T(8,128)(2,1)S(1)}, bf16[80,1152]{1,0:T(8,128)(2,1)S(1)}, u32[]{:S(2)}, u32[]{:S(2)}) collective-permute-start(bf16[80,1152]{1,0:T(8,128)(2,1)S(1)} %get-tuple-element.26.refs_4_), channel_id=1, source_target_pairs={{0,8},{8,12},{12,4},{4,0},{1,9},{9,13},{13,5},{5,1},{2,10},{10,14}... | collective-permute-start | bytes 552968 | tf_op jit(solution)/shard_map/ppermute | solution.py:105
  31.3 2.3 %collective-permute-done.6.refs_5_ = bf16[80,1152]{1,0:T(8,128)(2,1)S(1)} collective-permute-done((bf16[80,1152]{1,0:T(8,128)(2,1)S(1)}, bf16[80,1152]{1,0:T(8,128)(2,1)S(1)}, u32[]{:S(2)}, u32[]{:S(2)}) %collective-permute-start.6) | collective-permute-done | bytes 184352 | tf_op jit(solution)/shard_map/ppermute | solution.py:108
  34.6 2.1 %collective-permute-start.5 = (bf16[80,1152]{1,0:T(8,128)(2,1)S(1)}, bf16[80,1152]{1,0:T(8,128)(2,1)S(1)}, u32[]{:S(2)}, u32[]{:S(2)}) collective-permute-start(bf16[80,1152]{1,0:T(8,128)(2,1)S(1)} %get-tuple-element.25), channel_id=1, source_target_pairs={{0,2},{2,0},{1,3},{3,1},{4,6},{6,4},{5,7},{7,5},{8,10},{10,8},{9,1... | collective-permute-start | bytes 552968 | tf_op jit(solution)/shard_map/ppermute | solution.py:88
  37.6 2.2 %collective-permute-start.10 = (bf16[80,1152]{1,0:T(8,128)(2,1)S(1)}, bf16[80,1152]{1,0:T(8,128)(2,1)S(1)}, u32[]{:S(2)}, u32[]{:S(2)}) collective-permute-start(bf16[80,1152]{1,0:T(8,128)(2,1)S(1)} %collective-permute-done.7.refs_6_), channel_id=1, source_target_pairs={{0,8},{8,12},{12,4},{4,0},{1,9},{9,13},{13,5},{5,1},{2,10},{10,14}... | collective-permute-start | bytes 552968 | tf_op jit(solution)/shard_map/ppermute | solution.py:105
  39.8 1.8 %collective-permute-done.8.refs_7_ = bf16[80,1152]{1,0:T(8,128)(2,1)S(1)} collective-permute-done((bf16[80,1152]{1,0:T(8,128)(2,1)S(1)}, bf16[80,1152]{1,0:T(8,128)(2,1)S(1)}, u32[]{:S(2)}, u32[]{:S(2)}) %collective-permute-start.8) | collective-permute-done | bytes 184352 | tf_op jit(solution)/shard_map/ppermute | solution.py:105
  41.6 2.2 %collective-permute-start.11 = (bf16[80,1152]{1,0:T(8,128)(2,1)S(1)}, bf16[80,1152]{1,0:T(8,128)(2,1)S(1)}, u32[]{:S(2)}, u32[]{:S(2)}) collective-permute-start(bf16[80,1152]{1,0:T(8,128)(2,1)S(1)} %collective-permute-done.8.refs_7_), channel_id=1, source_target_pairs={{0,8},{8,12},{12,4},{4,0},{1,9},{9,13},{13,5},{5,1},{2,10},{10,14}... | collective-permute-start | bytes 552968 | tf_op jit(solution)/shard_map/ppermute | solution.py:105
  45.0 2.1 %collective-permute-done.11.refs_4_ = bf16[80,1152]{1,0:T(8,128)(2,1)S(1)} collective-permute-done((bf16[80,1152]{1,0:T(8,128)(2,1)S(1)}, bf16[80,1152]{1,0:T(8,128)(2,1)S(1)}, u32[]{:S(2)}, u32[]{:S(2)}) %collective-permute-start.11) | collective-permute-done | bytes 184352 | tf_op jit(solution)/shard_map/ppermute | solution.py:105
  48.1 1.4 %collective-permute-done.12 = f32[80,448]{1,0:T(8,128)S(1)} collective-permute-done((f32[80,448]{1,0:T(8,128)S(1)}, f32[80,448]{1,0:T(8,128)S(1)}, u32[]{:S(2)}, u32[]{:S(2)}) %collective-permute-start.12) | collective-permute-done | bytes 143392 | tf_op jit(solution)/shard_map/ppermute | solution.py:88
  49.5 3.1 %collective-permute-start.13 = (bf16[80,448]{1,0:T(8,128)(2,1)S(1)}, bf16[80,448]{1,0:T(8,128)(2,1)S(1)}, u32[]{:S(2)}, u32[]{:S(2)}) collective-permute-start(bf16[80,448]{1,0:T(8,128)(2,1)S(1)} %add_convert_fusion.refs_4_), channel_id=1, source_target_pairs={{0,8},{8,12},{12,4},{4,0},{1,9},{9,13},{13,5},{5,1},{2,10},{10,14}... | collective-permute-start | bytes 215048 | tf_op jit(solution)/shard_map/ppermute | solution.py:115
  54.0 1.4 %collective-permute-done.13.refs_5_ = bf16[80,448]{1,0:T(8,128)(2,1)S(1)} collective-permute-done((bf16[80,448]{1,0:T(8,128)(2,1)S(1)}, bf16[80,448]{1,0:T(8,128)(2,1)S(1)}, u32[]{:S(2)}, u32[]{:S(2)}) %collective-permute-start.13) | collective-permute-done | bytes 71712 | tf_op jit(solution)/shard_map/ppermute | solution.py:115
  55.5 4.1 %collective-permute-done.14.refs_6_ = bf16[80,448]{1,0:T(8,128)(2,1)S(1)} collective-permute-done((bf16[80,448]{1,0:T(8,128)(2,1)S(1)}, bf16[80,448]{1,0:T(8,128)(2,1)S(1)}, u32[]{:S(2)}, u32[]{:S(2)}) %collective-permute-start.14) | collective-permute-done | bytes 71712 | tf_op jit(solution)/shard_map/ppermute | solution.py:115
  59.6 1.4 %collective-permute-done.15.refs_7_ = bf16[80,448]{1,0:T(8,128)(2,1)S(1)} collective-permute-done((bf16[80,448]{1,0:T(8,128)(2,1)S(1)}, bf16[80,448]{1,0:T(8,128)(2,1)S(1)}, u32[]{:S(2)}, u32[]{:S(2)}) %collective-permute-start.15) | collective-permute-done | bytes 71712 | tf_op jit(solution)/shard_map/ppermute | solution.py:115
  62.2 2.5 %shard_map.85 = (bf16[1,56,448]{2,1,0:T(8,128)(2,1)}, f32[1,56,128]{2,1,0:T(8,128)}) custom-call(bf16[448,640]{1,0:T(8,128)(2,1)S(1)} %get-tuple-element.20.refs_0_, bf16[448,448]{1,0:T(8,128)(2,1)S(1)} %get-tuple-element.21.refs_1_, f32[56,448]{1,0:T(8,128)S(1)} %get-tuple-element.22.refs_2_, s32[1,128]{1,0:T(1,128)S(1)} %copy-done.5, ...), custom_call_target="tpu_custom_call" | custom-call | tf_op jit(solution)/shard_map/pallas_call | solution.py:83
  (38 shorter events, 11.9 us)
Async XLA Ops:
  0.6 27.5 %copy-start.2 = (s32[1,4,4]{2,1,0:T(4,128)S(1)}, s32[1,4,4]{2,1,0:T(4,128)}, u32[]{:S(2)}) copy-start(s32[1,4,4]{2,1,0:T(4,128)} %refs_1_.5) | copy-start | bytes 196
  0.6 4.8 %collective-permute-start = (s32[1,4,28]{2,1,0:T(4,128)}, s32[1,4,28]{2,1,0:T(4,128)S(1)}, u32[]{:S(2)}, u32[]{:S(2)}) collective-permute-start(s32[1,4,28]{2,1,0:T(4,128)} %refs_0_.1), channel_id=1, source_target_pairs={{0,2},{2,0},{1,3},{3,1},{4,6},{6,4},{5,7},{7,5},{8,10},{10,8},{9,1... | collective-permute-start | bytes 1352 | tf_op jit(solution)/shard_map/ppermute | solution.py:92
  3.6 3.8 %collective-permute-start.1 = (f32[1,4,28]{2,1,0:T(4,128)}, f32[1,4,28]{2,1,0:T(4,128)S(1)}, u32[]{:S(2)}, u32[]{:S(2)}) collective-permute-start(f32[1,4,28]{2,1,0:T(4,128)} %refs_1_.3), channel_id=1, source_target_pairs={{0,2},{2,0},{1,3},{3,1},{4,6},{6,4},{5,7},{7,5},{8,10},{10,8},{9,1... | collective-permute-start | bytes 1352 | tf_op jit(solution)/shard_map/ppermute | solution.py:92
  8.8 3.7 %collective-permute-start.2 = (f32[2,8,128]{2,1,0:T(8,128)S(1)}, f32[2,8,128]{2,1,0:T(8,128)S(1)}, u32[]{:S(2)}, u32[]{:S(2)}) collective-permute-start(f32[2,8,128]{2,1,0:T(8,128)S(1)} %shard_map.77.refs_0_), channel_id=1, source_target_pairs={{0,4},{4,0},{8,12},{12,8},{1,5},{5,1},{9,13},{13,9},{2,6},{6,2},{1... | collective-permute-start | bytes 24584 | tf_op jit(solution)/shard_map/ppermute | solution.py:92
  12.5 4.6 %collective-permute-start.3 = (f32[4,8,128]{2,1,0:T(8,128)S(1)}, f32[4,8,128]{2,1,0:T(8,128)S(1)}, u32[]{:S(2)}, u32[]{:S(2)}) collective-permute-start(f32[4,8,128]{2,1,0:T(8,128)S(1)} %shard_map.78.refs_0_), channel_id=1, source_target_pairs={{0,8},{4,12},{8,0},{12,4},{1,9},{5,13},{9,1},{13,5},{2,10},{6,14},... | collective-permute-start | bytes 49160 | tf_op jit(solution)/shard_map/ppermute | solution.py:92
  17.8 1.3 %copy-start.1 = (bf16[512,1152]{1,0:T(8,128)(2,1)S(1)}, bf16[512,1152]{1,0:T(8,128)(2,1)}, u32[]{:S(2)}) copy-start(bf16[512,1152]{1,0:T(8,128)(2,1)} %refs_1_.4) | copy-start | bytes 3538948
  19.5 8.7 %collective-permute-start.4 = (bf16[80,1152]{1,0:T(8,128)(2,1)S(1)}, bf16[80,1152]{1,0:T(8,128)(2,1)S(1)}, u32[]{:S(2)}, u32[]{:S(2)}) collective-permute-start(bf16[80,1152]{1,0:T(8,128)(2,1)S(1)} %get-tuple-element.19.refs_2_), channel_id=1, source_target_pairs={{0,8},{2,10},{8,12},{10,14},{12,4},{14,6},{4,0},{6,2},{1,9},{3,11}... | collective-permute-start | bytes 552968 | tf_op jit(solution)/shard_map/ppermute | solution.py:108
  22.2 2.0 %copy-start = (bf16[512,3,1152]{2,0,1:T(8,128)(2,1)S(1)}, bf16[512,3,1152]{2,0,1:T(8,128)(2,1)}, u32[]{:S(2)}) copy-start(bf16[512,3,1152]{2,0,1:T(8,128)(2,1)} %param.11) | copy-start | bytes 10616836
  25.0 37.3 %copy-start.5 = (s32[1,128]{1,0:T(1,128)S(1)}, s32[1,128]{1,0:T(1,128)}, u32[]{:S(2)}) copy-start(s32[1,128]{1,0:T(1,128)} %refs_3_.1) | copy-start | bytes 1540
  25.0 18.8 %collective-permute-start.9 = (bf16[3,80,1152]{2,1,0:T(8,128)(2,1)S(1)}, bf16[3,80,1152]{2,1,0:T(8,128)(2,1)S(1)}, u32[]{:S(2)}, u32[]{:S(2)}) collective-permute-start(bf16[3,80,1152]{2,1,0:T(8,128)(2,1)S(1)} %get-tuple-element.29), channel_id=1, source_target_pairs={{0,2},{2,0},{1,3},{3,1},{4,6},{6,4},{5,7},{7,5},{8,10},{10,8},{9,1... | collective-permute-start | bytes 1658888 | tf_op jit(solution)/shard_map/ppermute | solution.py:88
  25.5 8.1 %collective-permute-start.6 = (bf16[80,1152]{1,0:T(8,128)(2,1)S(1)}, bf16[80,1152]{1,0:T(8,128)(2,1)S(1)}, u32[]{:S(2)}, u32[]{:S(2)}) collective-permute-start(bf16[80,1152]{1,0:T(8,128)(2,1)S(1)} %get-tuple-element.25), channel_id=1, source_target_pairs={{0,10},{2,8},{8,14},{10,12},{12,6},{14,4},{4,2},{6,0},{1,11},{3,9}... | collective-permute-start | bytes 552968 | tf_op jit(solution)/shard_map/ppermute | solution.py:108
  29.5 8.1 %collective-permute-start.7 = (bf16[80,1152]{1,0:T(8,128)(2,1)S(1)}, bf16[80,1152]{1,0:T(8,128)(2,1)S(1)}, u32[]{:S(2)}, u32[]{:S(2)}) collective-permute-start(bf16[80,1152]{1,0:T(8,128)(2,1)S(1)} %get-tuple-element.26.refs_4_), channel_id=1, source_target_pairs={{0,8},{8,12},{12,4},{4,0},{1,9},{9,13},{13,5},{5,1},{2,10},{10,14}... | collective-permute-start | bytes 552968 | tf_op jit(solution)/shard_map/ppermute | solution.py:105
  33.6 8.0 %collective-permute-start.8 = (bf16[80,1152]{1,0:T(8,128)(2,1)S(1)}, bf16[80,1152]{1,0:T(8,128)(2,1)S(1)}, u32[]{:S(2)}, u32[]{:S(2)}) collective-permute-start(bf16[80,1152]{1,0:T(8,128)(2,1)S(1)} %collective-permute-done.6.refs_5_), channel_id=1, source_target_pairs={{0,8},{8,12},{12,4},{4,0},{1,9},{9,13},{13,5},{5,1},{2,10},{10,14}... | collective-permute-start | bytes 552968 | tf_op jit(solution)/shard_map/ppermute | solution.py:105
  34.6 9.1 %collective-permute-start.5 = (bf16[80,1152]{1,0:T(8,128)(2,1)S(1)}, bf16[80,1152]{1,0:T(8,128)(2,1)S(1)}, u32[]{:S(2)}, u32[]{:S(2)}) collective-permute-start(bf16[80,1152]{1,0:T(8,128)(2,1)S(1)} %get-tuple-element.25), channel_id=1, source_target_pairs={{0,2},{2,0},{1,3},{3,1},{4,6},{6,4},{5,7},{7,5},{8,10},{10,8},{9,1... | collective-permute-start | bytes 552968 | tf_op jit(solution)/shard_map/ppermute | solution.py:88
  37.6 7.4 %collective-permute-start.10 = (bf16[80,1152]{1,0:T(8,128)(2,1)S(1)}, bf16[80,1152]{1,0:T(8,128)(2,1)S(1)}, u32[]{:S(2)}, u32[]{:S(2)}) collective-permute-start(bf16[80,1152]{1,0:T(8,128)(2,1)S(1)} %collective-permute-done.7.refs_6_), channel_id=1, source_target_pairs={{0,8},{8,12},{12,4},{4,0},{1,9},{9,13},{13,5},{5,1},{2,10},{10,14}... | collective-permute-start | bytes 552968 | tf_op jit(solution)/shard_map/ppermute | solution.py:105
  41.6 5.5 %collective-permute-start.11 = (bf16[80,1152]{1,0:T(8,128)(2,1)S(1)}, bf16[80,1152]{1,0:T(8,128)(2,1)S(1)}, u32[]{:S(2)}, u32[]{:S(2)}) collective-permute-start(bf16[80,1152]{1,0:T(8,128)(2,1)S(1)} %collective-permute-done.8.refs_7_), channel_id=1, source_target_pairs={{0,8},{8,12},{12,4},{4,0},{1,9},{9,13},{13,5},{5,1},{2,10},{10,14}... | collective-permute-start | bytes 552968 | tf_op jit(solution)/shard_map/ppermute | solution.py:105
  48.1 1.5 %collective-permute-start.12 = (f32[80,448]{1,0:T(8,128)S(1)}, f32[80,448]{1,0:T(8,128)S(1)}, u32[]{:S(2)}, u32[]{:S(2)}) collective-permute-start(f32[80,448]{1,0:T(8,128)S(1)} %get-tuple-element.31), channel_id=1, source_target_pairs={{0,1},{1,0},{2,3},{3,2},{4,5},{5,4},{6,7},{7,6},{8,9},{9,8},{10,11... | collective-permute-start | bytes 430088 | tf_op jit(solution)/shard_map/ppermute | solution.py:88
  49.5 5.9 %collective-permute-start.13 = (bf16[80,448]{1,0:T(8,128)(2,1)S(1)}, bf16[80,448]{1,0:T(8,128)(2,1)S(1)}, u32[]{:S(2)}, u32[]{:S(2)}) collective-permute-start(bf16[80,448]{1,0:T(8,128)(2,1)S(1)} %add_convert_fusion.refs_4_), channel_id=1, source_target_pairs={{0,8},{8,12},{12,4},{4,0},{1,9},{9,13},{13,5},{5,1},{2,10},{10,14}... | collective-permute-start | bytes 215048 | tf_op jit(solution)/shard_map/ppermute | solution.py:115
  52.7 6.9 %collective-permute-start.14 = (bf16[80,448]{1,0:T(8,128)(2,1)S(1)}, bf16[80,448]{1,0:T(8,128)(2,1)S(1)}, u32[]{:S(2)}, u32[]{:S(2)}) collective-permute-start(bf16[80,448]{1,0:T(8,128)(2,1)S(1)} %add_convert_fusion.refs_4_), channel_id=1, source_target_pairs={{0,12},{8,4},{12,0},{4,8},{1,13},{9,5},{13,1},{5,9},{2,14},{10,6},... | collective-permute-start | bytes 215048 | tf_op jit(solution)/shard_map/ppermute | solution.py:115
  54.0 6.9 %collective-permute-start.15 = (bf16[80,448]{1,0:T(8,128)(2,1)S(1)}, bf16[80,448]{1,0:T(8,128)(2,1)S(1)}, u32[]{:S(2)}, u32[]{:S(2)}) collective-permute-start(bf16[80,448]{1,0:T(8,128)(2,1)S(1)} %add_convert_fusion.refs_4_), channel_id=1, source_target_pairs={{0,4},{8,0},{12,8},{4,12},{1,5},{9,1},{13,9},{5,13},{2,6},{10,2},{... | collective-permute-start | bytes 215048 | tf_op jit(solution)/shard_map/ppermute | solution.py:115
  54.0 6.9 %collective-permute-start.16 = (bf16[80,448]{1,0:T(8,128)(2,1)S(1)}, bf16[80,448]{1,0:T(8,128)(2,1)S(1)}, u32[]{:S(2)}, u32[]{:S(2)}) collective-permute-start(bf16[80,448]{1,0:T(8,128)(2,1)S(1)} %add_convert_fusion.refs_4_), channel_id=1, source_target_pairs={{0,1},{1,0},{2,3},{3,2},{4,5},{5,4},{6,7},{7,6},{8,9},{9,8},{10,11... | collective-permute-start | bytes 215048 | tf_op jit(solution)/shard_map/ppermute | solution.py:88
  55.5 5.5 %collective-permute-start.17 = (bf16[80,448]{1,0:T(8,128)(2,1)S(1)}, bf16[80,448]{1,0:T(8,128)(2,1)S(1)}, u32[]{:S(2)}, u32[]{:S(2)}) collective-permute-start(bf16[80,448]{1,0:T(8,128)(2,1)S(1)} %collective-permute-done.13.refs_5_), channel_id=1, source_target_pairs={{0,1},{1,0},{2,3},{3,2},{4,5},{5,4},{6,7},{7,6},{8,9},{9,8},{10,11... | collective-permute-start | bytes 215048 | tf_op jit(solution)/shard_map/ppermute | solution.py:88
  59.6 1.4 %collective-permute-start.18 = (bf16[80,448]{1,0:T(8,128)(2,1)S(1)}, bf16[80,448]{1,0:T(8,128)(2,1)S(1)}, u32[]{:S(2)}, u32[]{:S(2)}) collective-permute-start(bf16[80,448]{1,0:T(8,128)(2,1)S(1)} %collective-permute-done.14.refs_6_), channel_id=1, source_target_pairs={{0,1},{1,0},{2,3},{3,2},{4,5},{5,4},{6,7},{7,6},{8,9},{9,8},{10,11... | collective-permute-start | bytes 215048 | tf_op jit(solution)/shard_map/ppermute | solution.py:88
  60.9 1.3 %collective-permute-start.19 = (bf16[80,448]{1,0:T(8,128)(2,1)S(1)}, bf16[80,448]{1,0:T(8,128)(2,1)S(1)}, u32[]{:S(2)}, u32[]{:S(2)}) collective-permute-start(bf16[80,448]{1,0:T(8,128)(2,1)S(1)} %collective-permute-done.15.refs_7_), channel_id=1, source_target_pairs={{0,1},{1,0},{2,3},{3,2},{4,5},{5,4},{6,7},{7,6},{8,9},{9,8},{10,11... | collective-permute-start | bytes 215048 | tf_op jit(solution)/shard_map/ppermute | solution.py:88
  (2 other events, 1.4 us)

commit v7 on v5

--- a/solution.py
+++ b/solution.py
@@ -238,31 +238,17 @@
         small,
     )
 
-    def encode(picks, enc):
-        rows = dot(picks, enc).astype(BF16)
-        return [rows[k * listed : (k + 1) * listed] for k in range(poses)]
-
-    enc_rows = on_core(
-        encode, [picks, encoder], [shape(listed, width, dtype=BF16)] * poses, small
-    )
+    enc_rows = dot(picks, encoder).astype(BF16)
+    enc_rows = [enc_rows[k * listed : (k + 1) * listed] for k in range(poses)]
 
     ring = [[enc_rows[0]] + [rotate(enc_rows[k], "pos", k) for k in range(1, poses)]]
     ring.append([ring_next(enc_rows[k], "feat", "pos", k) for k in range(poses)])
 
-    def decode(picks, gains, dec):
-        rows = [(dot(picks, dec[l]) * gains[:, l : l + 1]).astype(BF16) for l in range(depth)]
-        return [
-            jnp.stack([row[k * listed : (k + 1) * listed] for row in rows], axis=0)
-            for k in range(poses)
-        ]
-
-    dec_rows = on_core(
-        decode,
-        [picks, gains, jnp.transpose(decoder, (1, 0, 2))],
-        [shape(depth, listed, width, dtype=BF16)] * poses,
-        small,
-        cost=(1, 1),
-    )
+    dec_rows = lax.dot_general(
+        picks, decoder, (((1,), (0,)), ((), ())), preferred_element_type=F32
+    )
+    dec_rows = (jnp.transpose(dec_rows, (1, 0, 2)) * gains.T[:, :, None]).astype(BF16)
+    dec_rows = [dec_rows[:, k * listed : (k + 1) * listed] for k in range(poses)]
     dec_rows = [dec_rows[0]] + [rotate(dec_rows[k], "pos", k) for k in range(1, poses)]
 
     def places(table, pattern):

time: 63.4 us -> 63.1 us (level)
  matrix products: 0 us -> 2.58 us
  waiting for transfers between devices: 20.9 us -> 19.2 us
  Pallas kernels: 9.23 us -> 8.16 us
    ppermute x4, waiting for transfers between devices: 7 us -> 4.09 us  [ring_next(): return lax.ppermute(x, axis, steps)]
    dot_general x0 -> x2, matrix products: none -> 2.58 us  [the longest x1 1.77 us: dot(): return lax.dot_general(a, b, dims, preferred_element_type=F32)]
    unnamed x8 -> x14, local copies, waits for them, and re-layouts: 3.28 us -> 1.32 us
    transpose x0 -> x1, local copies, waits for them, and re-layouts: none -> 1.56 us  [per_device(): gains.T[:, :, None]]
    ppermute x2, waiting for transfers between devices: 4.46 us -> 5.89 us  [ring_next(): return lax.ppermute(x, (axis, across), pairs)]
    ppermute x3, starting transfers between devices: 5.34 us -> 4.1 us  [ring_spread(): lax.ppermute(x, axis, [(order[i], order[(i + k) % count]) for i in range(...]
    ppermute x3, waiting for transfers between devices: 6.77 us -> 5.67 us  [ring_spread(): lax.ppermute(x, axis, [(order[i], order[(i + k) % count]) for i in range(...]
    pallas_call x8 -> x6, Pallas kernels: 9.23 us -> 8.16 us  [on_core(): return list(call(*args, *streams, *through))]
  transfers between devices with their start and end apart: 16 -> 16, of which waited for: 10 -> 11; matrix products, arithmetic and copies ran while one was open for 0% -> 1% of each run, Pallas kernels for 5% -> 4%
where the time goes in v7:
time: 63.1 us; the launch traced here: 62.9 us
  waiting for transfers between devices  19.2 us (30%)
  starting transfers between devices  15.2 us (24%)
  blocking collectives  13.9 us (22%)
  Pallas kernels  8.16 us (13%)
  local copies, waits for them, and re-layouts  2.99 us (5%)
  matrix products  2.58 us (4%)
  between operations  0.77 us (1%)
    all_to_all x1, blocking collectives, per_device(): lax.all_to_all(packed, ('feat', 'pos'), split_axis=0, concat_axis=0, tile...  13.9 us
    pallas_call x6, Pallas kernels, on_core(): return list(call(*args, *streams, *through))  8.16 us
    ppermute x4, starting transfers between devices, ring_next(): return lax.ppermute(x, axis, steps)  6.62 us
    ppermute x2, waiting for transfers between devices, ring_next(): return lax.ppermute(x, (axis, across), pairs)  5.89 us
    ppermute x3, waiting for transfers between devices, ring_spread(): lax.ppermute(x, axis, [(order[i], order[(i + k) % count]) for i in range(...  5.67 us
    ppermute x3, starting transfers between devices, ring_spread(): lax.ppermute(x, axis, [(order[i], order[(i + k) % count]) for i in range(...  4.1 us
    ppermute x4, waiting for transfers between devices, ring_next(): return lax.ppermute(x, axis, steps)  4.09 us
    ppermute x7, waiting for transfers between devices, rotate(): lax.ppermute(x, axis, [(i, (i + step) % count) for i in range(count)])  3.58 us
  transfers between devices with their start and end apart: 16, of which 11 were waited for; matrix products, arithmetic and copies ran while one was open for 1% of the time, Pallas kernels for 4%

profile of v7, /device:TPU:0, one launch (start us, length us, event | category | flops | bytes accessed | tf_op | source)
XLA Modules:
  0.0 62.9 jit_solution(14842577007727328407)
XLA Ops:
  0.6 1.5 %shard_map.77 = f32[8,8,128]{2,1,0:T(8,128)} custom-call(s32[1,4,28]{2,1,0:T(4,128)} %refs_0_.1, f32[1,4,28]{2,1,0:T(4,128)} %refs_1_.2), custom_call_target="tpu_custom_call" | custom-call | tf_op jit(solution)/shard_map/pallas_call | solution.py:83
  2.1 13.9 %all_to_all.5.refs_0_ = f32[8,8,128]{2,1,0:T(8,128)S(1)} all-to-all(f32[8,8,128]{2,1,0:T(8,128)} %shard_map.77), channel_id=1, replica_groups=mesh['grp'=2,'feat'=4,'pos'=2,'rep'=2] {'feat','pos'}, dimensions={0} | all-to-all | bytes 65536 | tf_op jit(solution)/shard_map/all_to_all | solution.py:159
  18.0 1.6 %copy.9 = f32[3,160]{1,0:T(4,128)} copy(f32[3,160]{0,1:T(8,128)} %bitcast.13) | data formatting | bytes 3840 | tf_op jit(solution)/shard_map/transpose | solution.py:250
  19.6 1.8 %convolution_convert_fusion = bf16[160,1152]{1,0:T(8,128)(2,1)S(1)} fusion(bf16[160,512]{1,0:T(8,128)(2,1)} %copy-done.1, bf16[512,1152]{1,0:T(8,128)(2,1)} %param.10), kind=kOutput, calls=%fused_computation.3 | convolution fusion | flops 188928000 | bytes 1712128 | tf_op jit(solution)/shard_map/dot_general | solution.py:18
  23.6 1.4 %collective-permute-start.5 = (bf16[3,80,1152]{2,1,0:T(8,128)(2,1)S(1)}, bf16[3,80,1152]{2,1,0:T(8,128)(2,1)S(1)}, u32[]{:S(2)}, u32[]{:S(2)}) collective-permute-start(bf16[3,80,1152]{2,1,0:T(8,128)(2,1)S(1)} %get-tuple-element.24), channel_id=1, source_target_pairs={{0,2},{2,0},{1,3},{3,1},{4,6},{6,4},{5,7},{7,5},{8,10},{10,8},{9,1... | collective-permute-start | bytes 1658888 | tf_op jit(solution)/shard_map/ppermute | solution.py:88
  25.0 4.0 %collective-permute-done.2.refs_4_ = bf16[80,1152]{1,0:T(8,128)(2,1)S(1)} collective-permute-done((bf16[80,1152]{1,0:T(8,128)(2,1)S(1)}, bf16[80,1152]{1,0:T(8,128)(2,1)S(1)}, u32[]{:S(2)}, u32[]{:S(2)}) %collective-permute-start.2) | collective-permute-done | bytes 184352 | tf_op jit(solution)/shard_map/ppermute | solution.py:104
  29.0 1.4 %collective-permute-start.3 = (bf16[80,1152]{1,0:T(8,128)(2,1)S(1)}, bf16[80,1152]{1,0:T(8,128)(2,1)S(1)}, u32[]{:S(2)}, u32[]{:S(2)}) collective-permute-start(bf16[80,1152]{1,0:T(8,128)(2,1)S(1)} %collective-permute-done.2.refs_4_), channel_id=1, source_target_pairs={{0,8},{8,12},{12,4},{4,0},{1,9},{9,13},{13,5},{5,1},{2,10},{10,14}... | collective-permute-start | bytes 552968 | tf_op jit(solution)/shard_map/ppermute | solution.py:101
  30.4 1.9 %collective-permute-done.refs_2_ = bf16[80,1152]{1,0:T(8,128)(2,1)S(1)} collective-permute-done((bf16[80,1152]{1,0:T(8,128)(2,1)S(1)}, bf16[80,1152]{1,0:T(8,128)(2,1)S(1)}, u32[]{:S(2)}, u32[]{:S(2)}) %collective-permute-start) | collective-permute-done | bytes 184352 | tf_op jit(solution)/shard_map/ppermute | solution.py:104
  32.3 1.4 %shard_map.79 = (bf16[448,640]{1,0:T(8,128)(2,1)S(1)}, bf16[640,448]{1,0:T(8,128)(2,1)S(1)}, f32[1,640]{1,0:T(1,128)S(1)}, bf16[448,448]{1,0:T(8,128)(2,1)S(1)},...) custom-call(f32[32,28]{1,0:T(8,128)S(1)} %get-tuple-element.13.refs_0_, ...), custom_call_target="tpu_custom_call", output_to_operand_aliasing={{5}: (2, {})} | custom-call | flops 1 | bytes 1 | tf_op jit(solution)/shard_map/pallas_call | solution.py:83
  33.7 1.8 %collective-permute-start.4 = (bf16[80,1152]{1,0:T(8,128)(2,1)S(1)}, bf16[80,1152]{1,0:T(8,128)(2,1)S(1)}, u32[]{:S(2)}, u32[]{:S(2)}) collective-permute-start(bf16[80,1152]{1,0:T(8,128)(2,1)S(1)} %get-tuple-element.20.refs_5_), channel_id=1, source_target_pairs={{0,8},{8,12},{12,4},{4,0},{1,9},{9,13},{13,5},{5,1},{2,10},{10,14}... | collective-permute-start | bytes 552968 | tf_op jit(solution)/shard_map/ppermute | solution.py:101
  35.5 1.6 %collective-permute-start.1 = (bf16[80,1152]{1,0:T(8,128)(2,1)S(1)}, bf16[80,1152]{1,0:T(8,128)(2,1)S(1)}, u32[]{:S(2)}, u32[]{:S(2)}) collective-permute-start(bf16[80,1152]{1,0:T(8,128)(2,1)S(1)} %get-tuple-element.27), channel_id=1, source_target_pairs={{0,2},{2,0},{1,3},{3,1},{4,6},{6,4},{5,7},{7,5},{8,10},{10,8},{9,1... | collective-permute-start | bytes 552968 | tf_op jit(solution)/shard_map/ppermute | solution.py:88
  37.0 1.8 %collective-permute-start.6 = (bf16[80,1152]{1,0:T(8,128)(2,1)S(1)}, bf16[80,1152]{1,0:T(8,128)(2,1)S(1)}, u32[]{:S(2)}, u32[]{:S(2)}) collective-permute-start(bf16[80,1152]{1,0:T(8,128)(2,1)S(1)} %collective-permute-done.3.refs_6_), channel_id=1, source_target_pairs={{0,8},{8,12},{12,4},{4,0},{1,9},{9,13},{13,5},{5,1},{2,10},{10,14}... | collective-permute-start | bytes 552968 | tf_op jit(solution)/shard_map/ppermute | solution.py:101
  38.8 2.5 %collective-permute-done.4.refs_7_ = bf16[80,1152]{1,0:T(8,128)(2,1)S(1)} collective-permute-done((bf16[80,1152]{1,0:T(8,128)(2,1)S(1)}, bf16[80,1152]{1,0:T(8,128)(2,1)S(1)}, u32[]{:S(2)}, u32[]{:S(2)}) %collective-permute-start.4) | collective-permute-done | bytes 184352 | tf_op jit(solution)/shard_map/ppermute | solution.py:101
  41.3 1.7 %collective-permute-start.7 = (bf16[80,1152]{1,0:T(8,128)(2,1)S(1)}, bf16[80,1152]{1,0:T(8,128)(2,1)S(1)}, u32[]{:S(2)}, u32[]{:S(2)}) collective-permute-start(bf16[80,1152]{1,0:T(8,128)(2,1)S(1)} %collective-permute-done.4.refs_7_), channel_id=1, source_target_pairs={{0,8},{8,12},{12,4},{4,0},{1,9},{9,13},{13,5},{5,1},{2,10},{10,14}... | collective-permute-start | bytes 552968 | tf_op jit(solution)/shard_map/ppermute | solution.py:101
  43.0 1.1 %collective-permute-done.1.refs_3_ = bf16[80,1152]{1,0:T(8,128)(2,1)S(1)} collective-permute-done((bf16[80,1152]{1,0:T(8,128)(2,1)S(1)}, bf16[80,1152]{1,0:T(8,128)(2,1)S(1)}, u32[]{:S(2)}, u32[]{:S(2)}) %collective-permute-start.1) | collective-permute-done | bytes 184352 | tf_op jit(solution)/shard_map/ppermute | solution.py:88
  44.1 1.2 %shard_map.80.refs_0_ = f32[160,448]{1,0:T(8,128)S(1)} custom-call(f32[1,640]{1,0:T(1,128)S(1)} %get-tuple-element.18.refs_0_.refs_1_, bf16[640,448]{1,0:T(8,128)(2,1)S(1)} %get-tuple-element.19.refs_1_.refs_2_, bf16[80,1152]{1,0:T(8,128)(2,1)S(1)} %get-tuple-element.26.refs_2_, bf16[80,1152]{1,0:T(8,128)(2,1)S(1)} %collective-permute-done.1.refs_3_, ...), custom_call_target="tpu_custom_call" | custom-call | flops 1 | bytes 1 | tf_op jit(solution)/shard_map/pallas_call | solution.py:83
  45.3 1.5 %collective-permute-done.7.refs_4_ = bf16[80,1152]{1,0:T(8,128)(2,1)S(1)} collective-permute-done((bf16[80,1152]{1,0:T(8,128)(2,1)S(1)}, bf16[80,1152]{1,0:T(8,128)(2,1)S(1)}, u32[]{:S(2)}, u32[]{:S(2)}) %collective-permute-start.7) | collective-permute-done | bytes 184352 | tf_op jit(solution)/shard_map/ppermute | solution.py:101
  46.9 0.9 %shard_map.81 = (f32[80,448]{1,0:T(8,128)S(1)}, f32[80,448]{1,0:T(8,128)S(1)}) custom-call(f32[160,448]{1,0:T(8,128)S(1)} %shard_map.80.refs_0_, f32[1,640]{1,0:T(1,128)S(1)} %get-tuple-element.18.refs_0_.refs_1_, bf16[640,448]{1,0:T(8,128)(2,1)S(1)} %get-tuple-element.19.refs_1_.refs_2_, bf16[80,1152]{1,0:T(8,128)(2,1)S(1)} %collective-permute-done.6.refs_3_, ...), custom_call_target="tpu_custom_call" | custom-call | tf_op jit(solution)/shard_map/pallas_call | solution.py:83
  47.9 1.4 %collective-permute-done.8 = f32[80,448]{1,0:T(8,128)S(1)} collective-permute-done((f32[80,448]{1,0:T(8,128)S(1)}, f32[80,448]{1,0:T(8,128)S(1)}, u32[]{:S(2)}, u32[]{:S(2)}) %collective-permute-start.8) | collective-permute-done | bytes 143392 | tf_op jit(solution)/shard_map/ppermute | solution.py:88
  49.3 2.4 %collective-permute-start.11 = (bf16[80,448]{1,0:T(8,128)(2,1)S(1)}, bf16[80,448]{1,0:T(8,128)(2,1)S(1)}, u32[]{:S(2)}, u32[]{:S(2)}) collective-permute-start(bf16[80,448]{1,0:T(8,128)(2,1)S(1)} %add_convert_fusion.refs_4_), channel_id=1, source_target_pairs={{0,4},{8,0},{12,8},{4,12},{1,5},{9,1},{13,9},{5,13},{2,6},{10,2},{... | collective-permute-start | bytes 215048 | tf_op jit(solution)/shard_map/ppermute | solution.py:111
  51.7 1.7 %collective-permute-start.10 = (bf16[80,448]{1,0:T(8,128)(2,1)S(1)}, bf16[80,448]{1,0:T(8,128)(2,1)S(1)}, u32[]{:S(2)}, u32[]{:S(2)}) collective-permute-start(bf16[80,448]{1,0:T(8,128)(2,1)S(1)} %add_convert_fusion.refs_4_), channel_id=1, source_target_pairs={{0,12},{8,4},{12,0},{4,8},{1,13},{9,5},{13,1},{5,9},{2,14},{10,6},... | collective-permute-start | bytes 215048 | tf_op jit(solution)/shard_map/ppermute | solution.py:111
  53.4 2.1 %collective-permute-done.11.refs_7_ = bf16[80,448]{1,0:T(8,128)(2,1)S(1)} collective-permute-done((bf16[80,448]{1,0:T(8,128)(2,1)S(1)}, bf16[80,448]{1,0:T(8,128)(2,1)S(1)}, u32[]{:S(2)}, u32[]{:S(2)}) %collective-permute-start.11) | collective-permute-done | bytes 71712 | tf_op jit(solution)/shard_map/ppermute | solution.py:111
  55.5 3.2 %collective-permute-done.10.refs_6_ = bf16[80,448]{1,0:T(8,128)(2,1)S(1)} collective-permute-done((bf16[80,448]{1,0:T(8,128)(2,1)S(1)}, bf16[80,448]{1,0:T(8,128)(2,1)S(1)}, u32[]{:S(2)}, u32[]{:S(2)}) %collective-permute-start.10) | collective-permute-done | bytes 71712 | tf_op jit(solution)/shard_map/ppermute | solution.py:111
  60.4 2.5 %shard_map.82 = (bf16[1,56,448]{2,1,0:T(8,128)(2,1)}, f32[1,56,128]{2,1,0:T(8,128)}) custom-call(bf16[448,640]{1,0:T(8,128)(2,1)S(1)} %get-tuple-element.15.refs_0_, bf16[448,448]{1,0:T(8,128)(2,1)S(1)} %get-tuple-element.16.refs_1_, f32[56,448]{1,0:T(8,128)S(1)} %get-tuple-element.17.refs_2_, s32[1,128]{1,0:T(1,128)S(1)} %copy-done.5, ...), custom_call_target="tpu_custom_call" | custom-call | tf_op jit(solution)/shard_map/pallas_call | solution.py:83
  (35 shorter events, 5.9 us)
Async XLA Ops:
  0.6 22.1 %copy-start = (bf16[512,3,1152]{2,0,1:T(8,128)(2,1)S(1)}, bf16[512,3,1152]{2,0,1:T(8,128)(2,1)}, u32[]{:S(2)}) copy-start(bf16[512,3,1152]{2,0,1:T(8,128)(2,1)} %param.11) | copy-start | bytes 10616836
  16.7 0.7 %copy-start.1 = (bf16[160,512]{1,0:T(8,128)(2,1)}, bf16[160,512]{1,0:T(8,128)(2,1)S(1)}, u32[]{:S(2)}) copy-start(bf16[160,512]{1,0:T(8,128)(2,1)S(1)} %get-tuple-element.14) | copy-start | bytes 491524
  17.4 0.6 copy-start.3
  19.6 3.1 %copy-start.2 = (bf16[160,512]{1,0:T(8,128)(2,1)S(1)}, bf16[160,512]{1,0:T(8,128)(2,1)}, u32[]{:S(2)}) copy-start(bf16[160,512]{1,0:T(8,128)(2,1)} %copy-done.1) | copy-start | bytes 491524
  19.6 3.1 %copy-start.6 = (f32[3,160]{1,0:T(4,128)S(1)}, f32[3,160]{1,0:T(4,128)}, u32[]{:S(2)}) copy-start(f32[3,160]{1,0:T(4,128)} %copy.9) | copy-start | bytes 5764
  21.4 7.6 %collective-permute-start.2 = (bf16[80,1152]{1,0:T(8,128)(2,1)S(1)}, bf16[80,1152]{1,0:T(8,128)(2,1)S(1)}, u32[]{:S(2)}, u32[]{:S(2)}) collective-permute-start(bf16[80,1152]{1,0:T(8,128)(2,1)S(1)} %get-tuple-element.26.refs_2_), channel_id=1, source_target_pairs={{0,8},{2,10},{8,12},{10,14},{12,4},{14,6},{4,0},{6,2},{1,9},{3,11}... | collective-permute-start | bytes 552968 | tf_op jit(solution)/shard_map/ppermute | solution.py:104
  22.0 10.4 %collective-permute-start = (bf16[80,1152]{1,0:T(8,128)(2,1)S(1)}, bf16[80,1152]{1,0:T(8,128)(2,1)S(1)}, u32[]{:S(2)}, u32[]{:S(2)}) collective-permute-start(bf16[80,1152]{1,0:T(8,128)(2,1)S(1)} %get-tuple-element.27), channel_id=1, source_target_pairs={{0,10},{2,8},{8,14},{10,12},{12,6},{14,4},{4,2},{6,0},{1,11},{3,9}... | collective-permute-start | bytes 552968 | tf_op jit(solution)/shard_map/ppermute | solution.py:104
  23.5 8.8 %copy-start.4 = (s32[1,4,4]{2,1,0:T(4,128)S(1)}, s32[1,4,4]{2,1,0:T(4,128)}, u32[]{:S(2)}) copy-start(s32[1,4,4]{2,1,0:T(4,128)} %refs_1_.3) | copy-start | bytes 196
  23.6 20.4 %collective-permute-start.5 = (bf16[3,80,1152]{2,1,0:T(8,128)(2,1)S(1)}, bf16[3,80,1152]{2,1,0:T(8,128)(2,1)S(1)}, u32[]{:S(2)}, u32[]{:S(2)}) collective-permute-start(bf16[3,80,1152]{2,1,0:T(8,128)(2,1)S(1)} %get-tuple-element.24), channel_id=1, source_target_pairs={{0,2},{2,0},{1,3},{3,1},{4,6},{6,4},{5,7},{7,5},{8,10},{10,8},{9,1... | collective-permute-start | bytes 1658888 | tf_op jit(solution)/shard_map/ppermute | solution.py:88
  29.0 8.0 %collective-permute-start.3 = (bf16[80,1152]{1,0:T(8,128)(2,1)S(1)}, bf16[80,1152]{1,0:T(8,128)(2,1)S(1)}, u32[]{:S(2)}, u32[]{:S(2)}) collective-permute-start(bf16[80,1152]{1,0:T(8,128)(2,1)S(1)} %collective-permute-done.2.refs_4_), channel_id=1, source_target_pairs={{0,8},{8,12},{12,4},{4,0},{1,9},{9,13},{13,5},{5,1},{2,10},{10,14}... | collective-permute-start | bytes 552968 | tf_op jit(solution)/shard_map/ppermute | solution.py:101
  33.7 7.6 %collective-permute-start.4 = (bf16[80,1152]{1,0:T(8,128)(2,1)S(1)}, bf16[80,1152]{1,0:T(8,128)(2,1)S(1)}, u32[]{:S(2)}, u32[]{:S(2)}) collective-permute-start(bf16[80,1152]{1,0:T(8,128)(2,1)S(1)} %get-tuple-element.20.refs_5_), channel_id=1, source_target_pairs={{0,8},{8,12},{12,4},{4,0},{1,9},{9,13},{13,5},{5,1},{2,10},{10,14}... | collective-permute-start | bytes 552968 | tf_op jit(solution)/shard_map/ppermute | solution.py:101
  35.5 8.6 %collective-permute-start.1 = (bf16[80,1152]{1,0:T(8,128)(2,1)S(1)}, bf16[80,1152]{1,0:T(8,128)(2,1)S(1)}, u32[]{:S(2)}, u32[]{:S(2)}) collective-permute-start(bf16[80,1152]{1,0:T(8,128)(2,1)S(1)} %get-tuple-element.27), channel_id=1, source_target_pairs={{0,2},{2,0},{1,3},{3,1},{4,6},{6,4},{5,7},{7,5},{8,10},{10,8},{9,1... | collective-permute-start | bytes 552968 | tf_op jit(solution)/shard_map/ppermute | solution.py:88
  37.0 8.3 %collective-permute-start.6 = (bf16[80,1152]{1,0:T(8,128)(2,1)S(1)}, bf16[80,1152]{1,0:T(8,128)(2,1)S(1)}, u32[]{:S(2)}, u32[]{:S(2)}) collective-permute-start(bf16[80,1152]{1,0:T(8,128)(2,1)S(1)} %collective-permute-done.3.refs_6_), channel_id=1, source_target_pairs={{0,8},{8,12},{12,4},{4,0},{1,9},{9,13},{13,5},{5,1},{2,10},{10,14}... | collective-permute-start | bytes 552968 | tf_op jit(solution)/shard_map/ppermute | solution.py:101
  41.3 5.5 %collective-permute-start.7 = (bf16[80,1152]{1,0:T(8,128)(2,1)S(1)}, bf16[80,1152]{1,0:T(8,128)(2,1)S(1)}, u32[]{:S(2)}, u32[]{:S(2)}) collective-permute-start(bf16[80,1152]{1,0:T(8,128)(2,1)S(1)} %collective-permute-done.4.refs_7_), channel_id=1, source_target_pairs={{0,8},{8,12},{12,4},{4,0},{1,9},{9,13},{13,5},{5,1},{2,10},{10,14}... | collective-permute-start | bytes 552968 | tf_op jit(solution)/shard_map/ppermute | solution.py:101
  45.3 15.1 %copy-start.5 = (s32[1,128]{1,0:T(1,128)S(1)}, s32[1,128]{1,0:T(1,128)}, u32[]{:S(2)}) copy-start(s32[1,128]{1,0:T(1,128)} %refs_3_.1) | copy-start | bytes 1540
  47.8 1.5 %collective-permute-start.8 = (f32[80,448]{1,0:T(8,128)S(1)}, f32[80,448]{1,0:T(8,128)S(1)}, u32[]{:S(2)}, u32[]{:S(2)}) collective-permute-start(f32[80,448]{1,0:T(8,128)S(1)} %get-tuple-element.23), channel_id=1, source_target_pairs={{0,1},{1,0},{2,3},{3,2},{4,5},{5,4},{6,7},{7,6},{8,9},{9,8},{10,11... | collective-permute-start | bytes 430088 | tf_op jit(solution)/shard_map/ppermute | solution.py:88
  49.3 6.2 %collective-permute-start.11 = (bf16[80,448]{1,0:T(8,128)(2,1)S(1)}, bf16[80,448]{1,0:T(8,128)(2,1)S(1)}, u32[]{:S(2)}, u32[]{:S(2)}) collective-permute-start(bf16[80,448]{1,0:T(8,128)(2,1)S(1)} %add_convert_fusion.refs_4_), channel_id=1, source_target_pairs={{0,4},{8,0},{12,8},{4,12},{1,5},{9,1},{13,9},{5,13},{2,6},{10,2},{... | collective-permute-start | bytes 215048 | tf_op jit(solution)/shard_map/ppermute | solution.py:111
  51.7 7.0 %collective-permute-start.10 = (bf16[80,448]{1,0:T(8,128)(2,1)S(1)}, bf16[80,448]{1,0:T(8,128)(2,1)S(1)}, u32[]{:S(2)}, u32[]{:S(2)}) collective-permute-start(bf16[80,448]{1,0:T(8,128)(2,1)S(1)} %add_convert_fusion.refs_4_), channel_id=1, source_target_pairs={{0,12},{8,4},{12,0},{4,8},{1,13},{9,5},{13,1},{5,9},{2,14},{10,6},... | collective-permute-start | bytes 215048 | tf_op jit(solution)/shard_map/ppermute | solution.py:111
  53.4 5.7 %collective-permute-start.9 = (bf16[80,448]{1,0:T(8,128)(2,1)S(1)}, bf16[80,448]{1,0:T(8,128)(2,1)S(1)}, u32[]{:S(2)}, u32[]{:S(2)}) collective-permute-start(bf16[80,448]{1,0:T(8,128)(2,1)S(1)} %add_convert_fusion.refs_4_), channel_id=1, source_target_pairs={{0,8},{8,12},{12,4},{4,0},{1,9},{9,13},{13,5},{5,1},{2,10},{10,14}... | collective-permute-start | bytes 215048 | tf_op jit(solution)/shard_map/ppermute | solution.py:111
  53.4 5.8 %collective-permute-start.12 = (bf16[80,448]{1,0:T(8,128)(2,1)S(1)}, bf16[80,448]{1,0:T(8,128)(2,1)S(1)}, u32[]{:S(2)}, u32[]{:S(2)}) collective-permute-start(bf16[80,448]{1,0:T(8,128)(2,1)S(1)} %add_convert_fusion.refs_4_), channel_id=1, source_target_pairs={{0,1},{1,0},{2,3},{3,2},{4,5},{5,4},{6,7},{7,6},{8,9},{9,8},{10,11... | collective-permute-start | bytes 215048 | tf_op jit(solution)/shard_map/ppermute | solution.py:88
  55.5 3.7 %collective-permute-start.15 = (bf16[80,448]{1,0:T(8,128)(2,1)S(1)}, bf16[80,448]{1,0:T(8,128)(2,1)S(1)}, u32[]{:S(2)}, u32[]{:S(2)}) collective-permute-start(bf16[80,448]{1,0:T(8,128)(2,1)S(1)} %collective-permute-done.11.refs_7_), channel_id=1, source_target_pairs={{0,1},{1,0},{2,3},{3,2},{4,5},{5,4},{6,7},{7,6},{8,9},{9,8},{10,11... | collective-permute-start | bytes 215048 | tf_op jit(solution)/shard_map/ppermute | solution.py:88
  58.7 1.3 %collective-permute-start.14 = (bf16[80,448]{1,0:T(8,128)(2,1)S(1)}, bf16[80,448]{1,0:T(8,128)(2,1)S(1)}, u32[]{:S(2)}, u32[]{:S(2)}) collective-permute-start(bf16[80,448]{1,0:T(8,128)(2,1)S(1)} %collective-permute-done.10.refs_6_), channel_id=1, source_target_pairs={{0,1},{1,0},{2,3},{3,2},{4,5},{5,4},{6,7},{7,6},{8,9},{9,8},{10,11... | collective-permute-start | bytes 215048 | tf_op jit(solution)/shard_map/ppermute | solution.py:88
  59.1 1.3 %collective-permute-start.13 = (bf16[80,448]{1,0:T(8,128)(2,1)S(1)}, bf16[80,448]{1,0:T(8,128)(2,1)S(1)}, u32[]{:S(2)}, u32[]{:S(2)}) collective-permute-start(bf16[80,448]{1,0:T(8,128)(2,1)S(1)} %collective-permute-done.9.refs_5_), channel_id=1, source_target_pairs={{0,1},{1,0},{2,3},{3,2},{4,5},{5,4},{6,7},{7,6},{8,9},{9,8},{10,11... | collective-permute-start | bytes 215048 | tf_op jit(solution)/shard_map/ppermute | solution.py:88

commit v8 on v7

--- a/solution.py
+++ b/solution.py
@@ -205,41 +205,36 @@
         for k in range(poses):
             prompt = jnp.where(pos + k >= poses, pos + k - poses, pos + k)
             tables.append(list_of(values, prompt))
-            rows.append(as_rows(tables[k]))
-        hits = [floor_div(ids, table_rows) == own for ids, _ in rows]
+            rows.append(as_rows(tables[k])[0])
+        hits = [floor_div(ids, table_rows) == own for ids in rows]
         earlier = (iota((slots, slots), 0) < iota((slots, slots), 1)).astype(BF16)
         ranks = dot(jnp.concatenate([h.astype(BF16) for h in hits], axis=0), earlier)
-        picks, gains, ids_of = [], [], []
+        picks = []
         for k in range(poses):
             chosen = jnp.where(
                 hits[k] & (ranks[k : k + 1] == iota((listed, slots), 0)), 1.0, 0.0
             )
-            ids = jnp.sum(chosen * rows[k][0], axis=1, keepdims=True)
-            ids_of.append(ids)
-            gains.append(jnp.sum(chosen * rows[k][1], axis=1, keepdims=True))
-            live = jnp.sum(chosen, axis=1, keepdims=True) > 0.0
-            local = jnp.where(live, ids - own * table_rows, -1.0)
-            picks.append((local == iota((listed, table_rows), 1)).astype(BF16))
-        picks = jnp.concatenate(picks, axis=0)
-        gains = jnp.concatenate(gains, axis=0)
-        ids_of = jnp.concatenate(ids_of, axis=0)
-        layer = ids_of - floor_div(ids_of, layers) * layers
-        gains = jnp.concatenate([jnp.where(layer <= l, gains, 0.0) for l in range(depth)], axis=1)
-        return picks, gains, tables[0]
-
-    picks, gains, my_list = on_core(
+            local = jnp.sum(chosen * (rows[k] - own * table_rows + 1.0), axis=1, keepdims=True)
+            picks.append((local - 1.0 == iota((listed, table_rows), 1)).astype(BF16))
+        return jnp.concatenate(picks, axis=0), tables[0]
+
+    picks, my_list = on_core(
         choose,
         [lists],
-        [
-            shape(column, table_rows, dtype=BF16),
-            shape(column, depth),
-            shape(2 * positions * feats, kslots),
-        ],
-        small,
-    )
-
-    enc_rows = dot(picks, encoder).astype(BF16)
-    enc_rows = [enc_rows[k * listed : (k + 1) * listed] for k in range(poses)]
+        [shape(column, table_rows, dtype=BF16), shape(2 * positions * feats, kslots)],
+        small,
+    )
+
+    def encode(picks, enc):
+        rows = dot(picks, enc).astype(BF16)
+        return [rows[k * listed : (k + 1) * listed] for k in range(poses)] + [picks]
+
+    *enc_rows, picks = on_core(
+        encode,
+        [picks, encoder],
+        [shape(listed, width, dtype=BF16)] * poses + [shape(column, table_rows, dtype=BF16)],
+        small,
+    )
 
     ring = [[enc_rows[0]] + [rotate(enc_rows[k], "pos", k) for k in range(1, poses)]]
     ring.append([ring_next(enc_rows[k], "feat", "pos", k) for k in range(poses)])
@@ -247,7 +242,7 @@
     dec_rows = lax.dot_general(
         picks, decoder, (((1,), (0,)), ((), ())), preferred_element_type=F32
     )
-    dec_rows = (jnp.transpose(dec_rows, (1, 0, 2)) * gains.T[:, :, None]).astype(BF16)
+    dec_rows = jnp.transpose(dec_rows, (1, 0, 2)).astype(BF16)
     dec_rows = [dec_rows[:, k * listed : (k + 1) * listed] for k in range(poses)]
     dec_rows = [dec_rows[0]] + [rotate(dec_rows[k], "pos", k) for k in range(1, poses)]
 
@@ -262,7 +257,7 @@
             turn = jnp.where(turn < 0.0, turn + poses, turn)
             return (step * poses + turn) * listed + rank
 
-        ids_row = as_rows(table)[0]
+        ids_row, vals_row = as_rows(table)
         ids_col = as_col(table)
         owner_row = floor_div(ids_row, table_rows)
         owner_col = floor_div(ids_col, table_rows)
@@ -275,6 +270,13 @@
         placing_t = padded(owner_row, rank_row) == iota((total, slots), 0)
         layer = ids_col - floor_div(ids_col, layers) * layers
         layer_row = jnp.sum(jnp.where(placing, layer, 0.0), axis=0, keepdims=True)
+        mine = placing_t[:column]
+        gain = jnp.sum(jnp.where(mine, vals_row, 0.0), axis=1, keepdims=True)
+        source_layer = ids_row - floor_div(ids_row, layers) * layers
+        source_layer = jnp.sum(jnp.where(mine, source_layer, 0.0), axis=1, keepdims=True)
+        gains = jnp.concatenate(
+            [jnp.where(source_layer <= l, gain, 0.0) for l in range(depth)], axis=0
+        )
         allowed = jnp.where(pattern[0] == 1, 1.0, 0.0).astype(BF16)
 
         def in_block(slot, dim, extent):
@@ -293,15 +295,17 @@
             first + iota((result_rows, slots), 0), kslots
         )
         own_mask = jnp.where(own_causal, own_mask, 0.0)
-        return placing.astype(BF16), placing_t.astype(BF16), layer_row, mask.astype(BF16), own_mask
-
-    placing, placing_t, layer_row, mask, own_mask, ring[1][-1] = on_core(
+        placing, placing_t = placing.astype(BF16), placing_t.astype(BF16)
+        return placing, placing_t, layer_row, gains, mask.astype(BF16), own_mask
+
+    placing, placing_t, layer_row, gains, mask, own_mask, ring[1][-1] = on_core(
         places,
         [my_list, block_pattern],
         [
             shape(slots, holders * listed, dtype=BF16),
             shape(holders * listed, slots, dtype=BF16),
             shape(1, holders * listed),
+            shape(depth * column, 1),
             shape(slots, slots, dtype=BF16),
             shape(result_rows, slots),
         ],
@@ -312,11 +316,9 @@
     for _ in range(2, feats):
         ring.append([ring_next(rows, "feat") for rows in ring[-1]])
 
-    def products(first, count, layer_row, placing_t, *values):
-        enc = jnp.concatenate(values[: count * poses], axis=0)
-        dec = values[count * poses : count * poses + poses]
-        dec = jnp.concatenate([d[l] for l in range(depth) for d in dec], axis=0)
-        every = dot(dec, enc, NT)
+    def products(first, enc, dec, layer_row, placing_t):
+        count = len(enc) // poses
+        every = dot(dec, jnp.concatenate(enc, axis=0), NT)
         lanes = slice(first * column, (first + count) * column)
         raw = jnp.zeros((column, count * column), F32)
         for l in range(depth):
@@ -325,28 +327,29 @@
         split = dot(jnp.concatenate(pieces(raw), axis=0), placing_t[lanes])
         return split[:column] + (split[column : 2 * column] + split[2 * column :])
 
-    def early(*values):
-        return (products(0, feats - 1, *values),)
-
-    def late(so_far, *values):
-        raw = so_far + products(feats - 1, 1, *values)
+    def early(layer_row, placing_t, gains, *values):
+        dec = jnp.concatenate([d[l] for l in range(depth) for d in values[:poses]], axis=0)
+        dec = (dec.astype(F32) * gains).astype(BF16)
+        return products(0, values[poses:], dec, layer_row, placing_t), dec
+
+    def late(layer_row, placing_t, so_far, dec, *values):
+        raw = so_far + products(feats - 1, values, dec, layer_row, placing_t)
         first = place()[2] == 0.0
         return (
             jnp.where(first, raw[:half], raw[half:]),
             jnp.where(first, raw[half:], raw[:half]),
         )
 
-    early_enc = [rows for step in ring[:-1] for rows in step]
-    (so_far,) = on_core(
+    so_far, scaled = on_core(
         early,
-        [layer_row, placing_t] + early_enc + list(dec_rows),
-        [shape(column, slots)],
+        [layer_row, placing_t, gains] + dec_rows + [rows for step in ring[:-1] for rows in step],
+        [shape(column, slots), shape(depth * column, width, dtype=BF16)],
         small,
         cost=(1, 1),
     )
     keep, send = on_core(
         late,
-        [so_far, layer_row, placing_t] + list(ring[-1]) + list(dec_rows),
+        [layer_row, placing_t, so_far, scaled] + ring[-1],
         [shape(half, slots)] * 2,
         small,
     )

time: 63.1 us -> 64 us (1.014)
  waiting for transfers between devices: 19.2 us -> 26 us
  starting transfers between devices: 15.2 us -> 12.4 us
  matrix products: 2.58 us -> 0.77 us
  local copies, waits for them, and re-layouts: 2.99 us -> 1.37 us
    ppermute x4, waiting for transfers between devices: 4.09 us -> 7.47 us  [ring_next(): return lax.ppermute(x, axis, steps)]
    ppermute x2, waiting for transfers between devices: 5.89 us -> 9.08 us  [ring_next(): return lax.ppermute(x, (axis, across), pairs)]
    ppermute x7, starting transfers between devices: 3.17 us -> 1.22 us  [rotate(): lax.ppermute(x, axis, [(i, (i + step) % count) for i in range(count)])]
    ppermute x4, starting transfers between devices: 6.62 us -> 4.77 us  [ring_next(): return lax.ppermute(x, axis, steps)]
    dot_general x1 -> x0, matrix products: 1.77 us -> none  [dot(): return lax.dot_general(a, b, dims, preferred_element_type=F32)]
    transpose x1 -> x0, local copies, waits for them, and re-layouts: 1.56 us -> none  [per_device(): gains.T[:, :, None]]
    ppermute x3, waiting for transfers between devices: 5.67 us -> 6.77 us  [ring_spread(): lax.ppermute(x, axis, [(order[i], order[(i + k) % count]) for i in range(...]
    ppermute x7, waiting for transfers between devices: 3.58 us -> 2.65 us  [rotate(): lax.ppermute(x, axis, [(i, (i + step) % count) for i in range(count)])]
  transfers between devices with their start and end apart: 16 -> 16, of which waited for: 11 -> 9; matrix products, arithmetic and copies ran while one was open for 1% -> 0% of each run, Pallas kernels for 4% -> 4%
where the time goes in v8:
time: 64 us; the launch traced here: 63.8 us
  waiting for transfers between devices  26 us (41%)
  blocking collectives  13.9 us (22%)
  starting transfers between devices  12.4 us (19%)
  Pallas kernels  8.53 us (13%)
  local copies, waits for them, and re-layouts  1.37 us (2%)
  between operations  0.78 us (1%)
  matrix products  0.77 us (1%)
    all_to_all x1, blocking collectives, per_device(): lax.all_to_all(packed, ('feat', 'pos'), split_axis=0, concat_axis=0, tile...  13.9 us
    ppermute x2, waiting for transfers between devices, ring_next(): return lax.ppermute(x, (axis, across), pairs)  9.08 us
    pallas_call x7, Pallas kernels, on_core(): return list(call(*args, *streams, *through))  8.53 us
    ppermute x4, waiting for transfers between devices, ring_next(): return lax.ppermute(x, axis, steps)  7.47 us
    ppermute x3, waiting for transfers between devices, ring_spread(): lax.ppermute(x, axis, [(order[i], order[(i + k) % count]) for i in range(...  6.77 us
    ppermute x4, starting transfers between devices, ring_next(): return lax.ppermute(x, axis, steps)  4.77 us
    ppermute x3, starting transfers between devices, ring_spread(): lax.ppermute(x, axis, [(order[i], order[(i + k) % count]) for i in range(...  4.26 us
    ppermute x7, waiting for transfers between devices, rotate(): lax.ppermute(x, axis, [(i, (i + step) % count) for i in range(count)])  2.65 us
  transfers between devices with their start and end apart: 16, of which 9 were waited for; matrix products, arithmetic and copies ran while one was open for 0% of the time, Pallas kernels for 4%

profile of v8, /device:TPU:0, one launch (start us, length us, event | category | flops | bytes accessed | tf_op | source)
XLA Modules:
  0.0 63.8 jit_solution(11195323848497665889)
XLA Ops:
  0.6 1.5 %shard_map.77 = f32[8,8,128]{2,1,0:T(8,128)} custom-call(s32[1,4,28]{2,1,0:T(4,128)} %refs_0_.1, f32[1,4,28]{2,1,0:T(4,128)} %refs_1_.3), custom_call_target="tpu_custom_call" | custom-call | tf_op jit(solution)/shard_map/pallas_call | solution.py:83
  2.1 13.9 %all_to_all.5.refs_0_ = f32[8,8,128]{2,1,0:T(8,128)S(1)} all-to-all(f32[8,8,128]{2,1,0:T(8,128)} %shard_map.77), channel_id=1, replica_groups=mesh['grp'=2,'feat'=4,'pos'=2,'rep'=2] {'feat','pos'}, dimensions={0} | all-to-all | bytes 65536 | tf_op jit(solution)/shard_map/all_to_all | solution.py:159
  16.6 1.3 %copy-done.1 = bf16[512,1152]{1,0:T(8,128)(2,1)S(1)} copy-done((bf16[512,1152]{1,0:T(8,128)(2,1)S(1)}, bf16[512,1152]{1,0:T(8,128)(2,1)}, u32[]{:S(2)}) %copy-start.1) | copy-done | bytes 1179672
  18.2 0.8 %fusion = bf16[3,160,1152]{2,1,0:T(8,128)(2,1)S(1)} fusion(bf16[512,3,1152]{2,0,1:T(8,128)(2,1)S(1)} %copy-done, bf16[160,512]{1,0:T(8,128)(2,1)S(1)} %get-tuple-element.27), kind=kOutput, calls=%fused_computation.1 | convolution fusion | flops 566784000 | bytes 4808704 | tf_op jit(solution)/shard_map/dot_general | solution.py:242
  19.1 0.5 collective-permute-start.1
  20.2 1.6 %collective-permute-start = (bf16[80,1152]{1,0:T(8,128)(2,1)S(1)}, bf16[80,1152]{1,0:T(8,128)(2,1)S(1)}, u32[]{:S(2)}, u32[]{:S(2)}) collective-permute-start(bf16[80,1152]{1,0:T(8,128)(2,1)S(1)} %get-tuple-element.20), channel_id=1, source_target_pairs={{0,10},{2,8},{8,14},{10,12},{12,6},{14,4},{4,2},{6,0},{1,11},{3,9}... | collective-permute-start | bytes 552968 | tf_op jit(solution)/shard_map/ppermute | solution.py:104
  21.8 5.5 %collective-permute-done.3.refs_7_ = bf16[80,1152]{1,0:T(8,128)(2,1)S(1)} collective-permute-done((bf16[80,1152]{1,0:T(8,128)(2,1)S(1)}, bf16[80,1152]{1,0:T(8,128)(2,1)S(1)}, u32[]{:S(2)}, u32[]{:S(2)}) %collective-permute-start.3) | collective-permute-done | bytes 184352 | tf_op jit(solution)/shard_map/ppermute | solution.py:104
  27.3 1.3 %collective-permute-start.4 = (bf16[80,1152]{1,0:T(8,128)(2,1)S(1)}, bf16[80,1152]{1,0:T(8,128)(2,1)S(1)}, u32[]{:S(2)}, u32[]{:S(2)}) collective-permute-start(bf16[80,1152]{1,0:T(8,128)(2,1)S(1)} %collective-permute-done.3.refs_7_), channel_id=1, source_target_pairs={{0,8},{8,12},{12,4},{4,0},{1,9},{9,13},{13,5},{5,1},{2,10},{10,14}... | collective-permute-start | bytes 552968 | tf_op jit(solution)/shard_map/ppermute | solution.py:101
  28.6 3.6 %collective-permute-done.refs_2_ = bf16[80,1152]{1,0:T(8,128)(2,1)S(1)} collective-permute-done((bf16[80,1152]{1,0:T(8,128)(2,1)S(1)}, bf16[80,1152]{1,0:T(8,128)(2,1)S(1)}, u32[]{:S(2)}, u32[]{:S(2)}) %collective-permute-start) | collective-permute-done | bytes 184352 | tf_op jit(solution)/shard_map/ppermute | solution.py:104
  32.2 1.4 %shard_map.80 = (bf16[448,640]{1,0:T(8,128)(2,1)S(1)}, bf16[640,448]{1,0:T(8,128)(2,1)S(1)}, f32[1,640]{1,0:T(1,128)S(1)}, f32[480,1]{1,0:T(8,128)S(1)}, bf16[44...) custom-call(f32[32,28]{1,0:T(8,128)S(1)} %get-tuple-element.18.refs_, ...), custom_call_target="tpu_custom_call", output_to_operand_aliasing={{6}: (2, {})} | custom-call | flops 1 | bytes 1 | tf_op jit(solution)/shard_map/pallas_call | solution.py:83
  33.6 0.9 %collective-permute-start.5 = (bf16[80,1152]{1,0:T(8,128)(2,1)S(1)}, bf16[80,1152]{1,0:T(8,128)(2,1)S(1)}, u32[]{:S(2)}, u32[]{:S(2)}) collective-permute-start(bf16[80,1152]{1,0:T(8,128)(2,1)S(1)} %get-tuple-element.29.refs_8_), channel_id=1, source_target_pairs={{0,8},{8,12},{12,4},{4,0},{1,9},{9,13},{13,5},{5,1},{2,10},{10,14}... | collective-permute-start | bytes 552968 | tf_op jit(solution)/shard_map/ppermute | solution.py:101
  35.1 1.8 %collective-permute-start.6 = (bf16[80,1152]{1,0:T(8,128)(2,1)S(1)}, bf16[80,1152]{1,0:T(8,128)(2,1)S(1)}, u32[]{:S(2)}, u32[]{:S(2)}) collective-permute-start(bf16[80,1152]{1,0:T(8,128)(2,1)S(1)} %collective-permute-done.4.refs_9_), channel_id=1, source_target_pairs={{0,8},{8,12},{12,4},{4,0},{1,9},{9,13},{13,5},{5,1},{2,10},{10,14}... | collective-permute-start | bytes 552968 | tf_op jit(solution)/shard_map/ppermute | solution.py:101
  36.9 3.9 %collective-permute-done.5.refs_10_ = bf16[80,1152]{1,0:T(8,128)(2,1)S(1)} collective-permute-done((bf16[80,1152]{1,0:T(8,128)(2,1)S(1)}, bf16[80,1152]{1,0:T(8,128)(2,1)S(1)}, u32[]{:S(2)}, u32[]{:S(2)}) %collective-permute-start.5) | collective-permute-done | bytes 184352 | tf_op jit(solution)/shard_map/ppermute | solution.py:101
  40.8 0.7 %collective-permute-start.7 = (bf16[80,1152]{1,0:T(8,128)(2,1)S(1)}, bf16[80,1152]{1,0:T(8,128)(2,1)S(1)}, u32[]{:S(2)}, u32[]{:S(2)}) collective-permute-start(bf16[80,1152]{1,0:T(8,128)(2,1)S(1)} %collective-permute-done.5.refs_10_), channel_id=1, source_target_pairs={{0,8},{8,12},{12,4},{4,0},{1,9},{9,13},{13,5},{5,1},{2,10},{10,14}... | collective-permute-start | bytes 552968 | tf_op jit(solution)/shard_map/ppermute | solution.py:101
  41.5 1.3 %shard_map.81 = (f32[160,448]{1,0:T(8,128)S(1)}, bf16[480,1152]{1,0:T(8,128)(2,1)S(1)}) custom-call(f32[1,640]{1,0:T(1,128)S(1)} %get-tuple-element.24.refs_0_, bf16[640,448]{1,0:T(8,128)(2,1)S(1)} %get-tuple-element.25.refs_1_, f32[480,1]{1,0:T(8,128)S(1)} %get-tuple-element.26.refs_2_, bf16[3,80,1152]{2,1,0:T(8,128)(2,1)S(1)} %get-tuple-element.35.refs_3_, ...), custom_call_target="tpu_custom_call" | custom-call | flops 1 | bytes 1 | tf_op jit(solution)/shard_map/pallas_call | solution.py:83
  42.8 3.5 %collective-permute-done.7.refs_5_ = bf16[80,1152]{1,0:T(8,128)(2,1)S(1)} collective-permute-done((bf16[80,1152]{1,0:T(8,128)(2,1)S(1)}, bf16[80,1152]{1,0:T(8,128)(2,1)S(1)}, u32[]{:S(2)}, u32[]{:S(2)}) %collective-permute-start.7) | collective-permute-done | bytes 184352 | tf_op jit(solution)/shard_map/ppermute | solution.py:101
  46.3 0.9 %shard_map.82 = (f32[80,448]{1,0:T(8,128)S(1)}, f32[80,448]{1,0:T(8,128)S(1)}) custom-call(f32[1,640]{1,0:T(1,128)S(1)} %get-tuple-element.24.refs_0_, bf16[640,448]{1,0:T(8,128)(2,1)S(1)} %get-tuple-element.25.refs_1_, f32[160,448]{1,0:T(8,128)S(1)} %get-tuple-element.30.refs_2_, bf16[480,1152]{1,0:T(8,128)(2,1)S(1)} %get-tuple-element.31.refs_3_, ...), custom_call_target="tpu_custom_call" | custom-call | tf_op jit(solution)/shard_map/pallas_call | solution.py:83
  47.4 1.4 %collective-permute-done.8 = f32[80,448]{1,0:T(8,128)S(1)} collective-permute-done((f32[80,448]{1,0:T(8,128)S(1)}, f32[80,448]{1,0:T(8,128)S(1)}, u32[]{:S(2)}, u32[]{:S(2)}) %collective-permute-start.8) | collective-permute-done | bytes 143392 | tf_op jit(solution)/shard_map/ppermute | solution.py:88
  48.8 1.7 %collective-permute-start.9 = (bf16[80,448]{1,0:T(8,128)(2,1)S(1)}, bf16[80,448]{1,0:T(8,128)(2,1)S(1)}, u32[]{:S(2)}, u32[]{:S(2)}) collective-permute-start(bf16[80,448]{1,0:T(8,128)(2,1)S(1)} %add_convert_fusion.refs_4_), channel_id=1, source_target_pairs={{0,8},{8,12},{12,4},{4,0},{1,9},{9,13},{13,5},{5,1},{2,10},{10,14}... | collective-permute-start | bytes 215048 | tf_op jit(solution)/shard_map/ppermute | solution.py:111
  50.4 2.6 %collective-permute-start.10 = (bf16[80,448]{1,0:T(8,128)(2,1)S(1)}, bf16[80,448]{1,0:T(8,128)(2,1)S(1)}, u32[]{:S(2)}, u32[]{:S(2)}) collective-permute-start(bf16[80,448]{1,0:T(8,128)(2,1)S(1)} %add_convert_fusion.refs_4_), channel_id=1, source_target_pairs={{0,12},{8,4},{12,0},{4,8},{1,13},{9,5},{13,1},{5,9},{2,14},{10,6},... | collective-permute-start | bytes 215048 | tf_op jit(solution)/shard_map/ppermute | solution.py:111
  53.5 4.5 %collective-permute-done.10.refs_6_ = bf16[80,448]{1,0:T(8,128)(2,1)S(1)} collective-permute-done((bf16[80,448]{1,0:T(8,128)(2,1)S(1)}, bf16[80,448]{1,0:T(8,128)(2,1)S(1)}, u32[]{:S(2)}, u32[]{:S(2)}) %collective-permute-start.10) | collective-permute-done | bytes 71712 | tf_op jit(solution)/shard_map/ppermute | solution.py:111
  58.1 1.8 %collective-permute-done.11.refs_7_ = bf16[80,448]{1,0:T(8,128)(2,1)S(1)} collective-permute-done((bf16[80,448]{1,0:T(8,128)(2,1)S(1)}, bf16[80,448]{1,0:T(8,128)(2,1)S(1)}, u32[]{:S(2)}, u32[]{:S(2)}) %collective-permute-start.11) | collective-permute-done | bytes 71712 | tf_op jit(solution)/shard_map/ppermute | solution.py:111
  60.0 1.3 %collective-permute-done.15.refs_11_ = bf16[80,448]{1,0:T(8,128)(2,1)S(1)} collective-permute-done((bf16[80,448]{1,0:T(8,128)(2,1)S(1)}, bf16[80,448]{1,0:T(8,128)(2,1)S(1)}, u32[]{:S(2)}, u32[]{:S(2)}) %collective-permute-start.15) | collective-permute-done | bytes 71712 | tf_op jit(solution)/shard_map/ppermute | solution.py:88
  61.2 2.5 %shard_map.83 = (bf16[1,56,448]{2,1,0:T(8,128)(2,1)}, f32[1,56,128]{2,1,0:T(8,128)}) custom-call(bf16[448,640]{1,0:T(8,128)(2,1)S(1)} %get-tuple-element.21.refs_0_, bf16[448,448]{1,0:T(8,128)(2,1)S(1)} %get-tuple-element.22.refs_1_, f32[56,448]{1,0:T(8,128)S(1)} %get-tuple-element.23.refs_2_, s32[1,128]{1,0:T(1,128)S(1)} %copy-done.3, ...), custom_call_target="tpu_custom_call" | custom-call | tf_op jit(solution)/shard_map/pallas_call | solution.py:83
  (27 shorter events, 2.6 us)
Async XLA Ops:
  0.6 17.6 %copy-start = (bf16[512,3,1152]{2,0,1:T(8,128)(2,1)S(1)}, bf16[512,3,1152]{2,0,1:T(8,128)(2,1)}, u32[]{:S(2)}) copy-start(bf16[512,3,1152]{2,0,1:T(8,128)(2,1)} %param.11) | copy-start | bytes 10616836
  16.6 1.3 %copy-start.1 = (bf16[512,1152]{1,0:T(8,128)(2,1)S(1)}, bf16[512,1152]{1,0:T(8,128)(2,1)}, u32[]{:S(2)}) copy-start(bf16[512,1152]{1,0:T(8,128)(2,1)} %refs_1_.4) | copy-start | bytes 3538948
  19.0 13.2 %copy-start.2 = (s32[1,4,4]{2,1,0:T(4,128)S(1)}, s32[1,4,4]{2,1,0:T(4,128)}, u32[]{:S(2)}) copy-start(s32[1,4,4]{2,1,0:T(4,128)} %refs_1_.5) | copy-start | bytes 196
  19.1 22.4 %collective-permute-start.1 = (bf16[3,80,1152]{2,1,0:T(8,128)(2,1)S(1)}, bf16[3,80,1152]{2,1,0:T(8,128)(2,1)S(1)}, u32[]{:S(2)}, u32[]{:S(2)}) collective-permute-start(bf16[3,80,1152]{2,1,0:T(8,128)(2,1)S(1)} %get-tuple-element.34), channel_id=1, source_target_pairs={{0,2},{2,0},{1,3},{3,1},{4,6},{6,4},{5,7},{7,5},{8,10},{10,8},{9,1... | collective-permute-start | bytes 1658888 | tf_op jit(solution)/shard_map/ppermute | solution.py:88
  19.7 7.6 %collective-permute-start.3 = (bf16[80,1152]{1,0:T(8,128)(2,1)S(1)}, bf16[80,1152]{1,0:T(8,128)(2,1)S(1)}, u32[]{:S(2)}, u32[]{:S(2)}) collective-permute-start(bf16[80,1152]{1,0:T(8,128)(2,1)S(1)} %get-tuple-element.28.refs_5_), channel_id=1, source_target_pairs={{0,8},{2,10},{8,12},{10,14},{12,4},{14,6},{4,0},{6,2},{1,9},{3,11}... | collective-permute-start | bytes 552968 | tf_op jit(solution)/shard_map/ppermute | solution.py:104
  20.2 12.0 %collective-permute-start = (bf16[80,1152]{1,0:T(8,128)(2,1)S(1)}, bf16[80,1152]{1,0:T(8,128)(2,1)S(1)}, u32[]{:S(2)}, u32[]{:S(2)}) collective-permute-start(bf16[80,1152]{1,0:T(8,128)(2,1)S(1)} %get-tuple-element.20), channel_id=1, source_target_pairs={{0,10},{2,8},{8,14},{10,12},{12,6},{14,4},{4,2},{6,0},{1,11},{3,9}... | collective-permute-start | bytes 552968 | tf_op jit(solution)/shard_map/ppermute | solution.py:104
  27.3 7.8 %collective-permute-start.4 = (bf16[80,1152]{1,0:T(8,128)(2,1)S(1)}, bf16[80,1152]{1,0:T(8,128)(2,1)S(1)}, u32[]{:S(2)}, u32[]{:S(2)}) collective-permute-start(bf16[80,1152]{1,0:T(8,128)(2,1)S(1)} %collective-permute-done.3.refs_7_), channel_id=1, source_target_pairs={{0,8},{8,12},{12,4},{4,0},{1,9},{9,13},{13,5},{5,1},{2,10},{10,14}... | collective-permute-start | bytes 552968 | tf_op jit(solution)/shard_map/ppermute | solution.py:101
  33.6 7.1 %collective-permute-start.5 = (bf16[80,1152]{1,0:T(8,128)(2,1)S(1)}, bf16[80,1152]{1,0:T(8,128)(2,1)S(1)}, u32[]{:S(2)}, u32[]{:S(2)}) collective-permute-start(bf16[80,1152]{1,0:T(8,128)(2,1)S(1)} %get-tuple-element.29.refs_8_), channel_id=1, source_target_pairs={{0,8},{8,12},{12,4},{4,0},{1,9},{9,13},{13,5},{5,1},{2,10},{10,14}... | collective-permute-start | bytes 552968 | tf_op jit(solution)/shard_map/ppermute | solution.py:101
  34.6 6.9 %collective-permute-start.2 = (bf16[80,1152]{1,0:T(8,128)(2,1)S(1)}, bf16[80,1152]{1,0:T(8,128)(2,1)S(1)}, u32[]{:S(2)}, u32[]{:S(2)}) collective-permute-start(bf16[80,1152]{1,0:T(8,128)(2,1)S(1)} %get-tuple-element.20), channel_id=1, source_target_pairs={{0,2},{2,0},{1,3},{3,1},{4,6},{6,4},{5,7},{7,5},{8,10},{10,8},{9,1... | collective-permute-start | bytes 552968 | tf_op jit(solution)/shard_map/ppermute | solution.py:88
  35.1 7.7 %collective-permute-start.6 = (bf16[80,1152]{1,0:T(8,128)(2,1)S(1)}, bf16[80,1152]{1,0:T(8,128)(2,1)S(1)}, u32[]{:S(2)}, u32[]{:S(2)}) collective-permute-start(bf16[80,1152]{1,0:T(8,128)(2,1)S(1)} %collective-permute-done.4.refs_9_), channel_id=1, source_target_pairs={{0,8},{8,12},{12,4},{4,0},{1,9},{9,13},{13,5},{5,1},{2,10},{10,14}... | collective-permute-start | bytes 552968 | tf_op jit(solution)/shard_map/ppermute | solution.py:101
  40.8 5.5 %collective-permute-start.7 = (bf16[80,1152]{1,0:T(8,128)(2,1)S(1)}, bf16[80,1152]{1,0:T(8,128)(2,1)S(1)}, u32[]{:S(2)}, u32[]{:S(2)}) collective-permute-start(bf16[80,1152]{1,0:T(8,128)(2,1)S(1)} %collective-permute-done.5.refs_10_), channel_id=1, source_target_pairs={{0,8},{8,12},{12,4},{4,0},{1,9},{9,13},{13,5},{5,1},{2,10},{10,14}... | collective-permute-start | bytes 552968 | tf_op jit(solution)/shard_map/ppermute | solution.py:101
  42.8 18.4 %copy-start.3 = (s32[1,128]{1,0:T(1,128)S(1)}, s32[1,128]{1,0:T(1,128)}, u32[]{:S(2)}) copy-start(s32[1,128]{1,0:T(1,128)} %refs_3_.1) | copy-start | bytes 1540
  47.3 1.5 %collective-permute-start.8 = (f32[80,448]{1,0:T(8,128)S(1)}, f32[80,448]{1,0:T(8,128)S(1)}, u32[]{:S(2)}, u32[]{:S(2)}) collective-permute-start(f32[80,448]{1,0:T(8,128)S(1)} %get-tuple-element.33), channel_id=1, source_target_pairs={{0,1},{1,0},{2,3},{3,2},{4,5},{5,4},{6,7},{7,6},{8,9},{9,8},{10,11... | collective-permute-start | bytes 430088 | tf_op jit(solution)/shard_map/ppermute | solution.py:88
  48.8 4.6 %collective-permute-start.9 = (bf16[80,448]{1,0:T(8,128)(2,1)S(1)}, bf16[80,448]{1,0:T(8,128)(2,1)S(1)}, u32[]{:S(2)}, u32[]{:S(2)}) collective-permute-start(bf16[80,448]{1,0:T(8,128)(2,1)S(1)} %add_convert_fusion.refs_4_), channel_id=1, source_target_pairs={{0,8},{8,12},{12,4},{4,0},{1,9},{9,13},{13,5},{5,1},{2,10},{10,14}... | collective-permute-start | bytes 215048 | tf_op jit(solution)/shard_map/ppermute | solution.py:111
  50.4 7.7 %collective-permute-start.10 = (bf16[80,448]{1,0:T(8,128)(2,1)S(1)}, bf16[80,448]{1,0:T(8,128)(2,1)S(1)}, u32[]{:S(2)}, u32[]{:S(2)}) collective-permute-start(bf16[80,448]{1,0:T(8,128)(2,1)S(1)} %add_convert_fusion.refs_4_), channel_id=1, source_target_pairs={{0,12},{8,4},{12,0},{4,8},{1,13},{9,5},{13,1},{5,9},{2,14},{10,6},... | collective-permute-start | bytes 215048 | tf_op jit(solution)/shard_map/ppermute | solution.py:111
  53.0 6.9 %collective-permute-start.11 = (bf16[80,448]{1,0:T(8,128)(2,1)S(1)}, bf16[80,448]{1,0:T(8,128)(2,1)S(1)}, u32[]{:S(2)}, u32[]{:S(2)}) collective-permute-start(bf16[80,448]{1,0:T(8,128)(2,1)S(1)} %add_convert_fusion.refs_4_), channel_id=1, source_target_pairs={{0,4},{8,0},{12,8},{4,12},{1,5},{9,1},{13,9},{5,13},{2,6},{10,2},{... | collective-permute-start | bytes 215048 | tf_op jit(solution)/shard_map/ppermute | solution.py:111
  53.0 6.9 %collective-permute-start.12 = (bf16[80,448]{1,0:T(8,128)(2,1)S(1)}, bf16[80,448]{1,0:T(8,128)(2,1)S(1)}, u32[]{:S(2)}, u32[]{:S(2)}) collective-permute-start(bf16[80,448]{1,0:T(8,128)(2,1)S(1)} %add_convert_fusion.refs_4_), channel_id=1, source_target_pairs={{0,1},{1,0},{2,3},{3,2},{4,5},{5,4},{6,7},{7,6},{8,9},{9,8},{10,11... | collective-permute-start | bytes 215048 | tf_op jit(solution)/shard_map/ppermute | solution.py:88
  53.4 6.5 %collective-permute-start.13 = (bf16[80,448]{1,0:T(8,128)(2,1)S(1)}, bf16[80,448]{1,0:T(8,128)(2,1)S(1)}, u32[]{:S(2)}, u32[]{:S(2)}) collective-permute-start(bf16[80,448]{1,0:T(8,128)(2,1)S(1)} %collective-permute-done.9.refs_5_), channel_id=1, source_target_pairs={{0,1},{1,0},{2,3},{3,2},{4,5},{5,4},{6,7},{7,6},{8,9},{9,8},{10,11... | collective-permute-start | bytes 215048 | tf_op jit(solution)/shard_map/ppermute | solution.py:88
  58.1 1.9 %collective-permute-start.14 = (bf16[80,448]{1,0:T(8,128)(2,1)S(1)}, bf16[80,448]{1,0:T(8,128)(2,1)S(1)}, u32[]{:S(2)}, u32[]{:S(2)}) collective-permute-start(bf16[80,448]{1,0:T(8,128)(2,1)S(1)} %collective-permute-done.10.refs_6_), channel_id=1, source_target_pairs={{0,1},{1,0},{2,3},{3,2},{4,5},{5,4},{6,7},{7,6},{8,9},{9,8},{10,11... | collective-permute-start | bytes 215048 | tf_op jit(solution)/shard_map/ppermute | solution.py:88
  59.9 1.3 %collective-permute-start.15 = (bf16[80,448]{1,0:T(8,128)(2,1)S(1)}, bf16[80,448]{1,0:T(8,128)(2,1)S(1)}, u32[]{:S(2)}, u32[]{:S(2)}) collective-permute-start(bf16[80,448]{1,0:T(8,128)(2,1)S(1)} %collective-permute-done.11.refs_7_), channel_id=1, source_target_pairs={{0,1},{1,0},{2,3},{3,2},{4,5},{5,4},{6,7},{7,6},{8,9},{9,8},{10,11... | collective-permute-start | bytes 215048 | tf_op jit(solution)/shard_map/ppermute | solution.py:88

commit v9 on v8

--- a/solution.py
+++ b/solution.py
@@ -88,29 +88,8 @@
     return lax.ppermute(x, axis, [(i, (i + step) % count) for i in range(count)])
 
 
-def ring_place(index, count):
-    low = floor_div(index, 2)
-    return jnp.where(index > 2 * low, count - 1 - low, low)
-
-
-def ring_next(x, axis, across=None, turn=0):
-    count = lax.axis_size(axis)
-    order = list(range(0, count, 2)) + list(range(1, count, 2))[::-1]
-    steps = [(order[i], order[(i + 1) % count]) for i in range(count)]
-    if across is None:
-        return lax.ppermute(x, axis, steps)
-    wide = lax.axis_size(across)
-    pairs = [(a * wide + i, b * wide + (i + turn) % wide) for a, b in steps for i in range(wide)]
-    return lax.ppermute(x, (axis, across), pairs)
-
-
-def ring_spread(x, axis):
-    count = lax.axis_size(axis)
-    order = list(range(0, count, 2)) + list(range(1, count, 2))[::-1]
-    return [x] + [
-        lax.ppermute(x, axis, [(order[i], order[(i + k) % count]) for i in range(count)])
-        for k in range(1, count)
-    ]
+def swap(x, axis, bits):
+    return lax.ppermute(x, axis, [(i, i ^ bits) for i in range(lax.axis_size(axis))])
 
 
 def part(x, kernel):
@@ -236,8 +215,8 @@
         small,
     )
 
-    ring = [[enc_rows[0]] + [rotate(enc_rows[k], "pos", k) for k in range(1, poses)]]
-    ring.append([ring_next(enc_rows[k], "feat", "pos", k) for k in range(poses)])
+    enc_rows = [enc_rows[0]] + [rotate(enc_rows[k], "pos", k) for k in range(1, poses)]
+    far = [swap(rows, "feat", feats // 2) for rows in enc_rows]
 
     dec_rows = lax.dot_general(
         picks, decoder, (((1,), (0,)), ((), ())), preferred_element_type=F32
@@ -251,8 +230,7 @@
 
         def padded(owner, rank):
             feat_of = floor_div(owner, poses)
-            step = ring_place(feat, feats) - ring_place(feat_of, feats)
-            step = jnp.where(step < 0.0, step + feats, step)
+            step = (feat.astype(jnp.int32) ^ feat_of.astype(jnp.int32)).astype(F32)
             turn = pos - (owner - feat_of * poses)
             turn = jnp.where(turn < 0.0, turn + poses, turn)
             return (step * poses + turn) * listed + rank
@@ -298,7 +276,7 @@
         placing, placing_t = placing.astype(BF16), placing_t.astype(BF16)
         return placing, placing_t, layer_row, gains, mask.astype(BF16), own_mask
 
-    placing, placing_t, layer_row, gains, mask, own_mask, ring[1][-1] = on_core(
+    placing, placing_t, layer_row, gains, mask, own_mask, far[0] = on_core(
         places,
         [my_list, block_pattern],
         [
@@ -310,15 +288,24 @@
             shape(result_rows, slots),
         ],
         small,
-        through=ring[1][-1:],
+        through=far[:1],
         cost=(1, 1),
     )
-    for _ in range(2, feats):
-        ring.append([ring_next(rows, "feat") for rows in ring[-1]])
+    shards = []
+    for m in range(feats):
+        if m == 0 or m == feats // 2:
+            shards.append(far if m else enc_rows)
+        elif feats == 4 and m == 3:
+            inner = [lax.ppermute(rows, "feat", [(1, 2), (2, 1)]) for rows in enc_rows]
+            outer = [lax.ppermute(rows, "feat", [(2, 3), (1, 0)]) for rows in far]
+            shards.append(inner + outer)
+        else:
+            shards.append([swap(rows, "feat", m) for rows in enc_rows])
 
     def products(first, enc, dec, layer_row, placing_t):
-        count = len(enc) // poses
-        every = dot(dec, jnp.concatenate(enc, axis=0), NT)
+        enc = jnp.concatenate(enc, axis=0)
+        count = enc.shape[0] // column
+        every = dot(dec, enc, NT)
         lanes = slice(first * column, (first + count) * column)
         raw = jnp.zeros((column, count * column), F32)
         for l in range(depth):
@@ -333,6 +320,8 @@
         return products(0, values[poses:], dec, layer_row, placing_t), dec
 
     def late(layer_row, placing_t, so_far, dec, *values):
+        if len(values) > poses:
+            values = [a + b for a, b in zip(values[:poses], values[poses:])]
         raw = so_far + products(feats - 1, values, dec, layer_row, placing_t)
         first = place()[2] == 0.0
         return (
@@ -342,20 +331,20 @@
 
     so_far, scaled = on_core(
         early,
-        [layer_row, placing_t, gains] + dec_rows + [rows for step in ring[:-1] for rows in step],
+        [layer_row, placing_t, gains] + dec_rows + [rows for step in shards[:-1] for rows in step],
         [shape(column, slots), shape(depth * column, width, dtype=BF16)],
         small,
         cost=(1, 1),
     )
     keep, send = on_core(
         late,
-        [layer_row, placing_t, so_far, scaled] + ring[-1],
+        [layer_row, placing_t, so_far, scaled] + shards[-1],
         [shape(half, slots)] * 2,
         small,
     )
     own_edges = (keep + rotate(send, "rep", 1)).astype(BF16)
-    shards = ring_spread(own_edges, "feat")
-    others = [rotate(shard, "rep", 1) for shard in shards]
+    edges = [own_edges] + [swap(own_edges, "feat", m) for m in range(1, feats)]
+    others = [rotate(shard, "rep", 1) for shard in edges]
 
     def finish(placing, mask, own_mask, targets, *values):
         feat, _, rep = place()
@@ -392,7 +381,7 @@
 
     edges, influence = on_core(
         finish,
-        [placing, mask, own_mask, target_slots] + shards + others,
+        [placing, mask, own_mask, target_slots] + edges + others,
         [shape(1, result_rows, slots, dtype=BF16), shape(1, result_rows, panel)],
         small,
     )

time: 64 us -> 71.1 us (1.11)
  waiting for transfers between devices: 26 us -> 31.9 us
  starting transfers between devices: 12.4 us -> 13.4 us
    ppermute x7, waiting for transfers between devices: 2.65 us -> 16 us  [rotate(): lax.ppermute(x, axis, [(i, (i + step) % count) for i in range(count)])]
    ppermute x9 -> x11, waiting for transfers between devices: 23.3 us -> 16 us  [the longest x7 11.2 us: swap(): lax.ppermute(x, axis, [(i, i ^ bits) for i in range(lax.axis_size(axis))])]
    ppermute x7, starting transfers between devices: 1.22 us -> 2.68 us  [rotate(): lax.ppermute(x, axis, [(i, (i + step) % count) for i in range(count)])]
    ppermute x9 -> x11, starting transfers between devices: 11.1 us -> 10.8 us  [the longest x7 6.86 us: swap(): lax.ppermute(x, axis, [(i, i ^ bits) for i in range(lax.axis_size(axis))])]
  transfers between devices with their start and end apart: 16 -> 18, of which waited for: 9 -> 10; matrix products, arithmetic and copies ran while one was open for 0% -> 0% of each run, Pallas kernels for 4% -> 4%
where the time goes in v9:
time: 71.1 us; the launch traced here: 70.8 us
  waiting for transfers between devices  31.9 us (45%)
  blocking collectives  13.9 us (20%)
  starting transfers between devices  13.4 us (19%)
  Pallas kernels  8.48 us (12%)
  local copies, waits for them, and re-layouts  1.37 us (2%)
  between operations  0.84 us (1%)
  matrix products  0.77 us (1%)
    ppermute x7, waiting for transfers between devices, rotate(): lax.ppermute(x, axis, [(i, (i + step) % count) for i in range(count)])  16 us
    all_to_all x1, blocking collectives, per_device(): lax.all_to_all(packed, ('feat', 'pos'), split_axis=0, concat_axis=0, tile...  13.9 us
    ppermute x7, waiting for transfers between devices, swap(): lax.ppermute(x, axis, [(i, i ^ bits) for i in range(lax.axis_size(axis))])  11.2 us
    pallas_call x7, Pallas kernels, on_core(): return list(call(*args, *streams, *through))  8.48 us
    ppermute x7, starting transfers between devices, swap(): lax.ppermute(x, axis, [(i, i ^ bits) for i in range(lax.axis_size(axis))])  6.86 us
    ppermute x2, waiting for transfers between devices, per_device(): outer = [lax.ppermute(rows, 'feat', [(2, 3), (1, 0)]) for rows in far]  4.82 us
    ppermute x7, starting transfers between devices, rotate(): lax.ppermute(x, axis, [(i, (i + step) % count) for i in range(count)])  2.68 us
    ppermute x2, starting transfers between devices, per_device(): outer = [lax.ppermute(rows, 'feat', [(2, 3), (1, 0)]) for rows in far]  2.57 us
  transfers between devices with their start and end apart: 18, of which 10 were waited for; matrix products, arithmetic and copies ran while one was open for 0% of the time, Pallas kernels for 4%

profile of v9, /device:TPU:0, one launch (start us, length us, event | category | flops | bytes accessed | tf_op | source)
XLA Modules:
  0.0 70.8 jit_solution(10512556749830837044)
XLA Ops:
  0.6 1.5 %shard_map.77 = f32[8,8,128]{2,1,0:T(8,128)} custom-call(s32[1,4,28]{2,1,0:T(4,128)} %refs_0_.1, f32[1,4,28]{2,1,0:T(4,128)} %refs_1_.3), custom_call_target="tpu_custom_call" | custom-call | tf_op jit(solution)/shard_map/pallas_call | solution.py:83
  2.1 13.9 %all_to_all.5.refs_0_ = f32[8,8,128]{2,1,0:T(8,128)S(1)} all-to-all(f32[8,8,128]{2,1,0:T(8,128)} %shard_map.77), channel_id=1, replica_groups=mesh['grp'=2,'feat'=4,'pos'=2,'rep'=2] {'feat','pos'}, dimensions={0} | all-to-all | bytes 65536 | tf_op jit(solution)/shard_map/all_to_all | solution.py:138
  16.6 1.3 %copy-done.1 = bf16[512,1152]{1,0:T(8,128)(2,1)S(1)} copy-done((bf16[512,1152]{1,0:T(8,128)(2,1)S(1)}, bf16[512,1152]{1,0:T(8,128)(2,1)}, u32[]{:S(2)}) %copy-start.1) | copy-done | bytes 1179672
  18.2 0.8 %fusion = bf16[3,160,1152]{2,1,0:T(8,128)(2,1)S(1)} fusion(bf16[512,3,1152]{2,0,1:T(8,128)(2,1)S(1)} %copy-done, bf16[160,512]{1,0:T(8,128)(2,1)S(1)} %get-tuple-element.27), kind=kOutput, calls=%fused_computation.1 | convolution fusion | flops 566784000 | bytes 4808704 | tf_op jit(solution)/shard_map/dot_general | solution.py:221
  19.7 1.6 %collective-permute-start.2 = (bf16[80,1152]{1,0:T(8,128)(2,1)S(1)}, bf16[80,1152]{1,0:T(8,128)(2,1)S(1)}, u32[]{:S(2)}, u32[]{:S(2)}) collective-permute-start(bf16[80,1152]{1,0:T(8,128)(2,1)S(1)} %get-tuple-element.28), channel_id=1, source_target_pairs={{0,2},{2,0},{1,3},{3,1},{4,6},{6,4},{5,7},{7,5},{8,10},{10,8},{9,1... | collective-permute-start | bytes 552968 | tf_op jit(solution)/shard_map/ppermute | solution.py:88
  22.3 13.6 %collective-permute-done.2.refs_6_ = bf16[80,1152]{1,0:T(8,128)(2,1)S(1)} collective-permute-done((bf16[80,1152]{1,0:T(8,128)(2,1)S(1)}, bf16[80,1152]{1,0:T(8,128)(2,1)S(1)}, u32[]{:S(2)}, u32[]{:S(2)}) %collective-permute-start.2) | collective-permute-done | bytes 184352 | tf_op jit(solution)/shard_map/ppermute | solution.py:88
  36.4 0.9 %collective-permute-start.5 = (bf16[80,1152]{1,0:T(8,128)(2,1)S(1)}, bf16[80,1152]{1,0:T(8,128)(2,1)S(1)}, u32[]{:S(2)}, u32[]{:S(2)}) collective-permute-start(bf16[80,1152]{1,0:T(8,128)(2,1)S(1)} %collective-permute-done.2.refs_6_), channel_id=1, source_target_pairs={{0,8},{4,12},{8,0},{12,4},{1,9},{5,13},{9,1},{13,5},{2,10},{6,14},... | collective-permute-start | bytes 552968 | tf_op jit(solution)/shard_map/ppermute | solution.py:92
  37.3 0.7 collective-permute-start.6
  38.0 1.4 %shard_map.80 = (bf16[448,640]{1,0:T(8,128)(2,1)S(1)}, bf16[640,448]{1,0:T(8,128)(2,1)S(1)}, f32[1,640]{1,0:T(1,128)S(1)}, f32[480,1]{1,0:T(8,128)S(1)}, bf16[44...) custom-call(f32[32,28]{1,0:T(8,128)S(1)} %get-tuple-element.18.refs_, ...), custom_call_target="tpu_custom_call", output_to_operand_aliasing={{6}: (2, {})} | custom-call | flops 1 | bytes 1 | tf_op jit(solution)/shard_map/pallas_call | solution.py:83
  39.4 1.3 %collective-permute-start.8 = (bf16[80,1152]{1,0:T(8,128)(2,1)S(1)}, bf16[80,1152]{1,0:T(8,128)(2,1)S(1)}, u32[]{:S(2)}, u32[]{:S(2)}) collective-permute-start(bf16[80,1152]{1,0:T(8,128)(2,1)S(1)} %get-tuple-element.29.refs_9_), channel_id=1, source_target_pairs={{8,12},{4,0},{9,13},{5,1},{10,14},{6,2},{11,15},{7,3},{24,28},{20,... | collective-permute-start | bytes 552968 | tf_op jit(solution)/shard_map/ppermute | solution.py:300
  40.7 2.4 %collective-permute-done.4.refs_8_ = bf16[80,1152]{1,0:T(8,128)(2,1)S(1)} collective-permute-done((bf16[80,1152]{1,0:T(8,128)(2,1)S(1)}, bf16[80,1152]{1,0:T(8,128)(2,1)S(1)}, u32[]{:S(2)}, u32[]{:S(2)}) %collective-permute-start.4) | collective-permute-done | bytes 184352 | tf_op jit(solution)/shard_map/ppermute | solution.py:92
  43.8 3.3 %collective-permute-done.5.refs_10_ = bf16[80,1152]{1,0:T(8,128)(2,1)S(1)} collective-permute-done((bf16[80,1152]{1,0:T(8,128)(2,1)S(1)}, bf16[80,1152]{1,0:T(8,128)(2,1)S(1)}, u32[]{:S(2)}, u32[]{:S(2)}) %collective-permute-start.5) | collective-permute-done | bytes 184352 | tf_op jit(solution)/shard_map/ppermute | solution.py:92
  47.1 1.3 %collective-permute-start.9 = (bf16[80,1152]{1,0:T(8,128)(2,1)S(1)}, bf16[80,1152]{1,0:T(8,128)(2,1)S(1)}, u32[]{:S(2)}, u32[]{:S(2)}) collective-permute-start(bf16[80,1152]{1,0:T(8,128)(2,1)S(1)} %collective-permute-done.5.refs_10_), channel_id=1, source_target_pairs={{8,12},{4,0},{9,13},{5,1},{10,14},{6,2},{11,15},{7,3},{24,28},{20,... | collective-permute-start | bytes 552968 | tf_op jit(solution)/shard_map/ppermute | solution.py:300
  48.4 1.3 %shard_map.81 = (f32[160,448]{1,0:T(8,128)S(1)}, bf16[480,1152]{1,0:T(8,128)(2,1)S(1)}) custom-call(f32[1,640]{1,0:T(1,128)S(1)} %get-tuple-element.24.refs_0_, bf16[640,448]{1,0:T(8,128)(2,1)S(1)} %get-tuple-element.25.refs_1_, f32[480,1]{1,0:T(8,128)S(1)} %get-tuple-element.26.refs_2_, bf16[3,80,1152]{2,1,0:T(8,128)(2,1)S(1)} %get-tuple-element.35.refs_3_, ...), custom_call_target="tpu_custom_call" | custom-call | flops 1 | bytes 1 | tf_op jit(solution)/shard_map/pallas_call | solution.py:83
  49.7 0.7 collective-permute-done.8.refs_6_
  50.4 4.1 %collective-permute-done.9.refs_7_ = bf16[80,1152]{1,0:T(8,128)(2,1)S(1)} collective-permute-done((bf16[80,1152]{1,0:T(8,128)(2,1)S(1)}, bf16[80,1152]{1,0:T(8,128)(2,1)S(1)}, u32[]{:S(2)}, u32[]{:S(2)}) %collective-permute-start.9) | collective-permute-done | bytes 184352 | tf_op jit(solution)/shard_map/ppermute | solution.py:300
  54.5 1.0 %shard_map.82 = (f32[80,448]{1,0:T(8,128)S(1)}, f32[80,448]{1,0:T(8,128)S(1)}) custom-call(f32[1,640]{1,0:T(1,128)S(1)} %get-tuple-element.24.refs_0_, bf16[640,448]{1,0:T(8,128)(2,1)S(1)} %get-tuple-element.25.refs_1_, f32[160,448]{1,0:T(8,128)S(1)} %get-tuple-element.30.refs_2_, bf16[480,1152]{1,0:T(8,128)(2,1)S(1)} %get-tuple-element.31.refs_3_, ...), custom_call_target="tpu_custom_call" | custom-call | tf_op jit(solution)/shard_map/pallas_call | solution.py:83
  55.5 1.4 %collective-permute-done.10 = f32[80,448]{1,0:T(8,128)S(1)} collective-permute-done((f32[80,448]{1,0:T(8,128)S(1)}, f32[80,448]{1,0:T(8,128)S(1)}, u32[]{:S(2)}, u32[]{:S(2)}) %collective-permute-start.10) | collective-permute-done | bytes 143392 | tf_op jit(solution)/shard_map/ppermute | solution.py:88
  57.0 2.2 %collective-permute-start.12 = (bf16[80,448]{1,0:T(8,128)(2,1)S(1)}, bf16[80,448]{1,0:T(8,128)(2,1)S(1)}, u32[]{:S(2)}, u32[]{:S(2)}) collective-permute-start(bf16[80,448]{1,0:T(8,128)(2,1)S(1)} %add_convert_fusion.refs_4_), channel_id=1, source_target_pairs={{0,8},{4,12},{8,0},{12,4},{1,9},{5,13},{9,1},{13,5},{2,10},{6,14},... | collective-permute-start | bytes 215048 | tf_op jit(solution)/shard_map/ppermute | solution.py:92
  59.2 2.2 %collective-permute-start.13 = (bf16[80,448]{1,0:T(8,128)(2,1)S(1)}, bf16[80,448]{1,0:T(8,128)(2,1)S(1)}, u32[]{:S(2)}, u32[]{:S(2)}) collective-permute-start(bf16[80,448]{1,0:T(8,128)(2,1)S(1)} %add_convert_fusion.refs_4_), channel_id=1, source_target_pairs={{0,12},{4,8},{8,4},{12,0},{1,13},{5,9},{9,5},{13,1},{2,14},{6,10},... | collective-permute-start | bytes 215048 | tf_op jit(solution)/shard_map/ppermute | solution.py:92
  61.4 1.2 %collective-permute-done.11.refs_5_ = bf16[80,448]{1,0:T(8,128)(2,1)S(1)} collective-permute-done((bf16[80,448]{1,0:T(8,128)(2,1)S(1)}, bf16[80,448]{1,0:T(8,128)(2,1)S(1)}, u32[]{:S(2)}, u32[]{:S(2)}) %collective-permute-start.11) | collective-permute-done | bytes 71712 | tf_op jit(solution)/shard_map/ppermute | solution.py:92
  62.6 4.3 %collective-permute-done.12.refs_6_ = bf16[80,448]{1,0:T(8,128)(2,1)S(1)} collective-permute-done((bf16[80,448]{1,0:T(8,128)(2,1)S(1)}, bf16[80,448]{1,0:T(8,128)(2,1)S(1)}, u32[]{:S(2)}, u32[]{:S(2)}) %collective-permute-start.12) | collective-permute-done | bytes 71712 | tf_op jit(solution)/shard_map/ppermute | solution.py:92
  67.3 0.8 %collective-permute-done.16.refs_10_ = bf16[80,448]{1,0:T(8,128)(2,1)S(1)} collective-permute-done((bf16[80,448]{1,0:T(8,128)(2,1)S(1)}, bf16[80,448]{1,0:T(8,128)(2,1)S(1)}, u32[]{:S(2)}, u32[]{:S(2)}) %collective-permute-start.16) | collective-permute-done | bytes 71712 | tf_op jit(solution)/shard_map/ppermute | solution.py:88
  68.3 2.5 %shard_map.83 = (bf16[1,56,448]{2,1,0:T(8,128)(2,1)}, f32[1,56,128]{2,1,0:T(8,128)}) custom-call(bf16[448,640]{1,0:T(8,128)(2,1)S(1)} %get-tuple-element.21.refs_0_, bf16[448,448]{1,0:T(8,128)(2,1)S(1)} %get-tuple-element.22.refs_1_, f32[56,448]{1,0:T(8,128)S(1)} %get-tuple-element.23.refs_2_, s32[1,128]{1,0:T(1,128)S(1)} %copy-done.3, ...), custom_call_target="tpu_custom_call" | custom-call | tf_op jit(solution)/shard_map/pallas_call | solution.py:83
  (31 shorter events, 4.5 us)
Async XLA Ops:
  0.6 17.6 %copy-start = (bf16[512,3,1152]{2,0,1:T(8,128)(2,1)S(1)}, bf16[512,3,1152]{2,0,1:T(8,128)(2,1)}, u32[]{:S(2)}) copy-start(bf16[512,3,1152]{2,0,1:T(8,128)(2,1)} %param.11) | copy-start | bytes 10616836
  16.6 1.3 %copy-start.1 = (bf16[512,1152]{1,0:T(8,128)(2,1)S(1)}, bf16[512,1152]{1,0:T(8,128)(2,1)}, u32[]{:S(2)}) copy-start(bf16[512,1152]{1,0:T(8,128)(2,1)} %refs_1_.4) | copy-start | bytes 3538948
  19.0 18.9 %copy-start.2 = (s32[1,4,4]{2,1,0:T(4,128)S(1)}, s32[1,4,4]{2,1,0:T(4,128)}, u32[]{:S(2)}) copy-start(s32[1,4,4]{2,1,0:T(4,128)} %refs_1_.5) | copy-start | bytes 196
  19.1 29.2 %collective-permute-start.1 = (bf16[3,80,1152]{2,1,0:T(8,128)(2,1)S(1)}, bf16[3,80,1152]{2,1,0:T(8,128)(2,1)S(1)}, u32[]{:S(2)}, u32[]{:S(2)}) collective-permute-start(bf16[3,80,1152]{2,1,0:T(8,128)(2,1)S(1)} %get-tuple-element.34), channel_id=1, source_target_pairs={{0,2},{2,0},{1,3},{3,1},{4,6},{6,4},{5,7},{7,5},{8,10},{10,8},{9,1... | collective-permute-start | bytes 1658888 | tf_op jit(solution)/shard_map/ppermute | solution.py:88
  19.7 16.3 %collective-permute-start.2 = (bf16[80,1152]{1,0:T(8,128)(2,1)S(1)}, bf16[80,1152]{1,0:T(8,128)(2,1)S(1)}, u32[]{:S(2)}, u32[]{:S(2)}) collective-permute-start(bf16[80,1152]{1,0:T(8,128)(2,1)S(1)} %get-tuple-element.28), channel_id=1, source_target_pairs={{0,2},{2,0},{1,3},{3,1},{4,6},{6,4},{5,7},{7,5},{8,10},{10,8},{9,1... | collective-permute-start | bytes 552968 | tf_op jit(solution)/shard_map/ppermute | solution.py:88
  21.2 16.1 %collective-permute-start = (bf16[80,1152]{1,0:T(8,128)(2,1)S(1)}, bf16[80,1152]{1,0:T(8,128)(2,1)S(1)}, u32[]{:S(2)}, u32[]{:S(2)}) collective-permute-start(bf16[80,1152]{1,0:T(8,128)(2,1)S(1)} %get-tuple-element.20.refs_5_), channel_id=1, source_target_pairs={{0,8},{4,12},{8,0},{12,4},{1,9},{5,13},{9,1},{13,5},{2,10},{6,14},... | collective-permute-start | bytes 552968 | tf_op jit(solution)/shard_map/ppermute | solution.py:92
  21.7 17.6 %collective-permute-start.3 = (bf16[80,1152]{1,0:T(8,128)(2,1)S(1)}, bf16[80,1152]{1,0:T(8,128)(2,1)S(1)}, u32[]{:S(2)}, u32[]{:S(2)}) collective-permute-start(bf16[80,1152]{1,0:T(8,128)(2,1)S(1)} %get-tuple-element.20.refs_5_), channel_id=1, source_target_pairs={{0,4},{4,0},{8,12},{12,8},{1,5},{5,1},{9,13},{13,9},{2,6},{6,2},{1... | collective-permute-start | bytes 552968 | tf_op jit(solution)/shard_map/ppermute | solution.py:92
  36.0 7.1 %collective-permute-start.4 = (bf16[80,1152]{1,0:T(8,128)(2,1)S(1)}, bf16[80,1152]{1,0:T(8,128)(2,1)S(1)}, u32[]{:S(2)}, u32[]{:S(2)}) collective-permute-start(bf16[80,1152]{1,0:T(8,128)(2,1)S(1)} %collective-permute-done.2.refs_6_), channel_id=1, source_target_pairs={{0,4},{4,0},{8,12},{12,8},{1,5},{5,1},{9,13},{13,9},{2,6},{6,2},{1... | collective-permute-start | bytes 552968 | tf_op jit(solution)/shard_map/ppermute | solution.py:92
  36.4 10.7 %collective-permute-start.5 = (bf16[80,1152]{1,0:T(8,128)(2,1)S(1)}, bf16[80,1152]{1,0:T(8,128)(2,1)S(1)}, u32[]{:S(2)}, u32[]{:S(2)}) collective-permute-start(bf16[80,1152]{1,0:T(8,128)(2,1)S(1)} %collective-permute-done.2.refs_6_), channel_id=1, source_target_pairs={{0,8},{4,12},{8,0},{12,4},{1,9},{5,13},{9,1},{13,5},{2,10},{6,14},... | collective-permute-start | bytes 552968 | tf_op jit(solution)/shard_map/ppermute | solution.py:92
  37.3 12.4 %collective-permute-start.6 = (bf16[80,1152]{1,0:T(8,128)(2,1)S(1)}, bf16[80,1152]{1,0:T(8,128)(2,1)S(1)}, u32[]{:S(2)}, u32[]{:S(2)}) collective-permute-start(bf16[80,1152]{1,0:T(8,128)(2,1)S(1)} %get-tuple-element.20.refs_5_), channel_id=1, source_target_pairs={{4,8},{8,4},{5,9},{9,5},{6,10},{10,6},{7,11},{11,7},{20,24},{24,20... | collective-permute-start | bytes 552968 | tf_op jit(solution)/shard_map/ppermute | solution.py:299
  39.4 11.0 %collective-permute-start.8 = (bf16[80,1152]{1,0:T(8,128)(2,1)S(1)}, bf16[80,1152]{1,0:T(8,128)(2,1)S(1)}, u32[]{:S(2)}, u32[]{:S(2)}) collective-permute-start(bf16[80,1152]{1,0:T(8,128)(2,1)S(1)} %get-tuple-element.29.refs_9_), channel_id=1, source_target_pairs={{8,12},{4,0},{9,13},{5,1},{10,14},{6,2},{11,15},{7,3},{24,28},{20,... | collective-permute-start | bytes 552968 | tf_op jit(solution)/shard_map/ppermute | solution.py:300
  43.1 6.6 %collective-permute-start.7 = (bf16[80,1152]{1,0:T(8,128)(2,1)S(1)}, bf16[80,1152]{1,0:T(8,128)(2,1)S(1)}, u32[]{:S(2)}, u32[]{:S(2)}) collective-permute-start(bf16[80,1152]{1,0:T(8,128)(2,1)S(1)} %collective-permute-done.2.refs_6_), channel_id=1, source_target_pairs={{4,8},{8,4},{5,9},{9,5},{6,10},{10,6},{7,11},{11,7},{20,24},{24,20... | collective-permute-start | bytes 552968 | tf_op jit(solution)/shard_map/ppermute | solution.py:299
  47.1 7.4 %collective-permute-start.9 = (bf16[80,1152]{1,0:T(8,128)(2,1)S(1)}, bf16[80,1152]{1,0:T(8,128)(2,1)S(1)}, u32[]{:S(2)}, u32[]{:S(2)}) collective-permute-start(bf16[80,1152]{1,0:T(8,128)(2,1)S(1)} %collective-permute-done.5.refs_10_), channel_id=1, source_target_pairs={{8,12},{4,0},{9,13},{5,1},{10,14},{6,2},{11,15},{7,3},{24,28},{20,... | collective-permute-start | bytes 552968 | tf_op jit(solution)/shard_map/ppermute | solution.py:300
  49.6 18.6 %copy-start.3 = (s32[1,128]{1,0:T(1,128)S(1)}, s32[1,128]{1,0:T(1,128)}, u32[]{:S(2)}) copy-start(s32[1,128]{1,0:T(1,128)} %refs_3_.1) | copy-start | bytes 1540
  55.5 1.5 %collective-permute-start.10 = (f32[80,448]{1,0:T(8,128)S(1)}, f32[80,448]{1,0:T(8,128)S(1)}, u32[]{:S(2)}, u32[]{:S(2)}) collective-permute-start(f32[80,448]{1,0:T(8,128)S(1)} %get-tuple-element.33), channel_id=1, source_target_pairs={{0,1},{1,0},{2,3},{3,2},{4,5},{5,4},{6,7},{7,6},{8,9},{9,8},{10,11... | collective-permute-start | bytes 430088 | tf_op jit(solution)/shard_map/ppermute | solution.py:88
  56.9 5.6 %collective-permute-start.11 = (bf16[80,448]{1,0:T(8,128)(2,1)S(1)}, bf16[80,448]{1,0:T(8,128)(2,1)S(1)}, u32[]{:S(2)}, u32[]{:S(2)}) collective-permute-start(bf16[80,448]{1,0:T(8,128)(2,1)S(1)} %add_convert_fusion.refs_4_), channel_id=1, source_target_pairs={{0,4},{4,0},{8,12},{12,8},{1,5},{5,1},{9,13},{13,9},{2,6},{6,2},{1... | collective-permute-start | bytes 215048 | tf_op jit(solution)/shard_map/ppermute | solution.py:92
  57.0 9.8 %collective-permute-start.12 = (bf16[80,448]{1,0:T(8,128)(2,1)S(1)}, bf16[80,448]{1,0:T(8,128)(2,1)S(1)}, u32[]{:S(2)}, u32[]{:S(2)}) collective-permute-start(bf16[80,448]{1,0:T(8,128)(2,1)S(1)} %add_convert_fusion.refs_4_), channel_id=1, source_target_pairs={{0,8},{4,12},{8,0},{12,4},{1,9},{5,13},{9,1},{13,5},{2,10},{6,14},... | collective-permute-start | bytes 215048 | tf_op jit(solution)/shard_map/ppermute | solution.py:92
  59.2 7.6 %collective-permute-start.13 = (bf16[80,448]{1,0:T(8,128)(2,1)S(1)}, bf16[80,448]{1,0:T(8,128)(2,1)S(1)}, u32[]{:S(2)}, u32[]{:S(2)}) collective-permute-start(bf16[80,448]{1,0:T(8,128)(2,1)S(1)} %add_convert_fusion.refs_4_), channel_id=1, source_target_pairs={{0,12},{4,8},{8,4},{12,0},{1,13},{5,9},{9,5},{13,1},{2,14},{6,10},... | collective-permute-start | bytes 215048 | tf_op jit(solution)/shard_map/ppermute | solution.py:92
  61.4 5.9 %collective-permute-start.14 = (bf16[80,448]{1,0:T(8,128)(2,1)S(1)}, bf16[80,448]{1,0:T(8,128)(2,1)S(1)}, u32[]{:S(2)}, u32[]{:S(2)}) collective-permute-start(bf16[80,448]{1,0:T(8,128)(2,1)S(1)} %add_convert_fusion.refs_4_), channel_id=1, source_target_pairs={{0,1},{1,0},{2,3},{3,2},{4,5},{5,4},{6,7},{7,6},{8,9},{9,8},{10,11... | collective-permute-start | bytes 215048 | tf_op jit(solution)/shard_map/ppermute | solution.py:88
  62.6 4.8 %collective-permute-start.15 = (bf16[80,448]{1,0:T(8,128)(2,1)S(1)}, bf16[80,448]{1,0:T(8,128)(2,1)S(1)}, u32[]{:S(2)}, u32[]{:S(2)}) collective-permute-start(bf16[80,448]{1,0:T(8,128)(2,1)S(1)} %collective-permute-done.11.refs_5_), channel_id=1, source_target_pairs={{0,1},{1,0},{2,3},{3,2},{4,5},{5,4},{6,7},{7,6},{8,9},{9,8},{10,11... | collective-permute-start | bytes 215048 | tf_op jit(solution)/shard_map/ppermute | solution.py:88
  66.8 1.3 %collective-permute-start.16 = (bf16[80,448]{1,0:T(8,128)(2,1)S(1)}, bf16[80,448]{1,0:T(8,128)(2,1)S(1)}, u32[]{:S(2)}, u32[]{:S(2)}) collective-permute-start(bf16[80,448]{1,0:T(8,128)(2,1)S(1)} %collective-permute-done.12.refs_6_), channel_id=1, source_target_pairs={{0,1},{1,0},{2,3},{3,2},{4,5},{5,4},{6,7},{7,6},{8,9},{9,8},{10,11... | collective-permute-start | bytes 215048 | tf_op jit(solution)/shard_map/ppermute | solution.py:88
  66.8 1.4 %collective-permute-start.17 = (bf16[80,448]{1,0:T(8,128)(2,1)S(1)}, bf16[80,448]{1,0:T(8,128)(2,1)S(1)}, u32[]{:S(2)}, u32[]{:S(2)}) collective-permute-start(bf16[80,448]{1,0:T(8,128)(2,1)S(1)} %collective-permute-done.13.refs_7_), channel_id=1, source_target_pairs={{0,1},{1,0},{2,3},{3,2},{4,5},{5,4},{6,7},{7,6},{8,9},{9,8},{10,11... | collective-permute-start | bytes 215048 | tf_op jit(solution)/shard_map/ppermute | solution.py:88

commit v10 on v9

--- a/solution.py
+++ b/solution.py
@@ -216,14 +216,20 @@
     )
 
     enc_rows = [enc_rows[0]] + [rotate(enc_rows[k], "pos", k) for k in range(1, poses)]
-    far = [swap(rows, "feat", feats // 2) for rows in enc_rows]
+    far = [swap(enc_rows[0], "feat", feats // 2)]
 
     dec_rows = lax.dot_general(
         picks, decoder, (((1,), (0,)), ((), ())), preferred_element_type=F32
     )
     dec_rows = jnp.transpose(dec_rows, (1, 0, 2)).astype(BF16)
     dec_rows = [dec_rows[:, k * listed : (k + 1) * listed] for k in range(poses)]
+    near = [swap(enc_rows[0], "feat", 1)]
+    *dec_rows, enc_rows[-1], near[0], far[0] = lax.optimization_barrier(
+        (*dec_rows, enc_rows[-1], near[0], far[0])
+    )
     dec_rows = [dec_rows[0]] + [rotate(dec_rows[k], "pos", k) for k in range(1, poses)]
+
+    far += [swap(rows, "feat", feats // 2) for rows in enc_rows[1:]]
 
     def places(table, pattern):
         feat, pos, rep = place()
@@ -301,6 +307,8 @@
             shards.append(inner + outer)
         else:
             shards.append([swap(rows, "feat", m) for rows in enc_rows])
+        if m == 1:
+            shards[1][0] = near[0]
 
     def products(first, enc, dec, layer_row, placing_t):
         enc = jnp.concatenate(enc, axis=0)

time: 71.1 us -> 63.5 us (0.89)
  waiting for transfers between devices: 31.9 us -> 24.1 us
    ppermute x7, waiting for transfers between devices: 16 us -> 6.27 us  [rotate(): lax.ppermute(x, axis, [(i, (i + step) % count) for i in range(count)])]
    ppermute x7, waiting for transfers between devices: 11.2 us -> 13.1 us  [swap(): lax.ppermute(x, axis, [(i, i ^ bits) for i in range(lax.axis_size(axis))])]
    ppermute x7, starting transfers between devices: 6.86 us -> 7.8 us  [swap(): lax.ppermute(x, axis, [(i, i ^ bits) for i in range(lax.axis_size(axis))])]
    ppermute x7, starting transfers between devices: 2.68 us -> 1.94 us  [rotate(): lax.ppermute(x, axis, [(i, (i + step) % count) for i in range(count)])]
  transfers between devices with their start and end apart: 18 -> 18, of which waited for: 10 -> 12; matrix products, arithmetic and copies ran while one was open for 0% -> 1% of each run, Pallas kernels for 4% -> 4%
where the time goes in v10:
time: 63.5 us; the launch traced here: 63.2 us
  waiting for transfers between devices  24.1 us (38%)
  blocking collectives  13.9 us (22%)
  starting transfers between devices  13.6 us (21%)
  Pallas kernels  8.49 us (13%)
  local copies, waits for them, and re-layouts  1.37 us (2%)
  between operations  0.82 us (1%)
  matrix products  0.77 us (1%)
    all_to_all x1, blocking collectives, per_device(): lax.all_to_all(packed, ('feat', 'pos'), split_axis=0, concat_axis=0, tile...  13.9 us
    ppermute x7, waiting for transfers between devices, swap(): lax.ppermute(x, axis, [(i, i ^ bits) for i in range(lax.axis_size(axis))])  13.1 us
    pallas_call x7, Pallas kernels, on_core(): return list(call(*args, *streams, *through))  8.49 us
    ppermute x7, starting transfers between devices, swap(): lax.ppermute(x, axis, [(i, i ^ bits) for i in range(lax.axis_size(axis))])  7.8 us
    ppermute x7, waiting for transfers between devices, rotate(): lax.ppermute(x, axis, [(i, (i + step) % count) for i in range(count)])  6.27 us
    ppermute x2, waiting for transfers between devices, per_device(): outer = [lax.ppermute(rows, 'feat', [(2, 3), (1, 0)]) for rows in far]  4.81 us
    ppermute x2, starting transfers between devices, per_device(): outer = [lax.ppermute(rows, 'feat', [(2, 3), (1, 0)]) for rows in far]  2.56 us
    ppermute x7, starting transfers between devices, rotate(): lax.ppermute(x, axis, [(i, (i + step) % count) for i in range(count)])  1.94 us
  transfers between devices with their start and end apart: 18, of which 12 were waited for; matrix products, arithmetic and copies ran while one was open for 1% of the time, Pallas kernels for 4%

profile of v10, /device:TPU:0, one launch (start us, length us, event | category | flops | bytes accessed | tf_op | source)
XLA Modules:
  0.0 63.2 jit_solution(11581861048939240243)
XLA Ops:
  0.6 1.5 %shard_map.77 = f32[8,8,128]{2,1,0:T(8,128)} custom-call(s32[1,4,28]{2,1,0:T(4,128)} %refs_0_.1, f32[1,4,28]{2,1,0:T(4,128)} %refs_1_.3), custom_call_target="tpu_custom_call" | custom-call | tf_op jit(solution)/shard_map/pallas_call | solution.py:83
  2.1 13.9 %all_to_all.5.refs_0_ = f32[8,8,128]{2,1,0:T(8,128)S(1)} all-to-all(f32[8,8,128]{2,1,0:T(8,128)} %shard_map.77), channel_id=1, replica_groups=mesh['grp'=2,'feat'=4,'pos'=2,'rep'=2] {'feat','pos'}, dimensions={0} | all-to-all | bytes 65536 | tf_op jit(solution)/shard_map/all_to_all | solution.py:138
  16.6 1.3 %copy-done.1 = bf16[512,1152]{1,0:T(8,128)(2,1)S(1)} copy-done((bf16[512,1152]{1,0:T(8,128)(2,1)S(1)}, bf16[512,1152]{1,0:T(8,128)(2,1)}, u32[]{:S(2)}) %copy-start.1) | copy-done | bytes 1179672
  20.1 0.8 %fusion = bf16[3,160,1152]{2,1,0:T(8,128)(2,1)S(1)} fusion(bf16[512,3,1152]{2,0,1:T(8,128)(2,1)S(1)} %copy-done, bf16[160,512]{1,0:T(8,128)(2,1)S(1)} %get-tuple-element.25), kind=kOutput, calls=%fused_computation.1 | convolution fusion | flops 566784000 | bytes 4808704 | tf_op jit(solution)/shard_map/dot_general | solution.py:221
  21.0 4.0 %collective-permute-done.refs_6_ = bf16[80,1152]{1,0:T(8,128)(2,1)S(1)} collective-permute-done((bf16[80,1152]{1,0:T(8,128)(2,1)S(1)}, bf16[80,1152]{1,0:T(8,128)(2,1)S(1)}, u32[]{:S(2)}, u32[]{:S(2)}) %collective-permute-start) | collective-permute-done | bytes 184352 | tf_op jit(solution)/shard_map/ppermute | solution.py:88
  25.0 1.4 %collective-permute-done.1.refs_7_ = bf16[80,1152]{1,0:T(8,128)(2,1)S(1)} collective-permute-done((bf16[80,1152]{1,0:T(8,128)(2,1)S(1)}, bf16[80,1152]{1,0:T(8,128)(2,1)S(1)}, u32[]{:S(2)}, u32[]{:S(2)}) %collective-permute-start.1) | collective-permute-done | bytes 184352 | tf_op jit(solution)/shard_map/ppermute | solution.py:92
  26.4 2.0 %collective-permute-done.2.refs_2_ = bf16[80,1152]{1,0:T(8,128)(2,1)S(1)} collective-permute-done((bf16[80,1152]{1,0:T(8,128)(2,1)S(1)}, bf16[80,1152]{1,0:T(8,128)(2,1)S(1)}, u32[]{:S(2)}, u32[]{:S(2)}) %collective-permute-start.2) | collective-permute-done | bytes 184352 | tf_op jit(solution)/shard_map/ppermute | solution.py:92
  29.0 2.2 %collective-permute-start.5 = (bf16[80,1152]{1,0:T(8,128)(2,1)S(1)}, bf16[80,1152]{1,0:T(8,128)(2,1)S(1)}, u32[]{:S(2)}, u32[]{:S(2)}) collective-permute-start(bf16[80,1152]{1,0:T(8,128)(2,1)S(1)} %collective-permute-done.refs_6_), channel_id=1, source_target_pairs={{0,8},{4,12},{8,0},{12,4},{1,9},{5,13},{9,1},{13,5},{2,10},{6,14},... | collective-permute-start | bytes 552968 | tf_op jit(solution)/shard_map/ppermute | solution.py:92
  32.5 1.4 %shard_map.80 = (bf16[448,640]{1,0:T(8,128)(2,1)S(1)}, bf16[640,448]{1,0:T(8,128)(2,1)S(1)}, f32[1,640]{1,0:T(1,128)S(1)}, f32[480,1]{1,0:T(8,128)S(1)}, bf16[44...) custom-call(f32[32,28]{1,0:T(8,128)S(1)} %get-tuple-element.23.refs_, ...), custom_call_target="tpu_custom_call", output_to_operand_aliasing={{6}: (2, {})} | custom-call | flops 1 | bytes 1 | tf_op jit(solution)/shard_map/pallas_call | solution.py:83
  33.9 1.7 %collective-permute-done.4.refs_8_ = bf16[80,1152]{1,0:T(8,128)(2,1)S(1)} collective-permute-done((bf16[80,1152]{1,0:T(8,128)(2,1)S(1)}, bf16[80,1152]{1,0:T(8,128)(2,1)S(1)}, u32[]{:S(2)}, u32[]{:S(2)}) %collective-permute-start.4) | collective-permute-done | bytes 184352 | tf_op jit(solution)/shard_map/ppermute | solution.py:92
  35.6 1.3 %collective-permute-start.8 = (bf16[80,1152]{1,0:T(8,128)(2,1)S(1)}, bf16[80,1152]{1,0:T(8,128)(2,1)S(1)}, u32[]{:S(2)}, u32[]{:S(2)}) collective-permute-start(bf16[80,1152]{1,0:T(8,128)(2,1)S(1)} %get-tuple-element.39.refs_9_), channel_id=1, source_target_pairs={{8,12},{4,0},{9,13},{5,1},{10,14},{6,2},{11,15},{7,3},{24,28},{20,... | collective-permute-start | bytes 552968 | tf_op jit(solution)/shard_map/ppermute | solution.py:306
  36.9 2.6 %collective-permute-done.5.refs_10_ = bf16[80,1152]{1,0:T(8,128)(2,1)S(1)} collective-permute-done((bf16[80,1152]{1,0:T(8,128)(2,1)S(1)}, bf16[80,1152]{1,0:T(8,128)(2,1)S(1)}, u32[]{:S(2)}, u32[]{:S(2)}) %collective-permute-start.5) | collective-permute-done | bytes 184352 | tf_op jit(solution)/shard_map/ppermute | solution.py:92
  39.5 1.3 %collective-permute-start.9 = (bf16[80,1152]{1,0:T(8,128)(2,1)S(1)}, bf16[80,1152]{1,0:T(8,128)(2,1)S(1)}, u32[]{:S(2)}, u32[]{:S(2)}) collective-permute-start(bf16[80,1152]{1,0:T(8,128)(2,1)S(1)} %collective-permute-done.5.refs_10_), channel_id=1, source_target_pairs={{8,12},{4,0},{9,13},{5,1},{10,14},{6,2},{11,15},{7,3},{24,28},{20,... | collective-permute-start | bytes 552968 | tf_op jit(solution)/shard_map/ppermute | solution.py:306
  40.8 1.3 %shard_map.81 = (f32[160,448]{1,0:T(8,128)S(1)}, bf16[480,1152]{1,0:T(8,128)(2,1)S(1)}) custom-call(f32[1,640]{1,0:T(1,128)S(1)} %get-tuple-element.32.refs_0_, bf16[640,448]{1,0:T(8,128)(2,1)S(1)} %get-tuple-element.33.refs_1_, f32[480,1]{1,0:T(8,128)S(1)} %get-tuple-element.34.refs_2_, bf16[3,80,1152]{2,1,0:T(8,128)(2,1)S(1)} %get-tuple-element.35.refs_3_, ...), custom_call_target="tpu_custom_call" | custom-call | flops 1 | bytes 1 | tf_op jit(solution)/shard_map/pallas_call | solution.py:83
  42.1 1.5 %collective-permute-done.8.refs_6_ = bf16[80,1152]{1,0:T(8,128)(2,1)S(1)} collective-permute-done((bf16[80,1152]{1,0:T(8,128)(2,1)S(1)}, bf16[80,1152]{1,0:T(8,128)(2,1)S(1)}, u32[]{:S(2)}, u32[]{:S(2)}) %collective-permute-start.8) | collective-permute-done | bytes 184352 | tf_op jit(solution)/shard_map/ppermute | solution.py:306
  43.6 3.3 %collective-permute-done.9.refs_7_ = bf16[80,1152]{1,0:T(8,128)(2,1)S(1)} collective-permute-done((bf16[80,1152]{1,0:T(8,128)(2,1)S(1)}, bf16[80,1152]{1,0:T(8,128)(2,1)S(1)}, u32[]{:S(2)}, u32[]{:S(2)}) %collective-permute-start.9) | collective-permute-done | bytes 184352 | tf_op jit(solution)/shard_map/ppermute | solution.py:306
  46.9 1.0 %shard_map.82 = (f32[80,448]{1,0:T(8,128)S(1)}, f32[80,448]{1,0:T(8,128)S(1)}) custom-call(f32[1,640]{1,0:T(1,128)S(1)} %get-tuple-element.32.refs_0_, bf16[640,448]{1,0:T(8,128)(2,1)S(1)} %get-tuple-element.33.refs_1_, f32[160,448]{1,0:T(8,128)S(1)} %get-tuple-element.40.refs_2_, bf16[480,1152]{1,0:T(8,128)(2,1)S(1)} %get-tuple-element.41.refs_3_, ...), custom_call_target="tpu_custom_call" | custom-call | tf_op jit(solution)/shard_map/pallas_call | solution.py:83
  47.9 1.4 %collective-permute-done.10 = f32[80,448]{1,0:T(8,128)S(1)} collective-permute-done((f32[80,448]{1,0:T(8,128)S(1)}, f32[80,448]{1,0:T(8,128)S(1)}, u32[]{:S(2)}, u32[]{:S(2)}) %collective-permute-start.10) | collective-permute-done | bytes 143392 | tf_op jit(solution)/shard_map/ppermute | solution.py:88
  49.4 2.4 %collective-permute-start.12 = (bf16[80,448]{1,0:T(8,128)(2,1)S(1)}, bf16[80,448]{1,0:T(8,128)(2,1)S(1)}, u32[]{:S(2)}, u32[]{:S(2)}) collective-permute-start(bf16[80,448]{1,0:T(8,128)(2,1)S(1)} %add_convert_fusion.refs_4_), channel_id=1, source_target_pairs={{0,8},{4,12},{8,0},{12,4},{1,9},{5,13},{9,1},{13,5},{2,10},{6,14},... | collective-permute-start | bytes 215048 | tf_op jit(solution)/shard_map/ppermute | solution.py:92
  51.8 2.0 %collective-permute-start.13 = (bf16[80,448]{1,0:T(8,128)(2,1)S(1)}, bf16[80,448]{1,0:T(8,128)(2,1)S(1)}, u32[]{:S(2)}, u32[]{:S(2)}) collective-permute-start(bf16[80,448]{1,0:T(8,128)(2,1)S(1)} %add_convert_fusion.refs_4_), channel_id=1, source_target_pairs={{0,12},{4,8},{8,4},{12,0},{1,13},{5,9},{9,5},{13,1},{2,14},{6,10},... | collective-permute-start | bytes 215048 | tf_op jit(solution)/shard_map/ppermute | solution.py:92
  53.8 1.2 %collective-permute-done.11.refs_5_ = bf16[80,448]{1,0:T(8,128)(2,1)S(1)} collective-permute-done((bf16[80,448]{1,0:T(8,128)(2,1)S(1)}, bf16[80,448]{1,0:T(8,128)(2,1)S(1)}, u32[]{:S(2)}, u32[]{:S(2)}) %collective-permute-start.11) | collective-permute-done | bytes 71712 | tf_op jit(solution)/shard_map/ppermute | solution.py:92
  55.0 4.3 %collective-permute-done.12.refs_6_ = bf16[80,448]{1,0:T(8,128)(2,1)S(1)} collective-permute-done((bf16[80,448]{1,0:T(8,128)(2,1)S(1)}, bf16[80,448]{1,0:T(8,128)(2,1)S(1)}, u32[]{:S(2)}, u32[]{:S(2)}) %collective-permute-start.12) | collective-permute-done | bytes 71712 | tf_op jit(solution)/shard_map/ppermute | solution.py:92
  59.8 0.8 %collective-permute-done.16.refs_10_ = bf16[80,448]{1,0:T(8,128)(2,1)S(1)} collective-permute-done((bf16[80,448]{1,0:T(8,128)(2,1)S(1)}, bf16[80,448]{1,0:T(8,128)(2,1)S(1)}, u32[]{:S(2)}, u32[]{:S(2)}) %collective-permute-start.16) | collective-permute-done | bytes 71712 | tf_op jit(solution)/shard_map/ppermute | solution.py:88
  60.7 2.5 %shard_map.83 = (bf16[1,56,448]{2,1,0:T(8,128)(2,1)}, f32[1,56,128]{2,1,0:T(8,128)}) custom-call(bf16[448,640]{1,0:T(8,128)(2,1)S(1)} %get-tuple-element.29.refs_0_, bf16[448,448]{1,0:T(8,128)(2,1)S(1)} %get-tuple-element.30.refs_1_, f32[56,448]{1,0:T(8,128)S(1)} %get-tuple-element.31.refs_2_, s32[1,128]{1,0:T(1,128)S(1)} %copy-done.3, ...), custom_call_target="tpu_custom_call" | custom-call | tf_op jit(solution)/shard_map/pallas_call | solution.py:83
  (31 shorter events, 5.7 us)
Async XLA Ops:
  0.6 19.5 %copy-start = (bf16[512,3,1152]{2,0,1:T(8,128)(2,1)S(1)}, bf16[512,3,1152]{2,0,1:T(8,128)(2,1)}, u32[]{:S(2)}) copy-start(bf16[512,3,1152]{2,0,1:T(8,128)(2,1)} %param.11) | copy-start | bytes 10616836
  16.6 1.3 %copy-start.1 = (bf16[512,1152]{1,0:T(8,128)(2,1)S(1)}, bf16[512,1152]{1,0:T(8,128)(2,1)}, u32[]{:S(2)}) copy-start(bf16[512,1152]{1,0:T(8,128)(2,1)} %refs_1_.4) | copy-start | bytes 3538948
  18.2 8.2 %collective-permute-start.1 = (bf16[80,1152]{1,0:T(8,128)(2,1)S(1)}, bf16[80,1152]{1,0:T(8,128)(2,1)S(1)}, u32[]{:S(2)}, u32[]{:S(2)}) collective-permute-start(bf16[80,1152]{1,0:T(8,128)(2,1)S(1)} %get-tuple-element.27.refs_5_), channel_id=1, source_target_pairs={{0,4},{4,0},{8,12},{12,8},{1,5},{5,1},{9,13},{13,9},{2,6},{6,2},{1... | collective-permute-start | bytes 552968 | tf_op jit(solution)/shard_map/ppermute | solution.py:92
  18.7 9.7 %collective-permute-start.2 = (bf16[80,1152]{1,0:T(8,128)(2,1)S(1)}, bf16[80,1152]{1,0:T(8,128)(2,1)S(1)}, u32[]{:S(2)}, u32[]{:S(2)}) collective-permute-start(bf16[80,1152]{1,0:T(8,128)(2,1)S(1)} %get-tuple-element.27.refs_5_), channel_id=1, source_target_pairs={{0,8},{4,12},{8,0},{12,4},{1,9},{5,13},{9,1},{13,5},{2,10},{6,14},... | collective-permute-start | bytes 552968 | tf_op jit(solution)/shard_map/ppermute | solution.py:92
  19.4 5.5 %collective-permute-start = (bf16[80,1152]{1,0:T(8,128)(2,1)S(1)}, bf16[80,1152]{1,0:T(8,128)(2,1)S(1)}, u32[]{:S(2)}, u32[]{:S(2)}) collective-permute-start(bf16[80,1152]{1,0:T(8,128)(2,1)S(1)} %get-tuple-element.26), channel_id=1, source_target_pairs={{0,2},{2,0},{1,3},{3,1},{4,6},{6,4},{5,7},{7,5},{8,10},{10,8},{9,1... | collective-permute-start | bytes 552968 | tf_op jit(solution)/shard_map/ppermute | solution.py:88
  20.9 11.6 %copy-start.2 = (s32[1,4,4]{2,1,0:T(4,128)S(1)}, s32[1,4,4]{2,1,0:T(4,128)}, u32[]{:S(2)}) copy-start(s32[1,4,4]{2,1,0:T(4,128)} %refs_1_.5) | copy-start | bytes 196
  28.4 12.4 %collective-permute-start.3 = (bf16[3,80,1152]{2,1,0:T(8,128)(2,1)S(1)}, bf16[3,80,1152]{2,1,0:T(8,128)(2,1)S(1)}, u32[]{:S(2)}, u32[]{:S(2)}) collective-permute-start(bf16[3,80,1152]{2,1,0:T(8,128)(2,1)S(1)} %get-tuple-element.36), channel_id=1, source_target_pairs={{0,2},{2,0},{1,3},{3,1},{4,6},{6,4},{5,7},{7,5},{8,10},{10,8},{9,1... | collective-permute-start | bytes 1658888 | tf_op jit(solution)/shard_map/ppermute | solution.py:88
  29.0 6.6 %collective-permute-start.4 = (bf16[80,1152]{1,0:T(8,128)(2,1)S(1)}, bf16[80,1152]{1,0:T(8,128)(2,1)S(1)}, u32[]{:S(2)}, u32[]{:S(2)}) collective-permute-start(bf16[80,1152]{1,0:T(8,128)(2,1)S(1)} %collective-permute-done.refs_6_), channel_id=1, source_target_pairs={{0,4},{4,0},{8,12},{12,8},{1,5},{5,1},{9,13},{13,9},{2,6},{6,2},{1... | collective-permute-start | bytes 552968 | tf_op jit(solution)/shard_map/ppermute | solution.py:92
  29.0 10.5 %collective-permute-start.5 = (bf16[80,1152]{1,0:T(8,128)(2,1)S(1)}, bf16[80,1152]{1,0:T(8,128)(2,1)S(1)}, u32[]{:S(2)}, u32[]{:S(2)}) collective-permute-start(bf16[80,1152]{1,0:T(8,128)(2,1)S(1)} %collective-permute-done.refs_6_), channel_id=1, source_target_pairs={{0,8},{4,12},{8,0},{12,4},{1,9},{5,13},{9,1},{13,5},{2,10},{6,14},... | collective-permute-start | bytes 552968 | tf_op jit(solution)/shard_map/ppermute | solution.py:92
  31.2 10.9 %collective-permute-start.6 = (bf16[80,1152]{1,0:T(8,128)(2,1)S(1)}, bf16[80,1152]{1,0:T(8,128)(2,1)S(1)}, u32[]{:S(2)}, u32[]{:S(2)}) collective-permute-start(bf16[80,1152]{1,0:T(8,128)(2,1)S(1)} %get-tuple-element.27.refs_5_), channel_id=1, source_target_pairs={{4,8},{8,4},{5,9},{9,5},{6,10},{10,6},{7,11},{11,7},{20,24},{24,20... | collective-permute-start | bytes 552968 | tf_op jit(solution)/shard_map/ppermute | solution.py:305
  31.9 10.2 %collective-permute-start.7 = (bf16[80,1152]{1,0:T(8,128)(2,1)S(1)}, bf16[80,1152]{1,0:T(8,128)(2,1)S(1)}, u32[]{:S(2)}, u32[]{:S(2)}) collective-permute-start(bf16[80,1152]{1,0:T(8,128)(2,1)S(1)} %collective-permute-done.refs_6_), channel_id=1, source_target_pairs={{4,8},{8,4},{5,9},{9,5},{6,10},{10,6},{7,11},{11,7},{20,24},{24,20... | collective-permute-start | bytes 552968 | tf_op jit(solution)/shard_map/ppermute | solution.py:305
  35.6 8.0 %collective-permute-start.8 = (bf16[80,1152]{1,0:T(8,128)(2,1)S(1)}, bf16[80,1152]{1,0:T(8,128)(2,1)S(1)}, u32[]{:S(2)}, u32[]{:S(2)}) collective-permute-start(bf16[80,1152]{1,0:T(8,128)(2,1)S(1)} %get-tuple-element.39.refs_9_), channel_id=1, source_target_pairs={{8,12},{4,0},{9,13},{5,1},{10,14},{6,2},{11,15},{7,3},{24,28},{20,... | collective-permute-start | bytes 552968 | tf_op jit(solution)/shard_map/ppermute | solution.py:306
  39.5 7.4 %collective-permute-start.9 = (bf16[80,1152]{1,0:T(8,128)(2,1)S(1)}, bf16[80,1152]{1,0:T(8,128)(2,1)S(1)}, u32[]{:S(2)}, u32[]{:S(2)}) collective-permute-start(bf16[80,1152]{1,0:T(8,128)(2,1)S(1)} %collective-permute-done.5.refs_10_), channel_id=1, source_target_pairs={{8,12},{4,0},{9,13},{5,1},{10,14},{6,2},{11,15},{7,3},{24,28},{20,... | collective-permute-start | bytes 552968 | tf_op jit(solution)/shard_map/ppermute | solution.py:306
  42.1 18.6 %copy-start.3 = (s32[1,128]{1,0:T(1,128)S(1)}, s32[1,128]{1,0:T(1,128)}, u32[]{:S(2)}) copy-start(s32[1,128]{1,0:T(1,128)} %refs_3_.1) | copy-start | bytes 1540
  47.9 1.5 %collective-permute-start.10 = (f32[80,448]{1,0:T(8,128)S(1)}, f32[80,448]{1,0:T(8,128)S(1)}, u32[]{:S(2)}, u32[]{:S(2)}) collective-permute-start(f32[80,448]{1,0:T(8,128)S(1)} %get-tuple-element.43), channel_id=1, source_target_pairs={{0,1},{1,0},{2,3},{3,2},{4,5},{5,4},{6,7},{7,6},{8,9},{9,8},{10,11... | collective-permute-start | bytes 430088 | tf_op jit(solution)/shard_map/ppermute | solution.py:88
  49.4 5.6 %collective-permute-start.11 = (bf16[80,448]{1,0:T(8,128)(2,1)S(1)}, bf16[80,448]{1,0:T(8,128)(2,1)S(1)}, u32[]{:S(2)}, u32[]{:S(2)}) collective-permute-start(bf16[80,448]{1,0:T(8,128)(2,1)S(1)} %add_convert_fusion.refs_4_), channel_id=1, source_target_pairs={{0,4},{4,0},{8,12},{12,8},{1,5},{5,1},{9,13},{13,9},{2,6},{6,2},{1... | collective-permute-start | bytes 215048 | tf_op jit(solution)/shard_map/ppermute | solution.py:92
  49.4 9.8 %collective-permute-start.12 = (bf16[80,448]{1,0:T(8,128)(2,1)S(1)}, bf16[80,448]{1,0:T(8,128)(2,1)S(1)}, u32[]{:S(2)}, u32[]{:S(2)}) collective-permute-start(bf16[80,448]{1,0:T(8,128)(2,1)S(1)} %add_convert_fusion.refs_4_), channel_id=1, source_target_pairs={{0,8},{4,12},{8,0},{12,4},{1,9},{5,13},{9,1},{13,5},{2,10},{6,14},... | collective-permute-start | bytes 215048 | tf_op jit(solution)/shard_map/ppermute | solution.py:92
  51.8 7.4 %collective-permute-start.13 = (bf16[80,448]{1,0:T(8,128)(2,1)S(1)}, bf16[80,448]{1,0:T(8,128)(2,1)S(1)}, u32[]{:S(2)}, u32[]{:S(2)}) collective-permute-start(bf16[80,448]{1,0:T(8,128)(2,1)S(1)} %add_convert_fusion.refs_4_), channel_id=1, source_target_pairs={{0,12},{4,8},{8,4},{12,0},{1,13},{5,9},{9,5},{13,1},{2,14},{6,10},... | collective-permute-start | bytes 215048 | tf_op jit(solution)/shard_map/ppermute | solution.py:92
  53.8 5.9 %collective-permute-start.14 = (bf16[80,448]{1,0:T(8,128)(2,1)S(1)}, bf16[80,448]{1,0:T(8,128)(2,1)S(1)}, u32[]{:S(2)}, u32[]{:S(2)}) collective-permute-start(bf16[80,448]{1,0:T(8,128)(2,1)S(1)} %add_convert_fusion.refs_4_), channel_id=1, source_target_pairs={{0,1},{1,0},{2,3},{3,2},{4,5},{5,4},{6,7},{7,6},{8,9},{9,8},{10,11... | collective-permute-start | bytes 215048 | tf_op jit(solution)/shard_map/ppermute | solution.py:88
  55.0 4.8 %collective-permute-start.15 = (bf16[80,448]{1,0:T(8,128)(2,1)S(1)}, bf16[80,448]{1,0:T(8,128)(2,1)S(1)}, u32[]{:S(2)}, u32[]{:S(2)}) collective-permute-start(bf16[80,448]{1,0:T(8,128)(2,1)S(1)} %collective-permute-done.11.refs_5_), channel_id=1, source_target_pairs={{0,1},{1,0},{2,3},{3,2},{4,5},{5,4},{6,7},{7,6},{8,9},{9,8},{10,11... | collective-permute-start | bytes 215048 | tf_op jit(solution)/shard_map/ppermute | solution.py:88
  59.2 1.3 %collective-permute-start.16 = (bf16[80,448]{1,0:T(8,128)(2,1)S(1)}, bf16[80,448]{1,0:T(8,128)(2,1)S(1)}, u32[]{:S(2)}, u32[]{:S(2)}) collective-permute-start(bf16[80,448]{1,0:T(8,128)(2,1)S(1)} %collective-permute-done.12.refs_6_), channel_id=1, source_target_pairs={{0,1},{1,0},{2,3},{3,2},{4,5},{5,4},{6,7},{7,6},{8,9},{9,8},{10,11... | collective-permute-start | bytes 215048 | tf_op jit(solution)/shard_map/ppermute | solution.py:88
  59.2 1.4 %collective-permute-start.17 = (bf16[80,448]{1,0:T(8,128)(2,1)S(1)}, bf16[80,448]{1,0:T(8,128)(2,1)S(1)}, u32[]{:S(2)}, u32[]{:S(2)}) collective-permute-start(bf16[80,448]{1,0:T(8,128)(2,1)S(1)} %collective-permute-done.13.refs_7_), channel_id=1, source_target_pairs={{0,1},{1,0},{2,3},{3,2},{4,5},{5,4},{6,7},{7,6},{8,9},{9,8},{10,11... | collective-permute-start | bytes 215048 | tf_op jit(solution)/shard_map/ppermute | solution.py:88

commit v11 on v8

--- a/solution.py
+++ b/solution.py
@@ -223,6 +223,7 @@
         [lists],
         [shape(column, table_rows, dtype=BF16), shape(2 * positions * feats, kslots)],
         small,
+        cost=(10**9, 10**7),
     )
 
     def encode(picks, enc):
@@ -244,7 +245,15 @@
     )
     dec_rows = jnp.transpose(dec_rows, (1, 0, 2)).astype(BF16)
     dec_rows = [dec_rows[:, k * listed : (k + 1) * listed] for k in range(poses)]
+    *dec_rows, ring[1][-1] = lax.optimization_barrier((*dec_rows, ring[1][-1]))
     dec_rows = [dec_rows[0]] + [rotate(dec_rows[k], "pos", k) for k in range(1, poses)]
+
+    ring.append([ring_next(rows, "feat") for rows in ring[-1]])
+
+    order = [(0, 0)] + [(k, q) for k in range(1, feats - 1) for q in range(poses)]
+    soon = len(order)
+    order += [(0, q) for q in range(1, poses)] + [(feats - 1, q) for q in range(poses)]
+    own_lists = [order.index((0, q)) for q in range(poses)]
 
     def places(table, pattern):
         feat, pos, rep = place()
@@ -255,7 +264,11 @@
             step = jnp.where(step < 0.0, step + feats, step)
             turn = pos - (owner - feat_of * poses)
             turn = jnp.where(turn < 0.0, turn + poses, turn)
-            return (step * poses + turn) * listed + rank
+            at = step * poses + turn
+            at = jnp.where(step < feats - 1.0, at - (poses - 1), at)
+            at = jnp.where(step == 0.0, turn + (feats - 2) * poses, at)
+            at = jnp.where((step == 0.0) & (turn == 0.0), 0.0, at)
+            return at * listed + rank
 
         ids_row, vals_row = as_rows(table)
         ids_col = as_col(table)
@@ -270,7 +283,8 @@
         placing_t = padded(owner_row, rank_row) == iota((total, slots), 0)
         layer = ids_col - floor_div(ids_col, layers) * layers
         layer_row = jnp.sum(jnp.where(placing, layer, 0.0), axis=0, keepdims=True)
-        mine = placing_t[:column]
+        mine = [placing_t[at * listed : (at + 1) * listed] for at in own_lists]
+        mine = jnp.concatenate(mine, axis=0)
         gain = jnp.sum(jnp.where(mine, vals_row, 0.0), axis=1, keepdims=True)
         source_layer = ids_row - floor_div(ids_row, layers) * layers
         source_layer = jnp.sum(jnp.where(mine, source_layer, 0.0), axis=1, keepdims=True)
@@ -298,7 +312,7 @@
         placing, placing_t = placing.astype(BF16), placing_t.astype(BF16)
         return placing, placing_t, layer_row, gains, mask.astype(BF16), own_mask
 
-    placing, placing_t, layer_row, gains, mask, own_mask, ring[1][-1] = on_core(
+    placing, placing_t, layer_row, gains, mask, own_mask, ring[2][0] = on_core(
         places,
         [my_list, block_pattern],
         [
@@ -310,17 +324,17 @@
             shape(result_rows, slots),
         ],
         small,
-        through=ring[1][-1:],
+        through=[ring[2][0]],
         cost=(1, 1),
     )
-    for _ in range(2, feats):
+    for _ in range(3, feats):
         ring.append([ring_next(rows, "feat") for rows in ring[-1]])
 
     def products(first, enc, dec, layer_row, placing_t):
-        count = len(enc) // poses
-        every = dot(dec, jnp.concatenate(enc, axis=0), NT)
-        lanes = slice(first * column, (first + count) * column)
-        raw = jnp.zeros((column, count * column), F32)
+        enc = jnp.concatenate(enc, axis=0)
+        every = dot(dec, enc, NT)
+        lanes = slice(first * listed, first * listed + enc.shape[0])
+        raw = jnp.zeros((column, enc.shape[0]), F32)
         for l in range(depth):
             rows = every[l * column : (l + 1) * column]
             raw = raw + jnp.where(layer_row[:, lanes] == l + 1.0, rows, 0.0)
@@ -333,7 +347,7 @@
         return products(0, values[poses:], dec, layer_row, placing_t), dec
 
     def late(layer_row, placing_t, so_far, dec, *values):
-        raw = so_far + products(feats - 1, values, dec, layer_row, placing_t)
+        raw = so_far + products(soon, values, dec, layer_row, placing_t)
         first = place()[2] == 0.0
         return (
             jnp.where(first, raw[:half], raw[half:]),
@@ -342,14 +356,14 @@
 
     so_far, scaled = on_core(
         early,
-        [layer_row, placing_t, gains] + dec_rows + [rows for step in ring[:-1] for rows in step],
+        [layer_row, placing_t, gains] + dec_rows + [ring[k][q] for k, q in order[:soon]],
         [shape(column, slots), shape(depth * column, width, dtype=BF16)],
         small,
         cost=(1, 1),
     )
     keep, send = on_core(
         late,
-        [layer_row, placing_t, so_far, scaled] + ring[-1],
+        [layer_row, placing_t, so_far, scaled] + [ring[k][q] for k, q in order[soon:]],
         [shape(half, slots)] * 2,
         small,
     )
@@ -360,10 +374,12 @@
     def finish(placing, mask, own_mask, targets, *values):
         feat, _, rep = place()
         first = rep == 0.0
-        parts = []
+        chips = []
         for mine, other in zip(values[:feats], values[feats:]):
-            parts += [jnp.where(first, mine, other), jnp.where(first, other, mine)]
-        padded = jnp.concatenate(parts, axis=0)
+            chips.append((jnp.where(first, mine, other), jnp.where(first, other, mine)))
+        chips = [jnp.concatenate(chip, axis=0) for chip in chips]
+        padded = [chips[k][q * listed : (q + 1) * listed] for k, q in order]
+        padded = jnp.concatenate(padded, axis=0)
         magnitude = jnp.abs(dot(placing, padded) * mask.astype(F32))
         total = jnp.maximum(jnp.sum(magnitude, axis=0, keepdims=True), 1.0)
         magnitude = magnitude.astype(BF16)

time: 64 us -> 61.1 us (0.955)
  waiting for transfers between devices: 26 us -> 22.3 us
  starting transfers between devices: 12.4 us -> 14.2 us
  local copies, waits for them, and re-layouts: 1.37 us -> 0.12 us
    ppermute x4, waiting for transfers between devices: 7.47 us -> 4.37 us  [ring_next(): return lax.ppermute(x, axis, steps)]
    ppermute x2, waiting for transfers between devices: 9.08 us -> 6.69 us  [ring_next(): return lax.ppermute(x, (axis, across), pairs)]
    ppermute x7, waiting for transfers between devices: 2.65 us -> 4.31 us  [rotate(): lax.ppermute(x, axis, [(i, (i + step) % count) for i in range(count)])]
    unnamed x8, local copies, waits for them, and re-layouts: 1.29 us -> 0.03 us
    ppermute x4, starting transfers between devices: 4.77 us -> 5.89 us  [ring_next(): return lax.ppermute(x, axis, steps)]
    ppermute x7, starting transfers between devices: 1.22 us -> 2.3 us  [rotate(): lax.ppermute(x, axis, [(i, (i + step) % count) for i in range(count)])]
    ppermute x2, starting transfers between devices: 2.11 us -> 1.31 us  [ring_next(): return lax.ppermute(x, (axis, across), pairs)]
  transfers between devices with their start and end apart: 16 -> 16, of which waited for: 9 -> 10; matrix products, arithmetic and copies ran while one was open for 0% -> 1% of each run, Pallas kernels for 4% -> 5%
where the time goes in v11:
time: 61.1 us; the launch traced here: 60.9 us
  waiting for transfers between devices  22.3 us (36%)
  starting transfers between devices  14.2 us (23%)
  blocking collectives  14.1 us (23%)
  Pallas kernels  8.67 us (14%)
  matrix products  0.77 us (1%)
  between operations  0.77 us (1%)
    all_to_all x1, blocking collectives, per_device(): lax.all_to_all(packed, ('feat', 'pos'), split_axis=0, concat_axis=0, tile...  14.1 us
    pallas_call x7, Pallas kernels, on_core(): return list(call(*args, *streams, *through))  8.67 us
    ppermute x3, waiting for transfers between devices, ring_spread(): lax.ppermute(x, axis, [(order[i], order[(i + k) % count]) for i in range(...  6.9 us
    ppermute x2, waiting for transfers between devices, ring_next(): return lax.ppermute(x, (axis, across), pairs)  6.69 us
    ppermute x4, starting transfers between devices, ring_next(): return lax.ppermute(x, axis, steps)  5.89 us
    ppermute x3, starting transfers between devices, ring_spread(): lax.ppermute(x, axis, [(order[i], order[(i + k) % count]) for i in range(...  4.7 us
    ppermute x4, waiting for transfers between devices, ring_next(): return lax.ppermute(x, axis, steps)  4.37 us
    ppermute x7, waiting for transfers between devices, rotate(): lax.ppermute(x, axis, [(i, (i + step) % count) for i in range(count)])  4.31 us
  transfers between devices with their start and end apart: 16, of which 10 were waited for; matrix products, arithmetic and copies ran while one was open for 1% of the time, Pallas kernels for 5%

profile of v11, /device:TPU:0, one launch (start us, length us, event | category | flops | bytes accessed | tf_op | source)
XLA Modules:
  0.0 60.9 jit_solution(5171654902915083742)
XLA Ops:
  0.6 1.5 %shard_map.77 = f32[8,8,128]{2,1,0:T(8,128)} custom-call(s32[1,4,28]{2,1,0:T(4,128)} %refs_0_.1, f32[1,4,28]{2,1,0:T(4,128)} %refs_1_.3), custom_call_target="tpu_custom_call" | custom-call | tf_op jit(solution)/shard_map/pallas_call | solution.py:83
  2.1 14.1 %all_to_all.5.refs_0_ = f32[8,8,128]{2,1,0:T(8,128)S(1)} all-to-all(f32[8,8,128]{2,1,0:T(8,128)} %shard_map.77), channel_id=1, replica_groups=mesh['grp'=2,'feat'=4,'pos'=2,'rep'=2] {'feat','pos'}, dimensions={0} | all-to-all | bytes 65536 | tf_op jit(solution)/shard_map/all_to_all | solution.py:159
  17.7 0.7 %collective-permute-start.2 = (bf16[80,1152]{1,0:T(8,128)(2,1)S(1)}, bf16[80,1152]{1,0:T(8,128)(2,1)S(1)}, u32[]{:S(2)}, u32[]{:S(2)}) collective-permute-start(bf16[80,1152]{1,0:T(8,128)(2,1)S(1)} %get-tuple-element.31), channel_id=1, source_target_pairs={{0,10},{2,8},{8,14},{10,12},{12,6},{14,4},{4,2},{6,0},{1,11},{3,9}... | collective-permute-start | bytes 552968 | tf_op jit(solution)/shard_map/ppermute | solution.py:104
  18.4 0.8 %fusion = bf16[3,160,1152]{2,1,0:T(8,128)(2,1)S(1)} fusion(bf16[512,3,1152]{2,0,1:T(8,128)(2,1)S(1)} %copy-done, bf16[160,512]{1,0:T(8,128)(2,1)S(1)} %get-tuple-element.30), kind=kOutput, calls=%fused_computation.1 | convolution fusion | flops 566784000 | bytes 4808704 | tf_op jit(solution)/shard_map/dot_general | solution.py:243
  19.3 6.7 %collective-permute-done.2.refs_7_ = bf16[80,1152]{1,0:T(8,128)(2,1)S(1)} collective-permute-done((bf16[80,1152]{1,0:T(8,128)(2,1)S(1)}, bf16[80,1152]{1,0:T(8,128)(2,1)S(1)}, u32[]{:S(2)}, u32[]{:S(2)}) %collective-permute-start.2) | collective-permute-done | bytes 184352 | tf_op jit(solution)/shard_map/ppermute | solution.py:104
  26.0 1.6 %collective-permute-start.3 = (bf16[3,80,1152]{2,1,0:T(8,128)(2,1)S(1)}, bf16[3,80,1152]{2,1,0:T(8,128)(2,1)S(1)}, u32[]{:S(2)}, u32[]{:S(2)}) collective-permute-start(bf16[3,80,1152]{2,1,0:T(8,128)(2,1)S(1)} %get-tuple-element.33), channel_id=1, source_target_pairs={{0,2},{2,0},{1,3},{3,1},{4,6},{6,4},{5,7},{7,5},{8,10},{10,8},{9,1... | collective-permute-start | bytes 1658888 | tf_op jit(solution)/shard_map/ppermute | solution.py:88
  27.6 1.7 %collective-permute-start.1 = (bf16[80,1152]{1,0:T(8,128)(2,1)S(1)}, bf16[80,1152]{1,0:T(8,128)(2,1)S(1)}, u32[]{:S(2)}, u32[]{:S(2)}) collective-permute-start(bf16[80,1152]{1,0:T(8,128)(2,1)S(1)} %collective-permute-done.refs_6_), channel_id=1, source_target_pairs={{0,8},{8,12},{12,4},{4,0},{1,9},{9,13},{13,5},{5,1},{2,10},{10,14}... | collective-permute-start | bytes 552968 | tf_op jit(solution)/shard_map/ppermute | solution.py:101
  29.3 0.7 %collective-permute-start.5 = (bf16[80,1152]{1,0:T(8,128)(2,1)S(1)}, bf16[80,1152]{1,0:T(8,128)(2,1)S(1)}, u32[]{:S(2)}, u32[]{:S(2)}) collective-permute-start(bf16[80,1152]{1,0:T(8,128)(2,1)S(1)} %get-tuple-element.31), channel_id=1, source_target_pairs={{0,2},{2,0},{1,3},{3,1},{4,6},{6,4},{5,7},{7,5},{8,10},{10,8},{9,1... | collective-permute-start | bytes 552968 | tf_op jit(solution)/shard_map/ppermute | solution.py:88
  29.9 3.2 %collective-permute-done.1.refs_2_ = bf16[80,1152]{1,0:T(8,128)(2,1)S(1)} collective-permute-done((bf16[80,1152]{1,0:T(8,128)(2,1)S(1)}, bf16[80,1152]{1,0:T(8,128)(2,1)S(1)}, u32[]{:S(2)}, u32[]{:S(2)}) %collective-permute-start.1) | collective-permute-done | bytes 184352 | tf_op jit(solution)/shard_map/ppermute | solution.py:101
  33.1 1.5 %shard_map.80 = (bf16[448,640]{1,0:T(8,128)(2,1)S(1)}, bf16[640,448]{1,0:T(8,128)(2,1)S(1)}, f32[1,640]{1,0:T(1,128)S(1)}, f32[480,1]{1,0:T(8,128)S(1)}, bf16[44...) custom-call(f32[32,28]{1,0:T(8,128)S(1)} %get-tuple-element.21.refs_, ...), custom_call_target="tpu_custom_call", output_to_operand_aliasing={{6}: (2, {})} | custom-call | flops 1 | bytes 1 | tf_op jit(solution)/shard_map/pallas_call | solution.py:83
  34.6 2.8 %collective-permute-start.6 = (bf16[80,1152]{1,0:T(8,128)(2,1)S(1)}, bf16[80,1152]{1,0:T(8,128)(2,1)S(1)}, u32[]{:S(2)}, u32[]{:S(2)}) collective-permute-start(bf16[80,1152]{1,0:T(8,128)(2,1)S(1)} %get-tuple-element.35.refs_8_), channel_id=1, source_target_pairs={{0,8},{8,12},{12,4},{4,0},{1,9},{9,13},{13,5},{5,1},{2,10},{10,14}... | collective-permute-start | bytes 552968 | tf_op jit(solution)/shard_map/ppermute | solution.py:101
  37.5 1.3 %collective-permute-start.7 = (bf16[80,1152]{1,0:T(8,128)(2,1)S(1)}, bf16[80,1152]{1,0:T(8,128)(2,1)S(1)}, u32[]{:S(2)}, u32[]{:S(2)}) collective-permute-start(bf16[80,1152]{1,0:T(8,128)(2,1)S(1)} %collective-permute-done.4.refs_9_), channel_id=1, source_target_pairs={{0,8},{8,12},{12,4},{4,0},{1,9},{9,13},{13,5},{5,1},{2,10},{10,14}... | collective-permute-start | bytes 552968 | tf_op jit(solution)/shard_map/ppermute | solution.py:101
  38.8 1.0 %collective-permute-done.3.refs_4_ = bf16[3,80,1152]{2,1,0:T(8,128)(2,1)S(1)} collective-permute-done((bf16[3,80,1152]{2,1,0:T(8,128)(2,1)S(1)}, bf16[3,80,1152]{2,1,0:T(8,128)(2,1)S(1)}, u32[]{:S(2)}, u32[]{:S(2)}) %collective-permute-start.3) | collective-permute-done | bytes 552992 | tf_op jit(solution)/shard_map/ppermute | solution.py:88
  39.8 1.3 %shard_map.81 = (f32[160,448]{1,0:T(8,128)S(1)}, bf16[480,1152]{1,0:T(8,128)(2,1)S(1)}) custom-call(f32[1,640]{1,0:T(1,128)S(1)} %get-tuple-element.27.refs_0_, bf16[640,448]{1,0:T(8,128)(2,1)S(1)} %get-tuple-element.28.refs_1_, f32[480,1]{1,0:T(8,128)S(1)} %get-tuple-element.29.refs_2_, bf16[3,80,1152]{2,1,0:T(8,128)(2,1)S(1)} %get-tuple-element.32.refs_3_, ...), custom_call_target="tpu_custom_call" | custom-call | flops 1 | bytes 1 | tf_op jit(solution)/shard_map/pallas_call | solution.py:83
  41.1 0.7 %collective-permute-done.5.refs_4_ = bf16[80,1152]{1,0:T(8,128)(2,1)S(1)} collective-permute-done((bf16[80,1152]{1,0:T(8,128)(2,1)S(1)}, bf16[80,1152]{1,0:T(8,128)(2,1)S(1)}, u32[]{:S(2)}, u32[]{:S(2)}) %collective-permute-start.5) | collective-permute-done | bytes 184352 | tf_op jit(solution)/shard_map/ppermute | solution.py:88
  41.8 1.2 %collective-permute-done.7.refs_6_ = bf16[80,1152]{1,0:T(8,128)(2,1)S(1)} collective-permute-done((bf16[80,1152]{1,0:T(8,128)(2,1)S(1)}, bf16[80,1152]{1,0:T(8,128)(2,1)S(1)}, u32[]{:S(2)}, u32[]{:S(2)}) %collective-permute-start.7) | collective-permute-done | bytes 184352 | tf_op jit(solution)/shard_map/ppermute | solution.py:101
  43.0 1.0 %shard_map.82 = (f32[80,448]{1,0:T(8,128)S(1)}, f32[80,448]{1,0:T(8,128)S(1)}) custom-call(f32[1,640]{1,0:T(1,128)S(1)} %get-tuple-element.27.refs_0_, bf16[640,448]{1,0:T(8,128)(2,1)S(1)} %get-tuple-element.28.refs_1_, f32[160,448]{1,0:T(8,128)S(1)} %get-tuple-element.36.refs_2_, bf16[480,1152]{1,0:T(8,128)(2,1)S(1)} %get-tuple-element.37.refs_3_, ...), custom_call_target="tpu_custom_call" | custom-call | tf_op jit(solution)/shard_map/pallas_call | solution.py:83
  44.0 1.4 %collective-permute-done.8 = f32[80,448]{1,0:T(8,128)S(1)} collective-permute-done((f32[80,448]{1,0:T(8,128)S(1)}, f32[80,448]{1,0:T(8,128)S(1)}, u32[]{:S(2)}, u32[]{:S(2)}) %collective-permute-start.8) | collective-permute-done | bytes 143392 | tf_op jit(solution)/shard_map/ppermute | solution.py:88
  45.5 2.9 %collective-permute-start.9 = (bf16[80,448]{1,0:T(8,128)(2,1)S(1)}, bf16[80,448]{1,0:T(8,128)(2,1)S(1)}, u32[]{:S(2)}, u32[]{:S(2)}) collective-permute-start(bf16[80,448]{1,0:T(8,128)(2,1)S(1)} %add_convert_fusion.refs_4_), channel_id=1, source_target_pairs={{0,8},{8,12},{12,4},{4,0},{1,9},{9,13},{13,5},{5,1},{2,10},{10,14}... | collective-permute-start | bytes 215048 | tf_op jit(solution)/shard_map/ppermute | solution.py:111
  48.4 1.8 %collective-permute-start.10 = (bf16[80,448]{1,0:T(8,128)(2,1)S(1)}, bf16[80,448]{1,0:T(8,128)(2,1)S(1)}, u32[]{:S(2)}, u32[]{:S(2)}) collective-permute-start(bf16[80,448]{1,0:T(8,128)(2,1)S(1)} %add_convert_fusion.refs_4_), channel_id=1, source_target_pairs={{0,12},{8,4},{12,0},{4,8},{1,13},{9,5},{13,1},{5,9},{2,14},{10,6},... | collective-permute-start | bytes 215048 | tf_op jit(solution)/shard_map/ppermute | solution.py:111
  50.8 4.5 %collective-permute-done.10.refs_6_ = bf16[80,448]{1,0:T(8,128)(2,1)S(1)} collective-permute-done((bf16[80,448]{1,0:T(8,128)(2,1)S(1)}, bf16[80,448]{1,0:T(8,128)(2,1)S(1)}, u32[]{:S(2)}, u32[]{:S(2)}) %collective-permute-start.10) | collective-permute-done | bytes 71712 | tf_op jit(solution)/shard_map/ppermute | solution.py:111
  55.3 1.8 %collective-permute-done.11.refs_7_ = bf16[80,448]{1,0:T(8,128)(2,1)S(1)} collective-permute-done((bf16[80,448]{1,0:T(8,128)(2,1)S(1)}, bf16[80,448]{1,0:T(8,128)(2,1)S(1)}, u32[]{:S(2)}, u32[]{:S(2)}) %collective-permute-start.11) | collective-permute-done | bytes 71712 | tf_op jit(solution)/shard_map/ppermute | solution.py:111
  57.1 1.3 %collective-permute-done.15.refs_11_ = bf16[80,448]{1,0:T(8,128)(2,1)S(1)} collective-permute-done((bf16[80,448]{1,0:T(8,128)(2,1)S(1)}, bf16[80,448]{1,0:T(8,128)(2,1)S(1)}, u32[]{:S(2)}, u32[]{:S(2)}) %collective-permute-start.15) | collective-permute-done | bytes 71712 | tf_op jit(solution)/shard_map/ppermute | solution.py:88
  58.3 2.5 %shard_map.83 = (bf16[1,56,448]{2,1,0:T(8,128)(2,1)}, f32[1,56,128]{2,1,0:T(8,128)}) custom-call(bf16[448,640]{1,0:T(8,128)(2,1)S(1)} %get-tuple-element.24.refs_0_, bf16[448,448]{1,0:T(8,128)(2,1)S(1)} %get-tuple-element.25.refs_1_, f32[56,448]{1,0:T(8,128)S(1)} %get-tuple-element.26.refs_2_, s32[1,128]{1,0:T(1,128)S(1)} %copy-done.3, ...), custom_call_target="tpu_custom_call" | custom-call | tf_op jit(solution)/shard_map/pallas_call | solution.py:83
  (27 shorter events, 2.4 us)
Async XLA Ops:
  0.6 17.8 %copy-start = (bf16[512,3,1152]{2,0,1:T(8,128)(2,1)S(1)}, bf16[512,3,1152]{2,0,1:T(8,128)(2,1)}, u32[]{:S(2)}) copy-start(bf16[512,3,1152]{2,0,1:T(8,128)(2,1)} %param.11) | copy-start | bytes 10616836
  2.1 14.6 %copy-start.1 = (bf16[512,1152]{1,0:T(8,128)(2,1)S(1)}, bf16[512,1152]{1,0:T(8,128)(2,1)}, u32[]{:S(2)}) copy-start(bf16[512,1152]{1,0:T(8,128)(2,1)} %refs_1_.4) | copy-start | bytes 3538948
  17.1 10.4 %collective-permute-start = (bf16[80,1152]{1,0:T(8,128)(2,1)S(1)}, bf16[80,1152]{1,0:T(8,128)(2,1)S(1)}, u32[]{:S(2)}, u32[]{:S(2)}) collective-permute-start(bf16[80,1152]{1,0:T(8,128)(2,1)S(1)} %get-tuple-element.23.refs_5_), channel_id=1, source_target_pairs={{0,8},{2,10},{8,12},{10,14},{12,4},{14,6},{4,0},{6,2},{1,9},{3,11}... | collective-permute-start | bytes 552968 | tf_op jit(solution)/shard_map/ppermute | solution.py:104
  17.7 8.3 %collective-permute-start.2 = (bf16[80,1152]{1,0:T(8,128)(2,1)S(1)}, bf16[80,1152]{1,0:T(8,128)(2,1)S(1)}, u32[]{:S(2)}, u32[]{:S(2)}) collective-permute-start(bf16[80,1152]{1,0:T(8,128)(2,1)S(1)} %get-tuple-element.31), channel_id=1, source_target_pairs={{0,10},{2,8},{8,14},{10,12},{12,6},{14,4},{4,2},{6,0},{1,11},{3,9}... | collective-permute-start | bytes 552968 | tf_op jit(solution)/shard_map/ppermute | solution.py:104
  19.2 13.9 %copy-start.2 = (s32[1,4,4]{2,1,0:T(4,128)S(1)}, s32[1,4,4]{2,1,0:T(4,128)}, u32[]{:S(2)}) copy-start(s32[1,4,4]{2,1,0:T(4,128)} %refs_1_.5) | copy-start | bytes 196
  26.0 13.8 %collective-permute-start.3 = (bf16[3,80,1152]{2,1,0:T(8,128)(2,1)S(1)}, bf16[3,80,1152]{2,1,0:T(8,128)(2,1)S(1)}, u32[]{:S(2)}, u32[]{:S(2)}) collective-permute-start(bf16[3,80,1152]{2,1,0:T(8,128)(2,1)S(1)} %get-tuple-element.33), channel_id=1, source_target_pairs={{0,2},{2,0},{1,3},{3,1},{4,6},{6,4},{5,7},{7,5},{8,10},{10,8},{9,1... | collective-permute-start | bytes 1658888 | tf_op jit(solution)/shard_map/ppermute | solution.py:88
  27.6 5.5 %collective-permute-start.1 = (bf16[80,1152]{1,0:T(8,128)(2,1)S(1)}, bf16[80,1152]{1,0:T(8,128)(2,1)S(1)}, u32[]{:S(2)}, u32[]{:S(2)}) collective-permute-start(bf16[80,1152]{1,0:T(8,128)(2,1)S(1)} %collective-permute-done.refs_6_), channel_id=1, source_target_pairs={{0,8},{8,12},{12,4},{4,0},{1,9},{9,13},{13,5},{5,1},{2,10},{10,14}... | collective-permute-start | bytes 552968 | tf_op jit(solution)/shard_map/ppermute | solution.py:101
  29.3 8.2 %collective-permute-start.4 = (bf16[80,1152]{1,0:T(8,128)(2,1)S(1)}, bf16[80,1152]{1,0:T(8,128)(2,1)S(1)}, u32[]{:S(2)}, u32[]{:S(2)}) collective-permute-start(bf16[80,1152]{1,0:T(8,128)(2,1)S(1)} %collective-permute-done.2.refs_7_), channel_id=1, source_target_pairs={{0,8},{8,12},{12,4},{4,0},{1,9},{9,13},{13,5},{5,1},{2,10},{10,14}... | collective-permute-start | bytes 552968 | tf_op jit(solution)/shard_map/ppermute | solution.py:101
  29.3 12.5 %collective-permute-start.5 = (bf16[80,1152]{1,0:T(8,128)(2,1)S(1)}, bf16[80,1152]{1,0:T(8,128)(2,1)S(1)}, u32[]{:S(2)}, u32[]{:S(2)}) collective-permute-start(bf16[80,1152]{1,0:T(8,128)(2,1)S(1)} %get-tuple-element.31), channel_id=1, source_target_pairs={{0,2},{2,0},{1,3},{3,1},{4,6},{6,4},{5,7},{7,5},{8,10},{10,8},{9,1... | collective-permute-start | bytes 552968 | tf_op jit(solution)/shard_map/ppermute | solution.py:88
  34.6 7.2 %collective-permute-start.6 = (bf16[80,1152]{1,0:T(8,128)(2,1)S(1)}, bf16[80,1152]{1,0:T(8,128)(2,1)S(1)}, u32[]{:S(2)}, u32[]{:S(2)}) collective-permute-start(bf16[80,1152]{1,0:T(8,128)(2,1)S(1)} %get-tuple-element.35.refs_8_), channel_id=1, source_target_pairs={{0,8},{8,12},{12,4},{4,0},{1,9},{9,13},{13,5},{5,1},{2,10},{10,14}... | collective-permute-start | bytes 552968 | tf_op jit(solution)/shard_map/ppermute | solution.py:101
  37.5 5.5 %collective-permute-start.7 = (bf16[80,1152]{1,0:T(8,128)(2,1)S(1)}, bf16[80,1152]{1,0:T(8,128)(2,1)S(1)}, u32[]{:S(2)}, u32[]{:S(2)}) collective-permute-start(bf16[80,1152]{1,0:T(8,128)(2,1)S(1)} %collective-permute-done.4.refs_9_), channel_id=1, source_target_pairs={{0,8},{8,12},{12,4},{4,0},{1,9},{9,13},{13,5},{5,1},{2,10},{10,14}... | collective-permute-start | bytes 552968 | tf_op jit(solution)/shard_map/ppermute | solution.py:101
  41.1 17.2 %copy-start.3 = (s32[1,128]{1,0:T(1,128)S(1)}, s32[1,128]{1,0:T(1,128)}, u32[]{:S(2)}) copy-start(s32[1,128]{1,0:T(1,128)} %refs_3_.1) | copy-start | bytes 1540
  44.0 1.5 %collective-permute-start.8 = (f32[80,448]{1,0:T(8,128)S(1)}, f32[80,448]{1,0:T(8,128)S(1)}, u32[]{:S(2)}, u32[]{:S(2)}) collective-permute-start(f32[80,448]{1,0:T(8,128)S(1)} %get-tuple-element.39), channel_id=1, source_target_pairs={{0,1},{1,0},{2,3},{3,2},{4,5},{5,4},{6,7},{7,6},{8,9},{9,8},{10,11... | collective-permute-start | bytes 430088 | tf_op jit(solution)/shard_map/ppermute | solution.py:88
  45.5 5.3 %collective-permute-start.9 = (bf16[80,448]{1,0:T(8,128)(2,1)S(1)}, bf16[80,448]{1,0:T(8,128)(2,1)S(1)}, u32[]{:S(2)}, u32[]{:S(2)}) collective-permute-start(bf16[80,448]{1,0:T(8,128)(2,1)S(1)} %add_convert_fusion.refs_4_), channel_id=1, source_target_pairs={{0,8},{8,12},{12,4},{4,0},{1,9},{9,13},{13,5},{5,1},{2,10},{10,14}... | collective-permute-start | bytes 215048 | tf_op jit(solution)/shard_map/ppermute | solution.py:111
  48.4 6.9 %collective-permute-start.10 = (bf16[80,448]{1,0:T(8,128)(2,1)S(1)}, bf16[80,448]{1,0:T(8,128)(2,1)S(1)}, u32[]{:S(2)}, u32[]{:S(2)}) collective-permute-start(bf16[80,448]{1,0:T(8,128)(2,1)S(1)} %add_convert_fusion.refs_4_), channel_id=1, source_target_pairs={{0,12},{8,4},{12,0},{4,8},{1,13},{9,5},{13,1},{5,9},{2,14},{10,6},... | collective-permute-start | bytes 215048 | tf_op jit(solution)/shard_map/ppermute | solution.py:111
  50.2 6.9 %collective-permute-start.11 = (bf16[80,448]{1,0:T(8,128)(2,1)S(1)}, bf16[80,448]{1,0:T(8,128)(2,1)S(1)}, u32[]{:S(2)}, u32[]{:S(2)}) collective-permute-start(bf16[80,448]{1,0:T(8,128)(2,1)S(1)} %add_convert_fusion.refs_4_), channel_id=1, source_target_pairs={{0,4},{8,0},{12,8},{4,12},{1,5},{9,1},{13,9},{5,13},{2,6},{10,2},{... | collective-permute-start | bytes 215048 | tf_op jit(solution)/shard_map/ppermute | solution.py:111
  50.2 6.9 %collective-permute-start.12 = (bf16[80,448]{1,0:T(8,128)(2,1)S(1)}, bf16[80,448]{1,0:T(8,128)(2,1)S(1)}, u32[]{:S(2)}, u32[]{:S(2)}) collective-permute-start(bf16[80,448]{1,0:T(8,128)(2,1)S(1)} %add_convert_fusion.refs_4_), channel_id=1, source_target_pairs={{0,1},{1,0},{2,3},{3,2},{4,5},{5,4},{6,7},{7,6},{8,9},{9,8},{10,11... | collective-permute-start | bytes 215048 | tf_op jit(solution)/shard_map/ppermute | solution.py:88
  50.8 6.3 %collective-permute-start.13 = (bf16[80,448]{1,0:T(8,128)(2,1)S(1)}, bf16[80,448]{1,0:T(8,128)(2,1)S(1)}, u32[]{:S(2)}, u32[]{:S(2)}) collective-permute-start(bf16[80,448]{1,0:T(8,128)(2,1)S(1)} %collective-permute-done.9.refs_5_), channel_id=1, source_target_pairs={{0,1},{1,0},{2,3},{3,2},{4,5},{5,4},{6,7},{7,6},{8,9},{9,8},{10,11... | collective-permute-start | bytes 215048 | tf_op jit(solution)/shard_map/ppermute | solution.py:88
  55.3 1.8 %collective-permute-start.14 = (bf16[80,448]{1,0:T(8,128)(2,1)S(1)}, bf16[80,448]{1,0:T(8,128)(2,1)S(1)}, u32[]{:S(2)}, u32[]{:S(2)}) collective-permute-start(bf16[80,448]{1,0:T(8,128)(2,1)S(1)} %collective-permute-done.10.refs_6_), channel_id=1, source_target_pairs={{0,1},{1,0},{2,3},{3,2},{4,5},{5,4},{6,7},{7,6},{8,9},{9,8},{10,11... | collective-permute-start | bytes 215048 | tf_op jit(solution)/shard_map/ppermute | solution.py:88
  57.1 1.3 %collective-permute-start.15 = (bf16[80,448]{1,0:T(8,128)(2,1)S(1)}, bf16[80,448]{1,0:T(8,128)(2,1)S(1)}, u32[]{:S(2)}, u32[]{:S(2)}) collective-permute-start(bf16[80,448]{1,0:T(8,128)(2,1)S(1)} %collective-permute-done.11.refs_7_), channel_id=1, source_target_pairs={{0,1},{1,0},{2,3},{3,2},{4,5},{5,4},{6,7},{7,6},{8,9},{9,8},{10,11... | collective-permute-start | bytes 215048 | tf_op jit(solution)/shard_map/ppermute | solution.py:88

commit v12 on v11

--- a/solution.py
+++ b/solution.py
@@ -11,6 +11,7 @@
 NN = (((1,), (0,)), ((), ()))
 NT = (((1,), (1,)), ((), ()))
 LANES = 128
+GROUP = 8
 KERNEL_SLOTS = 1024
 
 
@@ -139,6 +140,42 @@
     result_rows = block_rows // reps
     panel = target_slots.shape[1]
     small = slots <= KERNEL_SLOTS
+    span = -(-block_rows // LANES) * LANES if small else block_rows
+    wide = feats * span
+
+    rests = []
+    for row in range(0, half, GROUP):
+        rests.append((row, row % listed // capacity))
+    bins = []
+    for rest in sorted(rests, key=lambda rest: rest[1]):
+        for row in bins:
+            if sum(feats - block for _, block in row) + feats - rest[1] <= feats:
+                row.append(rest)
+                break
+        else:
+            bins.append([rest])
+
+    def pack_rests(x):
+        rows = []
+        for row in bins:
+            parts = [x[at : at + GROUP, block * span :] for at, block in row]
+            empty = wide - sum(part.shape[1] for part in parts)
+            parts += [jnp.zeros((GROUP, empty), x.dtype)] if empty else []
+            rows.append(jnp.concatenate(parts, axis=1) if len(parts) > 1 else parts[0])
+        return jnp.concatenate(rows, axis=0)
+
+    def unpack_rests(x):
+        x = x.astype(F32) if small else x
+        found = {}
+        for n, row in enumerate(bins):
+            lane = 0
+            for at, block in row:
+                rest = x[n * GROUP : (n + 1) * GROUP, lane : lane + wide - block * span]
+                lane += wide - block * span
+                if block:
+                    rest = jnp.concatenate([jnp.zeros((GROUP, block * span), x.dtype), rest], axis=1)
+                found[at] = rest
+        return jnp.concatenate([found[at] for at, _ in rests], axis=0).astype(BF16)
 
     def place():
         feat, pos = lax.axis_index("feat"), lax.axis_index("pos")
@@ -180,14 +217,20 @@
         middle = part(rest, small)
         return [high, middle, part(rest - middle.astype(F32), small)]
 
-    def as_rows(table):
-        spread = (iota((kslots, slots), 0) == slot_entry(iota((kslots, slots), 1))).astype(BF16)
-        wide = dot(jnp.concatenate(pieces(table), axis=0), spread)
+    def as_rows(table, slot_at, lanes):
+        entry = slot_entry(slot_at(iota((kslots, lanes), 1)))
+        spread = (iota((kslots, lanes), 0) == entry).astype(BF16)
+        every = dot(jnp.concatenate(pieces(table), axis=0), spread)
         count = table.shape[0]
-        wide = wide[:count] + (wide[count : 2 * count] + wide[2 * count :])
-        row = iota(wide.shape, 0) - list_row(iota(wide.shape, 1))
-        ids = jnp.sum(jnp.where(row == 0, wide, 0.0), axis=0, keepdims=True)
-        return ids, jnp.sum(jnp.where(row == positions, wide, 0.0), axis=0, keepdims=True)
+        every = every[:count] + (every[count : 2 * count] + every[2 * count :])
+        row = iota(every.shape, 0) - list_row(slot_at(iota(every.shape, 1)))
+        ids = jnp.sum(jnp.where(row == 0, every, 0.0), axis=0, keepdims=True)
+        return ids, jnp.sum(jnp.where(row == positions, every, 0.0), axis=0, keepdims=True)
+
+    def spread_slot(lane):
+        block = floor_div(lane, span)
+        inside = lane - block * span
+        return jnp.where(inside < block_rows, block * block_rows + inside, -1.0 * slots)
 
     def as_col(table):
         wide = (slots, table.shape[0])
@@ -205,7 +248,7 @@
         for k in range(poses):
             prompt = jnp.where(pos + k >= poses, pos + k - poses, pos + k)
             tables.append(list_of(values, prompt))
-            rows.append(as_rows(tables[k])[0])
+            rows.append(as_rows(tables[k], lambda lane: lane, slots)[0])
         hits = [floor_div(ids, table_rows) == own for ids in rows]
         earlier = (iota((slots, slots), 0) < iota((slots, slots), 1)).astype(BF16)
         ranks = dot(jnp.concatenate([h.astype(BF16) for h in hits], axis=0), earlier)
@@ -245,11 +288,6 @@
     )
     dec_rows = jnp.transpose(dec_rows, (1, 0, 2)).astype(BF16)
     dec_rows = [dec_rows[:, k * listed : (k + 1) * listed] for k in range(poses)]
-    *dec_rows, ring[1][-1] = lax.optimization_barrier((*dec_rows, ring[1][-1]))
-    dec_rows = [dec_rows[0]] + [rotate(dec_rows[k], "pos", k) for k in range(1, poses)]
-
-    ring.append([ring_next(rows, "feat") for rows in ring[-1]])
-
     order = [(0, 0)] + [(k, q) for k in range(1, feats - 1) for q in range(poses)]
     soon = len(order)
     order += [(0, q) for q in range(1, poses)] + [(feats - 1, q) for q in range(poses)]
@@ -270,17 +308,21 @@
             at = jnp.where((step == 0.0) & (turn == 0.0), 0.0, at)
             return at * listed + rank
 
-        ids_row, vals_row = as_rows(table)
+        ids_row, vals_row = as_rows(table, spread_slot, wide)
         ids_col = as_col(table)
         owner_row = floor_div(ids_row, table_rows)
         owner_col = floor_div(ids_col, table_rows)
-        same = owner_col == owner_row
         down, across = iota((slots, slots), 0), iota((slots, slots), 1)
+        same = owner_col == floor_div(as_rows(table, lambda lane: lane, slots)[0], table_rows)
         rank_col = jnp.sum(jnp.where(same & (across < down), 1.0, 0.0), axis=1, keepdims=True)
-        rank_row = jnp.sum(jnp.where(same & (down < across), 1.0, 0.0), axis=0, keepdims=True)
+        slot = spread_slot(iota((slots, wide), 1))
+        same = (owner_col == owner_row) & (iota((slots, wide), 0) < slot)
+        rank_row = jnp.sum(jnp.where(same, 1.0, 0.0), axis=0, keepdims=True)
         total = holders * listed
+        used = spread_slot(iota((1, wide), 1)) >= 0.0
+        place_row = jnp.where(used, padded(owner_row, rank_row), -1.0)
         placing = padded(owner_col, rank_col) == iota((slots, total), 1)
-        placing_t = padded(owner_row, rank_row) == iota((total, slots), 0)
+        placing_t = place_row == iota((total, wide), 0)
         layer = ids_col - floor_div(ids_col, layers) * layers
         layer_row = jnp.sum(jnp.where(placing, layer, 0.0), axis=0, keepdims=True)
         mine = [placing_t[at * listed : (at + 1) * listed] for at in own_lists]
@@ -297,14 +339,16 @@
             wide = (extent, feats) if dim == 0 else (feats, extent)
             return (floor_div(slot, block_rows) == iota(wide, 1 - dim)).astype(BF16)
 
-        sources = in_block(iota((slots, 1), 0), 0, slots)
-        targets = in_block(iota((1, slots), 1), 1, slots)
+        sources = (floor_div(iota((wide, 1), 0), span) == iota((wide, feats), 1)).astype(BF16)
+        targets = (floor_div(iota((1, wide), 1), span) == iota((feats, wide), 0)).astype(BF16)
         mask = dot(dot(sources, allowed, NT).astype(BF16), targets)
-        mask = jnp.where(floor_div(down, kslots) <= floor_div(across, kslots), mask, 0.0)
+        source = floor_div(spread_slot(iota((wide, wide), 0)), kslots)
+        target = floor_div(spread_slot(iota((wide, wide), 1)), kslots)
+        mask = jnp.where(source <= target, mask, 0.0)
         first = (feat * reps + rep) * result_rows
         own_slot = first + iota((result_rows, 1), 0)
         own_mask = dot(in_block(own_slot, 0, result_rows), allowed).astype(BF16)
-        own_mask = dot(own_mask, targets)
+        own_mask = dot(own_mask, in_block(iota((1, slots), 1), 1, slots))
         own_causal = floor_div(iota((result_rows, slots), 1), kslots) <= floor_div(
             first + iota((result_rows, slots), 0), kslots
         )
@@ -312,22 +356,27 @@
         placing, placing_t = placing.astype(BF16), placing_t.astype(BF16)
         return placing, placing_t, layer_row, gains, mask.astype(BF16), own_mask
 
-    placing, placing_t, layer_row, gains, mask, own_mask, ring[2][0] = on_core(
+    placing, placing_t, layer_row, gains, mask, own_mask, *dec_rows[1:] = on_core(
         places,
         [my_list, block_pattern],
         [
             shape(slots, holders * listed, dtype=BF16),
-            shape(holders * listed, slots, dtype=BF16),
+            shape(holders * listed, wide, dtype=BF16),
             shape(1, holders * listed),
             shape(depth * column, 1),
-            shape(slots, slots, dtype=BF16),
+            shape(wide, wide, dtype=BF16),
             shape(result_rows, slots),
         ],
         small,
-        through=[ring[2][0]],
+        through=dec_rows[1:],
         cost=(1, 1),
     )
-    for _ in range(3, feats):
+    *dec_rows, ring[1][0], ring[1][-1] = lax.optimization_barrier(
+        (*dec_rows, ring[1][0], ring[1][-1])
+    )
+    dec_rows = [dec_rows[0]] + [rotate(dec_rows[k], "pos", k) for k in range(1, poses)]
+
+    for _ in range(2, feats):
         ring.append([ring_next(rows, "feat") for rows in ring[-1]])
 
     def products(first, enc, dec, layer_row, placing_t):
@@ -349,22 +398,20 @@
     def late(layer_row, placing_t, so_far, dec, *values):
         raw = so_far + products(soon, values, dec, layer_row, placing_t)
         first = place()[2] == 0.0
-        return (
-            jnp.where(first, raw[:half], raw[half:]),
-            jnp.where(first, raw[half:], raw[:half]),
-        )
+        lower, higher = pack_rests(raw[:half]), pack_rests(raw[half:])
+        return jnp.where(first, lower, higher), jnp.where(first, higher, lower)
 
     so_far, scaled = on_core(
         early,
         [layer_row, placing_t, gains] + dec_rows + [ring[k][q] for k, q in order[:soon]],
-        [shape(column, slots), shape(depth * column, width, dtype=BF16)],
+        [shape(column, wide), shape(depth * column, width, dtype=BF16)],
         small,
         cost=(1, 1),
     )
     keep, send = on_core(
         late,
         [layer_row, placing_t, so_far, scaled] + [ring[k][q] for k, q in order[soon:]],
-        [shape(half, slots)] * 2,
+        [shape(len(bins) * GROUP, wide)] * 2,
         small,
     )
     own_edges = (keep + rotate(send, "rep", 1)).astype(BF16)
@@ -376,17 +423,25 @@
         first = rep == 0.0
         chips = []
         for mine, other in zip(values[:feats], values[feats:]):
-            chips.append((jnp.where(first, mine, other), jnp.where(first, other, mine)))
-        chips = [jnp.concatenate(chip, axis=0) for chip in chips]
+            lower, higher = jnp.where(first, mine, other), jnp.where(first, other, mine)
+            chips.append(jnp.concatenate([unpack_rests(lower), unpack_rests(higher)], axis=0))
         padded = [chips[k][q * listed : (q + 1) * listed] for k, q in order]
         padded = jnp.concatenate(padded, axis=0)
-        magnitude = jnp.abs(dot(placing, padded) * mask.astype(F32))
+        unused = [jnp.zeros((span - block_rows, holders * listed), BF16)]
+        unused = unused if span > block_rows else []
+        sources = []
+        for f in range(feats):
+            sources += [placing[f * block_rows : (f + 1) * block_rows]] + unused
+        sources = jnp.concatenate(sources, axis=0)
+        magnitude = jnp.abs(dot(sources, padded) * mask.astype(F32))
         total = jnp.maximum(jnp.sum(magnitude, axis=0, keepdims=True), 1.0)
         magnitude = magnitude.astype(BF16)
-        diagonal = iota((slots, slots), 0) == iota((slots, slots), 1)
+        diagonal = iota((wide, wide), 0) == iota((wide, wide), 1)
         scale = 1.0 / jnp.sum(jnp.where(diagonal, total, 0.0), axis=1, keepdims=True)
-        current = (iota((slots, panel), 0) == targets.astype(F32)).astype(F32)
-        accum = jnp.zeros((slots, panel), F32)
+        targets = targets.astype(F32)
+        targets = targets + floor_div(targets, block_rows) * (span - block_rows)
+        current = (iota((wide, panel), 0) == targets).astype(F32)
+        accum = jnp.zeros((wide, panel), F32)
         for _ in range(ITERS):
             scaled = current * scale
             high = part(scaled, small)
@@ -394,14 +449,14 @@
             both = dot(magnitude, jnp.concatenate([high, low], axis=1))
             current = both[:, :panel] + both[:, panel:]
             accum = accum + current
-        index = feat * reps + rep
         influence = accum[:result_rows]
-        for w in range(1, feats * reps):
-            influence = jnp.where(
-                index == w, accum[w * result_rows : (w + 1) * result_rows], influence
-            )
-        start = index * result_rows
-        own = start + iota((result_rows, slots), 0) == iota((result_rows, slots), 1)
+        for f in range(feats):
+            for r in range(reps):
+                at = f * span + r * result_rows
+                mine = (feat == f) & (rep == r)
+                influence = jnp.where(mine, accum[at : at + result_rows], influence)
+        start = feat * span + rep * result_rows
+        own = start + iota((result_rows, wide), 0) == iota((result_rows, wide), 1)
         rows = dot(own.astype(BF16), padded, NT).astype(BF16)
         edges = (dot(rows, placing, NT) * own_mask).astype(BF16)
         return edges[None], (influence * float(slots))[None]

time: 61.1 us -> 60.4 us (0.989)
  waiting for transfers between devices: 22.3 us -> 20.1 us
  starting transfers between devices: 14.2 us -> 15 us
    ppermute x4, waiting for transfers between devices: 4.37 us -> 8.34 us  [ring_next(): return lax.ppermute(x, axis, steps)]
    ppermute x3, waiting for transfers between devices: 6.9 us -> 4.56 us  [ring_spread(): lax.ppermute(x, axis, [(order[i], order[(i + k) % count]) for i in range(...]
    ppermute x2, waiting for transfers between devices: 6.69 us -> 4.54 us  [ring_next(): return lax.ppermute(x, (axis, across), pairs)]
    ppermute x7, waiting for transfers between devices: 4.31 us -> 2.63 us  [rotate(): lax.ppermute(x, axis, [(i, (i + step) % count) for i in range(count)])]
  transfers between devices with their start and end apart: 16 -> 16, of which waited for: 10 -> 11; matrix products, arithmetic and copies ran while one was open for 1% -> 1% of each run, Pallas kernels for 5% -> 5%
where the time goes in v12:
time: 60.4 us; the launch traced here: 60.1 us
  waiting for transfers between devices  20.1 us (33%)
  starting transfers between devices  15 us (25%)
  blocking collectives  14.1 us (23%)
  Pallas kernels  8.78 us (15%)
  matrix products  0.77 us (1%)
  between operations  0.76 us (1%)
  local copies, waits for them, and re-layouts  0.69 us (1%)
    all_to_all x1, blocking collectives, per_device(): lax.all_to_all(packed, ('feat', 'pos'), split_axis=0, concat_axis=0, tile...  14.1 us
    pallas_call x7, Pallas kernels, on_core(): return list(call(*args, *streams, *through))  8.78 us
    ppermute x4, waiting for transfers between devices, ring_next(): return lax.ppermute(x, axis, steps)  8.34 us
    ppermute x4, starting transfers between devices, ring_next(): return lax.ppermute(x, axis, steps)  5.89 us
    ppermute x3, starting transfers between devices, ring_spread(): lax.ppermute(x, axis, [(order[i], order[(i + k) % count]) for i in range(...  4.98 us
    ppermute x3, waiting for transfers between devices, ring_spread(): lax.ppermute(x, axis, [(order[i], order[(i + k) % count]) for i in range(...  4.56 us
    ppermute x2, waiting for transfers between devices, ring_next(): return lax.ppermute(x, (axis, across), pairs)  4.54 us
    ppermute x7, starting transfers between devices, rotate(): lax.ppermute(x, axis, [(i, (i + step) % count) for i in range(count)])  2.8 us
  transfers between devices with their start and end apart: 16, of which 11 were waited for; matrix products, arithmetic and copies ran while one was open for 1% of the time, Pallas kernels for 5%

profile of v12, /device:TPU:0, one launch (start us, length us, event | category | flops | bytes accessed | tf_op | source)
XLA Modules:
  0.0 60.1 jit_solution(9973363853616980854)
XLA Ops:
  0.6 1.5 %shard_map.77 = f32[8,8,128]{2,1,0:T(8,128)} custom-call(s32[1,4,28]{2,1,0:T(4,128)} %refs_0_.1, f32[1,4,28]{2,1,0:T(4,128)} %refs_1_.3), custom_call_target="tpu_custom_call" | custom-call | tf_op jit(solution)/shard_map/pallas_call | solution.py:84
  2.1 14.1 %all_to_all.5.refs_0_ = f32[8,8,128]{2,1,0:T(8,128)S(1)} all-to-all(f32[8,8,128]{2,1,0:T(8,128)} %shard_map.77), channel_id=1, replica_groups=mesh['grp'=2,'feat'=4,'pos'=2,'rep'=2] {'feat','pos'}, dimensions={0} | all-to-all | bytes 65536 | tf_op jit(solution)/shard_map/all_to_all | solution.py:196
  17.7 0.7 %collective-permute-start.1 = (bf16[80,1152]{1,0:T(8,128)(2,1)S(1)}, bf16[80,1152]{1,0:T(8,128)(2,1)S(1)}, u32[]{:S(2)}, u32[]{:S(2)}) collective-permute-start(bf16[80,1152]{1,0:T(8,128)(2,1)S(1)} %get-tuple-element.33), channel_id=1, source_target_pairs={{0,10},{2,8},{8,14},{10,12},{12,6},{14,4},{4,2},{6,0},{1,11},{3,9}... | collective-permute-start | bytes 552968 | tf_op jit(solution)/shard_map/ppermute | solution.py:105
  18.4 0.8 %fusion = bf16[3,160,1152]{2,1,0:T(8,128)(2,1)S(1)} fusion(bf16[512,3,1152]{2,0,1:T(8,128)(2,1)S(1)} %copy-done, bf16[160,512]{1,0:T(8,128)(2,1)S(1)} %get-tuple-element.24), kind=kOutput, calls=%fused_computation.1 | convolution fusion | flops 566784000 | bytes 4808704 | tf_op jit(solution)/shard_map/dot_general | solution.py:286
  19.9 1.6 %shard_map.80 = (bf16[448,640]{1,0:T(8,128)(2,1)S(1)}, bf16[640,512]{1,0:T(8,128)(2,1)S(1)}, f32[1,640]{1,0:T(1,128)S(1)}, f32[480,1]{1,0:T(8,128)S(1)}, bf16[51...) custom-call(f32[32,28]{1,0:T(8,128)S(1)} %get-tuple-element.22.refs_, ...), custom_call_target="tpu_custom_call", output_to_operand_aliasing={{6}: (2, {})} | custom-call | flops 1 | bytes 1 | tf_op jit(solution)/shard_map/pallas_call | solution.py:84
  21.5 2.6 %collective-permute-done.refs_6_ = bf16[80,1152]{1,0:T(8,128)(2,1)S(1)} collective-permute-done((bf16[80,1152]{1,0:T(8,128)(2,1)S(1)}, bf16[80,1152]{1,0:T(8,128)(2,1)S(1)}, u32[]{:S(2)}, u32[]{:S(2)}) %collective-permute-start) | collective-permute-done | bytes 184352 | tf_op jit(solution)/shard_map/ppermute | solution.py:105
  24.1 1.9 %collective-permute-done.1.refs_7_ = bf16[80,1152]{1,0:T(8,128)(2,1)S(1)} collective-permute-done((bf16[80,1152]{1,0:T(8,128)(2,1)S(1)}, bf16[80,1152]{1,0:T(8,128)(2,1)S(1)}, u32[]{:S(2)}, u32[]{:S(2)}) %collective-permute-start.1) | collective-permute-done | bytes 184352 | tf_op jit(solution)/shard_map/ppermute | solution.py:105
  26.0 1.6 %collective-permute-start.2 = (bf16[3,80,1152]{2,1,0:T(8,128)(2,1)S(1)}, bf16[3,80,1152]{2,1,0:T(8,128)(2,1)S(1)}, u32[]{:S(2)}, u32[]{:S(2)}) collective-permute-start(bf16[3,80,1152]{2,1,0:T(8,128)(2,1)S(1)} %get-tuple-element.35), channel_id=1, source_target_pairs={{0,2},{2,0},{1,3},{3,1},{4,6},{6,4},{5,7},{7,5},{8,10},{10,8},{9,1... | collective-permute-start | bytes 1658888 | tf_op jit(solution)/shard_map/ppermute | solution.py:89
  27.6 1.7 %collective-permute-start.3 = (bf16[80,1152]{1,0:T(8,128)(2,1)S(1)}, bf16[80,1152]{1,0:T(8,128)(2,1)S(1)}, u32[]{:S(2)}, u32[]{:S(2)}) collective-permute-start(bf16[80,1152]{1,0:T(8,128)(2,1)S(1)} %collective-permute-done.refs_6_), channel_id=1, source_target_pairs={{0,8},{8,12},{12,4},{4,0},{1,9},{9,13},{13,5},{5,1},{2,10},{10,14}... | collective-permute-start | bytes 552968 | tf_op jit(solution)/shard_map/ppermute | solution.py:102
  29.3 0.7 %collective-permute-start.5 = (bf16[80,1152]{1,0:T(8,128)(2,1)S(1)}, bf16[80,1152]{1,0:T(8,128)(2,1)S(1)}, u32[]{:S(2)}, u32[]{:S(2)}) collective-permute-start(bf16[80,1152]{1,0:T(8,128)(2,1)S(1)} %get-tuple-element.33), channel_id=1, source_target_pairs={{0,2},{2,0},{1,3},{3,1},{4,6},{6,4},{5,7},{7,5},{8,10},{10,8},{9,1... | collective-permute-start | bytes 552968 | tf_op jit(solution)/shard_map/ppermute | solution.py:89
  29.9 4.4 %collective-permute-done.3.refs_8_ = bf16[80,1152]{1,0:T(8,128)(2,1)S(1)} collective-permute-done((bf16[80,1152]{1,0:T(8,128)(2,1)S(1)}, bf16[80,1152]{1,0:T(8,128)(2,1)S(1)}, u32[]{:S(2)}, u32[]{:S(2)}) %collective-permute-start.3) | collective-permute-done | bytes 184352 | tf_op jit(solution)/shard_map/ppermute | solution.py:102
  34.4 2.1 %collective-permute-start.6 = (bf16[80,1152]{1,0:T(8,128)(2,1)S(1)}, bf16[80,1152]{1,0:T(8,128)(2,1)S(1)}, u32[]{:S(2)}, u32[]{:S(2)}) collective-permute-start(bf16[80,1152]{1,0:T(8,128)(2,1)S(1)} %collective-permute-done.3.refs_8_), channel_id=1, source_target_pairs={{0,8},{8,12},{12,4},{4,0},{1,9},{9,13},{13,5},{5,1},{2,10},{10,14}... | collective-permute-start | bytes 552968 | tf_op jit(solution)/shard_map/ppermute | solution.py:102
  36.4 1.9 %collective-permute-done.4.refs_9_ = bf16[80,1152]{1,0:T(8,128)(2,1)S(1)} collective-permute-done((bf16[80,1152]{1,0:T(8,128)(2,1)S(1)}, bf16[80,1152]{1,0:T(8,128)(2,1)S(1)}, u32[]{:S(2)}, u32[]{:S(2)}) %collective-permute-start.4) | collective-permute-done | bytes 184352 | tf_op jit(solution)/shard_map/ppermute | solution.py:102
  38.3 2.1 %collective-permute-start.7 = (bf16[80,1152]{1,0:T(8,128)(2,1)S(1)}, bf16[80,1152]{1,0:T(8,128)(2,1)S(1)}, u32[]{:S(2)}, u32[]{:S(2)}) collective-permute-start(bf16[80,1152]{1,0:T(8,128)(2,1)S(1)} %collective-permute-done.4.refs_9_), channel_id=1, source_target_pairs={{0,8},{8,12},{12,4},{4,0},{1,9},{9,13},{13,5},{5,1},{2,10},{10,14}... | collective-permute-start | bytes 552968 | tf_op jit(solution)/shard_map/ppermute | solution.py:102
  40.4 1.3 %shard_map.81 = (f32[160,512]{1,0:T(8,128)S(1)}, bf16[480,1152]{1,0:T(8,128)(2,1)S(1)}) custom-call(f32[1,640]{1,0:T(1,128)S(1)} %get-tuple-element.28.refs_0_, bf16[640,512]{1,0:T(8,128)(2,1)S(1)} %get-tuple-element.29.refs_1_, f32[480,1]{1,0:T(8,128)S(1)} %get-tuple-element.30.refs_2_, bf16[3,80,1152]{2,1,0:T(8,128)(2,1)S(1)} %get-tuple-element.34.refs_3_, ...), custom_call_target="tpu_custom_call" | custom-call | flops 1 | bytes 1 | tf_op jit(solution)/shard_map/pallas_call | solution.py:84
  41.8 2.1 %collective-permute-done.7.refs_6_ = bf16[80,1152]{1,0:T(8,128)(2,1)S(1)} collective-permute-done((bf16[80,1152]{1,0:T(8,128)(2,1)S(1)}, bf16[80,1152]{1,0:T(8,128)(2,1)S(1)}, u32[]{:S(2)}, u32[]{:S(2)}) %collective-permute-start.7) | collective-permute-done | bytes 184352 | tf_op jit(solution)/shard_map/ppermute | solution.py:102
  43.8 1.0 %shard_map.82 = (f32[56,512]{1,0:T(8,128)S(1)}, f32[56,512]{1,0:T(8,128)S(1)}) custom-call(f32[1,640]{1,0:T(1,128)S(1)} %get-tuple-element.28.refs_0_, bf16[640,512]{1,0:T(8,128)(2,1)S(1)} %get-tuple-element.29.refs_1_, f32[160,512]{1,0:T(8,128)S(1)} %get-tuple-element.38.refs_2_, bf16[480,1152]{1,0:T(8,128)(2,1)S(1)} %get-tuple-element.39.refs_3_, ...), custom_call_target="tpu_custom_call" | custom-call | tf_op jit(solution)/shard_map/pallas_call | solution.py:84
  44.9 1.3 %collective-permute-done.8 = f32[56,512]{1,0:T(8,128)S(1)} collective-permute-done((f32[56,512]{1,0:T(8,128)S(1)}, f32[56,512]{1,0:T(8,128)S(1)}, u32[]{:S(2)}, u32[]{:S(2)}) %collective-permute-start.8) | collective-permute-done | bytes 114720 | tf_op jit(solution)/shard_map/ppermute | solution.py:89
  46.2 3.0 %collective-permute-start.9 = (bf16[56,512]{1,0:T(8,128)(2,1)S(1)}, bf16[56,512]{1,0:T(8,128)(2,1)S(1)}, u32[]{:S(2)}, u32[]{:S(2)}) collective-permute-start(bf16[56,512]{1,0:T(8,128)(2,1)S(1)} %add_convert_fusion.refs_4_), channel_id=1, source_target_pairs={{0,8},{8,12},{12,4},{4,0},{1,9},{9,13},{13,5},{5,1},{2,10},{10,14}... | collective-permute-start | bytes 172040 | tf_op jit(solution)/shard_map/ppermute | solution.py:112
  49.3 1.9 %collective-permute-start.10 = (bf16[56,512]{1,0:T(8,128)(2,1)S(1)}, bf16[56,512]{1,0:T(8,128)(2,1)S(1)}, u32[]{:S(2)}, u32[]{:S(2)}) collective-permute-start(bf16[56,512]{1,0:T(8,128)(2,1)S(1)} %add_convert_fusion.refs_4_), channel_id=1, source_target_pairs={{0,12},{8,4},{12,0},{4,8},{1,13},{9,5},{13,1},{5,9},{2,14},{10,6},... | collective-permute-start | bytes 172040 | tf_op jit(solution)/shard_map/ppermute | solution.py:112
  51.7 3.6 %collective-permute-done.10.refs_6_ = bf16[56,512]{1,0:T(8,128)(2,1)S(1)} collective-permute-done((bf16[56,512]{1,0:T(8,128)(2,1)S(1)}, bf16[56,512]{1,0:T(8,128)(2,1)S(1)}, u32[]{:S(2)}, u32[]{:S(2)}) %collective-permute-start.10) | collective-permute-done | bytes 57376 | tf_op jit(solution)/shard_map/ppermute | solution.py:112
  55.4 0.9 %collective-permute-done.11.refs_7_ = bf16[56,512]{1,0:T(8,128)(2,1)S(1)} collective-permute-done((bf16[56,512]{1,0:T(8,128)(2,1)S(1)}, bf16[56,512]{1,0:T(8,128)(2,1)S(1)}, u32[]{:S(2)}, u32[]{:S(2)}) %collective-permute-start.11) | collective-permute-done | bytes 57376 | tf_op jit(solution)/shard_map/ppermute | solution.py:112
  56.6 0.9 %collective-permute-done.15.refs_11_ = bf16[56,512]{1,0:T(8,128)(2,1)S(1)} collective-permute-done((bf16[56,512]{1,0:T(8,128)(2,1)S(1)}, bf16[56,512]{1,0:T(8,128)(2,1)S(1)}, u32[]{:S(2)}, u32[]{:S(2)}) %collective-permute-start.15) | collective-permute-done | bytes 57376 | tf_op jit(solution)/shard_map/ppermute | solution.py:89
  57.5 2.6 %shard_map.83 = (bf16[1,56,448]{2,1,0:T(8,128)(2,1)}, f32[1,56,128]{2,1,0:T(8,128)}) custom-call(bf16[448,640]{1,0:T(8,128)(2,1)S(1)} %get-tuple-element.25.refs_0_, bf16[512,512]{1,0:T(8,128)(2,1)S(1)} %get-tuple-element.26.refs_1_, f32[56,448]{1,0:T(8,128)S(1)} %get-tuple-element.27.refs_2_, s32[1,128]{1,0:T(1,128)S(1)} %copy-done.3, ...), custom_call_target="tpu_custom_call" | custom-call | tf_op jit(solution)/shard_map/pallas_call | solution.py:84
  (27 shorter events, 3.2 us)
Async XLA Ops:
  0.6 17.8 %copy-start = (bf16[512,3,1152]{2,0,1:T(8,128)(2,1)S(1)}, bf16[512,3,1152]{2,0,1:T(8,128)(2,1)}, u32[]{:S(2)}) copy-start(bf16[512,3,1152]{2,0,1:T(8,128)(2,1)} %param.11) | copy-start | bytes 10616836
  2.1 14.6 %copy-start.1 = (bf16[512,1152]{1,0:T(8,128)(2,1)S(1)}, bf16[512,1152]{1,0:T(8,128)(2,1)}, u32[]{:S(2)}) copy-start(bf16[512,1152]{1,0:T(8,128)(2,1)} %refs_1_.4) | copy-start | bytes 3538948
  17.1 7.0 %collective-permute-start = (bf16[80,1152]{1,0:T(8,128)(2,1)S(1)}, bf16[80,1152]{1,0:T(8,128)(2,1)S(1)}, u32[]{:S(2)}, u32[]{:S(2)}) collective-permute-start(bf16[80,1152]{1,0:T(8,128)(2,1)S(1)} %get-tuple-element.32.refs_5_), channel_id=1, source_target_pairs={{0,8},{2,10},{8,12},{10,14},{12,4},{14,6},{4,0},{6,2},{1,9},{3,11}... | collective-permute-start | bytes 552968 | tf_op jit(solution)/shard_map/ppermute | solution.py:105
  17.7 8.3 %collective-permute-start.1 = (bf16[80,1152]{1,0:T(8,128)(2,1)S(1)}, bf16[80,1152]{1,0:T(8,128)(2,1)S(1)}, u32[]{:S(2)}, u32[]{:S(2)}) collective-permute-start(bf16[80,1152]{1,0:T(8,128)(2,1)S(1)} %get-tuple-element.33), channel_id=1, source_target_pairs={{0,10},{2,8},{8,14},{10,12},{12,6},{14,4},{4,2},{6,0},{1,11},{3,9}... | collective-permute-start | bytes 552968 | tf_op jit(solution)/shard_map/ppermute | solution.py:105
  19.2 0.7 %copy-start.2 = (s32[1,4,4]{2,1,0:T(4,128)S(1)}, s32[1,4,4]{2,1,0:T(4,128)}, u32[]{:S(2)}) copy-start(s32[1,4,4]{2,1,0:T(4,128)} %refs_1_.5) | copy-start | bytes 196
  26.0 14.4 %collective-permute-start.2 = (bf16[3,80,1152]{2,1,0:T(8,128)(2,1)S(1)}, bf16[3,80,1152]{2,1,0:T(8,128)(2,1)S(1)}, u32[]{:S(2)}, u32[]{:S(2)}) collective-permute-start(bf16[3,80,1152]{2,1,0:T(8,128)(2,1)S(1)} %get-tuple-element.35), channel_id=1, source_target_pairs={{0,2},{2,0},{1,3},{3,1},{4,6},{6,4},{5,7},{7,5},{8,10},{10,8},{9,1... | collective-permute-start | bytes 1658888 | tf_op jit(solution)/shard_map/ppermute | solution.py:89
  27.6 6.8 %collective-permute-start.3 = (bf16[80,1152]{1,0:T(8,128)(2,1)S(1)}, bf16[80,1152]{1,0:T(8,128)(2,1)S(1)}, u32[]{:S(2)}, u32[]{:S(2)}) collective-permute-start(bf16[80,1152]{1,0:T(8,128)(2,1)S(1)} %collective-permute-done.refs_6_), channel_id=1, source_target_pairs={{0,8},{8,12},{12,4},{4,0},{1,9},{9,13},{13,5},{5,1},{2,10},{10,14}... | collective-permute-start | bytes 552968 | tf_op jit(solution)/shard_map/ppermute | solution.py:102
  29.2 9.1 %collective-permute-start.4 = (bf16[80,1152]{1,0:T(8,128)(2,1)S(1)}, bf16[80,1152]{1,0:T(8,128)(2,1)S(1)}, u32[]{:S(2)}, u32[]{:S(2)}) collective-permute-start(bf16[80,1152]{1,0:T(8,128)(2,1)S(1)} %collective-permute-done.1.refs_7_), channel_id=1, source_target_pairs={{0,8},{8,12},{12,4},{4,0},{1,9},{9,13},{13,5},{5,1},{2,10},{10,14}... | collective-permute-start | bytes 552968 | tf_op jit(solution)/shard_map/ppermute | solution.py:102
  29.3 12.5 %collective-permute-start.5 = (bf16[80,1152]{1,0:T(8,128)(2,1)S(1)}, bf16[80,1152]{1,0:T(8,128)(2,1)S(1)}, u32[]{:S(2)}, u32[]{:S(2)}) collective-permute-start(bf16[80,1152]{1,0:T(8,128)(2,1)S(1)} %get-tuple-element.33), channel_id=1, source_target_pairs={{0,2},{2,0},{1,3},{3,1},{4,6},{6,4},{5,7},{7,5},{8,10},{10,8},{9,1... | collective-permute-start | bytes 552968 | tf_op jit(solution)/shard_map/ppermute | solution.py:89
  34.4 7.4 %collective-permute-start.6 = (bf16[80,1152]{1,0:T(8,128)(2,1)S(1)}, bf16[80,1152]{1,0:T(8,128)(2,1)S(1)}, u32[]{:S(2)}, u32[]{:S(2)}) collective-permute-start(bf16[80,1152]{1,0:T(8,128)(2,1)S(1)} %collective-permute-done.3.refs_8_), channel_id=1, source_target_pairs={{0,8},{8,12},{12,4},{4,0},{1,9},{9,13},{13,5},{5,1},{2,10},{10,14}... | collective-permute-start | bytes 552968 | tf_op jit(solution)/shard_map/ppermute | solution.py:102
  38.3 5.5 %collective-permute-start.7 = (bf16[80,1152]{1,0:T(8,128)(2,1)S(1)}, bf16[80,1152]{1,0:T(8,128)(2,1)S(1)}, u32[]{:S(2)}, u32[]{:S(2)}) collective-permute-start(bf16[80,1152]{1,0:T(8,128)(2,1)S(1)} %collective-permute-done.4.refs_9_), channel_id=1, source_target_pairs={{0,8},{8,12},{12,4},{4,0},{1,9},{9,13},{13,5},{5,1},{2,10},{10,14}... | collective-permute-start | bytes 552968 | tf_op jit(solution)/shard_map/ppermute | solution.py:102
  40.4 17.1 %copy-start.3 = (s32[1,128]{1,0:T(1,128)S(1)}, s32[1,128]{1,0:T(1,128)}, u32[]{:S(2)}) copy-start(s32[1,128]{1,0:T(1,128)} %refs_3_.1) | copy-start | bytes 1540
  44.8 1.4 %collective-permute-start.8 = (f32[56,512]{1,0:T(8,128)S(1)}, f32[56,512]{1,0:T(8,128)S(1)}, u32[]{:S(2)}, u32[]{:S(2)}) collective-permute-start(f32[56,512]{1,0:T(8,128)S(1)} %get-tuple-element.41), channel_id=1, source_target_pairs={{0,1},{1,0},{2,3},{3,2},{4,5},{5,4},{6,7},{7,6},{8,9},{9,8},{10,11... | collective-permute-start | bytes 344072 | tf_op jit(solution)/shard_map/ppermute | solution.py:89
  46.2 5.0 %collective-permute-start.9 = (bf16[56,512]{1,0:T(8,128)(2,1)S(1)}, bf16[56,512]{1,0:T(8,128)(2,1)S(1)}, u32[]{:S(2)}, u32[]{:S(2)}) collective-permute-start(bf16[56,512]{1,0:T(8,128)(2,1)S(1)} %add_convert_fusion.refs_4_), channel_id=1, source_target_pairs={{0,8},{8,12},{12,4},{4,0},{1,9},{9,13},{13,5},{5,1},{2,10},{10,14}... | collective-permute-start | bytes 172040 | tf_op jit(solution)/shard_map/ppermute | solution.py:112
  49.3 6.1 %collective-permute-start.10 = (bf16[56,512]{1,0:T(8,128)(2,1)S(1)}, bf16[56,512]{1,0:T(8,128)(2,1)S(1)}, u32[]{:S(2)}, u32[]{:S(2)}) collective-permute-start(bf16[56,512]{1,0:T(8,128)(2,1)S(1)} %add_convert_fusion.refs_4_), channel_id=1, source_target_pairs={{0,12},{8,4},{12,0},{4,8},{1,13},{9,5},{13,1},{5,9},{2,14},{10,6},... | collective-permute-start | bytes 172040 | tf_op jit(solution)/shard_map/ppermute | solution.py:112
  51.2 5.1 %collective-permute-start.11 = (bf16[56,512]{1,0:T(8,128)(2,1)S(1)}, bf16[56,512]{1,0:T(8,128)(2,1)S(1)}, u32[]{:S(2)}, u32[]{:S(2)}) collective-permute-start(bf16[56,512]{1,0:T(8,128)(2,1)S(1)} %add_convert_fusion.refs_4_), channel_id=1, source_target_pairs={{0,4},{8,0},{12,8},{4,12},{1,5},{9,1},{13,9},{5,13},{2,6},{10,2},{... | collective-permute-start | bytes 172040 | tf_op jit(solution)/shard_map/ppermute | solution.py:112
  51.2 5.1 %collective-permute-start.12 = (bf16[56,512]{1,0:T(8,128)(2,1)S(1)}, bf16[56,512]{1,0:T(8,128)(2,1)S(1)}, u32[]{:S(2)}, u32[]{:S(2)}) collective-permute-start(bf16[56,512]{1,0:T(8,128)(2,1)S(1)} %add_convert_fusion.refs_4_), channel_id=1, source_target_pairs={{0,1},{1,0},{2,3},{3,2},{4,5},{5,4},{6,7},{7,6},{8,9},{9,8},{10,11... | collective-permute-start | bytes 172040 | tf_op jit(solution)/shard_map/ppermute | solution.py:89
  51.2 5.1 %collective-permute-start.13 = (bf16[56,512]{1,0:T(8,128)(2,1)S(1)}, bf16[56,512]{1,0:T(8,128)(2,1)S(1)}, u32[]{:S(2)}, u32[]{:S(2)}) collective-permute-start(bf16[56,512]{1,0:T(8,128)(2,1)S(1)} %collective-permute-done.9.refs_5_), channel_id=1, source_target_pairs={{0,1},{1,0},{2,3},{3,2},{4,5},{5,4},{6,7},{7,6},{8,9},{9,8},{10,11... | collective-permute-start | bytes 172040 | tf_op jit(solution)/shard_map/ppermute | solution.py:89
  55.4 1.2 %collective-permute-start.14 = (bf16[56,512]{1,0:T(8,128)(2,1)S(1)}, bf16[56,512]{1,0:T(8,128)(2,1)S(1)}, u32[]{:S(2)}, u32[]{:S(2)}) collective-permute-start(bf16[56,512]{1,0:T(8,128)(2,1)S(1)} %collective-permute-done.10.refs_6_), channel_id=1, source_target_pairs={{0,1},{1,0},{2,3},{3,2},{4,5},{5,4},{6,7},{7,6},{8,9},{9,8},{10,11... | collective-permute-start | bytes 172040 | tf_op jit(solution)/shard_map/ppermute | solution.py:89
  56.3 1.2 %collective-permute-start.15 = (bf16[56,512]{1,0:T(8,128)(2,1)S(1)}, bf16[56,512]{1,0:T(8,128)(2,1)S(1)}, u32[]{:S(2)}, u32[]{:S(2)}) collective-permute-start(bf16[56,512]{1,0:T(8,128)(2,1)S(1)} %collective-permute-done.11.refs_7_), channel_id=1, source_target_pairs={{0,1},{1,0},{2,3},{3,2},{4,5},{5,4},{6,7},{7,6},{8,9},{9,8},{10,11... | collective-permute-start | bytes 172040 | tf_op jit(solution)/shard_map/ppermute | solution.py:89

commit v13 on v12

--- a/solution.py
+++ b/solution.py
@@ -287,7 +287,10 @@
         picks, decoder, (((1,), (0,)), ((), ())), preferred_element_type=F32
     )
     dec_rows = jnp.transpose(dec_rows, (1, 0, 2)).astype(BF16)
-    dec_rows = [dec_rows[:, k * listed : (k + 1) * listed] for k in range(poses)]
+    dec_rows = [
+        [dec_rows[l, k * listed : (k + 1) * listed] for l in range(depth)] for k in range(poses)
+    ]
+    away = [rows for k in range(1, poses) for rows in dec_rows[k]]
     order = [(0, 0)] + [(k, q) for k in range(1, feats - 1) for q in range(poses)]
     soon = len(order)
     order += [(0, q) for q in range(1, poses)] + [(feats - 1, q) for q in range(poses)]
@@ -356,7 +359,7 @@
         placing, placing_t = placing.astype(BF16), placing_t.astype(BF16)
         return placing, placing_t, layer_row, gains, mask.astype(BF16), own_mask
 
-    placing, placing_t, layer_row, gains, mask, own_mask, *dec_rows[1:] = on_core(
+    placing, placing_t, layer_row, gains, mask, own_mask, *away = on_core(
         places,
         [my_list, block_pattern],
         [
@@ -368,13 +371,14 @@
             shape(result_rows, slots),
         ],
         small,
-        through=dec_rows[1:],
+        through=away,
         cost=(1, 1),
     )
-    *dec_rows, ring[1][0], ring[1][-1] = lax.optimization_barrier(
-        (*dec_rows, ring[1][0], ring[1][-1])
-    )
-    dec_rows = [dec_rows[0]] + [rotate(dec_rows[k], "pos", k) for k in range(1, poses)]
+    *away, ring[1][0], ring[1][-1] = lax.optimization_barrier((*away, ring[1][0], ring[1][-1]))
+    for k in range(1, poses):
+        rows = away[(k - 1) * depth : k * depth]
+        dec_rows[k] = [rotate(row, "pos", k) for row in rows]
+    dec_rows = [dec_rows[k][l] for l in range(depth) for k in range(poses)]
 
     for _ in range(2, feats):
         ring.append([ring_next(rows, "feat") for rows in ring[-1]])
@@ -391,9 +395,9 @@
         return split[:column] + (split[column : 2 * column] + split[2 * column :])
 
     def early(layer_row, placing_t, gains, *values):
-        dec = jnp.concatenate([d[l] for l in range(depth) for d in values[:poses]], axis=0)
+        dec = jnp.concatenate(values[: depth * poses], axis=0)
         dec = (dec.astype(F32) * gains).astype(BF16)
-        return products(0, values[poses:], dec, layer_row, placing_t), dec
+        return products(0, values[depth * poses :], dec, layer_row, placing_t), dec
 
     def late(layer_row, placing_t, so_far, dec, *values):
         raw = so_far + products(soon, values, dec, layer_row, placing_t)

time: 60.4 us -> 60.4 us (level)
  waiting for transfers between devices: 20.1 us -> 17.5 us
  starting transfers between devices: 15 us -> 17.5 us
    ppermute x4, waiting for transfers between devices: 8.34 us -> 2.77 us  [ring_next(): return lax.ppermute(x, axis, steps)]
    ppermute x7 -> x9, waiting for transfers between devices: 2.63 us -> 5.66 us  [rotate(): lax.ppermute(x, axis, [(i, (i + step) % count) for i in range(count)])]
    ppermute x7 -> x9, starting transfers between devices: 2.8 us -> 5.78 us  [rotate(): lax.ppermute(x, axis, [(i, (i + step) % count) for i in range(count)])]
  transfers between devices with their start and end apart: 16 -> 18, of which waited for: 11 -> 12; matrix products, arithmetic and copies ran while one was open for 1% -> 1% of each run, Pallas kernels for 5% -> 5%
where the time goes in v13:
time: 60.4 us; the launch traced here: 60.1 us
  starting transfers between devices  17.5 us (29%)
  waiting for transfers between devices  17.5 us (29%)
  blocking collectives  14.1 us (23%)
  Pallas kernels  8.76 us (15%)
  matrix products  0.8 us (1%)
  between operations  0.76 us (1%)
  local copies, waits for them, and re-layouts  0.69 us (1%)
    all_to_all x1, blocking collectives, per_device(): lax.all_to_all(packed, ('feat', 'pos'), split_axis=0, concat_axis=0, tile...  14.1 us
    pallas_call x7, Pallas kernels, on_core(): return list(call(*args, *streams, *through))  8.76 us
    ppermute x9, starting transfers between devices, rotate(): lax.ppermute(x, axis, [(i, (i + step) % count) for i in range(count)])  5.78 us
    ppermute x9, waiting for transfers between devices, rotate(): lax.ppermute(x, axis, [(i, (i + step) % count) for i in range(count)])  5.66 us
    ppermute x4, starting transfers between devices, ring_next(): return lax.ppermute(x, axis, steps)  5.47 us
    ppermute x3, starting transfers between devices, ring_spread(): lax.ppermute(x, axis, [(order[i], order[(i + k) % count]) for i in range(...  4.97 us
    ppermute x3, waiting for transfers between devices, ring_spread(): lax.ppermute(x, axis, [(order[i], order[(i + k) % count]) for i in range(...  4.56 us
    ppermute x2, waiting for transfers between devices, ring_next(): return lax.ppermute(x, (axis, across), pairs)  4.5 us
  transfers between devices with their start and end apart: 18, of which 12 were waited for; matrix products, arithmetic and copies ran while one was open for 1% of the time, Pallas kernels for 5%

profile of v13, /device:TPU:0, one launch (start us, length us, event | category | flops | bytes accessed | tf_op | source)
XLA Modules:
  0.0 60.1 jit_solution(10795787714626012632)
XLA Ops:
  0.6 1.5 %shard_map.77 = f32[8,8,128]{2,1,0:T(8,128)} custom-call(s32[1,4,28]{2,1,0:T(4,128)} %refs_0_.1, f32[1,4,28]{2,1,0:T(4,128)} %refs_1_.3), custom_call_target="tpu_custom_call" | custom-call | tf_op jit(solution)/shard_map/pallas_call | solution.py:84
  2.1 14.1 %all_to_all.5.refs_0_ = f32[8,8,128]{2,1,0:T(8,128)S(1)} all-to-all(f32[8,8,128]{2,1,0:T(8,128)} %shard_map.77), channel_id=1, replica_groups=mesh['grp'=2,'feat'=4,'pos'=2,'rep'=2] {'feat','pos'}, dimensions={0} | all-to-all | bytes 65536 | tf_op jit(solution)/shard_map/all_to_all | solution.py:196
  18.4 0.8 %fusion = bf16[3,160,1152]{2,1,0:T(8,128)(2,1)S(1)} fusion(bf16[512,3,1152]{2,0,1:T(8,128)(2,1)S(1)} %copy-done, bf16[160,512]{1,0:T(8,128)(2,1)S(1)} %get-tuple-element.27), kind=kOutput, calls=%fused_computation.1 | convolution fusion | flops 566784000 | bytes 4808704 | tf_op jit(solution)/shard_map/dot_general | solution.py:286
  19.9 1.6 %shard_map.80 = (bf16[448,640]{1,0:T(8,128)(2,1)S(1)}, bf16[640,512]{1,0:T(8,128)(2,1)S(1)}, f32[1,640]{1,0:T(1,128)S(1)}, f32[480,1]{1,0:T(8,128)S(1)}, bf16[51...) custom-call(f32[32,28]{1,0:T(8,128)S(1)} %get-tuple-element.25.refs_, ...), custom_call_target="tpu_custom_call", output_to_operand_aliasing={{6}: (2, {}), {7}: (3, {}), {8}: (4, {})} | custom-call | flops 1 | bytes 1 | tf_op jit(solution)/shard_map/pallas_call | solution.py:84
  21.5 2.6 %collective-permute-done.refs_10_ = bf16[80,1152]{1,0:T(8,128)(2,1)S(1)} collective-permute-done((bf16[80,1152]{1,0:T(8,128)(2,1)S(1)}, bf16[80,1152]{1,0:T(8,128)(2,1)S(1)}, u32[]{:S(2)}, u32[]{:S(2)}) %collective-permute-start) | collective-permute-done | bytes 184352 | tf_op jit(solution)/shard_map/ppermute | solution.py:105
  24.1 1.9 %collective-permute-done.1.refs_11_ = bf16[80,1152]{1,0:T(8,128)(2,1)S(1)} collective-permute-done((bf16[80,1152]{1,0:T(8,128)(2,1)S(1)}, bf16[80,1152]{1,0:T(8,128)(2,1)S(1)}, u32[]{:S(2)}, u32[]{:S(2)}) %collective-permute-start.1) | collective-permute-done | bytes 184352 | tf_op jit(solution)/shard_map/ppermute | solution.py:105
  26.0 1.6 %collective-permute-start.2 = (bf16[80,1152]{1,0:T(8,128)(2,1)S(1)}, bf16[80,1152]{1,0:T(8,128)(2,1)S(1)}, u32[]{:S(2)}, u32[]{:S(2)}) collective-permute-start(bf16[80,1152]{1,0:T(8,128)(2,1)S(1)} %get-tuple-element.39), channel_id=1, source_target_pairs={{0,2},{2,0},{1,3},{3,1},{4,6},{6,4},{5,7},{7,5},{8,10},{10,8},{9,1... | collective-permute-start | bytes 552968 | tf_op jit(solution)/shard_map/ppermute | solution.py:89
  27.6 1.7 %collective-permute-start.5 = (bf16[80,1152]{1,0:T(8,128)(2,1)S(1)}, bf16[80,1152]{1,0:T(8,128)(2,1)S(1)}, u32[]{:S(2)}, u32[]{:S(2)}) collective-permute-start(bf16[80,1152]{1,0:T(8,128)(2,1)S(1)} %collective-permute-done.refs_10_), channel_id=1, source_target_pairs={{0,8},{8,12},{12,4},{4,0},{1,9},{9,13},{13,5},{5,1},{2,10},{10,14}... | collective-permute-start | bytes 552968 | tf_op jit(solution)/shard_map/ppermute | solution.py:102
  29.9 1.4 %collective-permute-start.4 = (bf16[80,1152]{1,0:T(8,128)(2,1)S(1)}, bf16[80,1152]{1,0:T(8,128)(2,1)S(1)}, u32[]{:S(2)}, u32[]{:S(2)}) collective-permute-start(bf16[80,1152]{1,0:T(8,128)(2,1)S(1)} %get-tuple-element.41), channel_id=1, source_target_pairs={{0,2},{2,0},{1,3},{3,1},{4,6},{6,4},{5,7},{7,5},{8,10},{10,8},{9,1... | collective-permute-start | bytes 552968 | tf_op jit(solution)/shard_map/ppermute | solution.py:89
  31.3 2.2 %collective-permute-done.2.refs_4_ = bf16[80,1152]{1,0:T(8,128)(2,1)S(1)} collective-permute-done((bf16[80,1152]{1,0:T(8,128)(2,1)S(1)}, bf16[80,1152]{1,0:T(8,128)(2,1)S(1)}, u32[]{:S(2)}, u32[]{:S(2)}) %collective-permute-start.2) | collective-permute-done | bytes 184352 | tf_op jit(solution)/shard_map/ppermute | solution.py:89
  33.5 1.6 %collective-permute-start.7 = (bf16[80,1152]{1,0:T(8,128)(2,1)S(1)}, bf16[80,1152]{1,0:T(8,128)(2,1)S(1)}, u32[]{:S(2)}, u32[]{:S(2)}) collective-permute-start(bf16[80,1152]{1,0:T(8,128)(2,1)S(1)} %get-tuple-element.38), channel_id=1, source_target_pairs={{0,2},{2,0},{1,3},{3,1},{4,6},{6,4},{5,7},{7,5},{8,10},{10,8},{9,1... | collective-permute-start | bytes 552968 | tf_op jit(solution)/shard_map/ppermute | solution.py:89
  35.1 1.7 %collective-permute-start.8 = (bf16[80,1152]{1,0:T(8,128)(2,1)S(1)}, bf16[80,1152]{1,0:T(8,128)(2,1)S(1)}, u32[]{:S(2)}, u32[]{:S(2)}) collective-permute-start(bf16[80,1152]{1,0:T(8,128)(2,1)S(1)} %collective-permute-done.5.refs_12_), channel_id=1, source_target_pairs={{0,8},{8,12},{12,4},{4,0},{1,9},{9,13},{13,5},{5,1},{2,10},{10,14}... | collective-permute-start | bytes 552968 | tf_op jit(solution)/shard_map/ppermute | solution.py:102
  36.8 1.5 %collective-permute-done.6.refs_13_ = bf16[80,1152]{1,0:T(8,128)(2,1)S(1)} collective-permute-done((bf16[80,1152]{1,0:T(8,128)(2,1)S(1)}, bf16[80,1152]{1,0:T(8,128)(2,1)S(1)}, u32[]{:S(2)}, u32[]{:S(2)}) %collective-permute-start.6) | collective-permute-done | bytes 184352 | tf_op jit(solution)/shard_map/ppermute | solution.py:102
  38.3 2.1 %collective-permute-start.9 = (bf16[80,1152]{1,0:T(8,128)(2,1)S(1)}, bf16[80,1152]{1,0:T(8,128)(2,1)S(1)}, u32[]{:S(2)}, u32[]{:S(2)}) collective-permute-start(bf16[80,1152]{1,0:T(8,128)(2,1)S(1)} %collective-permute-done.6.refs_13_), channel_id=1, source_target_pairs={{0,8},{8,12},{12,4},{4,0},{1,9},{9,13},{13,5},{5,1},{2,10},{10,14}... | collective-permute-start | bytes 552968 | tf_op jit(solution)/shard_map/ppermute | solution.py:102
  40.7 1.3 %shard_map.81 = (f32[160,512]{1,0:T(8,128)S(1)}, bf16[480,1152]{1,0:T(8,128)(2,1)S(1)}) custom-call(f32[1,640]{1,0:T(1,128)S(1)} %get-tuple-element.31.refs_0_, bf16[640,512]{1,0:T(8,128)(2,1)S(1)} %get-tuple-element.32.refs_1_, f32[480,1]{1,0:T(8,128)S(1)} %get-tuple-element.33.refs_2_, bf16[80,1152]{1,0:T(8,128)(2,1)S(1)} %get-tuple-element.50.refs_3_, ...), custom_call_target="tpu_custom_call" | custom-call | flops 1 | bytes 1 | tf_op jit(solution)/shard_map/pallas_call | solution.py:84
  42.6 1.2 %collective-permute-done.9.refs_6_ = bf16[80,1152]{1,0:T(8,128)(2,1)S(1)} collective-permute-done((bf16[80,1152]{1,0:T(8,128)(2,1)S(1)}, bf16[80,1152]{1,0:T(8,128)(2,1)S(1)}, u32[]{:S(2)}, u32[]{:S(2)}) %collective-permute-start.9) | collective-permute-done | bytes 184352 | tf_op jit(solution)/shard_map/ppermute | solution.py:102
  43.9 1.0 %shard_map.82 = (f32[56,512]{1,0:T(8,128)S(1)}, f32[56,512]{1,0:T(8,128)S(1)}) custom-call(f32[1,640]{1,0:T(1,128)S(1)} %get-tuple-element.31.refs_0_, bf16[640,512]{1,0:T(8,128)(2,1)S(1)} %get-tuple-element.32.refs_1_, f32[160,512]{1,0:T(8,128)S(1)} %get-tuple-element.44.refs_2_, bf16[480,1152]{1,0:T(8,128)(2,1)S(1)} %get-tuple-element.45.refs_3_, ...), custom_call_target="tpu_custom_call" | custom-call | tf_op jit(solution)/shard_map/pallas_call | solution.py:84
  44.9 1.3 %collective-permute-done.10 = f32[56,512]{1,0:T(8,128)S(1)} collective-permute-done((f32[56,512]{1,0:T(8,128)S(1)}, f32[56,512]{1,0:T(8,128)S(1)}, u32[]{:S(2)}, u32[]{:S(2)}) %collective-permute-start.10) | collective-permute-done | bytes 114720 | tf_op jit(solution)/shard_map/ppermute | solution.py:89
  46.2 3.0 %collective-permute-start.11 = (bf16[56,512]{1,0:T(8,128)(2,1)S(1)}, bf16[56,512]{1,0:T(8,128)(2,1)S(1)}, u32[]{:S(2)}, u32[]{:S(2)}) collective-permute-start(bf16[56,512]{1,0:T(8,128)(2,1)S(1)} %add_convert_fusion.refs_4_), channel_id=1, source_target_pairs={{0,8},{8,12},{12,4},{4,0},{1,9},{9,13},{13,5},{5,1},{2,10},{10,14}... | collective-permute-start | bytes 172040 | tf_op jit(solution)/shard_map/ppermute | solution.py:112
  49.3 1.9 %collective-permute-start.12 = (bf16[56,512]{1,0:T(8,128)(2,1)S(1)}, bf16[56,512]{1,0:T(8,128)(2,1)S(1)}, u32[]{:S(2)}, u32[]{:S(2)}) collective-permute-start(bf16[56,512]{1,0:T(8,128)(2,1)S(1)} %add_convert_fusion.refs_4_), channel_id=1, source_target_pairs={{0,12},{8,4},{12,0},{4,8},{1,13},{9,5},{13,1},{5,9},{2,14},{10,6},... | collective-permute-start | bytes 172040 | tf_op jit(solution)/shard_map/ppermute | solution.py:112
  51.7 3.6 %collective-permute-done.12.refs_6_ = bf16[56,512]{1,0:T(8,128)(2,1)S(1)} collective-permute-done((bf16[56,512]{1,0:T(8,128)(2,1)S(1)}, bf16[56,512]{1,0:T(8,128)(2,1)S(1)}, u32[]{:S(2)}, u32[]{:S(2)}) %collective-permute-start.12) | collective-permute-done | bytes 57376 | tf_op jit(solution)/shard_map/ppermute | solution.py:112
  55.4 0.9 %collective-permute-done.13.refs_7_ = bf16[56,512]{1,0:T(8,128)(2,1)S(1)} collective-permute-done((bf16[56,512]{1,0:T(8,128)(2,1)S(1)}, bf16[56,512]{1,0:T(8,128)(2,1)S(1)}, u32[]{:S(2)}, u32[]{:S(2)}) %collective-permute-start.13) | collective-permute-done | bytes 57376 | tf_op jit(solution)/shard_map/ppermute | solution.py:112
  56.6 0.9 %collective-permute-done.17.refs_11_ = bf16[56,512]{1,0:T(8,128)(2,1)S(1)} collective-permute-done((bf16[56,512]{1,0:T(8,128)(2,1)S(1)}, bf16[56,512]{1,0:T(8,128)(2,1)S(1)}, u32[]{:S(2)}, u32[]{:S(2)}) %collective-permute-start.17) | collective-permute-done | bytes 57376 | tf_op jit(solution)/shard_map/ppermute | solution.py:89
  57.5 2.6 %shard_map.83 = (bf16[1,56,448]{2,1,0:T(8,128)(2,1)}, f32[1,56,128]{2,1,0:T(8,128)}) custom-call(bf16[448,640]{1,0:T(8,128)(2,1)S(1)} %get-tuple-element.28.refs_0_, bf16[512,512]{1,0:T(8,128)(2,1)S(1)} %get-tuple-element.29.refs_1_, f32[56,448]{1,0:T(8,128)S(1)} %get-tuple-element.30.refs_2_, s32[1,128]{1,0:T(1,128)S(1)} %copy-done.3, ...), custom_call_target="tpu_custom_call" | custom-call | tf_op jit(solution)/shard_map/pallas_call | solution.py:84
  (31 shorter events, 5.4 us)
Async XLA Ops:
  0.6 17.8 %copy-start = (bf16[512,3,1152]{2,0,1:T(8,128)(2,1)S(1)}, bf16[512,3,1152]{2,0,1:T(8,128)(2,1)}, u32[]{:S(2)}) copy-start(bf16[512,3,1152]{2,0,1:T(8,128)(2,1)} %param.11) | copy-start | bytes 10616836
  2.1 14.6 %copy-start.1 = (bf16[512,1152]{1,0:T(8,128)(2,1)S(1)}, bf16[512,1152]{1,0:T(8,128)(2,1)}, u32[]{:S(2)}) copy-start(bf16[512,1152]{1,0:T(8,128)(2,1)} %refs_1_.4) | copy-start | bytes 3538948
  17.1 7.0 %collective-permute-start = (bf16[80,1152]{1,0:T(8,128)(2,1)S(1)}, bf16[80,1152]{1,0:T(8,128)(2,1)S(1)}, u32[]{:S(2)}, u32[]{:S(2)}) collective-permute-start(bf16[80,1152]{1,0:T(8,128)(2,1)S(1)} %get-tuple-element.37.refs_9_), channel_id=1, source_target_pairs={{0,8},{2,10},{8,12},{10,14},{12,4},{14,6},{4,0},{6,2},{1,9},{3,11}... | collective-permute-start | bytes 552968 | tf_op jit(solution)/shard_map/ppermute | solution.py:105
  17.7 8.3 %collective-permute-start.1 = (bf16[80,1152]{1,0:T(8,128)(2,1)S(1)}, bf16[80,1152]{1,0:T(8,128)(2,1)S(1)}, u32[]{:S(2)}, u32[]{:S(2)}) collective-permute-start(bf16[80,1152]{1,0:T(8,128)(2,1)S(1)} %get-tuple-element.38), channel_id=1, source_target_pairs={{0,10},{2,8},{8,14},{10,12},{12,6},{14,4},{4,2},{6,0},{1,11},{3,9}... | collective-permute-start | bytes 552968 | tf_op jit(solution)/shard_map/ppermute | solution.py:105
  19.2 0.7 %copy-start.2 = (s32[1,4,4]{2,1,0:T(4,128)S(1)}, s32[1,4,4]{2,1,0:T(4,128)}, u32[]{:S(2)}) copy-start(s32[1,4,4]{2,1,0:T(4,128)} %refs_1_.5) | copy-start | bytes 196
  26.0 7.5 %collective-permute-start.2 = (bf16[80,1152]{1,0:T(8,128)(2,1)S(1)}, bf16[80,1152]{1,0:T(8,128)(2,1)S(1)}, u32[]{:S(2)}, u32[]{:S(2)}) collective-permute-start(bf16[80,1152]{1,0:T(8,128)(2,1)S(1)} %get-tuple-element.39), channel_id=1, source_target_pairs={{0,2},{2,0},{1,3},{3,1},{4,6},{6,4},{5,7},{7,5},{8,10},{10,8},{9,1... | collective-permute-start | bytes 552968 | tf_op jit(solution)/shard_map/ppermute | solution.py:89
  27.6 7.5 %collective-permute-start.5 = (bf16[80,1152]{1,0:T(8,128)(2,1)S(1)}, bf16[80,1152]{1,0:T(8,128)(2,1)S(1)}, u32[]{:S(2)}, u32[]{:S(2)}) collective-permute-start(bf16[80,1152]{1,0:T(8,128)(2,1)S(1)} %collective-permute-done.refs_10_), channel_id=1, source_target_pairs={{0,8},{8,12},{12,4},{4,0},{1,9},{9,13},{13,5},{5,1},{2,10},{10,14}... | collective-permute-start | bytes 552968 | tf_op jit(solution)/shard_map/ppermute | solution.py:102
  29.3 9.1 %collective-permute-start.6 = (bf16[80,1152]{1,0:T(8,128)(2,1)S(1)}, bf16[80,1152]{1,0:T(8,128)(2,1)S(1)}, u32[]{:S(2)}, u32[]{:S(2)}) collective-permute-start(bf16[80,1152]{1,0:T(8,128)(2,1)S(1)} %collective-permute-done.1.refs_11_), channel_id=1, source_target_pairs={{0,8},{8,12},{12,4},{4,0},{1,9},{9,13},{13,5},{5,1},{2,10},{10,14}... | collective-permute-start | bytes 552968 | tf_op jit(solution)/shard_map/ppermute | solution.py:102
  29.3 11.1 %collective-permute-start.3 = (bf16[80,1152]{1,0:T(8,128)(2,1)S(1)}, bf16[80,1152]{1,0:T(8,128)(2,1)S(1)}, u32[]{:S(2)}, u32[]{:S(2)}) collective-permute-start(bf16[80,1152]{1,0:T(8,128)(2,1)S(1)} %get-tuple-element.40), channel_id=1, source_target_pairs={{0,2},{2,0},{1,3},{3,1},{4,6},{6,4},{5,7},{7,5},{8,10},{10,8},{9,1... | collective-permute-start | bytes 552968 | tf_op jit(solution)/shard_map/ppermute | solution.py:89
  29.9 10.7 %collective-permute-start.4 = (bf16[80,1152]{1,0:T(8,128)(2,1)S(1)}, bf16[80,1152]{1,0:T(8,128)(2,1)S(1)}, u32[]{:S(2)}, u32[]{:S(2)}) collective-permute-start(bf16[80,1152]{1,0:T(8,128)(2,1)S(1)} %get-tuple-element.41), channel_id=1, source_target_pairs={{0,2},{2,0},{1,3},{3,1},{4,6},{6,4},{5,7},{7,5},{8,10},{10,8},{9,1... | collective-permute-start | bytes 552968 | tf_op jit(solution)/shard_map/ppermute | solution.py:89
  33.5 9.1 %collective-permute-start.7 = (bf16[80,1152]{1,0:T(8,128)(2,1)S(1)}, bf16[80,1152]{1,0:T(8,128)(2,1)S(1)}, u32[]{:S(2)}, u32[]{:S(2)}) collective-permute-start(bf16[80,1152]{1,0:T(8,128)(2,1)S(1)} %get-tuple-element.38), channel_id=1, source_target_pairs={{0,2},{2,0},{1,3},{3,1},{4,6},{6,4},{5,7},{7,5},{8,10},{10,8},{9,1... | collective-permute-start | bytes 552968 | tf_op jit(solution)/shard_map/ppermute | solution.py:89
  35.1 7.5 %collective-permute-start.8 = (bf16[80,1152]{1,0:T(8,128)(2,1)S(1)}, bf16[80,1152]{1,0:T(8,128)(2,1)S(1)}, u32[]{:S(2)}, u32[]{:S(2)}) collective-permute-start(bf16[80,1152]{1,0:T(8,128)(2,1)S(1)} %collective-permute-done.5.refs_12_), channel_id=1, source_target_pairs={{0,8},{8,12},{12,4},{4,0},{1,9},{9,13},{13,5},{5,1},{2,10},{10,14}... | collective-permute-start | bytes 552968 | tf_op jit(solution)/shard_map/ppermute | solution.py:102
  38.3 5.5 %collective-permute-start.9 = (bf16[80,1152]{1,0:T(8,128)(2,1)S(1)}, bf16[80,1152]{1,0:T(8,128)(2,1)S(1)}, u32[]{:S(2)}, u32[]{:S(2)}) collective-permute-start(bf16[80,1152]{1,0:T(8,128)(2,1)S(1)} %collective-permute-done.6.refs_13_), channel_id=1, source_target_pairs={{0,8},{8,12},{12,4},{4,0},{1,9},{9,13},{13,5},{5,1},{2,10},{10,14}... | collective-permute-start | bytes 552968 | tf_op jit(solution)/shard_map/ppermute | solution.py:102
  40.7 16.9 %copy-start.3 = (s32[1,128]{1,0:T(1,128)S(1)}, s32[1,128]{1,0:T(1,128)}, u32[]{:S(2)}) copy-start(s32[1,128]{1,0:T(1,128)} %refs_3_.1) | copy-start | bytes 1540
  44.8 1.4 %collective-permute-start.10 = (f32[56,512]{1,0:T(8,128)S(1)}, f32[56,512]{1,0:T(8,128)S(1)}, u32[]{:S(2)}, u32[]{:S(2)}) collective-permute-start(f32[56,512]{1,0:T(8,128)S(1)} %get-tuple-element.47), channel_id=1, source_target_pairs={{0,1},{1,0},{2,3},{3,2},{4,5},{5,4},{6,7},{7,6},{8,9},{9,8},{10,11... | collective-permute-start | bytes 344072 | tf_op jit(solution)/shard_map/ppermute | solution.py:89
  46.2 5.0 %collective-permute-start.11 = (bf16[56,512]{1,0:T(8,128)(2,1)S(1)}, bf16[56,512]{1,0:T(8,128)(2,1)S(1)}, u32[]{:S(2)}, u32[]{:S(2)}) collective-permute-start(bf16[56,512]{1,0:T(8,128)(2,1)S(1)} %add_convert_fusion.refs_4_), channel_id=1, source_target_pairs={{0,8},{8,12},{12,4},{4,0},{1,9},{9,13},{13,5},{5,1},{2,10},{10,14}... | collective-permute-start | bytes 172040 | tf_op jit(solution)/shard_map/ppermute | solution.py:112
  49.3 6.1 %collective-permute-start.12 = (bf16[56,512]{1,0:T(8,128)(2,1)S(1)}, bf16[56,512]{1,0:T(8,128)(2,1)S(1)}, u32[]{:S(2)}, u32[]{:S(2)}) collective-permute-start(bf16[56,512]{1,0:T(8,128)(2,1)S(1)} %add_convert_fusion.refs_4_), channel_id=1, source_target_pairs={{0,12},{8,4},{12,0},{4,8},{1,13},{9,5},{13,1},{5,9},{2,14},{10,6},... | collective-permute-start | bytes 172040 | tf_op jit(solution)/shard_map/ppermute | solution.py:112
  51.2 5.1 %collective-permute-start.13 = (bf16[56,512]{1,0:T(8,128)(2,1)S(1)}, bf16[56,512]{1,0:T(8,128)(2,1)S(1)}, u32[]{:S(2)}, u32[]{:S(2)}) collective-permute-start(bf16[56,512]{1,0:T(8,128)(2,1)S(1)} %add_convert_fusion.refs_4_), channel_id=1, source_target_pairs={{0,4},{8,0},{12,8},{4,12},{1,5},{9,1},{13,9},{5,13},{2,6},{10,2},{... | collective-permute-start | bytes 172040 | tf_op jit(solution)/shard_map/ppermute | solution.py:112
  51.2 5.1 %collective-permute-start.14 = (bf16[56,512]{1,0:T(8,128)(2,1)S(1)}, bf16[56,512]{1,0:T(8,128)(2,1)S(1)}, u32[]{:S(2)}, u32[]{:S(2)}) collective-permute-start(bf16[56,512]{1,0:T(8,128)(2,1)S(1)} %add_convert_fusion.refs_4_), channel_id=1, source_target_pairs={{0,1},{1,0},{2,3},{3,2},{4,5},{5,4},{6,7},{7,6},{8,9},{9,8},{10,11... | collective-permute-start | bytes 172040 | tf_op jit(solution)/shard_map/ppermute | solution.py:89
  51.2 5.1 %collective-permute-start.15 = (bf16[56,512]{1,0:T(8,128)(2,1)S(1)}, bf16[56,512]{1,0:T(8,128)(2,1)S(1)}, u32[]{:S(2)}, u32[]{:S(2)}) collective-permute-start(bf16[56,512]{1,0:T(8,128)(2,1)S(1)} %collective-permute-done.11.refs_5_), channel_id=1, source_target_pairs={{0,1},{1,0},{2,3},{3,2},{4,5},{5,4},{6,7},{7,6},{8,9},{9,8},{10,11... | collective-permute-start | bytes 172040 | tf_op jit(solution)/shard_map/ppermute | solution.py:89
  55.4 1.2 %collective-permute-start.16 = (bf16[56,512]{1,0:T(8,128)(2,1)S(1)}, bf16[56,512]{1,0:T(8,128)(2,1)S(1)}, u32[]{:S(2)}, u32[]{:S(2)}) collective-permute-start(bf16[56,512]{1,0:T(8,128)(2,1)S(1)} %collective-permute-done.12.refs_6_), channel_id=1, source_target_pairs={{0,1},{1,0},{2,3},{3,2},{4,5},{5,4},{6,7},{7,6},{8,9},{9,8},{10,11... | collective-permute-start | bytes 172040 | tf_op jit(solution)/shard_map/ppermute | solution.py:89
  56.3 1.2 %collective-permute-start.17 = (bf16[56,512]{1,0:T(8,128)(2,1)S(1)}, bf16[56,512]{1,0:T(8,128)(2,1)S(1)}, u32[]{:S(2)}, u32[]{:S(2)}) collective-permute-start(bf16[56,512]{1,0:T(8,128)(2,1)S(1)} %collective-permute-done.13.refs_7_), channel_id=1, source_target_pairs={{0,1},{1,0},{2,3},{3,2},{4,5},{5,4},{6,7},{7,6},{8,9},{9,8},{10,11... | collective-permute-start | bytes 172040 | tf_op jit(solution)/shard_map/ppermute | solution.py:89

commit v14 on v12

--- a/solution.py
+++ b/solution.py
@@ -105,12 +105,10 @@
     return lax.ppermute(x, (axis, across), pairs)
 
 
-def ring_spread(x, axis):
+def spread(x, axis):
     count = lax.axis_size(axis)
-    order = list(range(0, count, 2)) + list(range(1, count, 2))[::-1]
     return [x] + [
-        lax.ppermute(x, axis, [(order[i], order[(i + k) % count]) for i in range(count)])
-        for k in range(1, count)
+        lax.ppermute(x, axis, [(i, i ^ bits) for i in range(count)]) for bits in range(1, count)
     ]
 
 
@@ -296,12 +294,20 @@
     def places(table, pattern):
         feat, pos, rep = place()
 
+        def turned(owner):
+            turn = pos - (owner - floor_div(owner, poses) * poses)
+            return jnp.where(turn < 0.0, turn + poses, turn)
+
+        def spread_place(owner, rank):
+            feat_of = floor_div(owner, poses).astype(jnp.int32)
+            bits = (feat.astype(jnp.int32) ^ feat_of).astype(F32)
+            return (bits * poses + turned(owner)) * listed + rank
+
         def padded(owner, rank):
             feat_of = floor_div(owner, poses)
+            turn = turned(owner)
             step = ring_place(feat, feats) - ring_place(feat_of, feats)
             step = jnp.where(step < 0.0, step + feats, step)
-            turn = pos - (owner - feat_of * poses)
-            turn = jnp.where(turn < 0.0, turn + poses, turn)
             at = step * poses + turn
             at = jnp.where(step < feats - 1.0, at - (poses - 1), at)
             at = jnp.where(step == 0.0, turn + (feats - 2) * poses, at)
@@ -321,10 +327,11 @@
         total = holders * listed
         used = spread_slot(iota((1, wide), 1)) >= 0.0
         place_row = jnp.where(used, padded(owner_row, rank_row), -1.0)
-        placing = padded(owner_col, rank_col) == iota((slots, total), 1)
+        placing = spread_place(owner_col, rank_col) == iota((slots, total), 1)
+        entry = padded(owner_col, rank_col) == iota((slots, total), 1)
         placing_t = place_row == iota((total, wide), 0)
         layer = ids_col - floor_div(ids_col, layers) * layers
-        layer_row = jnp.sum(jnp.where(placing, layer, 0.0), axis=0, keepdims=True)
+        layer_row = jnp.sum(jnp.where(entry, layer, 0.0), axis=0, keepdims=True)
         mine = [placing_t[at * listed : (at + 1) * listed] for at in own_lists]
         mine = jnp.concatenate(mine, axis=0)
         gain = jnp.sum(jnp.where(mine, vals_row, 0.0), axis=1, keepdims=True)
@@ -335,28 +342,17 @@
         )
         allowed = jnp.where(pattern[0] == 1, 1.0, 0.0).astype(BF16)
 
-        def in_block(slot, dim, extent):
-            wide = (extent, feats) if dim == 0 else (feats, extent)
-            return (floor_div(slot, block_rows) == iota(wide, 1 - dim)).astype(BF16)
-
         sources = (floor_div(iota((wide, 1), 0), span) == iota((wide, feats), 1)).astype(BF16)
         targets = (floor_div(iota((1, wide), 1), span) == iota((feats, wide), 0)).astype(BF16)
         mask = dot(dot(sources, allowed, NT).astype(BF16), targets)
         source = floor_div(spread_slot(iota((wide, wide), 0)), kslots)
         target = floor_div(spread_slot(iota((wide, wide), 1)), kslots)
         mask = jnp.where(source <= target, mask, 0.0)
-        first = (feat * reps + rep) * result_rows
-        own_slot = first + iota((result_rows, 1), 0)
-        own_mask = dot(in_block(own_slot, 0, result_rows), allowed).astype(BF16)
-        own_mask = dot(own_mask, in_block(iota((1, slots), 1), 1, slots))
-        own_causal = floor_div(iota((result_rows, slots), 1), kslots) <= floor_div(
-            first + iota((result_rows, slots), 0), kslots
-        )
-        own_mask = jnp.where(own_causal, own_mask, 0.0)
+        squeeze = spread_slot(iota((wide, slots), 0)) == iota((wide, slots), 1)
         placing, placing_t = placing.astype(BF16), placing_t.astype(BF16)
-        return placing, placing_t, layer_row, gains, mask.astype(BF16), own_mask
-
-    placing, placing_t, layer_row, gains, mask, own_mask, *dec_rows[1:] = on_core(
+        return placing, placing_t, layer_row, gains, mask.astype(BF16), squeeze.astype(BF16)
+
+    placing, placing_t, layer_row, gains, mask, squeeze, *dec_rows[1:] = on_core(
         places,
         [my_list, block_pattern],
         [
@@ -365,7 +361,7 @@
             shape(1, holders * listed),
             shape(depth * column, 1),
             shape(wide, wide, dtype=BF16),
-            shape(result_rows, slots),
+            shape(wide, slots, dtype=BF16),
         ],
         small,
         through=dec_rows[1:],
@@ -415,25 +411,25 @@
         small,
     )
     own_edges = (keep + rotate(send, "rep", 1)).astype(BF16)
-    shards = ring_spread(own_edges, "feat")
+    shards = spread(own_edges, "feat")
     others = [rotate(shard, "rep", 1) for shard in shards]
 
-    def finish(placing, mask, own_mask, targets, *values):
+    def finish(placing, mask, squeeze, targets, *values):
         feat, _, rep = place()
         first = rep == 0.0
         chips = []
         for mine, other in zip(values[:feats], values[feats:]):
             lower, higher = jnp.where(first, mine, other), jnp.where(first, other, mine)
             chips.append(jnp.concatenate([unpack_rests(lower), unpack_rests(higher)], axis=0))
-        padded = [chips[k][q * listed : (q + 1) * listed] for k, q in order]
-        padded = jnp.concatenate(padded, axis=0)
+        padded = jnp.concatenate(chips, axis=0)
         unused = [jnp.zeros((span - block_rows, holders * listed), BF16)]
         unused = unused if span > block_rows else []
         sources = []
         for f in range(feats):
             sources += [placing[f * block_rows : (f + 1) * block_rows]] + unused
         sources = jnp.concatenate(sources, axis=0)
-        magnitude = jnp.abs(dot(sources, padded) * mask.astype(F32))
+        edges = dot(sources, padded) * mask.astype(F32)
+        magnitude = jnp.abs(edges)
         total = jnp.maximum(jnp.sum(magnitude, axis=0, keepdims=True), 1.0)
         magnitude = magnitude.astype(BF16)
         diagonal = iota((wide, wide), 0) == iota((wide, wide), 1)
@@ -457,13 +453,13 @@
                 influence = jnp.where(mine, accum[at : at + result_rows], influence)
         start = feat * span + rep * result_rows
         own = start + iota((result_rows, wide), 0) == iota((result_rows, wide), 1)
-        rows = dot(own.astype(BF16), padded, NT).astype(BF16)
-        edges = (dot(rows, placing, NT) * own_mask).astype(BF16)
+        rows = dot(own.astype(BF16), edges.astype(BF16), NT).astype(BF16)
+        edges = dot(rows, squeeze).astype(BF16)
         return edges[None], (influence * float(slots))[None]
 
     edges, influence = on_core(
         finish,
-        [placing, mask, own_mask, target_slots] + shards + others,
+        [placing, mask, squeeze, target_slots] + shards + others,
         [shape(1, result_rows, slots, dtype=BF16), shape(1, result_rows, panel)],
         small,
     )

time: 60.4 us -> 60.5 us (level)
  waiting for transfers between devices: 20.1 us -> 19.4 us
  transfers between devices with their start and end apart: 16 -> 16, of which waited for: 11 -> 10; matrix products, arithmetic and copies ran while one was open for 1% -> 1% of each run, Pallas kernels for 5% -> 5%
where the time goes in v14:
time: 60.5 us; the launch traced here: 60.3 us
  waiting for transfers between devices  19.4 us (32%)
  starting transfers between devices  15.6 us (26%)
  blocking collectives  14.1 us (23%)
  Pallas kernels  8.94 us (15%)
  matrix products  0.77 us (1%)
  between operations  0.75 us (1%)
  local copies, waits for them, and re-layouts  0.69 us (1%)
    all_to_all x1, blocking collectives, per_device(): lax.all_to_all(packed, ('feat', 'pos'), split_axis=0, concat_axis=0, tile...  14.1 us
    pallas_call x7, Pallas kernels, on_core(): return list(call(*args, *streams, *through))  8.94 us
    ppermute x4, waiting for transfers between devices, ring_next(): return lax.ppermute(x, axis, steps)  8.34 us
    ppermute x4, starting transfers between devices, ring_next(): return lax.ppermute(x, axis, steps)  5.89 us
    ppermute x3, starting transfers between devices, spread(): lax.ppermute(x, axis, [(i, i ^ bits) for i in range(count)])  5.07 us
    ppermute x3, waiting for transfers between devices, spread(): lax.ppermute(x, axis, [(i, i ^ bits) for i in range(count)])  4.56 us
    ppermute x2, waiting for transfers between devices, ring_next(): return lax.ppermute(x, (axis, across), pairs)  4.24 us
    ppermute x7, starting transfers between devices, rotate(): lax.ppermute(x, axis, [(i, (i + step) % count) for i in range(count)])  3.31 us
  transfers between devices with their start and end apart: 16, of which 10 were waited for; matrix products, arithmetic and copies ran while one was open for 1% of the time, Pallas kernels for 5%

profile of v14, /device:TPU:0, one launch (start us, length us, event | category | flops | bytes accessed | tf_op | source)
XLA Modules:
  0.0 60.3 jit_solution(2775651313804437714)
XLA Ops:
  0.6 1.5 %shard_map.77 = f32[8,8,128]{2,1,0:T(8,128)} custom-call(s32[1,4,28]{2,1,0:T(4,128)} %refs_0_.1, f32[1,4,28]{2,1,0:T(4,128)} %refs_1_.3), custom_call_target="tpu_custom_call" | custom-call | tf_op jit(solution)/shard_map/pallas_call | solution.py:84
  2.1 14.1 %all_to_all.5.refs_0_ = f32[8,8,128]{2,1,0:T(8,128)S(1)} all-to-all(f32[8,8,128]{2,1,0:T(8,128)} %shard_map.77), channel_id=1, replica_groups=mesh['grp'=2,'feat'=4,'pos'=2,'rep'=2] {'feat','pos'}, dimensions={0} | all-to-all | bytes 65536 | tf_op jit(solution)/shard_map/all_to_all | solution.py:194
  17.7 0.7 %collective-permute-start.1 = (bf16[80,1152]{1,0:T(8,128)(2,1)S(1)}, bf16[80,1152]{1,0:T(8,128)(2,1)S(1)}, u32[]{:S(2)}, u32[]{:S(2)}) collective-permute-start(bf16[80,1152]{1,0:T(8,128)(2,1)S(1)} %get-tuple-element.33), channel_id=1, source_target_pairs={{0,10},{2,8},{8,14},{10,12},{12,6},{14,4},{4,2},{6,0},{1,11},{3,9}... | collective-permute-start | bytes 552968 | tf_op jit(solution)/shard_map/ppermute | solution.py:105
  18.4 0.8 %fusion = bf16[3,160,1152]{2,1,0:T(8,128)(2,1)S(1)} fusion(bf16[512,3,1152]{2,0,1:T(8,128)(2,1)S(1)} %copy-done, bf16[160,512]{1,0:T(8,128)(2,1)S(1)} %get-tuple-element.24), kind=kOutput, calls=%fused_computation.1 | convolution fusion | flops 566784000 | bytes 4808704 | tf_op jit(solution)/shard_map/dot_general | solution.py:284
  19.3 0.6 copy-done.2
  19.9 1.9 %shard_map.80 = (bf16[448,640]{1,0:T(8,128)(2,1)S(1)}, bf16[640,512]{1,0:T(8,128)(2,1)S(1)}, f32[1,640]{1,0:T(1,128)S(1)}, f32[480,1]{1,0:T(8,128)S(1)}, bf16[51...) custom-call(f32[32,28]{1,0:T(8,128)S(1)} %get-tuple-element.22.refs_, ...), custom_call_target="tpu_custom_call", output_to_operand_aliasing={{6}: (2, {})} | custom-call | flops 1 | bytes 1 | tf_op jit(solution)/shard_map/pallas_call | solution.py:84
  21.8 2.3 %collective-permute-done.refs_6_ = bf16[80,1152]{1,0:T(8,128)(2,1)S(1)} collective-permute-done((bf16[80,1152]{1,0:T(8,128)(2,1)S(1)}, bf16[80,1152]{1,0:T(8,128)(2,1)S(1)}, u32[]{:S(2)}, u32[]{:S(2)}) %collective-permute-start) | collective-permute-done | bytes 184352 | tf_op jit(solution)/shard_map/ppermute | solution.py:105
  24.1 1.9 %collective-permute-done.1.refs_7_ = bf16[80,1152]{1,0:T(8,128)(2,1)S(1)} collective-permute-done((bf16[80,1152]{1,0:T(8,128)(2,1)S(1)}, bf16[80,1152]{1,0:T(8,128)(2,1)S(1)}, u32[]{:S(2)}, u32[]{:S(2)}) %collective-permute-start.1) | collective-permute-done | bytes 184352 | tf_op jit(solution)/shard_map/ppermute | solution.py:105
  26.0 1.6 %collective-permute-start.2 = (bf16[3,80,1152]{2,1,0:T(8,128)(2,1)S(1)}, bf16[3,80,1152]{2,1,0:T(8,128)(2,1)S(1)}, u32[]{:S(2)}, u32[]{:S(2)}) collective-permute-start(bf16[3,80,1152]{2,1,0:T(8,128)(2,1)S(1)} %get-tuple-element.35), channel_id=1, source_target_pairs={{0,2},{2,0},{1,3},{3,1},{4,6},{6,4},{5,7},{7,5},{8,10},{10,8},{9,1... | collective-permute-start | bytes 1658888 | tf_op jit(solution)/shard_map/ppermute | solution.py:89
  27.6 1.7 %collective-permute-start.3 = (bf16[80,1152]{1,0:T(8,128)(2,1)S(1)}, bf16[80,1152]{1,0:T(8,128)(2,1)S(1)}, u32[]{:S(2)}, u32[]{:S(2)}) collective-permute-start(bf16[80,1152]{1,0:T(8,128)(2,1)S(1)} %collective-permute-done.refs_6_), channel_id=1, source_target_pairs={{0,8},{8,12},{12,4},{4,0},{1,9},{9,13},{13,5},{5,1},{2,10},{10,14}... | collective-permute-start | bytes 552968 | tf_op jit(solution)/shard_map/ppermute | solution.py:102
  29.3 0.7 %collective-permute-start.5 = (bf16[80,1152]{1,0:T(8,128)(2,1)S(1)}, bf16[80,1152]{1,0:T(8,128)(2,1)S(1)}, u32[]{:S(2)}, u32[]{:S(2)}) collective-permute-start(bf16[80,1152]{1,0:T(8,128)(2,1)S(1)} %get-tuple-element.33), channel_id=1, source_target_pairs={{0,2},{2,0},{1,3},{3,1},{4,6},{6,4},{5,7},{7,5},{8,10},{10,8},{9,1... | collective-permute-start | bytes 552968 | tf_op jit(solution)/shard_map/ppermute | solution.py:89
  29.9 4.4 %collective-permute-done.3.refs_8_ = bf16[80,1152]{1,0:T(8,128)(2,1)S(1)} collective-permute-done((bf16[80,1152]{1,0:T(8,128)(2,1)S(1)}, bf16[80,1152]{1,0:T(8,128)(2,1)S(1)}, u32[]{:S(2)}, u32[]{:S(2)}) %collective-permute-start.3) | collective-permute-done | bytes 184352 | tf_op jit(solution)/shard_map/ppermute | solution.py:102
  34.4 2.1 %collective-permute-start.6 = (bf16[80,1152]{1,0:T(8,128)(2,1)S(1)}, bf16[80,1152]{1,0:T(8,128)(2,1)S(1)}, u32[]{:S(2)}, u32[]{:S(2)}) collective-permute-start(bf16[80,1152]{1,0:T(8,128)(2,1)S(1)} %collective-permute-done.3.refs_8_), channel_id=1, source_target_pairs={{0,8},{8,12},{12,4},{4,0},{1,9},{9,13},{13,5},{5,1},{2,10},{10,14}... | collective-permute-start | bytes 552968 | tf_op jit(solution)/shard_map/ppermute | solution.py:102
  36.4 1.9 %collective-permute-done.4.refs_9_ = bf16[80,1152]{1,0:T(8,128)(2,1)S(1)} collective-permute-done((bf16[80,1152]{1,0:T(8,128)(2,1)S(1)}, bf16[80,1152]{1,0:T(8,128)(2,1)S(1)}, u32[]{:S(2)}, u32[]{:S(2)}) %collective-permute-start.4) | collective-permute-done | bytes 184352 | tf_op jit(solution)/shard_map/ppermute | solution.py:102
  38.3 2.1 %collective-permute-start.7 = (bf16[80,1152]{1,0:T(8,128)(2,1)S(1)}, bf16[80,1152]{1,0:T(8,128)(2,1)S(1)}, u32[]{:S(2)}, u32[]{:S(2)}) collective-permute-start(bf16[80,1152]{1,0:T(8,128)(2,1)S(1)} %collective-permute-done.4.refs_9_), channel_id=1, source_target_pairs={{0,8},{8,12},{12,4},{4,0},{1,9},{9,13},{13,5},{5,1},{2,10},{10,14}... | collective-permute-start | bytes 552968 | tf_op jit(solution)/shard_map/ppermute | solution.py:102
  40.4 1.3 %shard_map.81 = (f32[160,512]{1,0:T(8,128)S(1)}, bf16[480,1152]{1,0:T(8,128)(2,1)S(1)}) custom-call(f32[1,640]{1,0:T(1,128)S(1)} %get-tuple-element.28.refs_0_, bf16[640,512]{1,0:T(8,128)(2,1)S(1)} %get-tuple-element.29.refs_1_, f32[480,1]{1,0:T(8,128)S(1)} %get-tuple-element.30.refs_2_, bf16[3,80,1152]{2,1,0:T(8,128)(2,1)S(1)} %get-tuple-element.34.refs_3_, ...), custom_call_target="tpu_custom_call" | custom-call | flops 1 | bytes 1 | tf_op jit(solution)/shard_map/pallas_call | solution.py:84
  41.8 2.1 %collective-permute-done.7.refs_6_ = bf16[80,1152]{1,0:T(8,128)(2,1)S(1)} collective-permute-done((bf16[80,1152]{1,0:T(8,128)(2,1)S(1)}, bf16[80,1152]{1,0:T(8,128)(2,1)S(1)}, u32[]{:S(2)}, u32[]{:S(2)}) %collective-permute-start.7) | collective-permute-done | bytes 184352 | tf_op jit(solution)/shard_map/ppermute | solution.py:102
  43.8 1.0 %shard_map.82 = (f32[56,512]{1,0:T(8,128)S(1)}, f32[56,512]{1,0:T(8,128)S(1)}) custom-call(f32[1,640]{1,0:T(1,128)S(1)} %get-tuple-element.28.refs_0_, bf16[640,512]{1,0:T(8,128)(2,1)S(1)} %get-tuple-element.29.refs_1_, f32[160,512]{1,0:T(8,128)S(1)} %get-tuple-element.38.refs_2_, bf16[480,1152]{1,0:T(8,128)(2,1)S(1)} %get-tuple-element.39.refs_3_, ...), custom_call_target="tpu_custom_call" | custom-call | tf_op jit(solution)/shard_map/pallas_call | solution.py:84
  44.9 1.3 %collective-permute-done.8 = f32[56,512]{1,0:T(8,128)S(1)} collective-permute-done((f32[56,512]{1,0:T(8,128)S(1)}, f32[56,512]{1,0:T(8,128)S(1)}, u32[]{:S(2)}, u32[]{:S(2)}) %collective-permute-start.8) | collective-permute-done | bytes 114720 | tf_op jit(solution)/shard_map/ppermute | solution.py:89
  46.2 2.6 %collective-permute-start.9 = (bf16[56,512]{1,0:T(8,128)(2,1)S(1)}, bf16[56,512]{1,0:T(8,128)(2,1)S(1)}, u32[]{:S(2)}, u32[]{:S(2)}) collective-permute-start(bf16[56,512]{1,0:T(8,128)(2,1)S(1)} %add_convert_fusion.refs_4_), channel_id=1, source_target_pairs={{0,4},{4,0},{8,12},{12,8},{1,5},{5,1},{9,13},{13,9},{2,6},{6,2},{1... | collective-permute-start | bytes 172040 | tf_op jit(solution)/shard_map/ppermute | solution.py:111
  49.4 1.9 %collective-permute-start.11 = (bf16[56,512]{1,0:T(8,128)(2,1)S(1)}, bf16[56,512]{1,0:T(8,128)(2,1)S(1)}, u32[]{:S(2)}, u32[]{:S(2)}) collective-permute-start(bf16[56,512]{1,0:T(8,128)(2,1)S(1)} %add_convert_fusion.refs_4_), channel_id=1, source_target_pairs={{0,12},{4,8},{8,4},{12,0},{1,13},{5,9},{9,5},{13,1},{2,14},{6,10},... | collective-permute-start | bytes 172040 | tf_op jit(solution)/shard_map/ppermute | solution.py:111
  51.8 4.6 %collective-permute-done.10.refs_6_ = bf16[56,512]{1,0:T(8,128)(2,1)S(1)} collective-permute-done((bf16[56,512]{1,0:T(8,128)(2,1)S(1)}, bf16[56,512]{1,0:T(8,128)(2,1)S(1)}, u32[]{:S(2)}, u32[]{:S(2)}) %collective-permute-start.10) | collective-permute-done | bytes 57376 | tf_op jit(solution)/shard_map/ppermute | solution.py:111
  56.9 0.7 %collective-permute-done.14.refs_10_ = bf16[56,512]{1,0:T(8,128)(2,1)S(1)} collective-permute-done((bf16[56,512]{1,0:T(8,128)(2,1)S(1)}, bf16[56,512]{1,0:T(8,128)(2,1)S(1)}, u32[]{:S(2)}, u32[]{:S(2)}) %collective-permute-start.14) | collective-permute-done | bytes 57376 | tf_op jit(solution)/shard_map/ppermute | solution.py:89
  57.8 2.5 %shard_map.83 = (bf16[1,56,448]{2,1,0:T(8,128)(2,1)}, f32[1,56,128]{2,1,0:T(8,128)}) custom-call(bf16[448,640]{1,0:T(8,128)(2,1)S(1)} %get-tuple-element.25.refs_0_, bf16[512,512]{1,0:T(8,128)(2,1)S(1)} %get-tuple-element.26.refs_1_, bf16[512,448]{1,0:T(8,128)(2,1)S(1)} %get-tuple-element.27.refs_2_, s32[1,128]{1,0:T(1,128)S(1)} %copy-done.3, ...), custom_call_target="tpu_custom_call" | custom-call | tf_op jit(solution)/shard_map/pallas_call | solution.py:84
  (27 shorter events, 3.5 us)
Async XLA Ops:
  0.6 17.8 %copy-start = (bf16[512,3,1152]{2,0,1:T(8,128)(2,1)S(1)}, bf16[512,3,1152]{2,0,1:T(8,128)(2,1)}, u32[]{:S(2)}) copy-start(bf16[512,3,1152]{2,0,1:T(8,128)(2,1)} %param.11) | copy-start | bytes 10616836
  2.1 14.6 %copy-start.1 = (bf16[512,1152]{1,0:T(8,128)(2,1)S(1)}, bf16[512,1152]{1,0:T(8,128)(2,1)}, u32[]{:S(2)}) copy-start(bf16[512,1152]{1,0:T(8,128)(2,1)} %refs_1_.4) | copy-start | bytes 3538948
  17.1 7.0 %collective-permute-start = (bf16[80,1152]{1,0:T(8,128)(2,1)S(1)}, bf16[80,1152]{1,0:T(8,128)(2,1)S(1)}, u32[]{:S(2)}, u32[]{:S(2)}) collective-permute-start(bf16[80,1152]{1,0:T(8,128)(2,1)S(1)} %get-tuple-element.32.refs_5_), channel_id=1, source_target_pairs={{0,8},{2,10},{8,12},{10,14},{12,4},{14,6},{4,0},{6,2},{1,9},{3,11}... | collective-permute-start | bytes 552968 | tf_op jit(solution)/shard_map/ppermute | solution.py:105
  17.7 8.3 %collective-permute-start.1 = (bf16[80,1152]{1,0:T(8,128)(2,1)S(1)}, bf16[80,1152]{1,0:T(8,128)(2,1)S(1)}, u32[]{:S(2)}, u32[]{:S(2)}) collective-permute-start(bf16[80,1152]{1,0:T(8,128)(2,1)S(1)} %get-tuple-element.33), channel_id=1, source_target_pairs={{0,10},{2,8},{8,14},{10,12},{12,6},{14,4},{4,2},{6,0},{1,11},{3,9}... | collective-permute-start | bytes 552968 | tf_op jit(solution)/shard_map/ppermute | solution.py:105
  19.2 0.7 %copy-start.2 = (s32[1,4,4]{2,1,0:T(4,128)S(1)}, s32[1,4,4]{2,1,0:T(4,128)}, u32[]{:S(2)}) copy-start(s32[1,4,4]{2,1,0:T(4,128)} %refs_1_.5) | copy-start | bytes 196
  26.0 14.4 %collective-permute-start.2 = (bf16[3,80,1152]{2,1,0:T(8,128)(2,1)S(1)}, bf16[3,80,1152]{2,1,0:T(8,128)(2,1)S(1)}, u32[]{:S(2)}, u32[]{:S(2)}) collective-permute-start(bf16[3,80,1152]{2,1,0:T(8,128)(2,1)S(1)} %get-tuple-element.35), channel_id=1, source_target_pairs={{0,2},{2,0},{1,3},{3,1},{4,6},{6,4},{5,7},{7,5},{8,10},{10,8},{9,1... | collective-permute-start | bytes 1658888 | tf_op jit(solution)/shard_map/ppermute | solution.py:89
  27.6 6.8 %collective-permute-start.3 = (bf16[80,1152]{1,0:T(8,128)(2,1)S(1)}, bf16[80,1152]{1,0:T(8,128)(2,1)S(1)}, u32[]{:S(2)}, u32[]{:S(2)}) collective-permute-start(bf16[80,1152]{1,0:T(8,128)(2,1)S(1)} %collective-permute-done.refs_6_), channel_id=1, source_target_pairs={{0,8},{8,12},{12,4},{4,0},{1,9},{9,13},{13,5},{5,1},{2,10},{10,14}... | collective-permute-start | bytes 552968 | tf_op jit(solution)/shard_map/ppermute | solution.py:102
  29.2 9.1 %collective-permute-start.4 = (bf16[80,1152]{1,0:T(8,128)(2,1)S(1)}, bf16[80,1152]{1,0:T(8,128)(2,1)S(1)}, u32[]{:S(2)}, u32[]{:S(2)}) collective-permute-start(bf16[80,1152]{1,0:T(8,128)(2,1)S(1)} %collective-permute-done.1.refs_7_), channel_id=1, source_target_pairs={{0,8},{8,12},{12,4},{4,0},{1,9},{9,13},{13,5},{5,1},{2,10},{10,14}... | collective-permute-start | bytes 552968 | tf_op jit(solution)/shard_map/ppermute | solution.py:102
  29.3 12.5 %collective-permute-start.5 = (bf16[80,1152]{1,0:T(8,128)(2,1)S(1)}, bf16[80,1152]{1,0:T(8,128)(2,1)S(1)}, u32[]{:S(2)}, u32[]{:S(2)}) collective-permute-start(bf16[80,1152]{1,0:T(8,128)(2,1)S(1)} %get-tuple-element.33), channel_id=1, source_target_pairs={{0,2},{2,0},{1,3},{3,1},{4,6},{6,4},{5,7},{7,5},{8,10},{10,8},{9,1... | collective-permute-start | bytes 552968 | tf_op jit(solution)/shard_map/ppermute | solution.py:89
  34.4 7.4 %collective-permute-start.6 = (bf16[80,1152]{1,0:T(8,128)(2,1)S(1)}, bf16[80,1152]{1,0:T(8,128)(2,1)S(1)}, u32[]{:S(2)}, u32[]{:S(2)}) collective-permute-start(bf16[80,1152]{1,0:T(8,128)(2,1)S(1)} %collective-permute-done.3.refs_8_), channel_id=1, source_target_pairs={{0,8},{8,12},{12,4},{4,0},{1,9},{9,13},{13,5},{5,1},{2,10},{10,14}... | collective-permute-start | bytes 552968 | tf_op jit(solution)/shard_map/ppermute | solution.py:102
  38.3 5.5 %collective-permute-start.7 = (bf16[80,1152]{1,0:T(8,128)(2,1)S(1)}, bf16[80,1152]{1,0:T(8,128)(2,1)S(1)}, u32[]{:S(2)}, u32[]{:S(2)}) collective-permute-start(bf16[80,1152]{1,0:T(8,128)(2,1)S(1)} %collective-permute-done.4.refs_9_), channel_id=1, source_target_pairs={{0,8},{8,12},{12,4},{4,0},{1,9},{9,13},{13,5},{5,1},{2,10},{10,14}... | collective-permute-start | bytes 552968 | tf_op jit(solution)/shard_map/ppermute | solution.py:102
  40.4 17.4 %copy-start.3 = (s32[1,128]{1,0:T(1,128)S(1)}, s32[1,128]{1,0:T(1,128)}, u32[]{:S(2)}) copy-start(s32[1,128]{1,0:T(1,128)} %refs_3_.1) | copy-start | bytes 1540
  44.8 1.4 %collective-permute-start.8 = (f32[56,512]{1,0:T(8,128)S(1)}, f32[56,512]{1,0:T(8,128)S(1)}, u32[]{:S(2)}, u32[]{:S(2)}) collective-permute-start(f32[56,512]{1,0:T(8,128)S(1)} %get-tuple-element.41), channel_id=1, source_target_pairs={{0,1},{1,0},{2,3},{3,2},{4,5},{5,4},{6,7},{7,6},{8,9},{9,8},{10,11... | collective-permute-start | bytes 344072 | tf_op jit(solution)/shard_map/ppermute | solution.py:89
  46.2 5.1 %collective-permute-start.9 = (bf16[56,512]{1,0:T(8,128)(2,1)S(1)}, bf16[56,512]{1,0:T(8,128)(2,1)S(1)}, u32[]{:S(2)}, u32[]{:S(2)}) collective-permute-start(bf16[56,512]{1,0:T(8,128)(2,1)S(1)} %add_convert_fusion.refs_4_), channel_id=1, source_target_pairs={{0,4},{4,0},{8,12},{12,8},{1,5},{5,1},{9,13},{13,9},{2,6},{6,2},{1... | collective-permute-start | bytes 172040 | tf_op jit(solution)/shard_map/ppermute | solution.py:111
  48.9 7.5 %collective-permute-start.10 = (bf16[56,512]{1,0:T(8,128)(2,1)S(1)}, bf16[56,512]{1,0:T(8,128)(2,1)S(1)}, u32[]{:S(2)}, u32[]{:S(2)}) collective-permute-start(bf16[56,512]{1,0:T(8,128)(2,1)S(1)} %add_convert_fusion.refs_4_), channel_id=1, source_target_pairs={{0,8},{4,12},{8,0},{12,4},{1,9},{5,13},{9,1},{13,5},{2,10},{6,14},... | collective-permute-start | bytes 172040 | tf_op jit(solution)/shard_map/ppermute | solution.py:111
  49.4 7.0 %collective-permute-start.11 = (bf16[56,512]{1,0:T(8,128)(2,1)S(1)}, bf16[56,512]{1,0:T(8,128)(2,1)S(1)}, u32[]{:S(2)}, u32[]{:S(2)}) collective-permute-start(bf16[56,512]{1,0:T(8,128)(2,1)S(1)} %add_convert_fusion.refs_4_), channel_id=1, source_target_pairs={{0,12},{4,8},{8,4},{12,0},{1,13},{5,9},{9,5},{13,1},{2,14},{6,10},... | collective-permute-start | bytes 172040 | tf_op jit(solution)/shard_map/ppermute | solution.py:111
  51.3 5.6 %collective-permute-start.12 = (bf16[56,512]{1,0:T(8,128)(2,1)S(1)}, bf16[56,512]{1,0:T(8,128)(2,1)S(1)}, u32[]{:S(2)}, u32[]{:S(2)}) collective-permute-start(bf16[56,512]{1,0:T(8,128)(2,1)S(1)} %add_convert_fusion.refs_4_), channel_id=1, source_target_pairs={{0,1},{1,0},{2,3},{3,2},{4,5},{5,4},{6,7},{7,6},{8,9},{9,8},{10,11... | collective-permute-start | bytes 172040 | tf_op jit(solution)/shard_map/ppermute | solution.py:89
  51.3 5.6 %collective-permute-start.13 = (bf16[56,512]{1,0:T(8,128)(2,1)S(1)}, bf16[56,512]{1,0:T(8,128)(2,1)S(1)}, u32[]{:S(2)}, u32[]{:S(2)}) collective-permute-start(bf16[56,512]{1,0:T(8,128)(2,1)S(1)} %collective-permute-done.9.refs_5_), channel_id=1, source_target_pairs={{0,1},{1,0},{2,3},{3,2},{4,5},{5,4},{6,7},{7,6},{8,9},{9,8},{10,11... | collective-permute-start | bytes 172040 | tf_op jit(solution)/shard_map/ppermute | solution.py:89
  56.4 1.2 %collective-permute-start.14 = (bf16[56,512]{1,0:T(8,128)(2,1)S(1)}, bf16[56,512]{1,0:T(8,128)(2,1)S(1)}, u32[]{:S(2)}, u32[]{:S(2)}) collective-permute-start(bf16[56,512]{1,0:T(8,128)(2,1)S(1)} %collective-permute-done.10.refs_6_), channel_id=1, source_target_pairs={{0,1},{1,0},{2,3},{3,2},{4,5},{5,4},{6,7},{7,6},{8,9},{9,8},{10,11... | collective-permute-start | bytes 172040 | tf_op jit(solution)/shard_map/ppermute | solution.py:89
  56.4 1.4 %collective-permute-start.15 = (bf16[56,512]{1,0:T(8,128)(2,1)S(1)}, bf16[56,512]{1,0:T(8,128)(2,1)S(1)}, u32[]{:S(2)}, u32[]{:S(2)}) collective-permute-start(bf16[56,512]{1,0:T(8,128)(2,1)S(1)} %collective-permute-done.11.refs_7_), channel_id=1, source_target_pairs={{0,1},{1,0},{2,3},{3,2},{4,5},{5,4},{6,7},{7,6},{8,9},{9,8},{10,11... | collective-permute-start | bytes 172040 | tf_op jit(solution)/shard_map/ppermute | solution.py:89

commit v15 on v14

--- a/solution.py
+++ b/solution.py
@@ -107,9 +107,10 @@
 
 def spread(x, axis):
     count = lax.axis_size(axis)
-    return [x] + [
-        lax.ppermute(x, axis, [(i, i ^ bits) for i in range(count)]) for bits in range(1, count)
-    ]
+    found = {0: x}
+    for bits in sorted(range(1, count), key=lambda bits: bits < count // 2):
+        found[bits] = lax.ppermute(x, axis, [(i, i ^ bits) for i in range(count)])
+    return list(found.items())
 
 
 def part(x, kernel):
@@ -285,7 +286,10 @@
         picks, decoder, (((1,), (0,)), ((), ())), preferred_element_type=F32
     )
     dec_rows = jnp.transpose(dec_rows, (1, 0, 2)).astype(BF16)
-    dec_rows = [dec_rows[:, k * listed : (k + 1) * listed] for k in range(poses)]
+    dec_rows = [
+        [dec_rows[l, k * listed : (k + 1) * listed] for l in range(depth)] for k in range(poses)
+    ]
+    away = [rows for k in range(1, poses) for rows in dec_rows[k]]
     order = [(0, 0)] + [(k, q) for k in range(1, feats - 1) for q in range(poses)]
     soon = len(order)
     order += [(0, q) for q in range(1, poses)] + [(feats - 1, q) for q in range(poses)]
@@ -352,7 +356,7 @@
         placing, placing_t = placing.astype(BF16), placing_t.astype(BF16)
         return placing, placing_t, layer_row, gains, mask.astype(BF16), squeeze.astype(BF16)
 
-    placing, placing_t, layer_row, gains, mask, squeeze, *dec_rows[1:] = on_core(
+    placing, placing_t, layer_row, gains, mask, squeeze, *away = on_core(
         places,
         [my_list, block_pattern],
         [
@@ -364,13 +368,13 @@
             shape(wide, slots, dtype=BF16),
         ],
         small,
-        through=dec_rows[1:],
+        through=away,
         cost=(1, 1),
     )
-    *dec_rows, ring[1][0], ring[1][-1] = lax.optimization_barrier(
-        (*dec_rows, ring[1][0], ring[1][-1])
-    )
-    dec_rows = [dec_rows[0]] + [rotate(dec_rows[k], "pos", k) for k in range(1, poses)]
+    for k in range(1, poses):
+        rows = away[(k - 1) * depth : k * depth]
+        dec_rows[k] = [rotate(row, "pos", k) for row in rows]
+    dec_rows = [dec_rows[k][l] for l in range(depth) for k in range(poses)]
 
     for _ in range(2, feats):
         ring.append([ring_next(rows, "feat") for rows in ring[-1]])
@@ -387,9 +391,10 @@
         return split[:column] + (split[column : 2 * column] + split[2 * column :])
 
     def early(layer_row, placing_t, gains, *values):
-        dec = jnp.concatenate([d[l] for l in range(depth) for d in values[:poses]], axis=0)
+        count = depth * poses
+        dec = jnp.concatenate(values[-count:], axis=0)
         dec = (dec.astype(F32) * gains).astype(BF16)
-        return products(0, values[poses:], dec, layer_row, placing_t), dec
+        return products(0, values[:-count], dec, layer_row, placing_t), dec
 
     def late(layer_row, placing_t, so_far, dec, *values):
         raw = so_far + products(soon, values, dec, layer_row, placing_t)
@@ -399,7 +404,7 @@
 
     so_far, scaled = on_core(
         early,
-        [layer_row, placing_t, gains] + dec_rows + [ring[k][q] for k, q in order[:soon]],
+        [layer_row, placing_t, gains] + [ring[k][q] for k, q in order[:soon]] + dec_rows,
         [shape(column, wide), shape(depth * column, width, dtype=BF16)],
         small,
         cost=(1, 1),
@@ -411,7 +416,9 @@
         small,
     )
     own_edges = (keep + rotate(send, "rep", 1)).astype(BF16)
-    shards = spread(own_edges, "feat")
+    found = spread(own_edges, "feat")
+    arrival = [bits for bits, _ in found]
+    shards = [shard for _, shard in found]
     others = [rotate(shard, "rep", 1) for shard in shards]
 
     def finish(placing, mask, squeeze, targets, *values):
@@ -421,7 +428,7 @@
         for mine, other in zip(values[:feats], values[feats:]):
             lower, higher = jnp.where(first, mine, other), jnp.where(first, other, mine)
             chips.append(jnp.concatenate([unpack_rests(lower), unpack_rests(higher)], axis=0))
-        padded = jnp.concatenate(chips, axis=0)
+        padded = jnp.concatenate([chips[arrival.index(m)] for m in range(feats)], axis=0)
         unused = [jnp.zeros((span - block_rows, holders * listed), BF16)]
         unused = unused if span > block_rows else []
         sources = []

time: 60.5 us -> 57.4 us (0.949)
  waiting for transfers between devices: 19.4 us -> 17 us
  starting transfers between devices: 15.6 us -> 14.9 us
    ppermute x4, waiting for transfers between devices: 8.34 us -> 3.97 us  [ring_next(): return lax.ppermute(x, axis, steps)]
    ppermute x7 -> x9, waiting for transfers between devices: 2.29 us -> 4.87 us  [rotate(): lax.ppermute(x, axis, [(i, (i + step) % count) for i in range(count)])]
    ppermute x4, starting transfers between devices: 5.89 us -> 3.62 us  [ring_next(): return lax.ppermute(x, axis, steps)]
    ppermute x7 -> x9, starting transfers between devices: 3.31 us -> 5.33 us  [rotate(): lax.ppermute(x, axis, [(i, (i + step) % count) for i in range(count)])]
  transfers between devices with their start and end apart: 16 -> 18, of which waited for: 10 -> 12; matrix products, arithmetic and copies ran while one was open for 1% -> 2% of each run, Pallas kernels for 5% -> 6%
where the time goes in v15:
time: 57.4 us; the launch traced here: 57.1 us
  waiting for transfers between devices  17 us (30%)
  starting transfers between devices  14.9 us (26%)
  blocking collectives  14.1 us (25%)
  Pallas kernels  8.96 us (16%)
  matrix products  0.8 us (1%)
  between operations  0.75 us (1%)
  local copies, waits for them, and re-layouts  0.69 us (1%)
    all_to_all x1, blocking collectives, per_device(): lax.all_to_all(packed, ('feat', 'pos'), split_axis=0, concat_axis=0, tile...  14.1 us
    pallas_call x7, Pallas kernels, on_core(): return list(call(*args, *streams, *through))  8.96 us
    ppermute x9, starting transfers between devices, rotate(): lax.ppermute(x, axis, [(i, (i + step) % count) for i in range(count)])  5.33 us
    ppermute x9, waiting for transfers between devices, rotate(): lax.ppermute(x, axis, [(i, (i + step) % count) for i in range(count)])  4.87 us
    ppermute x3, starting transfers between devices, spread(): found[bits] = lax.ppermute(x, axis, [(i, i ^ bits) for i in range(count)])  4.62 us
    ppermute x3, waiting for transfers between devices, spread(): found[bits] = lax.ppermute(x, axis, [(i, i ^ bits) for i in range(count)])  4.39 us
    ppermute x4, waiting for transfers between devices, ring_next(): return lax.ppermute(x, axis, steps)  3.97 us
    ppermute x2, waiting for transfers between devices, ring_next(): return lax.ppermute(x, (axis, across), pairs)  3.73 us
  transfers between devices with their start and end apart: 18, of which 12 were waited for; matrix products, arithmetic and copies ran while one was open for 2% of the time, Pallas kernels for 6%

profile of v15, /device:TPU:0, one launch (start us, length us, event | category | flops | bytes accessed | tf_op | source)
XLA Modules:
  0.0 57.1 jit_solution(7870108076111336163)
XLA Ops:
  0.6 1.5 %shard_map.77 = f32[8,8,128]{2,1,0:T(8,128)} custom-call(s32[1,4,28]{2,1,0:T(4,128)} %refs_0_.1, f32[1,4,28]{2,1,0:T(4,128)} %refs_1_.3), custom_call_target="tpu_custom_call" | custom-call | tf_op jit(solution)/shard_map/pallas_call | solution.py:84
  2.1 14.1 %all_to_all.5.refs_0_ = f32[8,8,128]{2,1,0:T(8,128)S(1)} all-to-all(f32[8,8,128]{2,1,0:T(8,128)} %shard_map.77), channel_id=1, replica_groups=mesh['grp'=2,'feat'=4,'pos'=2,'rep'=2] {'feat','pos'}, dimensions={0} | all-to-all | bytes 65536 | tf_op jit(solution)/shard_map/all_to_all | solution.py:195
  17.7 0.7 %collective-permute-start.1 = (bf16[80,1152]{1,0:T(8,128)(2,1)S(1)}, bf16[80,1152]{1,0:T(8,128)(2,1)S(1)}, u32[]{:S(2)}, u32[]{:S(2)}) collective-permute-start(bf16[80,1152]{1,0:T(8,128)(2,1)S(1)} %get-tuple-element.30), channel_id=1, source_target_pairs={{0,10},{2,8},{8,14},{10,12},{12,6},{14,4},{4,2},{6,0},{1,11},{3,9}... | collective-permute-start | bytes 552968 | tf_op jit(solution)/shard_map/ppermute | solution.py:105
  18.4 0.8 %fusion = bf16[3,160,1152]{2,1,0:T(8,128)(2,1)S(1)} fusion(bf16[512,3,1152]{2,0,1:T(8,128)(2,1)S(1)} %copy-done, bf16[160,512]{1,0:T(8,128)(2,1)S(1)} %get-tuple-element.22), kind=kOutput, calls=%fused_computation.1 | convolution fusion | flops 566784000 | bytes 4808704 | tf_op jit(solution)/shard_map/dot_general | solution.py:285
  19.9 1.9 %shard_map.80 = (bf16[448,640]{1,0:T(8,128)(2,1)S(1)}, bf16[640,512]{1,0:T(8,128)(2,1)S(1)}, f32[1,640]{1,0:T(1,128)S(1)}, f32[480,1]{1,0:T(8,128)S(1)}, bf16[51...) custom-call(f32[32,28]{1,0:T(8,128)S(1)} %get-tuple-element.20.refs_, ...), custom_call_target="tpu_custom_call", output_to_operand_aliasing={{6}: (2, {}), {7}: (3, {}), {8}: (4, {})} | custom-call | flops 1 | bytes 1 | tf_op jit(solution)/shard_map/pallas_call | solution.py:84
  21.8 1.4 %collective-permute-start.4 = (bf16[80,1152]{1,0:T(8,128)(2,1)S(1)}, bf16[80,1152]{1,0:T(8,128)(2,1)S(1)}, u32[]{:S(2)}, u32[]{:S(2)}) collective-permute-start(bf16[80,1152]{1,0:T(8,128)(2,1)S(1)} %get-tuple-element.31), channel_id=1, source_target_pairs={{0,2},{2,0},{1,3},{3,1},{4,6},{6,4},{5,7},{7,5},{8,10},{10,8},{9,1... | collective-permute-start | bytes 552968 | tf_op jit(solution)/shard_map/ppermute | solution.py:89
  23.2 1.4 %collective-permute-done.refs_4_ = bf16[80,1152]{1,0:T(8,128)(2,1)S(1)} collective-permute-done((bf16[80,1152]{1,0:T(8,128)(2,1)S(1)}, bf16[80,1152]{1,0:T(8,128)(2,1)S(1)}, u32[]{:S(2)}, u32[]{:S(2)}) %collective-permute-start) | collective-permute-done | bytes 184352 | tf_op jit(solution)/shard_map/ppermute | solution.py:105
  24.6 1.2 %collective-permute-start.2 = (bf16[80,1152]{1,0:T(8,128)(2,1)S(1)}, bf16[80,1152]{1,0:T(8,128)(2,1)S(1)}, u32[]{:S(2)}, u32[]{:S(2)}) collective-permute-start(bf16[80,1152]{1,0:T(8,128)(2,1)S(1)} %collective-permute-done.refs_4_), channel_id=1, source_target_pairs={{0,8},{8,12},{12,4},{4,0},{1,9},{9,13},{13,5},{5,1},{2,10},{10,14}... | collective-permute-start | bytes 552968 | tf_op jit(solution)/shard_map/ppermute | solution.py:102
  25.8 2.3 %collective-permute-done.1.refs_5_ = bf16[80,1152]{1,0:T(8,128)(2,1)S(1)} collective-permute-done((bf16[80,1152]{1,0:T(8,128)(2,1)S(1)}, bf16[80,1152]{1,0:T(8,128)(2,1)S(1)}, u32[]{:S(2)}, u32[]{:S(2)}) %collective-permute-start.1) | collective-permute-done | bytes 184352 | tf_op jit(solution)/shard_map/ppermute | solution.py:105
  28.7 1.8 %collective-permute-start.5 = (bf16[80,1152]{1,0:T(8,128)(2,1)S(1)}, bf16[80,1152]{1,0:T(8,128)(2,1)S(1)}, u32[]{:S(2)}, u32[]{:S(2)}) collective-permute-start(bf16[80,1152]{1,0:T(8,128)(2,1)S(1)} %get-tuple-element.32), channel_id=1, source_target_pairs={{0,2},{2,0},{1,3},{3,1},{4,6},{6,4},{5,7},{7,5},{8,10},{10,8},{9,1... | collective-permute-start | bytes 552968 | tf_op jit(solution)/shard_map/ppermute | solution.py:89
  30.7 1.8 %collective-permute-start.7 = (bf16[80,1152]{1,0:T(8,128)(2,1)S(1)}, bf16[80,1152]{1,0:T(8,128)(2,1)S(1)}, u32[]{:S(2)}, u32[]{:S(2)}) collective-permute-start(bf16[80,1152]{1,0:T(8,128)(2,1)S(1)} %get-tuple-element.30), channel_id=1, source_target_pairs={{0,2},{2,0},{1,3},{3,1},{4,6},{6,4},{5,7},{7,5},{8,10},{10,8},{9,1... | collective-permute-start | bytes 552968 | tf_op jit(solution)/shard_map/ppermute | solution.py:89
  32.6 1.2 %collective-permute-start.8 = (bf16[80,1152]{1,0:T(8,128)(2,1)S(1)}, bf16[80,1152]{1,0:T(8,128)(2,1)S(1)}, u32[]{:S(2)}, u32[]{:S(2)}) collective-permute-start(bf16[80,1152]{1,0:T(8,128)(2,1)S(1)} %collective-permute-done.2.refs_6_), channel_id=1, source_target_pairs={{0,8},{8,12},{12,4},{4,0},{1,9},{9,13},{13,5},{5,1},{2,10},{10,14}... | collective-permute-start | bytes 552968 | tf_op jit(solution)/shard_map/ppermute | solution.py:102
  33.8 2.7 %collective-permute-done.3.refs_7_ = bf16[80,1152]{1,0:T(8,128)(2,1)S(1)} collective-permute-done((bf16[80,1152]{1,0:T(8,128)(2,1)S(1)}, bf16[80,1152]{1,0:T(8,128)(2,1)S(1)}, u32[]{:S(2)}, u32[]{:S(2)}) %collective-permute-start.3) | collective-permute-done | bytes 184352 | tf_op jit(solution)/shard_map/ppermute | solution.py:102
  37.1 1.6 %collective-permute-done.6.refs_13_ = bf16[80,1152]{1,0:T(8,128)(2,1)S(1)} collective-permute-done((bf16[80,1152]{1,0:T(8,128)(2,1)S(1)}, bf16[80,1152]{1,0:T(8,128)(2,1)S(1)}, u32[]{:S(2)}, u32[]{:S(2)}) %collective-permute-start.6) | collective-permute-done | bytes 184352 | tf_op jit(solution)/shard_map/ppermute | solution.py:89
  38.8 1.3 %shard_map.81 = (f32[160,512]{1,0:T(8,128)S(1)}, bf16[480,1152]{1,0:T(8,128)(2,1)S(1)}) custom-call(f32[1,640]{1,0:T(1,128)S(1)} %get-tuple-element.26.refs_0_, bf16[640,512]{1,0:T(8,128)(2,1)S(1)} %get-tuple-element.27.refs_1_, f32[480,1]{1,0:T(8,128)S(1)} %get-tuple-element.28.refs_2_, bf16[80,1152]{1,0:T(8,128)(2,1)S(1)} %get-tuple-element.29.refs_3_, ...), custom_call_target="tpu_custom_call" | custom-call | flops 1 | bytes 1 | tf_op jit(solution)/shard_map/pallas_call | solution.py:84
  40.1 0.7 %collective-permute-done.7.refs_4_ = bf16[80,1152]{1,0:T(8,128)(2,1)S(1)} collective-permute-done((bf16[80,1152]{1,0:T(8,128)(2,1)S(1)}, bf16[80,1152]{1,0:T(8,128)(2,1)S(1)}, u32[]{:S(2)}, u32[]{:S(2)}) %collective-permute-start.7) | collective-permute-done | bytes 184352 | tf_op jit(solution)/shard_map/ppermute | solution.py:89
  40.8 1.3 %collective-permute-done.9.refs_6_ = bf16[80,1152]{1,0:T(8,128)(2,1)S(1)} collective-permute-done((bf16[80,1152]{1,0:T(8,128)(2,1)S(1)}, bf16[80,1152]{1,0:T(8,128)(2,1)S(1)}, u32[]{:S(2)}, u32[]{:S(2)}) %collective-permute-start.9) | collective-permute-done | bytes 184352 | tf_op jit(solution)/shard_map/ppermute | solution.py:102
  42.0 1.0 %shard_map.82 = (f32[56,512]{1,0:T(8,128)S(1)}, f32[56,512]{1,0:T(8,128)S(1)}) custom-call(f32[1,640]{1,0:T(1,128)S(1)} %get-tuple-element.26.refs_0_, bf16[640,512]{1,0:T(8,128)(2,1)S(1)} %get-tuple-element.27.refs_1_, f32[160,512]{1,0:T(8,128)S(1)} %get-tuple-element.34.refs_2_, bf16[480,1152]{1,0:T(8,128)(2,1)S(1)} %get-tuple-element.35.refs_3_, ...), custom_call_target="tpu_custom_call" | custom-call | tf_op jit(solution)/shard_map/pallas_call | solution.py:84
  43.1 1.3 %collective-permute-done.10 = f32[56,512]{1,0:T(8,128)S(1)} collective-permute-done((f32[56,512]{1,0:T(8,128)S(1)}, f32[56,512]{1,0:T(8,128)S(1)}, u32[]{:S(2)}, u32[]{:S(2)}) %collective-permute-start.10) | collective-permute-done | bytes 114720 | tf_op jit(solution)/shard_map/ppermute | solution.py:89
  44.4 1.6 %collective-permute-start.11 = (bf16[56,512]{1,0:T(8,128)(2,1)S(1)}, bf16[56,512]{1,0:T(8,128)(2,1)S(1)}, u32[]{:S(2)}, u32[]{:S(2)}) collective-permute-start(bf16[56,512]{1,0:T(8,128)(2,1)S(1)} %add_convert_fusion.refs_4_), channel_id=1, source_target_pairs={{0,8},{4,12},{8,0},{12,4},{1,9},{5,13},{9,1},{13,5},{2,10},{6,14},... | collective-permute-start | bytes 172040 | tf_op jit(solution)/shard_map/ppermute | solution.py:112
  46.0 3.0 %collective-permute-start.12 = (bf16[56,512]{1,0:T(8,128)(2,1)S(1)}, bf16[56,512]{1,0:T(8,128)(2,1)S(1)}, u32[]{:S(2)}, u32[]{:S(2)}) collective-permute-start(bf16[56,512]{1,0:T(8,128)(2,1)S(1)} %add_convert_fusion.refs_4_), channel_id=1, source_target_pairs={{0,12},{4,8},{8,4},{12,0},{1,13},{5,9},{9,5},{13,1},{2,14},{6,10},... | collective-permute-start | bytes 172040 | tf_op jit(solution)/shard_map/ppermute | solution.py:112
  49.0 3.2 %collective-permute-done.11.refs_5_ = bf16[56,512]{1,0:T(8,128)(2,1)S(1)} collective-permute-done((bf16[56,512]{1,0:T(8,128)(2,1)S(1)}, bf16[56,512]{1,0:T(8,128)(2,1)S(1)}, u32[]{:S(2)}, u32[]{:S(2)}) %collective-permute-start.11) | collective-permute-done | bytes 57376 | tf_op jit(solution)/shard_map/ppermute | solution.py:112
  53.4 0.7 %collective-permute-done.16.refs_10_ = bf16[56,512]{1,0:T(8,128)(2,1)S(1)} collective-permute-done((bf16[56,512]{1,0:T(8,128)(2,1)S(1)}, bf16[56,512]{1,0:T(8,128)(2,1)S(1)}, u32[]{:S(2)}, u32[]{:S(2)}) %collective-permute-start.16) | collective-permute-done | bytes 57376 | tf_op jit(solution)/shard_map/ppermute | solution.py:89
  54.7 2.5 %shard_map.83 = (bf16[1,56,448]{2,1,0:T(8,128)(2,1)}, f32[1,56,128]{2,1,0:T(8,128)}) custom-call(bf16[448,640]{1,0:T(8,128)(2,1)S(1)} %get-tuple-element.23.refs_0_, bf16[512,512]{1,0:T(8,128)(2,1)S(1)} %get-tuple-element.24.refs_1_, bf16[512,448]{1,0:T(8,128)(2,1)S(1)} %get-tuple-element.25.refs_2_, s32[1,128]{1,0:T(1,128)S(1)} %copy-done.3, ...), custom_call_target="tpu_custom_call" | custom-call | tf_op jit(solution)/shard_map/pallas_call | solution.py:84
  (31 shorter events, 5.5 us)
Async XLA Ops:
  0.6 17.8 %copy-start = (bf16[512,3,1152]{2,0,1:T(8,128)(2,1)S(1)}, bf16[512,3,1152]{2,0,1:T(8,128)(2,1)}, u32[]{:S(2)}) copy-start(bf16[512,3,1152]{2,0,1:T(8,128)(2,1)} %param.11) | copy-start | bytes 10616836
  2.1 14.6 %copy-start.1 = (bf16[512,1152]{1,0:T(8,128)(2,1)S(1)}, bf16[512,1152]{1,0:T(8,128)(2,1)}, u32[]{:S(2)}) copy-start(bf16[512,1152]{1,0:T(8,128)(2,1)} %refs_1_.4) | copy-start | bytes 3538948
  17.1 7.5 %collective-permute-start = (bf16[80,1152]{1,0:T(8,128)(2,1)S(1)}, bf16[80,1152]{1,0:T(8,128)(2,1)S(1)}, u32[]{:S(2)}, u32[]{:S(2)}) collective-permute-start(bf16[80,1152]{1,0:T(8,128)(2,1)S(1)} %get-tuple-element.29.refs_3_), channel_id=1, source_target_pairs={{0,8},{2,10},{8,12},{10,14},{12,4},{14,6},{4,0},{6,2},{1,9},{3,11}... | collective-permute-start | bytes 552968 | tf_op jit(solution)/shard_map/ppermute | solution.py:105
  17.7 10.4 %collective-permute-start.1 = (bf16[80,1152]{1,0:T(8,128)(2,1)S(1)}, bf16[80,1152]{1,0:T(8,128)(2,1)S(1)}, u32[]{:S(2)}, u32[]{:S(2)}) collective-permute-start(bf16[80,1152]{1,0:T(8,128)(2,1)S(1)} %get-tuple-element.30), channel_id=1, source_target_pairs={{0,10},{2,8},{8,14},{10,12},{12,6},{14,4},{4,2},{6,0},{1,11},{3,9}... | collective-permute-start | bytes 552968 | tf_op jit(solution)/shard_map/ppermute | solution.py:105
  19.2 0.7 %copy-start.2 = (s32[1,4,4]{2,1,0:T(4,128)S(1)}, s32[1,4,4]{2,1,0:T(4,128)}, u32[]{:S(2)}) copy-start(s32[1,4,4]{2,1,0:T(4,128)} %refs_1_.5) | copy-start | bytes 196
  21.8 8.9 %collective-permute-start.4 = (bf16[80,1152]{1,0:T(8,128)(2,1)S(1)}, bf16[80,1152]{1,0:T(8,128)(2,1)S(1)}, u32[]{:S(2)}, u32[]{:S(2)}) collective-permute-start(bf16[80,1152]{1,0:T(8,128)(2,1)S(1)} %get-tuple-element.31), channel_id=1, source_target_pairs={{0,2},{2,0},{1,3},{3,1},{4,6},{6,4},{5,7},{7,5},{8,10},{10,8},{9,1... | collective-permute-start | bytes 552968 | tf_op jit(solution)/shard_map/ppermute | solution.py:89
  24.6 8.0 %collective-permute-start.2 = (bf16[80,1152]{1,0:T(8,128)(2,1)S(1)}, bf16[80,1152]{1,0:T(8,128)(2,1)S(1)}, u32[]{:S(2)}, u32[]{:S(2)}) collective-permute-start(bf16[80,1152]{1,0:T(8,128)(2,1)S(1)} %collective-permute-done.refs_4_), channel_id=1, source_target_pairs={{0,8},{8,12},{12,4},{4,0},{1,9},{9,13},{13,5},{5,1},{2,10},{10,14}... | collective-permute-start | bytes 552968 | tf_op jit(solution)/shard_map/ppermute | solution.py:102
  28.1 8.3 %collective-permute-start.3 = (bf16[80,1152]{1,0:T(8,128)(2,1)S(1)}, bf16[80,1152]{1,0:T(8,128)(2,1)S(1)}, u32[]{:S(2)}, u32[]{:S(2)}) collective-permute-start(bf16[80,1152]{1,0:T(8,128)(2,1)S(1)} %collective-permute-done.1.refs_5_), channel_id=1, source_target_pairs={{0,8},{8,12},{12,4},{4,0},{1,9},{9,13},{13,5},{5,1},{2,10},{10,14}... | collective-permute-start | bytes 552968 | tf_op jit(solution)/shard_map/ppermute | solution.py:102
  28.7 8.4 %collective-permute-start.5 = (bf16[80,1152]{1,0:T(8,128)(2,1)S(1)}, bf16[80,1152]{1,0:T(8,128)(2,1)S(1)}, u32[]{:S(2)}, u32[]{:S(2)}) collective-permute-start(bf16[80,1152]{1,0:T(8,128)(2,1)S(1)} %get-tuple-element.32), channel_id=1, source_target_pairs={{0,2},{2,0},{1,3},{3,1},{4,6},{6,4},{5,7},{7,5},{8,10},{10,8},{9,1... | collective-permute-start | bytes 552968 | tf_op jit(solution)/shard_map/ppermute | solution.py:89
  30.5 8.2 %collective-permute-start.6 = (bf16[80,1152]{1,0:T(8,128)(2,1)S(1)}, bf16[80,1152]{1,0:T(8,128)(2,1)S(1)}, u32[]{:S(2)}, u32[]{:S(2)}) collective-permute-start(bf16[80,1152]{1,0:T(8,128)(2,1)S(1)} %get-tuple-element.33), channel_id=1, source_target_pairs={{0,2},{2,0},{1,3},{3,1},{4,6},{6,4},{5,7},{7,5},{8,10},{10,8},{9,1... | collective-permute-start | bytes 552968 | tf_op jit(solution)/shard_map/ppermute | solution.py:89
  30.7 10.0 %collective-permute-start.7 = (bf16[80,1152]{1,0:T(8,128)(2,1)S(1)}, bf16[80,1152]{1,0:T(8,128)(2,1)S(1)}, u32[]{:S(2)}, u32[]{:S(2)}) collective-permute-start(bf16[80,1152]{1,0:T(8,128)(2,1)S(1)} %get-tuple-element.30), channel_id=1, source_target_pairs={{0,2},{2,0},{1,3},{3,1},{4,6},{6,4},{5,7},{7,5},{8,10},{10,8},{9,1... | collective-permute-start | bytes 552968 | tf_op jit(solution)/shard_map/ppermute | solution.py:89
  32.6 8.2 %collective-permute-start.8 = (bf16[80,1152]{1,0:T(8,128)(2,1)S(1)}, bf16[80,1152]{1,0:T(8,128)(2,1)S(1)}, u32[]{:S(2)}, u32[]{:S(2)}) collective-permute-start(bf16[80,1152]{1,0:T(8,128)(2,1)S(1)} %collective-permute-done.2.refs_6_), channel_id=1, source_target_pairs={{0,8},{8,12},{12,4},{4,0},{1,9},{9,13},{13,5},{5,1},{2,10},{10,14}... | collective-permute-start | bytes 552968 | tf_op jit(solution)/shard_map/ppermute | solution.py:102
  36.5 5.5 %collective-permute-start.9 = (bf16[80,1152]{1,0:T(8,128)(2,1)S(1)}, bf16[80,1152]{1,0:T(8,128)(2,1)S(1)}, u32[]{:S(2)}, u32[]{:S(2)}) collective-permute-start(bf16[80,1152]{1,0:T(8,128)(2,1)S(1)} %collective-permute-done.3.refs_7_), channel_id=1, source_target_pairs={{0,8},{8,12},{12,4},{4,0},{1,9},{9,13},{13,5},{5,1},{2,10},{10,14}... | collective-permute-start | bytes 552968 | tf_op jit(solution)/shard_map/ppermute | solution.py:102
  38.8 15.9 %copy-start.3 = (s32[1,128]{1,0:T(1,128)S(1)}, s32[1,128]{1,0:T(1,128)}, u32[]{:S(2)}) copy-start(s32[1,128]{1,0:T(1,128)} %refs_3_.1) | copy-start | bytes 1540
  43.0 1.4 %collective-permute-start.10 = (f32[56,512]{1,0:T(8,128)S(1)}, f32[56,512]{1,0:T(8,128)S(1)}, u32[]{:S(2)}, u32[]{:S(2)}) collective-permute-start(f32[56,512]{1,0:T(8,128)S(1)} %get-tuple-element.37), channel_id=1, source_target_pairs={{0,1},{1,0},{2,3},{3,2},{4,5},{5,4},{6,7},{7,6},{8,9},{9,8},{10,11... | collective-permute-start | bytes 344072 | tf_op jit(solution)/shard_map/ppermute | solution.py:89
  44.4 7.8 %collective-permute-start.11 = (bf16[56,512]{1,0:T(8,128)(2,1)S(1)}, bf16[56,512]{1,0:T(8,128)(2,1)S(1)}, u32[]{:S(2)}, u32[]{:S(2)}) collective-permute-start(bf16[56,512]{1,0:T(8,128)(2,1)S(1)} %add_convert_fusion.refs_4_), channel_id=1, source_target_pairs={{0,8},{4,12},{8,0},{12,4},{1,9},{5,13},{9,1},{13,5},{2,10},{6,14},... | collective-permute-start | bytes 172040 | tf_op jit(solution)/shard_map/ppermute | solution.py:112
  46.0 6.8 %collective-permute-start.12 = (bf16[56,512]{1,0:T(8,128)(2,1)S(1)}, bf16[56,512]{1,0:T(8,128)(2,1)S(1)}, u32[]{:S(2)}, u32[]{:S(2)}) collective-permute-start(bf16[56,512]{1,0:T(8,128)(2,1)S(1)} %add_convert_fusion.refs_4_), channel_id=1, source_target_pairs={{0,12},{4,8},{8,4},{12,0},{1,13},{5,9},{9,5},{13,1},{2,14},{6,10},... | collective-permute-start | bytes 172040 | tf_op jit(solution)/shard_map/ppermute | solution.py:112
  49.0 4.4 %collective-permute-start.13 = (bf16[56,512]{1,0:T(8,128)(2,1)S(1)}, bf16[56,512]{1,0:T(8,128)(2,1)S(1)}, u32[]{:S(2)}, u32[]{:S(2)}) collective-permute-start(bf16[56,512]{1,0:T(8,128)(2,1)S(1)} %add_convert_fusion.refs_4_), channel_id=1, source_target_pairs={{0,4},{4,0},{8,12},{12,8},{1,5},{5,1},{9,13},{13,9},{2,6},{6,2},{1... | collective-permute-start | bytes 172040 | tf_op jit(solution)/shard_map/ppermute | solution.py:112
  49.0 4.4 %collective-permute-start.14 = (bf16[56,512]{1,0:T(8,128)(2,1)S(1)}, bf16[56,512]{1,0:T(8,128)(2,1)S(1)}, u32[]{:S(2)}, u32[]{:S(2)}) collective-permute-start(bf16[56,512]{1,0:T(8,128)(2,1)S(1)} %add_convert_fusion.refs_4_), channel_id=1, source_target_pairs={{0,1},{1,0},{2,3},{3,2},{4,5},{5,4},{6,7},{7,6},{8,9},{9,8},{10,11... | collective-permute-start | bytes 172040 | tf_op jit(solution)/shard_map/ppermute | solution.py:89
  52.2 1.2 %collective-permute-start.15 = (bf16[56,512]{1,0:T(8,128)(2,1)S(1)}, bf16[56,512]{1,0:T(8,128)(2,1)S(1)}, u32[]{:S(2)}, u32[]{:S(2)}) collective-permute-start(bf16[56,512]{1,0:T(8,128)(2,1)S(1)} %collective-permute-done.11.refs_5_), channel_id=1, source_target_pairs={{0,1},{1,0},{2,3},{3,2},{4,5},{5,4},{6,7},{7,6},{8,9},{9,8},{10,11... | collective-permute-start | bytes 172040 | tf_op jit(solution)/shard_map/ppermute | solution.py:89
  52.9 1.2 %collective-permute-start.16 = (bf16[56,512]{1,0:T(8,128)(2,1)S(1)}, bf16[56,512]{1,0:T(8,128)(2,1)S(1)}, u32[]{:S(2)}, u32[]{:S(2)}) collective-permute-start(bf16[56,512]{1,0:T(8,128)(2,1)S(1)} %collective-permute-done.12.refs_6_), channel_id=1, source_target_pairs={{0,1},{1,0},{2,3},{3,2},{4,5},{5,4},{6,7},{7,6},{8,9},{9,8},{10,11... | collective-permute-start | bytes 172040 | tf_op jit(solution)/shard_map/ppermute | solution.py:89
  53.4 1.2 %collective-permute-start.17 = (bf16[56,512]{1,0:T(8,128)(2,1)S(1)}, bf16[56,512]{1,0:T(8,128)(2,1)S(1)}, u32[]{:S(2)}, u32[]{:S(2)}) collective-permute-start(bf16[56,512]{1,0:T(8,128)(2,1)S(1)} %collective-permute-done.13.refs_7_), channel_id=1, source_target_pairs={{0,1},{1,0},{2,3},{3,2},{4,5},{5,4},{6,7},{7,6},{8,9},{9,8},{10,11... | collective-permute-start | bytes 172040 | tf_op jit(solution)/shard_map/ppermute | solution.py:89

commit v16 on v15

--- a/solution.py
+++ b/solution.py
@@ -103,14 +103,6 @@
     wide = lax.axis_size(across)
     pairs = [(a * wide + i, b * wide + (i + turn) % wide) for a, b in steps for i in range(wide)]
     return lax.ppermute(x, (axis, across), pairs)
-
-
-def spread(x, axis):
-    count = lax.axis_size(axis)
-    found = {0: x}
-    for bits in sorted(range(1, count), key=lambda bits: bits < count // 2):
-        found[bits] = lax.ppermute(x, axis, [(i, i ^ bits) for i in range(count)])
-    return list(found.items())
 
 
 def part(x, kernel):
@@ -163,13 +155,13 @@
             rows.append(jnp.concatenate(parts, axis=1) if len(parts) > 1 else parts[0])
         return jnp.concatenate(rows, axis=0)
 
-    def unpack_rests(x):
-        x = x.astype(F32) if small else x
+    def unpack_rests(x, first):
         found = {}
         for n, row in enumerate(bins):
             lane = 0
             for at, block in row:
-                rest = x[n * GROUP : (n + 1) * GROUP, lane : lane + wide - block * span]
+                at_row = (first + n) * GROUP
+                rest = x[at_row : at_row + GROUP, lane : lane + wide - block * span]
                 lane += wide - block * span
                 if block:
                     rest = jnp.concatenate([jnp.zeros((GROUP, block * span), x.dtype), rest], axis=1)
@@ -398,9 +390,7 @@
 
     def late(layer_row, placing_t, so_far, dec, *values):
         raw = so_far + products(soon, values, dec, layer_row, placing_t)
-        first = place()[2] == 0.0
-        lower, higher = pack_rests(raw[:half]), pack_rests(raw[half:])
-        return jnp.where(first, lower, higher), jnp.where(first, higher, lower)
+        return (jnp.concatenate([pack_rests(raw[:half]), pack_rests(raw[half:])], axis=0),)
 
     so_far, scaled = on_core(
         early,
@@ -409,26 +399,34 @@
         small,
         cost=(1, 1),
     )
-    keep, send = on_core(
+    (partial,) = on_core(
         late,
         [layer_row, placing_t, so_far, scaled] + [ring[k][q] for k, q in order[soon:]],
-        [shape(len(bins) * GROUP, wide)] * 2,
-        small,
-    )
-    own_edges = (keep + rotate(send, "rep", 1)).astype(BF16)
-    found = spread(own_edges, "feat")
-    arrival = [bits for bits, _ in found]
-    shards = [shard for _, shard in found]
-    others = [rotate(shard, "rep", 1) for shard in shards]
+        [shape(reps * len(bins) * GROUP, wide)],
+        small,
+    )
+    columns = (partial + rotate(partial, "rep", 1)).astype(BF16)
+
+    far = []
+    for bits in range(2, feats, 2):
+        pairs = [
+            (f * reps + r, (f ^ (bits + r)) * reps + r) for f in range(feats) for r in range(reps)
+        ]
+        far.append(lax.ppermute(columns, ("feat", "rep"), pairs))
+    near = lax.ppermute(columns, "feat", [(f, f ^ 1) for f in range(feats)])
+    across = [rotate(shard, "rep", 1) for shard in far]
 
     def finish(placing, mask, squeeze, targets, *values):
         feat, _, rep = place()
         first = rep == 0.0
-        chips = []
-        for mine, other in zip(values[:feats], values[feats:]):
-            lower, higher = jnp.where(first, mine, other), jnp.where(first, other, mine)
-            chips.append(jnp.concatenate([unpack_rests(lower), unpack_rests(higher)], axis=0))
-        padded = jnp.concatenate([chips[arrival.index(m)] for m in range(feats)], axis=0)
+        chips = [values[0], values[len(far) + 1]]
+        for mine, other in zip(values[1 : len(far) + 1], values[len(far) + 2 :]):
+            chips += [jnp.where(first, mine, other), jnp.where(first, other, mine)]
+        padded = []
+        for chip in chips:
+            chip = chip.astype(F32) if small else chip
+            padded += [unpack_rests(chip, r * len(bins)) for r in range(reps)]
+        padded = jnp.concatenate(padded, axis=0)
         unused = [jnp.zeros((span - block_rows, holders * listed), BF16)]
         unused = unused if span > block_rows else []
         sources = []
@@ -466,7 +464,7 @@
 
     edges, influence = on_core(
         finish,
-        [placing, mask, squeeze, target_slots] + shards + others,
+        [placing, mask, squeeze, target_slots, columns] + far + [near] + across,
         [shape(1, result_rows, slots, dtype=BF16), shape(1, result_rows, panel)],
         small,
     )

time: 57.4 us -> 58 us (1.010)
  waiting for transfers between devices: 17 us -> 19.8 us
  starting transfers between devices: 14.9 us -> 12.6 us
    ppermute x3 -> x2, waiting for transfers between devices: 4.39 us -> 7 us  [the longest x1 7 us: per_device(): far.append(lax.ppermute(columns, ('feat', 'rep'), pairs))]
    ppermute x3 -> x2, starting transfers between devices: 4.62 us -> 2.34 us  [the longest x1 1.65 us: per_device(): far.append(lax.ppermute(columns, ('feat', 'rep'), pairs))]
    ppermute x9 -> x6, waiting for transfers between devices: 4.87 us -> 5.1 us  [rotate(): lax.ppermute(x, axis, [(i, (i + step) % count) for i in range(count)])]
    ppermute x9 -> x6, starting transfers between devices: 5.33 us -> 5.32 us  [rotate(): lax.ppermute(x, axis, [(i, (i + step) % count) for i in range(count)])]
  transfers between devices with their start and end apart: 18 -> 14, of which waited for: 12 -> 9; matrix products, arithmetic and copies ran while one was open for 2% -> 2% of each run, Pallas kernels for 6% -> 5%
where the time goes in v16:
time: 58 us; the launch traced here: 57.7 us
  waiting for transfers between devices  19.8 us (34%)
  blocking collectives  14.1 us (24%)
  starting transfers between devices  12.6 us (22%)
  Pallas kernels  8.95 us (15%)
  matrix products  0.8 us (1%)
  between operations  0.76 us (1%)
  local copies, waits for them, and re-layouts  0.69 us (1%)
    all_to_all x1, blocking collectives, per_device(): lax.all_to_all(packed, ('feat', 'pos'), split_axis=0, concat_axis=0, tile...  14.1 us
    pallas_call x7, Pallas kernels, on_core(): return list(call(*args, *streams, *through))  8.95 us
    ppermute x1, waiting for transfers between devices, per_device(): far.append(lax.ppermute(columns, ('feat', 'rep'), pairs))  7 us
    ppermute x6, starting transfers between devices, rotate(): lax.ppermute(x, axis, [(i, (i + step) % count) for i in range(count)])  5.32 us
    ppermute x6, waiting for transfers between devices, rotate(): lax.ppermute(x, axis, [(i, (i + step) % count) for i in range(count)])  5.1 us
    ppermute x4, waiting for transfers between devices, ring_next(): return lax.ppermute(x, axis, steps)  3.97 us
    ppermute x2, waiting for transfers between devices, ring_next(): return lax.ppermute(x, (axis, across), pairs)  3.73 us
    ppermute x4, starting transfers between devices, ring_next(): return lax.ppermute(x, axis, steps)  3.62 us
  transfers between devices with their start and end apart: 14, of which 9 were waited for; matrix products, arithmetic and copies ran while one was open for 2% of the time, Pallas kernels for 5%

profile of v16, /device:TPU:0, one launch (start us, length us, event | category | flops | bytes accessed | tf_op | source)
XLA Modules:
  0.0 57.7 jit_solution(3349943554830937128)
XLA Ops:
  0.6 1.5 %shard_map.77 = f32[8,8,128]{2,1,0:T(8,128)} custom-call(s32[1,4,28]{2,1,0:T(4,128)} %refs_0_.1, f32[1,4,28]{2,1,0:T(4,128)} %refs_1_.3), custom_call_target="tpu_custom_call" | custom-call | tf_op jit(solution)/shard_map/pallas_call | solution.py:84
  2.1 14.1 %all_to_all.5.refs_0_ = f32[8,8,128]{2,1,0:T(8,128)S(1)} all-to-all(f32[8,8,128]{2,1,0:T(8,128)} %shard_map.77), channel_id=1, replica_groups=mesh['grp'=2,'feat'=4,'pos'=2,'rep'=2] {'feat','pos'}, dimensions={0} | all-to-all | bytes 65536 | tf_op jit(solution)/shard_map/all_to_all | solution.py:187
  17.7 0.7 %collective-permute-start.1 = (bf16[80,1152]{1,0:T(8,128)(2,1)S(1)}, bf16[80,1152]{1,0:T(8,128)(2,1)S(1)}, u32[]{:S(2)}, u32[]{:S(2)}) collective-permute-start(bf16[80,1152]{1,0:T(8,128)(2,1)S(1)} %get-tuple-element.28), channel_id=1, source_target_pairs={{0,10},{2,8},{8,14},{10,12},{12,6},{14,4},{4,2},{6,0},{1,11},{3,9}... | collective-permute-start | bytes 552968 | tf_op jit(solution)/shard_map/ppermute | solution.py:105
  18.4 0.8 %fusion = bf16[3,160,1152]{2,1,0:T(8,128)(2,1)S(1)} fusion(bf16[512,3,1152]{2,0,1:T(8,128)(2,1)S(1)} %copy-done, bf16[160,512]{1,0:T(8,128)(2,1)S(1)} %get-tuple-element.20), kind=kOutput, calls=%fused_computation.1 | convolution fusion | flops 566784000 | bytes 4808704 | tf_op jit(solution)/shard_map/dot_general | solution.py:277
  19.9 1.9 %shard_map.80 = (bf16[448,640]{1,0:T(8,128)(2,1)S(1)}, bf16[640,512]{1,0:T(8,128)(2,1)S(1)}, f32[1,640]{1,0:T(1,128)S(1)}, f32[480,1]{1,0:T(8,128)S(1)}, bf16[51...) custom-call(f32[32,28]{1,0:T(8,128)S(1)} %get-tuple-element.18.refs_, ...), custom_call_target="tpu_custom_call", output_to_operand_aliasing={{6}: (2, {}), {7}: (3, {}), {8}: (4, {})} | custom-call | flops 1 | bytes 1 | tf_op jit(solution)/shard_map/pallas_call | solution.py:84
  21.8 1.4 %collective-permute-start.4 = (bf16[80,1152]{1,0:T(8,128)(2,1)S(1)}, bf16[80,1152]{1,0:T(8,128)(2,1)S(1)}, u32[]{:S(2)}, u32[]{:S(2)}) collective-permute-start(bf16[80,1152]{1,0:T(8,128)(2,1)S(1)} %get-tuple-element.29), channel_id=1, source_target_pairs={{0,2},{2,0},{1,3},{3,1},{4,6},{6,4},{5,7},{7,5},{8,10},{10,8},{9,1... | collective-permute-start | bytes 552968 | tf_op jit(solution)/shard_map/ppermute | solution.py:89
  23.2 1.4 %collective-permute-done.refs_4_ = bf16[80,1152]{1,0:T(8,128)(2,1)S(1)} collective-permute-done((bf16[80,1152]{1,0:T(8,128)(2,1)S(1)}, bf16[80,1152]{1,0:T(8,128)(2,1)S(1)}, u32[]{:S(2)}, u32[]{:S(2)}) %collective-permute-start) | collective-permute-done | bytes 184352 | tf_op jit(solution)/shard_map/ppermute | solution.py:105
  24.6 1.2 %collective-permute-start.2 = (bf16[80,1152]{1,0:T(8,128)(2,1)S(1)}, bf16[80,1152]{1,0:T(8,128)(2,1)S(1)}, u32[]{:S(2)}, u32[]{:S(2)}) collective-permute-start(bf16[80,1152]{1,0:T(8,128)(2,1)S(1)} %collective-permute-done.refs_4_), channel_id=1, source_target_pairs={{0,8},{8,12},{12,4},{4,0},{1,9},{9,13},{13,5},{5,1},{2,10},{10,14}... | collective-permute-start | bytes 552968 | tf_op jit(solution)/shard_map/ppermute | solution.py:102
  25.8 2.3 %collective-permute-done.1.refs_5_ = bf16[80,1152]{1,0:T(8,128)(2,1)S(1)} collective-permute-done((bf16[80,1152]{1,0:T(8,128)(2,1)S(1)}, bf16[80,1152]{1,0:T(8,128)(2,1)S(1)}, u32[]{:S(2)}, u32[]{:S(2)}) %collective-permute-start.1) | collective-permute-done | bytes 184352 | tf_op jit(solution)/shard_map/ppermute | solution.py:105
  28.7 1.8 %collective-permute-start.5 = (bf16[80,1152]{1,0:T(8,128)(2,1)S(1)}, bf16[80,1152]{1,0:T(8,128)(2,1)S(1)}, u32[]{:S(2)}, u32[]{:S(2)}) collective-permute-start(bf16[80,1152]{1,0:T(8,128)(2,1)S(1)} %get-tuple-element.30), channel_id=1, source_target_pairs={{0,2},{2,0},{1,3},{3,1},{4,6},{6,4},{5,7},{7,5},{8,10},{10,8},{9,1... | collective-permute-start | bytes 552968 | tf_op jit(solution)/shard_map/ppermute | solution.py:89
  30.7 1.8 %collective-permute-start.7 = (bf16[80,1152]{1,0:T(8,128)(2,1)S(1)}, bf16[80,1152]{1,0:T(8,128)(2,1)S(1)}, u32[]{:S(2)}, u32[]{:S(2)}) collective-permute-start(bf16[80,1152]{1,0:T(8,128)(2,1)S(1)} %get-tuple-element.28), channel_id=1, source_target_pairs={{0,2},{2,0},{1,3},{3,1},{4,6},{6,4},{5,7},{7,5},{8,10},{10,8},{9,1... | collective-permute-start | bytes 552968 | tf_op jit(solution)/shard_map/ppermute | solution.py:89
  32.6 1.2 %collective-permute-start.8 = (bf16[80,1152]{1,0:T(8,128)(2,1)S(1)}, bf16[80,1152]{1,0:T(8,128)(2,1)S(1)}, u32[]{:S(2)}, u32[]{:S(2)}) collective-permute-start(bf16[80,1152]{1,0:T(8,128)(2,1)S(1)} %collective-permute-done.2.refs_6_), channel_id=1, source_target_pairs={{0,8},{8,12},{12,4},{4,0},{1,9},{9,13},{13,5},{5,1},{2,10},{10,14}... | collective-permute-start | bytes 552968 | tf_op jit(solution)/shard_map/ppermute | solution.py:102
  33.8 2.7 %collective-permute-done.3.refs_7_ = bf16[80,1152]{1,0:T(8,128)(2,1)S(1)} collective-permute-done((bf16[80,1152]{1,0:T(8,128)(2,1)S(1)}, bf16[80,1152]{1,0:T(8,128)(2,1)S(1)}, u32[]{:S(2)}, u32[]{:S(2)}) %collective-permute-start.3) | collective-permute-done | bytes 184352 | tf_op jit(solution)/shard_map/ppermute | solution.py:102
  37.1 1.6 %collective-permute-done.6.refs_13_ = bf16[80,1152]{1,0:T(8,128)(2,1)S(1)} collective-permute-done((bf16[80,1152]{1,0:T(8,128)(2,1)S(1)}, bf16[80,1152]{1,0:T(8,128)(2,1)S(1)}, u32[]{:S(2)}, u32[]{:S(2)}) %collective-permute-start.6) | collective-permute-done | bytes 184352 | tf_op jit(solution)/shard_map/ppermute | solution.py:89
  38.8 1.3 %shard_map.81 = (f32[160,512]{1,0:T(8,128)S(1)}, bf16[480,1152]{1,0:T(8,128)(2,1)S(1)}) custom-call(f32[1,640]{1,0:T(1,128)S(1)} %get-tuple-element.24.refs_0_, bf16[640,512]{1,0:T(8,128)(2,1)S(1)} %get-tuple-element.25.refs_1_, f32[480,1]{1,0:T(8,128)S(1)} %get-tuple-element.26.refs_2_, bf16[80,1152]{1,0:T(8,128)(2,1)S(1)} %get-tuple-element.27.refs_3_, ...), custom_call_target="tpu_custom_call" | custom-call | flops 1 | bytes 1 | tf_op jit(solution)/shard_map/pallas_call | solution.py:84
  40.1 0.7 %collective-permute-done.7.refs_4_ = bf16[80,1152]{1,0:T(8,128)(2,1)S(1)} collective-permute-done((bf16[80,1152]{1,0:T(8,128)(2,1)S(1)}, bf16[80,1152]{1,0:T(8,128)(2,1)S(1)}, u32[]{:S(2)}, u32[]{:S(2)}) %collective-permute-start.7) | collective-permute-done | bytes 184352 | tf_op jit(solution)/shard_map/ppermute | solution.py:89
  40.8 1.3 %collective-permute-done.9.refs_6_ = bf16[80,1152]{1,0:T(8,128)(2,1)S(1)} collective-permute-done((bf16[80,1152]{1,0:T(8,128)(2,1)S(1)}, bf16[80,1152]{1,0:T(8,128)(2,1)S(1)}, u32[]{:S(2)}, u32[]{:S(2)}) %collective-permute-start.9) | collective-permute-done | bytes 184352 | tf_op jit(solution)/shard_map/ppermute | solution.py:102
  42.0 1.0 %shard_map.82 = f32[112,512]{1,0:T(8,128)S(1)} custom-call(f32[1,640]{1,0:T(1,128)S(1)} %get-tuple-element.24.refs_0_, bf16[640,512]{1,0:T(8,128)(2,1)S(1)} %get-tuple-element.25.refs_1_, f32[160,512]{1,0:T(8,128)S(1)} %get-tuple-element.32.refs_2_, bf16[480,1152]{1,0:T(8,128)(2,1)S(1)} %get-tuple-element.33.refs_3_, ...), custom_call_target="tpu_custom_call" | custom-call | tf_op jit(solution)/shard_map/pallas_call | solution.py:84
  43.1 1.5 %collective-permute-done.10 = f32[112,512]{1,0:T(8,128)S(1)} collective-permute-done((f32[112,512]{1,0:T(8,128)S(1)}, f32[112,512]{1,0:T(8,128)S(1)}, u32[]{:S(2)}, u32[]{:S(2)}) %collective-permute-start.10) | collective-permute-done | bytes 229408 | tf_op jit(solution)/shard_map/ppermute | solution.py:89
  44.6 1.6 %collective-permute-start.11 = (bf16[112,512]{1,0:T(8,128)(2,1)S(1)}, bf16[112,512]{1,0:T(8,128)(2,1)S(1)}, u32[]{:S(2)}, u32[]{:S(2)}) collective-permute-start(bf16[112,512]{1,0:T(8,128)(2,1)S(1)} %add_convert_fusion.refs_4_), channel_id=1, source_target_pairs={{0,8},{1,13},{4,12},{5,9},{8,0},{9,5},{12,4},{13,1},{2,10},{3,15},... | collective-permute-start | bytes 344072 | tf_op jit(solution)/shard_map/ppermute | solution.py:415
  46.2 0.7 %collective-permute-start.12 = (bf16[112,512]{1,0:T(8,128)(2,1)S(1)}, bf16[112,512]{1,0:T(8,128)(2,1)S(1)}, u32[]{:S(2)}, u32[]{:S(2)}) collective-permute-start(bf16[112,512]{1,0:T(8,128)(2,1)S(1)} %add_convert_fusion.refs_4_), channel_id=1, source_target_pairs={{0,4},{4,0},{8,12},{12,8},{1,5},{5,1},{9,13},{13,9},{2,6},{6,2},{1... | collective-permute-start | bytes 344072 | tf_op jit(solution)/shard_map/ppermute | solution.py:416
  46.9 7.0 %collective-permute-done.11.refs_5_ = bf16[112,512]{1,0:T(8,128)(2,1)S(1)} collective-permute-done((bf16[112,512]{1,0:T(8,128)(2,1)S(1)}, bf16[112,512]{1,0:T(8,128)(2,1)S(1)}, u32[]{:S(2)}, u32[]{:S(2)}) %collective-permute-start.11) | collective-permute-done | bytes 114720 | tf_op jit(solution)/shard_map/ppermute | solution.py:415
  53.9 1.3 %collective-permute-done.13.refs_7_ = bf16[112,512]{1,0:T(8,128)(2,1)S(1)} collective-permute-done((bf16[112,512]{1,0:T(8,128)(2,1)S(1)}, bf16[112,512]{1,0:T(8,128)(2,1)S(1)}, u32[]{:S(2)}, u32[]{:S(2)}) %collective-permute-start.13) | collective-permute-done | bytes 114720 | tf_op jit(solution)/shard_map/ppermute | solution.py:89
  55.2 2.5 %shard_map.83 = (bf16[1,56,448]{2,1,0:T(8,128)(2,1)}, f32[1,56,128]{2,1,0:T(8,128)}) custom-call(bf16[448,640]{1,0:T(8,128)(2,1)S(1)} %get-tuple-element.21.refs_0_, bf16[512,512]{1,0:T(8,128)(2,1)S(1)} %get-tuple-element.22.refs_1_, bf16[512,448]{1,0:T(8,128)(2,1)S(1)} %get-tuple-element.23.refs_2_, s32[1,128]{1,0:T(1,128)S(1)} %copy-done.3, ...), custom_call_target="tpu_custom_call" | custom-call | tf_op jit(solution)/shard_map/pallas_call | solution.py:84
  (23 shorter events, 3.7 us)
Async XLA Ops:
  0.6 17.8 %copy-start = (bf16[512,3,1152]{2,0,1:T(8,128)(2,1)S(1)}, bf16[512,3,1152]{2,0,1:T(8,128)(2,1)}, u32[]{:S(2)}) copy-start(bf16[512,3,1152]{2,0,1:T(8,128)(2,1)} %param.11) | copy-start | bytes 10616836
  2.1 14.6 %copy-start.1 = (bf16[512,1152]{1,0:T(8,128)(2,1)S(1)}, bf16[512,1152]{1,0:T(8,128)(2,1)}, u32[]{:S(2)}) copy-start(bf16[512,1152]{1,0:T(8,128)(2,1)} %refs_1_.4) | copy-start | bytes 3538948
  17.1 7.5 %collective-permute-start = (bf16[80,1152]{1,0:T(8,128)(2,1)S(1)}, bf16[80,1152]{1,0:T(8,128)(2,1)S(1)}, u32[]{:S(2)}, u32[]{:S(2)}) collective-permute-start(bf16[80,1152]{1,0:T(8,128)(2,1)S(1)} %get-tuple-element.27.refs_3_), channel_id=1, source_target_pairs={{0,8},{2,10},{8,12},{10,14},{12,4},{14,6},{4,0},{6,2},{1,9},{3,11}... | collective-permute-start | bytes 552968 | tf_op jit(solution)/shard_map/ppermute | solution.py:105
  17.7 10.4 %collective-permute-start.1 = (bf16[80,1152]{1,0:T(8,128)(2,1)S(1)}, bf16[80,1152]{1,0:T(8,128)(2,1)S(1)}, u32[]{:S(2)}, u32[]{:S(2)}) collective-permute-start(bf16[80,1152]{1,0:T(8,128)(2,1)S(1)} %get-tuple-element.28), channel_id=1, source_target_pairs={{0,10},{2,8},{8,14},{10,12},{12,6},{14,4},{4,2},{6,0},{1,11},{3,9}... | collective-permute-start | bytes 552968 | tf_op jit(solution)/shard_map/ppermute | solution.py:105
  19.2 0.7 %copy-start.2 = (s32[1,4,4]{2,1,0:T(4,128)S(1)}, s32[1,4,4]{2,1,0:T(4,128)}, u32[]{:S(2)}) copy-start(s32[1,4,4]{2,1,0:T(4,128)} %refs_1_.5) | copy-start | bytes 196
  21.8 8.9 %collective-permute-start.4 = (bf16[80,1152]{1,0:T(8,128)(2,1)S(1)}, bf16[80,1152]{1,0:T(8,128)(2,1)S(1)}, u32[]{:S(2)}, u32[]{:S(2)}) collective-permute-start(bf16[80,1152]{1,0:T(8,128)(2,1)S(1)} %get-tuple-element.29), channel_id=1, source_target_pairs={{0,2},{2,0},{1,3},{3,1},{4,6},{6,4},{5,7},{7,5},{8,10},{10,8},{9,1... | collective-permute-start | bytes 552968 | tf_op jit(solution)/shard_map/ppermute | solution.py:89
  24.6 8.0 %collective-permute-start.2 = (bf16[80,1152]{1,0:T(8,128)(2,1)S(1)}, bf16[80,1152]{1,0:T(8,128)(2,1)S(1)}, u32[]{:S(2)}, u32[]{:S(2)}) collective-permute-start(bf16[80,1152]{1,0:T(8,128)(2,1)S(1)} %collective-permute-done.refs_4_), channel_id=1, source_target_pairs={{0,8},{8,12},{12,4},{4,0},{1,9},{9,13},{13,5},{5,1},{2,10},{10,14}... | collective-permute-start | bytes 552968 | tf_op jit(solution)/shard_map/ppermute | solution.py:102
  28.1 8.3 %collective-permute-start.3 = (bf16[80,1152]{1,0:T(8,128)(2,1)S(1)}, bf16[80,1152]{1,0:T(8,128)(2,1)S(1)}, u32[]{:S(2)}, u32[]{:S(2)}) collective-permute-start(bf16[80,1152]{1,0:T(8,128)(2,1)S(1)} %collective-permute-done.1.refs_5_), channel_id=1, source_target_pairs={{0,8},{8,12},{12,4},{4,0},{1,9},{9,13},{13,5},{5,1},{2,10},{10,14}... | collective-permute-start | bytes 552968 | tf_op jit(solution)/shard_map/ppermute | solution.py:102
  28.7 8.4 %collective-permute-start.5 = (bf16[80,1152]{1,0:T(8,128)(2,1)S(1)}, bf16[80,1152]{1,0:T(8,128)(2,1)S(1)}, u32[]{:S(2)}, u32[]{:S(2)}) collective-permute-start(bf16[80,1152]{1,0:T(8,128)(2,1)S(1)} %get-tuple-element.30), channel_id=1, source_target_pairs={{0,2},{2,0},{1,3},{3,1},{4,6},{6,4},{5,7},{7,5},{8,10},{10,8},{9,1... | collective-permute-start | bytes 552968 | tf_op jit(solution)/shard_map/ppermute | solution.py:89
  30.5 8.2 %collective-permute-start.6 = (bf16[80,1152]{1,0:T(8,128)(2,1)S(1)}, bf16[80,1152]{1,0:T(8,128)(2,1)S(1)}, u32[]{:S(2)}, u32[]{:S(2)}) collective-permute-start(bf16[80,1152]{1,0:T(8,128)(2,1)S(1)} %get-tuple-element.31), channel_id=1, source_target_pairs={{0,2},{2,0},{1,3},{3,1},{4,6},{6,4},{5,7},{7,5},{8,10},{10,8},{9,1... | collective-permute-start | bytes 552968 | tf_op jit(solution)/shard_map/ppermute | solution.py:89
  30.7 10.0 %collective-permute-start.7 = (bf16[80,1152]{1,0:T(8,128)(2,1)S(1)}, bf16[80,1152]{1,0:T(8,128)(2,1)S(1)}, u32[]{:S(2)}, u32[]{:S(2)}) collective-permute-start(bf16[80,1152]{1,0:T(8,128)(2,1)S(1)} %get-tuple-element.28), channel_id=1, source_target_pairs={{0,2},{2,0},{1,3},{3,1},{4,6},{6,4},{5,7},{7,5},{8,10},{10,8},{9,1... | collective-permute-start | bytes 552968 | tf_op jit(solution)/shard_map/ppermute | solution.py:89
  32.6 8.2 %collective-permute-start.8 = (bf16[80,1152]{1,0:T(8,128)(2,1)S(1)}, bf16[80,1152]{1,0:T(8,128)(2,1)S(1)}, u32[]{:S(2)}, u32[]{:S(2)}) collective-permute-start(bf16[80,1152]{1,0:T(8,128)(2,1)S(1)} %collective-permute-done.2.refs_6_), channel_id=1, source_target_pairs={{0,8},{8,12},{12,4},{4,0},{1,9},{9,13},{13,5},{5,1},{2,10},{10,14}... | collective-permute-start | bytes 552968 | tf_op jit(solution)/shard_map/ppermute | solution.py:102
  36.5 5.5 %collective-permute-start.9 = (bf16[80,1152]{1,0:T(8,128)(2,1)S(1)}, bf16[80,1152]{1,0:T(8,128)(2,1)S(1)}, u32[]{:S(2)}, u32[]{:S(2)}) collective-permute-start(bf16[80,1152]{1,0:T(8,128)(2,1)S(1)} %collective-permute-done.3.refs_7_), channel_id=1, source_target_pairs={{0,8},{8,12},{12,4},{4,0},{1,9},{9,13},{13,5},{5,1},{2,10},{10,14}... | collective-permute-start | bytes 552968 | tf_op jit(solution)/shard_map/ppermute | solution.py:102
  40.1 15.2 %copy-start.3 = (s32[1,128]{1,0:T(1,128)S(1)}, s32[1,128]{1,0:T(1,128)}, u32[]{:S(2)}) copy-start(s32[1,128]{1,0:T(1,128)} %refs_3_.1) | copy-start | bytes 1540
  43.0 1.6 %collective-permute-start.10 = (f32[112,512]{1,0:T(8,128)S(1)}, f32[112,512]{1,0:T(8,128)S(1)}, u32[]{:S(2)}, u32[]{:S(2)}) collective-permute-start(f32[112,512]{1,0:T(8,128)S(1)} %shard_map.82), channel_id=1, source_target_pairs={{0,1},{1,0},{2,3},{3,2},{4,5},{5,4},{6,7},{7,6},{8,9},{9,8},{10,11... | collective-permute-start | bytes 688136 | tf_op jit(solution)/shard_map/ppermute | solution.py:89
  44.6 9.3 %collective-permute-start.11 = (bf16[112,512]{1,0:T(8,128)(2,1)S(1)}, bf16[112,512]{1,0:T(8,128)(2,1)S(1)}, u32[]{:S(2)}, u32[]{:S(2)}) collective-permute-start(bf16[112,512]{1,0:T(8,128)(2,1)S(1)} %add_convert_fusion.refs_4_), channel_id=1, source_target_pairs={{0,8},{1,13},{4,12},{5,9},{8,0},{9,5},{12,4},{13,1},{2,10},{3,15},... | collective-permute-start | bytes 344072 | tf_op jit(solution)/shard_map/ppermute | solution.py:415
  46.2 7.7 %collective-permute-start.12 = (bf16[112,512]{1,0:T(8,128)(2,1)S(1)}, bf16[112,512]{1,0:T(8,128)(2,1)S(1)}, u32[]{:S(2)}, u32[]{:S(2)}) collective-permute-start(bf16[112,512]{1,0:T(8,128)(2,1)S(1)} %add_convert_fusion.refs_4_), channel_id=1, source_target_pairs={{0,4},{4,0},{8,12},{12,8},{1,5},{5,1},{9,13},{13,9},{2,6},{6,2},{1... | collective-permute-start | bytes 344072 | tf_op jit(solution)/shard_map/ppermute | solution.py:416
  53.9 1.3 %collective-permute-start.13 = (bf16[112,512]{1,0:T(8,128)(2,1)S(1)}, bf16[112,512]{1,0:T(8,128)(2,1)S(1)}, u32[]{:S(2)}, u32[]{:S(2)}) collective-permute-start(bf16[112,512]{1,0:T(8,128)(2,1)S(1)} %collective-permute-done.11.refs_5_), channel_id=1, source_target_pairs={{0,1},{1,0},{2,3},{3,2},{4,5},{5,4},{6,7},{7,6},{8,9},{9,8},{10,11... | collective-permute-start | bytes 344072 | tf_op jit(solution)/shard_map/ppermute | solution.py:89

commit v17 on v16

--- a/solution.py
+++ b/solution.py
@@ -413,15 +413,18 @@
             (f * reps + r, (f ^ (bits + r)) * reps + r) for f in range(feats) for r in range(reps)
         ]
         far.append(lax.ppermute(columns, ("feat", "rep"), pairs))
-    near = lax.ppermute(columns, "feat", [(f, f ^ 1) for f in range(feats)])
-    across = [rotate(shard, "rep", 1) for shard in far]
+    rows = len(bins) * GROUP
+    own_half = jnp.where(lax.axis_index("rep") == 0, columns[:rows], columns[rows:])
+    near = lax.ppermute(own_half, "feat", [(f, f ^ 1) for f in range(feats)])
+    across = [rotate(shard, "rep", 1) for shard in far + [near]]
 
     def finish(placing, mask, squeeze, targets, *values):
         feat, _, rep = place()
         first = rep == 0.0
-        chips = [values[0], values[len(far) + 1]]
-        for mine, other in zip(values[1 : len(far) + 1], values[len(far) + 2 :]):
+        chips = []
+        for mine, other in zip(values[1 : len(far) + 2], values[len(far) + 2 :]):
             chips += [jnp.where(first, mine, other), jnp.where(first, other, mine)]
+        chips = [values[0], jnp.concatenate(chips[-reps:], axis=0)] + chips[:-reps]
         padded = []
         for chip in chips:
             chip = chip.astype(F32) if small else chip

time: 58 us -> 63.6 us (1.097)
  waiting for transfers between devices: 19.8 us -> 10.2 us
  starting transfers between devices: 12.6 us -> 20.5 us
  local copies, waits for them, and re-layouts: 0.69 us -> 6.27 us
  other arithmetic: 0.04 us -> 1.09 us
  Pallas kernels: 8.95 us -> 9.65 us
    ppermute x4, starting transfers between devices: 3.62 us -> 9.39 us  [ring_next(): return lax.ppermute(x, axis, steps)]
    unnamed x8 -> x20, local copies, waits for them, and re-layouts: 0.6 us -> 6.18 us
    ppermute x2, waiting for transfers between devices: 3.73 us -> 0.01 us  [ring_next(): return lax.ppermute(x, (axis, across), pairs)]
    ppermute x4, waiting for transfers between devices: 3.97 us -> 0.7 us  [ring_next(): return lax.ppermute(x, axis, steps)]
    ppermute x1, starting transfers between devices: 1.65 us -> 3.45 us  [per_device(): far.append(lax.ppermute(columns, ('feat', 'rep'), pairs))]
    ppermute x1, waiting for transfers between devices: 7 us -> 5.33 us  [per_device(): far.append(lax.ppermute(columns, ('feat', 'rep'), pairs))]
    convert_element_type x1, other arithmetic: 0.04 us -> 1.08 us  [per_device(): columns = (partial + rotate(partial, 'rep', 1)).astype(BF16)]
    ppermute x6 -> x7, waiting for transfers between devices: 5.1 us -> 4.14 us  [rotate(): lax.ppermute(x, axis, [(i, (i + step) % count) for i in range(count)])]
  transfers between devices with their start and end apart: 14 -> 15, of which waited for: 9 -> 7; matrix products, arithmetic and copies ran while one was open for 2% -> 1% of each run, Pallas kernels for 5% -> 5%
where the time goes in v17:
time: 63.6 us; the launch traced here: 63.2 us
  starting transfers between devices  20.5 us (32%)
  blocking collectives  14.1 us (22%)
  waiting for transfers between devices  10.2 us (16%)
  Pallas kernels  9.65 us (15%)
  local copies, waits for them, and re-layouts  6.27 us (10%)
  other arithmetic  1.09 us (2%)
  matrix products  0.77 us (1%)
  between operations  0.76 us (1%)
    all_to_all x1, blocking collectives, per_device(): lax.all_to_all(packed, ('feat', 'pos'), split_axis=0, concat_axis=0, tile...  14.1 us
    pallas_call x7, Pallas kernels, on_core(): return list(call(*args, *streams, *through))  9.65 us
    ppermute x4, starting transfers between devices, ring_next(): return lax.ppermute(x, axis, steps)  9.39 us
    unnamed x20, local copies, waits for them, and re-layouts  6.18 us
    ppermute x7, starting transfers between devices, rotate(): lax.ppermute(x, axis, [(i, (i + step) % count) for i in range(count)])  5.58 us
    ppermute x1, waiting for transfers between devices, per_device(): far.append(lax.ppermute(columns, ('feat', 'rep'), pairs))  5.33 us
    ppermute x7, waiting for transfers between devices, rotate(): lax.ppermute(x, axis, [(i, (i + step) % count) for i in range(count)])  4.14 us
    ppermute x1, starting transfers between devices, per_device(): far.append(lax.ppermute(columns, ('feat', 'rep'), pairs))  3.45 us
  transfers between devices with their start and end apart: 15, of which 7 were waited for; matrix products, arithmetic and copies ran while one was open for 1% of the time, Pallas kernels for 5%

profile of v17, /device:TPU:0, one launch (start us, length us, event | category | flops | bytes accessed | tf_op | source)
XLA Modules:
  0.0 63.2 jit_solution(1061403415000863990)
XLA Ops:
  0.6 1.5 %shard_map.77 = f32[8,8,128]{2,1,0:T(8,128)} custom-call(s32[1,4,28]{2,1,0:T(4,128)} %refs_0_.1, f32[1,4,28]{2,1,0:T(4,128)} %refs_1_.3), custom_call_target="tpu_custom_call" | custom-call | tf_op jit(solution)/shard_map/pallas_call | solution.py:84
  2.1 14.1 %all_to_all.5.refs_0_ = f32[8,8,128]{2,1,0:T(8,128)S(1)} all-to-all(f32[8,8,128]{2,1,0:T(8,128)} %shard_map.77), channel_id=1, replica_groups=mesh['grp'=2,'feat'=4,'pos'=2,'rep'=2] {'feat','pos'}, dimensions={0} | all-to-all | bytes 65536 | tf_op jit(solution)/shard_map/all_to_all | solution.py:187
  19.9 1.9 %shard_map.80 = (bf16[448,640]{1,0:T(8,128)(2,1)S(1)}, bf16[640,512]{1,0:T(8,128)(2,1)S(1)}, f32[1,640]{1,0:T(1,128)S(1)}, f32[480,1]{1,0:T(8,128)S(1)}, bf16[51...) custom-call(f32[32,28]{1,0:T(8,128)S(1)} %get-tuple-element.18.refs_, ...), custom_call_target="tpu_custom_call", output_to_operand_aliasing={{6}: (2, {}), {7}: (3, {}), {8}: (4, {})} | custom-call | flops 1 | bytes 1 | tf_op jit(solution)/shard_map/pallas_call | solution.py:84
  21.8 0.8 %copy-done.2 = bf16[448,640]{1,0:T(8,128)(2,1)} copy-done((bf16[448,640]{1,0:T(8,128)(2,1)}, bf16[448,640]{1,0:T(8,128)(2,1)S(1)}, u32[]{:S(2)}) %copy-start.2) | copy-done | bytes 573464
  22.6 0.8 %copy-done.4 = bf16[512,512]{1,0:T(8,128)(2,1)} copy-done((bf16[512,512]{1,0:T(8,128)(2,1)}, bf16[512,512]{1,0:T(8,128)(2,1)S(1)}, u32[]{:S(2)}) %copy-start.4) | copy-done | bytes 524312
  23.4 0.8 %copy-done.6 = bf16[512,448]{1,0:T(8,128)(2,1)} copy-done((bf16[512,448]{1,0:T(8,128)(2,1)}, bf16[512,448]{1,0:T(8,128)(2,1)S(1)}, u32[]{:S(2)}) %copy-start.6) | copy-done | bytes 458776
  24.2 1.3 %collective-permute-start.4 = (bf16[80,1152]{1,0:T(8,128)(2,1)S(1)}, bf16[80,1152]{1,0:T(8,128)(2,1)S(1)}, u32[]{:S(2)}, u32[]{:S(2)}) collective-permute-start(bf16[80,1152]{1,0:T(8,128)(2,1)S(1)} %get-tuple-element.29), channel_id=1, source_target_pairs={{0,2},{2,0},{1,3},{3,1},{4,6},{6,4},{5,7},{7,5},{8,10},{10,8},{9,1... | collective-permute-start | bytes 552968 | tf_op jit(solution)/shard_map/ppermute | solution.py:89
  25.5 2.2 %collective-permute-start.2 = (bf16[80,1152]{1,0:T(8,128)(2,1)S(1)}, bf16[80,1152]{1,0:T(8,128)(2,1)S(1)}, u32[]{:S(2)}, u32[]{:S(2)}) collective-permute-start(bf16[80,1152]{1,0:T(8,128)(2,1)S(1)} %collective-permute-done.refs_4_), channel_id=1, source_target_pairs={{0,8},{8,12},{12,4},{4,0},{1,9},{9,13},{13,5},{5,1},{2,10},{10,14}... | collective-permute-start | bytes 552968 | tf_op jit(solution)/shard_map/ppermute | solution.py:102
  27.7 1.6 %collective-permute-start.3 = (bf16[80,1152]{1,0:T(8,128)(2,1)S(1)}, bf16[80,1152]{1,0:T(8,128)(2,1)S(1)}, u32[]{:S(2)}, u32[]{:S(2)}) collective-permute-start(bf16[80,1152]{1,0:T(8,128)(2,1)S(1)} %collective-permute-done.1.refs_5_), channel_id=1, source_target_pairs={{0,8},{8,12},{12,4},{4,0},{1,9},{9,13},{13,5},{5,1},{2,10},{10,14}... | collective-permute-start | bytes 552968 | tf_op jit(solution)/shard_map/ppermute | solution.py:102
  29.8 1.6 %collective-permute-start.6 = (bf16[80,1152]{1,0:T(8,128)(2,1)S(1)}, bf16[80,1152]{1,0:T(8,128)(2,1)S(1)}, u32[]{:S(2)}, u32[]{:S(2)}) collective-permute-start(bf16[80,1152]{1,0:T(8,128)(2,1)S(1)} %get-tuple-element.31), channel_id=1, source_target_pairs={{0,2},{2,0},{1,3},{3,1},{4,6},{6,4},{5,7},{7,5},{8,10},{10,8},{9,1... | collective-permute-start | bytes 552968 | tf_op jit(solution)/shard_map/ppermute | solution.py:89
  31.4 1.7 %collective-permute-start.7 = (bf16[80,1152]{1,0:T(8,128)(2,1)S(1)}, bf16[80,1152]{1,0:T(8,128)(2,1)S(1)}, u32[]{:S(2)}, u32[]{:S(2)}) collective-permute-start(bf16[80,1152]{1,0:T(8,128)(2,1)S(1)} %get-tuple-element.28), channel_id=1, source_target_pairs={{0,2},{2,0},{1,3},{3,1},{4,6},{6,4},{5,7},{7,5},{8,10},{10,8},{9,1... | collective-permute-start | bytes 552968 | tf_op jit(solution)/shard_map/ppermute | solution.py:89
  33.1 2.2 %collective-permute-start.8 = (bf16[80,1152]{1,0:T(8,128)(2,1)S(1)}, bf16[80,1152]{1,0:T(8,128)(2,1)S(1)}, u32[]{:S(2)}, u32[]{:S(2)}) collective-permute-start(bf16[80,1152]{1,0:T(8,128)(2,1)S(1)} %collective-permute-done.2.refs_6_), channel_id=1, source_target_pairs={{0,8},{8,12},{12,4},{4,0},{1,9},{9,13},{13,5},{5,1},{2,10},{10,14}... | collective-permute-start | bytes 552968 | tf_op jit(solution)/shard_map/ppermute | solution.py:102
  35.7 3.4 %collective-permute-start.9 = (bf16[80,1152]{1,0:T(8,128)(2,1)S(1)}, bf16[80,1152]{1,0:T(8,128)(2,1)S(1)}, u32[]{:S(2)}, u32[]{:S(2)}) collective-permute-start(bf16[80,1152]{1,0:T(8,128)(2,1)S(1)} %collective-permute-done.3.refs_7_), channel_id=1, source_target_pairs={{0,8},{8,12},{12,4},{4,0},{1,9},{9,13},{13,5},{5,1},{2,10},{10,14}... | collective-permute-start | bytes 552968 | tf_op jit(solution)/shard_map/ppermute | solution.py:102
  39.8 1.3 %shard_map.81 = (f32[160,512]{1,0:T(8,128)S(1)}, bf16[480,1152]{1,0:T(8,128)(2,1)S(1)}) custom-call(f32[1,640]{1,0:T(1,128)S(1)} %get-tuple-element.24.refs_0_, bf16[640,512]{1,0:T(8,128)(2,1)S(1)} %get-tuple-element.25.refs_1_, f32[480,1]{1,0:T(8,128)S(1)} %get-tuple-element.26.refs_2_, bf16[80,1152]{1,0:T(8,128)(2,1)S(1)} %get-tuple-element.27.refs_3_, ...), custom_call_target="tpu_custom_call" | custom-call | flops 1 | bytes 1 | tf_op jit(solution)/shard_map/pallas_call | solution.py:84
  42.1 1.7 %shard_map.82 = f32[112,512]{1,0:T(8,128)} custom-call(f32[1,640]{1,0:T(1,128)S(1)} %get-tuple-element.24.refs_0_, bf16[640,512]{1,0:T(8,128)(2,1)S(1)} %get-tuple-element.25.refs_1_, f32[160,512]{1,0:T(8,128)S(1)} %get-tuple-element.32.refs_2_, bf16[480,1152]{1,0:T(8,128)(2,1)S(1)} %get-tuple-element.33.refs_3_, ...), custom_call_target="tpu_custom_call" | custom-call | tf_op jit(solution)/shard_map/pallas_call | solution.py:84
  43.8 1.8 %collective-permute-done.10 = f32[112,512]{1,0:T(8,128)} collective-permute-done((f32[112,512]{1,0:T(8,128)}, f32[112,512]{1,0:T(8,128)}, u32[]{:S(2)}, u32[]{:S(2)}) %collective-permute-start.10) | collective-permute-done | bytes 229408 | tf_op jit(solution)/shard_map/ppermute | solution.py:89
  45.6 1.1 %add_convert_fusion.refs_4_ = bf16[112,512]{1,0:T(8,128)(2,1)S(1)} fusion(f32[112,512]{1,0:T(8,128)} %shard_map.82, f32[112,512]{1,0:T(8,128)} %collective-permute-done.10), kind=kLoop, calls=%fused_computation.2 | loop fusion | flops 114688 | bytes 573440 | tf_op jit(solution)/shard_map/convert_element_type | solution.py:408
  46.7 3.4 %collective-permute-start.11 = (bf16[112,512]{1,0:T(8,128)(2,1)S(1)}, bf16[112,512]{1,0:T(8,128)(2,1)S(1)}, u32[]{:S(2)}, u32[]{:S(2)}) collective-permute-start(bf16[112,512]{1,0:T(8,128)(2,1)S(1)} %add_convert_fusion.refs_4_), channel_id=1, source_target_pairs={{0,8},{1,13},{4,12},{5,9},{8,0},{9,5},{12,4},{13,1},{2,10},{3,15},... | collective-permute-start | bytes 344072 | tf_op jit(solution)/shard_map/ppermute | solution.py:415
  50.9 5.3 %collective-permute-done.11.refs_5_ = bf16[112,512]{1,0:T(8,128)(2,1)S(1)} collective-permute-done((bf16[112,512]{1,0:T(8,128)(2,1)S(1)}, bf16[112,512]{1,0:T(8,128)(2,1)S(1)}, u32[]{:S(2)}, u32[]{:S(2)}) %collective-permute-start.11) | collective-permute-done | bytes 114720 | tf_op jit(solution)/shard_map/ppermute | solution.py:415
  56.7 0.9 %collective-permute-done.14.refs_8_ = bf16[56,512]{1,0:T(8,128)(2,1)S(1)} collective-permute-done((bf16[56,512]{1,0:T(8,128)(2,1)S(1)}, bf16[56,512]{1,0:T(8,128)(2,1)S(1)}, u32[]{:S(2)}, u32[]{:S(2)}) %collective-permute-start.14) | collective-permute-done | bytes 57376 | tf_op jit(solution)/shard_map/ppermute | solution.py:89
  57.6 1.1 %copy-done.3 = bf16[448,640]{1,0:T(8,128)(2,1)S(1)} copy-done((bf16[448,640]{1,0:T(8,128)(2,1)S(1)}, bf16[448,640]{1,0:T(8,128)(2,1)}, u32[]{:S(2)}) %copy-start.3) | copy-done | bytes 573464
  58.7 1.0 %copy-done.5 = bf16[512,512]{1,0:T(8,128)(2,1)S(1)} copy-done((bf16[512,512]{1,0:T(8,128)(2,1)S(1)}, bf16[512,512]{1,0:T(8,128)(2,1)}, u32[]{:S(2)}) %copy-start.5) | copy-done | bytes 524312
  59.7 1.0 %copy-done.7 = bf16[512,448]{1,0:T(8,128)(2,1)S(1)} copy-done((bf16[512,448]{1,0:T(8,128)(2,1)S(1)}, bf16[512,448]{1,0:T(8,128)(2,1)}, u32[]{:S(2)}) %copy-start.7) | copy-done | bytes 458776
  60.8 2.5 %shard_map.83 = (bf16[1,56,448]{2,1,0:T(8,128)(2,1)}, f32[1,56,128]{2,1,0:T(8,128)}) custom-call(bf16[448,640]{1,0:T(8,128)(2,1)S(1)} %copy-done.3, bf16[512,512]{1,0:T(8,128)(2,1)S(1)} %copy-done.5, bf16[512,448]{1,0:T(8,128)(2,1)S(1)} %copy-done.7, s32[1,128]{1,0:T(1,128)S(1)} %copy-done.9, bf16[112,512]{1,0:T(8,128)(2,1)S(1)} %add_convert_fusion.refs_4_, ...), custom_call_target="tpu_custom_call" | custom-call | tf_op jit(solution)/shard_map/pallas_call | solution.py:84
  (38 shorter events, 7.5 us)
Async XLA Ops:
  0.6 17.8 %copy-start = (bf16[512,3,1152]{2,0,1:T(8,128)(2,1)S(1)}, bf16[512,3,1152]{2,0,1:T(8,128)(2,1)}, u32[]{:S(2)}) copy-start(bf16[512,3,1152]{2,0,1:T(8,128)(2,1)} %param.11) | copy-start | bytes 10616836
  2.1 14.6 %copy-start.1 = (bf16[512,1152]{1,0:T(8,128)(2,1)S(1)}, bf16[512,1152]{1,0:T(8,128)(2,1)}, u32[]{:S(2)}) copy-start(bf16[512,1152]{1,0:T(8,128)(2,1)} %refs_1_.4) | copy-start | bytes 3538948
  17.1 8.4 %collective-permute-start = (bf16[80,1152]{1,0:T(8,128)(2,1)S(1)}, bf16[80,1152]{1,0:T(8,128)(2,1)S(1)}, u32[]{:S(2)}, u32[]{:S(2)}) collective-permute-start(bf16[80,1152]{1,0:T(8,128)(2,1)S(1)} %get-tuple-element.27.refs_3_), channel_id=1, source_target_pairs={{0,8},{2,10},{8,12},{10,14},{12,4},{14,6},{4,0},{6,2},{1,9},{3,11}... | collective-permute-start | bytes 552968 | tf_op jit(solution)/shard_map/ppermute | solution.py:105
  17.7 10.0 %collective-permute-start.1 = (bf16[80,1152]{1,0:T(8,128)(2,1)S(1)}, bf16[80,1152]{1,0:T(8,128)(2,1)S(1)}, u32[]{:S(2)}, u32[]{:S(2)}) collective-permute-start(bf16[80,1152]{1,0:T(8,128)(2,1)S(1)} %get-tuple-element.28), channel_id=1, source_target_pairs={{0,10},{2,8},{8,14},{10,12},{12,6},{14,4},{4,2},{6,0},{1,11},{3,9}... | collective-permute-start | bytes 552968 | tf_op jit(solution)/shard_map/ppermute | solution.py:105
  21.8 0.8 %copy-start.2 = (bf16[448,640]{1,0:T(8,128)(2,1)}, bf16[448,640]{1,0:T(8,128)(2,1)S(1)}, u32[]{:S(2)}) copy-start(bf16[448,640]{1,0:T(8,128)(2,1)S(1)} %get-tuple-element.21.refs_0_) | copy-start | bytes 1720324
  22.6 0.8 %copy-start.4 = (bf16[512,512]{1,0:T(8,128)(2,1)}, bf16[512,512]{1,0:T(8,128)(2,1)S(1)}, u32[]{:S(2)}) copy-start(bf16[512,512]{1,0:T(8,128)(2,1)S(1)} %get-tuple-element.22.refs_1_) | copy-start | bytes 1572868
  23.4 0.8 %copy-start.6 = (bf16[512,448]{1,0:T(8,128)(2,1)}, bf16[512,448]{1,0:T(8,128)(2,1)S(1)}, u32[]{:S(2)}) copy-start(bf16[512,448]{1,0:T(8,128)(2,1)S(1)} %get-tuple-element.23.refs_2_) | copy-start | bytes 1376260
  24.2 7.2 %collective-permute-start.4 = (bf16[80,1152]{1,0:T(8,128)(2,1)S(1)}, bf16[80,1152]{1,0:T(8,128)(2,1)S(1)}, u32[]{:S(2)}, u32[]{:S(2)}) collective-permute-start(bf16[80,1152]{1,0:T(8,128)(2,1)S(1)} %get-tuple-element.29), channel_id=1, source_target_pairs={{0,2},{2,0},{1,3},{3,1},{4,6},{6,4},{5,7},{7,5},{8,10},{10,8},{9,1... | collective-permute-start | bytes 552968 | tf_op jit(solution)/shard_map/ppermute | solution.py:89
  25.5 7.6 %collective-permute-start.2 = (bf16[80,1152]{1,0:T(8,128)(2,1)S(1)}, bf16[80,1152]{1,0:T(8,128)(2,1)S(1)}, u32[]{:S(2)}, u32[]{:S(2)}) collective-permute-start(bf16[80,1152]{1,0:T(8,128)(2,1)S(1)} %collective-permute-done.refs_4_), channel_id=1, source_target_pairs={{0,8},{8,12},{12,4},{4,0},{1,9},{9,13},{13,5},{5,1},{2,10},{10,14}... | collective-permute-start | bytes 552968 | tf_op jit(solution)/shard_map/ppermute | solution.py:102
  27.7 7.9 %collective-permute-start.3 = (bf16[80,1152]{1,0:T(8,128)(2,1)S(1)}, bf16[80,1152]{1,0:T(8,128)(2,1)S(1)}, u32[]{:S(2)}, u32[]{:S(2)}) collective-permute-start(bf16[80,1152]{1,0:T(8,128)(2,1)S(1)} %collective-permute-done.1.refs_5_), channel_id=1, source_target_pairs={{0,8},{8,12},{12,4},{4,0},{1,9},{9,13},{13,5},{5,1},{2,10},{10,14}... | collective-permute-start | bytes 552968 | tf_op jit(solution)/shard_map/ppermute | solution.py:102
  29.4 9.7 %collective-permute-start.5 = (bf16[80,1152]{1,0:T(8,128)(2,1)S(1)}, bf16[80,1152]{1,0:T(8,128)(2,1)S(1)}, u32[]{:S(2)}, u32[]{:S(2)}) collective-permute-start(bf16[80,1152]{1,0:T(8,128)(2,1)S(1)} %get-tuple-element.30), channel_id=1, source_target_pairs={{0,2},{2,0},{1,3},{3,1},{4,6},{6,4},{5,7},{7,5},{8,10},{10,8},{9,1... | collective-permute-start | bytes 552968 | tf_op jit(solution)/shard_map/ppermute | solution.py:89
  29.8 10.0 %collective-permute-start.6 = (bf16[80,1152]{1,0:T(8,128)(2,1)S(1)}, bf16[80,1152]{1,0:T(8,128)(2,1)S(1)}, u32[]{:S(2)}, u32[]{:S(2)}) collective-permute-start(bf16[80,1152]{1,0:T(8,128)(2,1)S(1)} %get-tuple-element.31), channel_id=1, source_target_pairs={{0,2},{2,0},{1,3},{3,1},{4,6},{6,4},{5,7},{7,5},{8,10},{10,8},{9,1... | collective-permute-start | bytes 552968 | tf_op jit(solution)/shard_map/ppermute | solution.py:89
  31.4 10.4 %collective-permute-start.7 = (bf16[80,1152]{1,0:T(8,128)(2,1)S(1)}, bf16[80,1152]{1,0:T(8,128)(2,1)S(1)}, u32[]{:S(2)}, u32[]{:S(2)}) collective-permute-start(bf16[80,1152]{1,0:T(8,128)(2,1)S(1)} %get-tuple-element.28), channel_id=1, source_target_pairs={{0,2},{2,0},{1,3},{3,1},{4,6},{6,4},{5,7},{7,5},{8,10},{10,8},{9,1... | collective-permute-start | bytes 552968 | tf_op jit(solution)/shard_map/ppermute | solution.py:89
  33.1 8.7 %collective-permute-start.8 = (bf16[80,1152]{1,0:T(8,128)(2,1)S(1)}, bf16[80,1152]{1,0:T(8,128)(2,1)S(1)}, u32[]{:S(2)}, u32[]{:S(2)}) collective-permute-start(bf16[80,1152]{1,0:T(8,128)(2,1)S(1)} %collective-permute-done.2.refs_6_), channel_id=1, source_target_pairs={{0,8},{8,12},{12,4},{4,0},{1,9},{9,13},{13,5},{5,1},{2,10},{10,14}... | collective-permute-start | bytes 552968 | tf_op jit(solution)/shard_map/ppermute | solution.py:102
  35.7 6.4 %collective-permute-start.9 = (bf16[80,1152]{1,0:T(8,128)(2,1)S(1)}, bf16[80,1152]{1,0:T(8,128)(2,1)S(1)}, u32[]{:S(2)}, u32[]{:S(2)}) collective-permute-start(bf16[80,1152]{1,0:T(8,128)(2,1)S(1)} %collective-permute-done.3.refs_7_), channel_id=1, source_target_pairs={{0,8},{8,12},{12,4},{4,0},{1,9},{9,13},{13,5},{5,1},{2,10},{10,14}... | collective-permute-start | bytes 552968 | tf_op jit(solution)/shard_map/ppermute | solution.py:102
  41.1 16.5 %copy-start.9 = (s32[1,128]{1,0:T(1,128)S(1)}, s32[1,128]{1,0:T(1,128)}, u32[]{:S(2)}) copy-start(s32[1,128]{1,0:T(1,128)} %refs_3_.1) | copy-start | bytes 1540
  43.8 1.8 %collective-permute-start.10 = (f32[112,512]{1,0:T(8,128)}, f32[112,512]{1,0:T(8,128)}, u32[]{:S(2)}, u32[]{:S(2)}) collective-permute-start(f32[112,512]{1,0:T(8,128)} %shard_map.82), channel_id=1, source_target_pairs={{0,1},{1,0},{2,3},{3,2},{4,5},{5,4},{6,7},{7,6},{8,9},{9,8},{10,11... | collective-permute-start | bytes 688136 | tf_op jit(solution)/shard_map/ppermute | solution.py:89
  46.7 9.5 %collective-permute-start.11 = (bf16[112,512]{1,0:T(8,128)(2,1)S(1)}, bf16[112,512]{1,0:T(8,128)(2,1)S(1)}, u32[]{:S(2)}, u32[]{:S(2)}) collective-permute-start(bf16[112,512]{1,0:T(8,128)(2,1)S(1)} %add_convert_fusion.refs_4_), channel_id=1, source_target_pairs={{0,8},{1,13},{4,12},{5,9},{8,0},{9,5},{12,4},{13,1},{2,10},{3,15},... | collective-permute-start | bytes 344072 | tf_op jit(solution)/shard_map/ppermute | solution.py:415
  50.2 6.1 %collective-permute-start.12 = (bf16[56,512]{1,0:T(8,128)(2,1)S(1)}, bf16[56,512]{1,0:T(8,128)(2,1)S(1)}, u32[]{:S(2)}, u32[]{:S(2)}) collective-permute-start(bf16[56,512]{1,0:T(8,128)(2,1)S(1)} %slice_select_fusion), channel_id=1, source_target_pairs={{0,4},{4,0},{8,12},{12,8},{1,5},{5,1},{9,13},{13,9},{2,6},{6,2},{1... | collective-permute-start | bytes 172040 | tf_op jit(solution)/shard_map/ppermute | solution.py:418
  56.2 1.4 %collective-permute-start.13 = (bf16[112,512]{1,0:T(8,128)(2,1)S(1)}, bf16[112,512]{1,0:T(8,128)(2,1)S(1)}, u32[]{:S(2)}, u32[]{:S(2)}) collective-permute-start(bf16[112,512]{1,0:T(8,128)(2,1)S(1)} %collective-permute-done.11.refs_5_), channel_id=1, source_target_pairs={{0,1},{1,0},{2,3},{3,2},{4,5},{5,4},{6,7},{7,6},{8,9},{9,8},{10,11... | collective-permute-start | bytes 344072 | tf_op jit(solution)/shard_map/ppermute | solution.py:89
  56.2 1.4 %collective-permute-start.14 = (bf16[56,512]{1,0:T(8,128)(2,1)S(1)}, bf16[56,512]{1,0:T(8,128)(2,1)S(1)}, u32[]{:S(2)}, u32[]{:S(2)}) collective-permute-start(bf16[56,512]{1,0:T(8,128)(2,1)S(1)} %collective-permute-done.12.refs_6_), channel_id=1, source_target_pairs={{0,1},{1,0},{2,3},{3,2},{4,5},{5,4},{6,7},{7,6},{8,9},{9,8},{10,11... | collective-permute-start | bytes 172040 | tf_op jit(solution)/shard_map/ppermute | solution.py:89
  57.6 1.1 %copy-start.3 = (bf16[448,640]{1,0:T(8,128)(2,1)S(1)}, bf16[448,640]{1,0:T(8,128)(2,1)}, u32[]{:S(2)}) copy-start(bf16[448,640]{1,0:T(8,128)(2,1)} %copy-done.2) | copy-start | bytes 1720324
  58.7 1.0 %copy-start.5 = (bf16[512,512]{1,0:T(8,128)(2,1)S(1)}, bf16[512,512]{1,0:T(8,128)(2,1)}, u32[]{:S(2)}) copy-start(bf16[512,512]{1,0:T(8,128)(2,1)} %copy-done.4) | copy-start | bytes 1572868
  59.7 1.0 %copy-start.7 = (bf16[512,448]{1,0:T(8,128)(2,1)S(1)}, bf16[512,448]{1,0:T(8,128)(2,1)}, u32[]{:S(2)}) copy-start(bf16[512,448]{1,0:T(8,128)(2,1)} %copy-done.6) | copy-start | bytes 1376260
  (1 other events, 0.7 us)

commit v18 on v17

--- a/solution.py
+++ b/solution.py
@@ -405,7 +405,19 @@
         [shape(reps * len(bins) * GROUP, wide)],
         small,
     )
-    columns = (partial + rotate(partial, "rep", 1)).astype(BF16)
+    rows = len(bins) * GROUP
+
+    def summed(mine, other):
+        both = mine + other
+        own = jnp.where(place()[2] == 0.0, both[:rows], both[rows:])
+        return both.astype(BF16), own.astype(BF16)
+
+    columns, own_half = on_core(
+        summed,
+        [partial, rotate(partial, "rep", 1)],
+        [shape(reps * rows, wide, dtype=BF16), shape(rows, wide, dtype=BF16)],
+        small,
+    )
 
     far = []
     for bits in range(2, feats, 2):
@@ -413,8 +425,6 @@
             (f * reps + r, (f ^ (bits + r)) * reps + r) for f in range(feats) for r in range(reps)
         ]
         far.append(lax.ppermute(columns, ("feat", "rep"), pairs))
-    rows = len(bins) * GROUP
-    own_half = jnp.where(lax.axis_index("rep") == 0, columns[:rows], columns[rows:])
     near = lax.ppermute(own_half, "feat", [(f, f ^ 1) for f in range(feats)])
     across = [rotate(shard, "rep", 1) for shard in far + [near]]
 

time: 63.6 us -> 58.1 us (0.914)
  waiting for transfers between devices: 10.2 us -> 19.4 us
  starting transfers between devices: 20.5 us -> 13.1 us
  local copies, waits for them, and re-layouts: 6.27 us -> 0.69 us
  other arithmetic: 1.09 us -> 0 us
  Pallas kernels: 9.65 us -> 9 us
    ppermute x4, starting transfers between devices: 9.39 us -> 3.62 us  [ring_next(): return lax.ppermute(x, axis, steps)]
    unnamed x20 -> x8, local copies, waits for them, and re-layouts: 6.18 us -> 0.6 us
    ppermute x2, waiting for transfers between devices: 0.01 us -> 3.73 us  [ring_next(): return lax.ppermute(x, (axis, across), pairs)]
    ppermute x4, waiting for transfers between devices: 0.7 us -> 3.97 us  [ring_next(): return lax.ppermute(x, axis, steps)]
    ppermute x1, starting transfers between devices: 3.45 us -> 1.65 us  [per_device(): far.append(lax.ppermute(columns, ('feat', 'rep'), pairs))]
    ppermute x1, waiting for transfers between devices: 5.33 us -> 7 us  [per_device(): far.append(lax.ppermute(columns, ('feat', 'rep'), pairs))]
    convert_element_type x1 -> x0, other arithmetic: 1.08 us -> none  [per_device(): columns = (partial + rotate(partial, 'rep', 1)).astype(BF16)]
    pallas_call x7 -> x8, Pallas kernels: 9.65 us -> 9 us  [on_core(): return list(call(*args, *streams, *through))]
  transfers between devices with their start and end apart: 15 -> 15, of which waited for: 7 -> 9; matrix products, arithmetic and copies ran while one was open for 1% -> 2% of each run, Pallas kernels for 5% -> 5%
where the time goes in v18:
time: 58.1 us; the launch traced here: 57.8 us
  waiting for transfers between devices  19.4 us (33%)
  blocking collectives  14.1 us (24%)
  starting transfers between devices  13.1 us (23%)
  Pallas kernels  9 us (15%)
  matrix products  0.8 us (1%)
  between operations  0.76 us (1%)
  local copies, waits for them, and re-layouts  0.69 us (1%)
    all_to_all x1, blocking collectives, per_device(): lax.all_to_all(packed, ('feat', 'pos'), split_axis=0, concat_axis=0, tile...  14.1 us
    pallas_call x8, Pallas kernels, on_core(): return list(call(*args, *streams, *through))  9 us
    ppermute x1, waiting for transfers between devices, per_device(): far.append(lax.ppermute(columns, ('feat', 'rep'), pairs))  7 us
    ppermute x7, starting transfers between devices, rotate(): lax.ppermute(x, axis, [(i, (i + step) % count) for i in range(count)])  5.83 us
    ppermute x7, waiting for transfers between devices, rotate(): lax.ppermute(x, axis, [(i, (i + step) % count) for i in range(count)])  4.68 us
    ppermute x4, waiting for transfers between devices, ring_next(): return lax.ppermute(x, axis, steps)  3.97 us
    ppermute x2, waiting for transfers between devices, ring_next(): return lax.ppermute(x, (axis, across), pairs)  3.73 us
    ppermute x4, starting transfers between devices, ring_next(): return lax.ppermute(x, axis, steps)  3.62 us
  transfers between devices with their start and end apart: 15, of which 9 were waited for; matrix products, arithmetic and copies ran while one was open for 2% of the time, Pallas kernels for 5%

profile of v18, /device:TPU:0, one launch (start us, length us, event | category | flops | bytes accessed | tf_op | source)
XLA Modules:
  0.0 57.8 jit_solution(7796836182580850835)
XLA Ops:
  0.6 1.5 %shard_map.77 = f32[8,8,128]{2,1,0:T(8,128)} custom-call(s32[1,4,28]{2,1,0:T(4,128)} %refs_0_.1, f32[1,4,28]{2,1,0:T(4,128)} %refs_1_.3), custom_call_target="tpu_custom_call" | custom-call | tf_op jit(solution)/shard_map/pallas_call | solution.py:84
  2.1 14.1 %all_to_all.5.refs_0_ = f32[8,8,128]{2,1,0:T(8,128)S(1)} all-to-all(f32[8,8,128]{2,1,0:T(8,128)} %shard_map.77), channel_id=1, replica_groups=mesh['grp'=2,'feat'=4,'pos'=2,'rep'=2] {'feat','pos'}, dimensions={0} | all-to-all | bytes 65536 | tf_op jit(solution)/shard_map/all_to_all | solution.py:187
  17.7 0.7 %collective-permute-start.1 = (bf16[80,1152]{1,0:T(8,128)(2,1)S(1)}, bf16[80,1152]{1,0:T(8,128)(2,1)S(1)}, u32[]{:S(2)}, u32[]{:S(2)}) collective-permute-start(bf16[80,1152]{1,0:T(8,128)(2,1)S(1)} %get-tuple-element.30), channel_id=1, source_target_pairs={{0,10},{2,8},{8,14},{10,12},{12,6},{14,4},{4,2},{6,0},{1,11},{3,9}... | collective-permute-start | bytes 552968 | tf_op jit(solution)/shard_map/ppermute | solution.py:105
  18.4 0.8 %fusion = bf16[3,160,1152]{2,1,0:T(8,128)(2,1)S(1)} fusion(bf16[512,3,1152]{2,0,1:T(8,128)(2,1)S(1)} %copy-done, bf16[160,512]{1,0:T(8,128)(2,1)S(1)} %get-tuple-element.22), kind=kOutput, calls=%fused_computation.1 | convolution fusion | flops 566784000 | bytes 4808704 | tf_op jit(solution)/shard_map/dot_general | solution.py:277
  19.9 1.9 %shard_map.80 = (bf16[448,640]{1,0:T(8,128)(2,1)S(1)}, bf16[640,512]{1,0:T(8,128)(2,1)S(1)}, f32[1,640]{1,0:T(1,128)S(1)}, f32[480,1]{1,0:T(8,128)S(1)}, bf16[51...) custom-call(f32[32,28]{1,0:T(8,128)S(1)} %get-tuple-element.20.refs_, ...), custom_call_target="tpu_custom_call", output_to_operand_aliasing={{6}: (2, {}), {7}: (3, {}), {8}: (4, {})} | custom-call | flops 1 | bytes 1 | tf_op jit(solution)/shard_map/pallas_call | solution.py:84
  21.8 1.4 %collective-permute-start.4 = (bf16[80,1152]{1,0:T(8,128)(2,1)S(1)}, bf16[80,1152]{1,0:T(8,128)(2,1)S(1)}, u32[]{:S(2)}, u32[]{:S(2)}) collective-permute-start(bf16[80,1152]{1,0:T(8,128)(2,1)S(1)} %get-tuple-element.31), channel_id=1, source_target_pairs={{0,2},{2,0},{1,3},{3,1},{4,6},{6,4},{5,7},{7,5},{8,10},{10,8},{9,1... | collective-permute-start | bytes 552968 | tf_op jit(solution)/shard_map/ppermute | solution.py:89
  23.2 1.4 %collective-permute-done.refs_4_ = bf16[80,1152]{1,0:T(8,128)(2,1)S(1)} collective-permute-done((bf16[80,1152]{1,0:T(8,128)(2,1)S(1)}, bf16[80,1152]{1,0:T(8,128)(2,1)S(1)}, u32[]{:S(2)}, u32[]{:S(2)}) %collective-permute-start) | collective-permute-done | bytes 184352 | tf_op jit(solution)/shard_map/ppermute | solution.py:105
  24.6 1.2 %collective-permute-start.2 = (bf16[80,1152]{1,0:T(8,128)(2,1)S(1)}, bf16[80,1152]{1,0:T(8,128)(2,1)S(1)}, u32[]{:S(2)}, u32[]{:S(2)}) collective-permute-start(bf16[80,1152]{1,0:T(8,128)(2,1)S(1)} %collective-permute-done.refs_4_), channel_id=1, source_target_pairs={{0,8},{8,12},{12,4},{4,0},{1,9},{9,13},{13,5},{5,1},{2,10},{10,14}... | collective-permute-start | bytes 552968 | tf_op jit(solution)/shard_map/ppermute | solution.py:102
  25.8 2.3 %collective-permute-done.1.refs_5_ = bf16[80,1152]{1,0:T(8,128)(2,1)S(1)} collective-permute-done((bf16[80,1152]{1,0:T(8,128)(2,1)S(1)}, bf16[80,1152]{1,0:T(8,128)(2,1)S(1)}, u32[]{:S(2)}, u32[]{:S(2)}) %collective-permute-start.1) | collective-permute-done | bytes 184352 | tf_op jit(solution)/shard_map/ppermute | solution.py:105
  28.7 1.8 %collective-permute-start.5 = (bf16[80,1152]{1,0:T(8,128)(2,1)S(1)}, bf16[80,1152]{1,0:T(8,128)(2,1)S(1)}, u32[]{:S(2)}, u32[]{:S(2)}) collective-permute-start(bf16[80,1152]{1,0:T(8,128)(2,1)S(1)} %get-tuple-element.32), channel_id=1, source_target_pairs={{0,2},{2,0},{1,3},{3,1},{4,6},{6,4},{5,7},{7,5},{8,10},{10,8},{9,1... | collective-permute-start | bytes 552968 | tf_op jit(solution)/shard_map/ppermute | solution.py:89
  30.7 1.8 %collective-permute-start.7 = (bf16[80,1152]{1,0:T(8,128)(2,1)S(1)}, bf16[80,1152]{1,0:T(8,128)(2,1)S(1)}, u32[]{:S(2)}, u32[]{:S(2)}) collective-permute-start(bf16[80,1152]{1,0:T(8,128)(2,1)S(1)} %get-tuple-element.30), channel_id=1, source_target_pairs={{0,2},{2,0},{1,3},{3,1},{4,6},{6,4},{5,7},{7,5},{8,10},{10,8},{9,1... | collective-permute-start | bytes 552968 | tf_op jit(solution)/shard_map/ppermute | solution.py:89
  32.6 1.2 %collective-permute-start.8 = (bf16[80,1152]{1,0:T(8,128)(2,1)S(1)}, bf16[80,1152]{1,0:T(8,128)(2,1)S(1)}, u32[]{:S(2)}, u32[]{:S(2)}) collective-permute-start(bf16[80,1152]{1,0:T(8,128)(2,1)S(1)} %collective-permute-done.2.refs_6_), channel_id=1, source_target_pairs={{0,8},{8,12},{12,4},{4,0},{1,9},{9,13},{13,5},{5,1},{2,10},{10,14}... | collective-permute-start | bytes 552968 | tf_op jit(solution)/shard_map/ppermute | solution.py:102
  33.8 2.7 %collective-permute-done.3.refs_7_ = bf16[80,1152]{1,0:T(8,128)(2,1)S(1)} collective-permute-done((bf16[80,1152]{1,0:T(8,128)(2,1)S(1)}, bf16[80,1152]{1,0:T(8,128)(2,1)S(1)}, u32[]{:S(2)}, u32[]{:S(2)}) %collective-permute-start.3) | collective-permute-done | bytes 184352 | tf_op jit(solution)/shard_map/ppermute | solution.py:102
  37.1 1.6 %collective-permute-done.6.refs_13_ = bf16[80,1152]{1,0:T(8,128)(2,1)S(1)} collective-permute-done((bf16[80,1152]{1,0:T(8,128)(2,1)S(1)}, bf16[80,1152]{1,0:T(8,128)(2,1)S(1)}, u32[]{:S(2)}, u32[]{:S(2)}) %collective-permute-start.6) | collective-permute-done | bytes 184352 | tf_op jit(solution)/shard_map/ppermute | solution.py:89
  38.8 1.3 %shard_map.81 = (f32[160,512]{1,0:T(8,128)S(1)}, bf16[480,1152]{1,0:T(8,128)(2,1)S(1)}) custom-call(f32[1,640]{1,0:T(1,128)S(1)} %get-tuple-element.26.refs_0_, bf16[640,512]{1,0:T(8,128)(2,1)S(1)} %get-tuple-element.27.refs_1_, f32[480,1]{1,0:T(8,128)S(1)} %get-tuple-element.28.refs_2_, bf16[80,1152]{1,0:T(8,128)(2,1)S(1)} %get-tuple-element.29.refs_3_, ...), custom_call_target="tpu_custom_call" | custom-call | flops 1 | bytes 1 | tf_op jit(solution)/shard_map/pallas_call | solution.py:84
  40.1 0.7 %collective-permute-done.7.refs_4_ = bf16[80,1152]{1,0:T(8,128)(2,1)S(1)} collective-permute-done((bf16[80,1152]{1,0:T(8,128)(2,1)S(1)}, bf16[80,1152]{1,0:T(8,128)(2,1)S(1)}, u32[]{:S(2)}, u32[]{:S(2)}) %collective-permute-start.7) | collective-permute-done | bytes 184352 | tf_op jit(solution)/shard_map/ppermute | solution.py:89
  40.8 1.3 %collective-permute-done.9.refs_6_ = bf16[80,1152]{1,0:T(8,128)(2,1)S(1)} collective-permute-done((bf16[80,1152]{1,0:T(8,128)(2,1)S(1)}, bf16[80,1152]{1,0:T(8,128)(2,1)S(1)}, u32[]{:S(2)}, u32[]{:S(2)}) %collective-permute-start.9) | collective-permute-done | bytes 184352 | tf_op jit(solution)/shard_map/ppermute | solution.py:102
  42.0 1.0 %shard_map.82.refs_0_ = f32[112,512]{1,0:T(8,128)S(1)} custom-call(f32[1,640]{1,0:T(1,128)S(1)} %get-tuple-element.26.refs_0_, bf16[640,512]{1,0:T(8,128)(2,1)S(1)} %get-tuple-element.27.refs_1_, f32[160,512]{1,0:T(8,128)S(1)} %get-tuple-element.34.refs_2_, bf16[480,1152]{1,0:T(8,128)(2,1)S(1)} %get-tuple-element.35.refs_3_, ...), custom_call_target="tpu_custom_call" | custom-call | tf_op jit(solution)/shard_map/pallas_call | solution.py:84
  43.1 1.5 %collective-permute-done.10.refs_1_ = f32[112,512]{1,0:T(8,128)S(1)} collective-permute-done((f32[112,512]{1,0:T(8,128)S(1)}, f32[112,512]{1,0:T(8,128)S(1)}, u32[]{:S(2)}, u32[]{:S(2)}) %collective-permute-start.10) | collective-permute-done | bytes 229408 | tf_op jit(solution)/shard_map/ppermute | solution.py:89
  44.6 1.6 %collective-permute-start.11 = (bf16[112,512]{1,0:T(8,128)(2,1)S(1)}, bf16[112,512]{1,0:T(8,128)(2,1)S(1)}, u32[]{:S(2)}, u32[]{:S(2)}) collective-permute-start(bf16[112,512]{1,0:T(8,128)(2,1)S(1)} %get-tuple-element.36.refs_4_), channel_id=1, source_target_pairs={{0,8},{1,13},{4,12},{5,9},{8,0},{9,5},{12,4},{13,1},{2,10},{3,15},... | collective-permute-start | bytes 344072 | tf_op jit(solution)/shard_map/ppermute | solution.py:427
  46.2 0.7 %collective-permute-start.12 = (bf16[56,512]{1,0:T(8,128)(2,1)S(1)}, bf16[56,512]{1,0:T(8,128)(2,1)S(1)}, u32[]{:S(2)}, u32[]{:S(2)}) collective-permute-start(bf16[56,512]{1,0:T(8,128)(2,1)S(1)} %get-tuple-element.37), channel_id=1, source_target_pairs={{0,4},{4,0},{8,12},{12,8},{1,5},{5,1},{9,13},{13,9},{2,6},{6,2},{1... | collective-permute-start | bytes 172040 | tf_op jit(solution)/shard_map/ppermute | solution.py:428
  46.9 7.0 %collective-permute-done.11.refs_5_ = bf16[112,512]{1,0:T(8,128)(2,1)S(1)} collective-permute-done((bf16[112,512]{1,0:T(8,128)(2,1)S(1)}, bf16[112,512]{1,0:T(8,128)(2,1)S(1)}, u32[]{:S(2)}, u32[]{:S(2)}) %collective-permute-start.11) | collective-permute-done | bytes 114720 | tf_op jit(solution)/shard_map/ppermute | solution.py:427
  54.4 0.9 %collective-permute-done.14.refs_8_ = bf16[56,512]{1,0:T(8,128)(2,1)S(1)} collective-permute-done((bf16[56,512]{1,0:T(8,128)(2,1)S(1)}, bf16[56,512]{1,0:T(8,128)(2,1)S(1)}, u32[]{:S(2)}, u32[]{:S(2)}) %collective-permute-start.14) | collective-permute-done | bytes 57376 | tf_op jit(solution)/shard_map/ppermute | solution.py:89
  55.3 2.5 %shard_map.84 = (bf16[1,56,448]{2,1,0:T(8,128)(2,1)}, f32[1,56,128]{2,1,0:T(8,128)}) custom-call(bf16[448,640]{1,0:T(8,128)(2,1)S(1)} %get-tuple-element.23.refs_0_, bf16[512,512]{1,0:T(8,128)(2,1)S(1)} %get-tuple-element.24.refs_1_, bf16[512,448]{1,0:T(8,128)(2,1)S(1)} %get-tuple-element.25.refs_2_, s32[1,128]{1,0:T(1,128)S(1)} %copy-done.3, ...), custom_call_target="tpu_custom_call" | custom-call | tf_op jit(solution)/shard_map/pallas_call | solution.py:84
  (25 shorter events, 4.2 us)
Async XLA Ops:
  0.6 17.8 %copy-start = (bf16[512,3,1152]{2,0,1:T(8,128)(2,1)S(1)}, bf16[512,3,1152]{2,0,1:T(8,128)(2,1)}, u32[]{:S(2)}) copy-start(bf16[512,3,1152]{2,0,1:T(8,128)(2,1)} %param.11) | copy-start | bytes 10616836
  2.1 14.6 %copy-start.1 = (bf16[512,1152]{1,0:T(8,128)(2,1)S(1)}, bf16[512,1152]{1,0:T(8,128)(2,1)}, u32[]{:S(2)}) copy-start(bf16[512,1152]{1,0:T(8,128)(2,1)} %refs_1_.4) | copy-start | bytes 3538948
  17.1 7.5 %collective-permute-start = (bf16[80,1152]{1,0:T(8,128)(2,1)S(1)}, bf16[80,1152]{1,0:T(8,128)(2,1)S(1)}, u32[]{:S(2)}, u32[]{:S(2)}) collective-permute-start(bf16[80,1152]{1,0:T(8,128)(2,1)S(1)} %get-tuple-element.29.refs_3_), channel_id=1, source_target_pairs={{0,8},{2,10},{8,12},{10,14},{12,4},{14,6},{4,0},{6,2},{1,9},{3,11}... | collective-permute-start | bytes 552968 | tf_op jit(solution)/shard_map/ppermute | solution.py:105
  17.7 10.4 %collective-permute-start.1 = (bf16[80,1152]{1,0:T(8,128)(2,1)S(1)}, bf16[80,1152]{1,0:T(8,128)(2,1)S(1)}, u32[]{:S(2)}, u32[]{:S(2)}) collective-permute-start(bf16[80,1152]{1,0:T(8,128)(2,1)S(1)} %get-tuple-element.30), channel_id=1, source_target_pairs={{0,10},{2,8},{8,14},{10,12},{12,6},{14,4},{4,2},{6,0},{1,11},{3,9}... | collective-permute-start | bytes 552968 | tf_op jit(solution)/shard_map/ppermute | solution.py:105
  19.2 0.7 %copy-start.2 = (s32[1,4,4]{2,1,0:T(4,128)S(1)}, s32[1,4,4]{2,1,0:T(4,128)}, u32[]{:S(2)}) copy-start(s32[1,4,4]{2,1,0:T(4,128)} %refs_1_.5) | copy-start | bytes 196
  21.8 8.9 %collective-permute-start.4 = (bf16[80,1152]{1,0:T(8,128)(2,1)S(1)}, bf16[80,1152]{1,0:T(8,128)(2,1)S(1)}, u32[]{:S(2)}, u32[]{:S(2)}) collective-permute-start(bf16[80,1152]{1,0:T(8,128)(2,1)S(1)} %get-tuple-element.31), channel_id=1, source_target_pairs={{0,2},{2,0},{1,3},{3,1},{4,6},{6,4},{5,7},{7,5},{8,10},{10,8},{9,1... | collective-permute-start | bytes 552968 | tf_op jit(solution)/shard_map/ppermute | solution.py:89
  24.6 8.0 %collective-permute-start.2 = (bf16[80,1152]{1,0:T(8,128)(2,1)S(1)}, bf16[80,1152]{1,0:T(8,128)(2,1)S(1)}, u32[]{:S(2)}, u32[]{:S(2)}) collective-permute-start(bf16[80,1152]{1,0:T(8,128)(2,1)S(1)} %collective-permute-done.refs_4_), channel_id=1, source_target_pairs={{0,8},{8,12},{12,4},{4,0},{1,9},{9,13},{13,5},{5,1},{2,10},{10,14}... | collective-permute-start | bytes 552968 | tf_op jit(solution)/shard_map/ppermute | solution.py:102
  28.1 8.3 %collective-permute-start.3 = (bf16[80,1152]{1,0:T(8,128)(2,1)S(1)}, bf16[80,1152]{1,0:T(8,128)(2,1)S(1)}, u32[]{:S(2)}, u32[]{:S(2)}) collective-permute-start(bf16[80,1152]{1,0:T(8,128)(2,1)S(1)} %collective-permute-done.1.refs_5_), channel_id=1, source_target_pairs={{0,8},{8,12},{12,4},{4,0},{1,9},{9,13},{13,5},{5,1},{2,10},{10,14}... | collective-permute-start | bytes 552968 | tf_op jit(solution)/shard_map/ppermute | solution.py:102
  28.7 8.4 %collective-permute-start.5 = (bf16[80,1152]{1,0:T(8,128)(2,1)S(1)}, bf16[80,1152]{1,0:T(8,128)(2,1)S(1)}, u32[]{:S(2)}, u32[]{:S(2)}) collective-permute-start(bf16[80,1152]{1,0:T(8,128)(2,1)S(1)} %get-tuple-element.32), channel_id=1, source_target_pairs={{0,2},{2,0},{1,3},{3,1},{4,6},{6,4},{5,7},{7,5},{8,10},{10,8},{9,1... | collective-permute-start | bytes 552968 | tf_op jit(solution)/shard_map/ppermute | solution.py:89
  30.5 8.2 %collective-permute-start.6 = (bf16[80,1152]{1,0:T(8,128)(2,1)S(1)}, bf16[80,1152]{1,0:T(8,128)(2,1)S(1)}, u32[]{:S(2)}, u32[]{:S(2)}) collective-permute-start(bf16[80,1152]{1,0:T(8,128)(2,1)S(1)} %get-tuple-element.33), channel_id=1, source_target_pairs={{0,2},{2,0},{1,3},{3,1},{4,6},{6,4},{5,7},{7,5},{8,10},{10,8},{9,1... | collective-permute-start | bytes 552968 | tf_op jit(solution)/shard_map/ppermute | solution.py:89
  30.7 10.0 %collective-permute-start.7 = (bf16[80,1152]{1,0:T(8,128)(2,1)S(1)}, bf16[80,1152]{1,0:T(8,128)(2,1)S(1)}, u32[]{:S(2)}, u32[]{:S(2)}) collective-permute-start(bf16[80,1152]{1,0:T(8,128)(2,1)S(1)} %get-tuple-element.30), channel_id=1, source_target_pairs={{0,2},{2,0},{1,3},{3,1},{4,6},{6,4},{5,7},{7,5},{8,10},{10,8},{9,1... | collective-permute-start | bytes 552968 | tf_op jit(solution)/shard_map/ppermute | solution.py:89
  32.6 8.2 %collective-permute-start.8 = (bf16[80,1152]{1,0:T(8,128)(2,1)S(1)}, bf16[80,1152]{1,0:T(8,128)(2,1)S(1)}, u32[]{:S(2)}, u32[]{:S(2)}) collective-permute-start(bf16[80,1152]{1,0:T(8,128)(2,1)S(1)} %collective-permute-done.2.refs_6_), channel_id=1, source_target_pairs={{0,8},{8,12},{12,4},{4,0},{1,9},{9,13},{13,5},{5,1},{2,10},{10,14}... | collective-permute-start | bytes 552968 | tf_op jit(solution)/shard_map/ppermute | solution.py:102
  36.5 5.5 %collective-permute-start.9 = (bf16[80,1152]{1,0:T(8,128)(2,1)S(1)}, bf16[80,1152]{1,0:T(8,128)(2,1)S(1)}, u32[]{:S(2)}, u32[]{:S(2)}) collective-permute-start(bf16[80,1152]{1,0:T(8,128)(2,1)S(1)} %collective-permute-done.3.refs_7_), channel_id=1, source_target_pairs={{0,8},{8,12},{12,4},{4,0},{1,9},{9,13},{13,5},{5,1},{2,10},{10,14}... | collective-permute-start | bytes 552968 | tf_op jit(solution)/shard_map/ppermute | solution.py:102
  40.1 15.2 %copy-start.3 = (s32[1,128]{1,0:T(1,128)S(1)}, s32[1,128]{1,0:T(1,128)}, u32[]{:S(2)}) copy-start(s32[1,128]{1,0:T(1,128)} %refs_3_.1) | copy-start | bytes 1540
  43.0 1.6 %collective-permute-start.10 = (f32[112,512]{1,0:T(8,128)S(1)}, f32[112,512]{1,0:T(8,128)S(1)}, u32[]{:S(2)}, u32[]{:S(2)}) collective-permute-start(f32[112,512]{1,0:T(8,128)S(1)} %shard_map.82.refs_0_), channel_id=1, source_target_pairs={{0,1},{1,0},{2,3},{3,2},{4,5},{5,4},{6,7},{7,6},{8,9},{9,8},{10,11... | collective-permute-start | bytes 688136 | tf_op jit(solution)/shard_map/ppermute | solution.py:89
  44.6 9.3 %collective-permute-start.11 = (bf16[112,512]{1,0:T(8,128)(2,1)S(1)}, bf16[112,512]{1,0:T(8,128)(2,1)S(1)}, u32[]{:S(2)}, u32[]{:S(2)}) collective-permute-start(bf16[112,512]{1,0:T(8,128)(2,1)S(1)} %get-tuple-element.36.refs_4_), channel_id=1, source_target_pairs={{0,8},{1,13},{4,12},{5,9},{8,0},{9,5},{12,4},{13,1},{2,10},{3,15},... | collective-permute-start | bytes 344072 | tf_op jit(solution)/shard_map/ppermute | solution.py:427
  46.2 7.7 %collective-permute-start.12 = (bf16[56,512]{1,0:T(8,128)(2,1)S(1)}, bf16[56,512]{1,0:T(8,128)(2,1)S(1)}, u32[]{:S(2)}, u32[]{:S(2)}) collective-permute-start(bf16[56,512]{1,0:T(8,128)(2,1)S(1)} %get-tuple-element.37), channel_id=1, source_target_pairs={{0,4},{4,0},{8,12},{12,8},{1,5},{5,1},{9,13},{13,9},{2,6},{6,2},{1... | collective-permute-start | bytes 172040 | tf_op jit(solution)/shard_map/ppermute | solution.py:428
  53.9 1.4 %collective-permute-start.13 = (bf16[112,512]{1,0:T(8,128)(2,1)S(1)}, bf16[112,512]{1,0:T(8,128)(2,1)S(1)}, u32[]{:S(2)}, u32[]{:S(2)}) collective-permute-start(bf16[112,512]{1,0:T(8,128)(2,1)S(1)} %collective-permute-done.11.refs_5_), channel_id=1, source_target_pairs={{0,1},{1,0},{2,3},{3,2},{4,5},{5,4},{6,7},{7,6},{8,9},{9,8},{10,11... | collective-permute-start | bytes 344072 | tf_op jit(solution)/shard_map/ppermute | solution.py:89
  53.9 1.4 %collective-permute-start.14 = (bf16[56,512]{1,0:T(8,128)(2,1)S(1)}, bf16[56,512]{1,0:T(8,128)(2,1)S(1)}, u32[]{:S(2)}, u32[]{:S(2)}) collective-permute-start(bf16[56,512]{1,0:T(8,128)(2,1)S(1)} %collective-permute-done.12.refs_6_), channel_id=1, source_target_pairs={{0,1},{1,0},{2,3},{3,2},{4,5},{5,4},{6,7},{7,6},{8,9},{9,8},{10,11... | collective-permute-start | bytes 172040 | tf_op jit(solution)/shard_map/ppermute | solution.py:89

commit v19 on v15

--- a/solution.py
+++ b/solution.py
@@ -354,13 +354,19 @@
         mask = jnp.where(source <= target, mask, 0.0)
         squeeze = spread_slot(iota((wide, slots), 0)) == iota((wide, slots), 1)
         placing, placing_t = placing.astype(BF16), placing_t.astype(BF16)
+        unused = [jnp.zeros((span - block_rows, holders * listed), BF16)]
+        unused = unused if span > block_rows else []
+        spaced = []
+        for f in range(feats):
+            spaced += [placing[f * block_rows : (f + 1) * block_rows]] + unused
+        placing = jnp.concatenate(spaced, axis=0)
         return placing, placing_t, layer_row, gains, mask.astype(BF16), squeeze.astype(BF16)
 
     placing, placing_t, layer_row, gains, mask, squeeze, *away = on_core(
         places,
         [my_list, block_pattern],
         [
-            shape(slots, holders * listed, dtype=BF16),
+            shape(wide, holders * listed, dtype=BF16),
             shape(holders * listed, wide, dtype=BF16),
             shape(1, holders * listed),
             shape(depth * column, 1),
@@ -429,18 +435,11 @@
             lower, higher = jnp.where(first, mine, other), jnp.where(first, other, mine)
             chips.append(jnp.concatenate([unpack_rests(lower), unpack_rests(higher)], axis=0))
         padded = jnp.concatenate([chips[arrival.index(m)] for m in range(feats)], axis=0)
-        unused = [jnp.zeros((span - block_rows, holders * listed), BF16)]
-        unused = unused if span > block_rows else []
-        sources = []
-        for f in range(feats):
-            sources += [placing[f * block_rows : (f + 1) * block_rows]] + unused
-        sources = jnp.concatenate(sources, axis=0)
-        edges = dot(sources, padded) * mask.astype(F32)
+        edges = dot(placing, padded) * mask.astype(F32)
         magnitude = jnp.abs(edges)
         total = jnp.maximum(jnp.sum(magnitude, axis=0, keepdims=True), 1.0)
         magnitude = magnitude.astype(BF16)
-        diagonal = iota((wide, wide), 0) == iota((wide, wide), 1)
-        scale = 1.0 / jnp.sum(jnp.where(diagonal, total, 0.0), axis=1, keepdims=True)
+        scale = 1.0 / jnp.transpose(jnp.broadcast_to(total, (GROUP, wide)))[:, :1]
         targets = targets.astype(F32)
         targets = targets + floor_div(targets, block_rows) * (span - block_rows)
         current = (iota((wide, panel), 0) == targets).astype(F32)

time: 57.4 us -> 57.5 us (level)
  transfers between devices with their start and end apart: 18 -> 18, of which waited for: 12 -> 12; matrix products, arithmetic and copies ran while one was open for 2% -> 1% of each run, Pallas kernels for 6% -> 6%
where the time goes in v19:
time: 57.5 us; the launch traced here: 57.3 us
  waiting for transfers between devices  17 us (30%)
  starting transfers between devices  14.9 us (26%)
  blocking collectives  14.1 us (25%)
  Pallas kernels  9.1 us (16%)
  matrix products  0.77 us (1%)
  between operations  0.75 us (1%)
  local copies, waits for them, and re-layouts  0.69 us (1%)
    all_to_all x1, blocking collectives, per_device(): lax.all_to_all(packed, ('feat', 'pos'), split_axis=0, concat_axis=0, tile...  14.1 us
    pallas_call x7, Pallas kernels, on_core(): return list(call(*args, *streams, *through))  9.1 us
    ppermute x9, starting transfers between devices, rotate(): lax.ppermute(x, axis, [(i, (i + step) % count) for i in range(count)])  5.32 us
    ppermute x9, waiting for transfers between devices, rotate(): lax.ppermute(x, axis, [(i, (i + step) % count) for i in range(count)])  4.82 us
    ppermute x3, starting transfers between devices, spread(): found[bits] = lax.ppermute(x, axis, [(i, i ^ bits) for i in range(count)])  4.62 us
    ppermute x3, waiting for transfers between devices, spread(): found[bits] = lax.ppermute(x, axis, [(i, i ^ bits) for i in range(count)])  4.39 us
    ppermute x4, waiting for transfers between devices, ring_next(): return lax.ppermute(x, axis, steps)  4.03 us
    ppermute x2, waiting for transfers between devices, ring_next(): return lax.ppermute(x, (axis, across), pairs)  3.81 us
  transfers between devices with their start and end apart: 18, of which 12 were waited for; matrix products, arithmetic and copies ran while one was open for 1% of the time, Pallas kernels for 6%

profile of v19, /device:TPU:0, one launch (start us, length us, event | category | flops | bytes accessed | tf_op | source)
XLA Modules:
  0.0 57.3 jit_solution(17341127959267417922)
XLA Ops:
  0.6 1.5 %shard_map.77 = f32[8,8,128]{2,1,0:T(8,128)} custom-call(s32[1,4,28]{2,1,0:T(4,128)} %refs_0_.1, f32[1,4,28]{2,1,0:T(4,128)} %refs_1_.3), custom_call_target="tpu_custom_call" | custom-call | tf_op jit(solution)/shard_map/pallas_call | solution.py:84
  2.1 14.1 %all_to_all.5.refs_0_ = f32[8,8,128]{2,1,0:T(8,128)S(1)} all-to-all(f32[8,8,128]{2,1,0:T(8,128)} %shard_map.77), channel_id=1, replica_groups=mesh['grp'=2,'feat'=4,'pos'=2,'rep'=2] {'feat','pos'}, dimensions={0} | all-to-all | bytes 65536 | tf_op jit(solution)/shard_map/all_to_all | solution.py:195
  17.7 0.7 %collective-permute-start.1 = (bf16[80,1152]{1,0:T(8,128)(2,1)S(1)}, bf16[80,1152]{1,0:T(8,128)(2,1)S(1)}, u32[]{:S(2)}, u32[]{:S(2)}) collective-permute-start(bf16[80,1152]{1,0:T(8,128)(2,1)S(1)} %get-tuple-element.30), channel_id=1, source_target_pairs={{0,10},{2,8},{8,14},{10,12},{12,6},{14,4},{4,2},{6,0},{1,11},{3,9}... | collective-permute-start | bytes 552968 | tf_op jit(solution)/shard_map/ppermute | solution.py:105
  18.4 0.8 %fusion = bf16[3,160,1152]{2,1,0:T(8,128)(2,1)S(1)} fusion(bf16[512,3,1152]{2,0,1:T(8,128)(2,1)S(1)} %copy-done, bf16[160,512]{1,0:T(8,128)(2,1)S(1)} %get-tuple-element.22), kind=kOutput, calls=%fused_computation.1 | convolution fusion | flops 566784000 | bytes 4808704 | tf_op jit(solution)/shard_map/dot_general | solution.py:285
  19.9 1.9 %shard_map.80 = (bf16[512,640]{1,0:T(8,128)(2,1)S(1)}, bf16[640,512]{1,0:T(8,128)(2,1)S(1)}, f32[1,640]{1,0:T(1,128)S(1)}, f32[480,1]{1,0:T(8,128)S(1)}, bf16[51...) custom-call(f32[32,28]{1,0:T(8,128)S(1)} %get-tuple-element.20.refs_, ...), custom_call_target="tpu_custom_call", output_to_operand_aliasing={{6}: (2, {}), {7}: (3, {}), {8}: (4, {})} | custom-call | flops 1 | bytes 1 | tf_op jit(solution)/shard_map/pallas_call | solution.py:84
  21.8 1.4 %collective-permute-start.4 = (bf16[80,1152]{1,0:T(8,128)(2,1)S(1)}, bf16[80,1152]{1,0:T(8,128)(2,1)S(1)}, u32[]{:S(2)}, u32[]{:S(2)}) collective-permute-start(bf16[80,1152]{1,0:T(8,128)(2,1)S(1)} %get-tuple-element.31), channel_id=1, source_target_pairs={{0,2},{2,0},{1,3},{3,1},{4,6},{6,4},{5,7},{7,5},{8,10},{10,8},{9,1... | collective-permute-start | bytes 552968 | tf_op jit(solution)/shard_map/ppermute | solution.py:89
  23.2 1.5 %collective-permute-done.refs_4_ = bf16[80,1152]{1,0:T(8,128)(2,1)S(1)} collective-permute-done((bf16[80,1152]{1,0:T(8,128)(2,1)S(1)}, bf16[80,1152]{1,0:T(8,128)(2,1)S(1)}, u32[]{:S(2)}, u32[]{:S(2)}) %collective-permute-start) | collective-permute-done | bytes 184352 | tf_op jit(solution)/shard_map/ppermute | solution.py:105
  24.6 1.2 %collective-permute-start.2 = (bf16[80,1152]{1,0:T(8,128)(2,1)S(1)}, bf16[80,1152]{1,0:T(8,128)(2,1)S(1)}, u32[]{:S(2)}, u32[]{:S(2)}) collective-permute-start(bf16[80,1152]{1,0:T(8,128)(2,1)S(1)} %collective-permute-done.refs_4_), channel_id=1, source_target_pairs={{0,8},{8,12},{12,4},{4,0},{1,9},{9,13},{13,5},{5,1},{2,10},{10,14}... | collective-permute-start | bytes 552968 | tf_op jit(solution)/shard_map/ppermute | solution.py:102
  25.8 2.3 %collective-permute-done.1.refs_5_ = bf16[80,1152]{1,0:T(8,128)(2,1)S(1)} collective-permute-done((bf16[80,1152]{1,0:T(8,128)(2,1)S(1)}, bf16[80,1152]{1,0:T(8,128)(2,1)S(1)}, u32[]{:S(2)}, u32[]{:S(2)}) %collective-permute-start.1) | collective-permute-done | bytes 184352 | tf_op jit(solution)/shard_map/ppermute | solution.py:105
  28.7 1.8 %collective-permute-start.5 = (bf16[80,1152]{1,0:T(8,128)(2,1)S(1)}, bf16[80,1152]{1,0:T(8,128)(2,1)S(1)}, u32[]{:S(2)}, u32[]{:S(2)}) collective-permute-start(bf16[80,1152]{1,0:T(8,128)(2,1)S(1)} %get-tuple-element.32), channel_id=1, source_target_pairs={{0,2},{2,0},{1,3},{3,1},{4,6},{6,4},{5,7},{7,5},{8,10},{10,8},{9,1... | collective-permute-start | bytes 552968 | tf_op jit(solution)/shard_map/ppermute | solution.py:89
  30.8 1.8 %collective-permute-start.7 = (bf16[80,1152]{1,0:T(8,128)(2,1)S(1)}, bf16[80,1152]{1,0:T(8,128)(2,1)S(1)}, u32[]{:S(2)}, u32[]{:S(2)}) collective-permute-start(bf16[80,1152]{1,0:T(8,128)(2,1)S(1)} %get-tuple-element.30), channel_id=1, source_target_pairs={{0,2},{2,0},{1,3},{3,1},{4,6},{6,4},{5,7},{7,5},{8,10},{10,8},{9,1... | collective-permute-start | bytes 552968 | tf_op jit(solution)/shard_map/ppermute | solution.py:89
  32.6 1.2 %collective-permute-start.8 = (bf16[80,1152]{1,0:T(8,128)(2,1)S(1)}, bf16[80,1152]{1,0:T(8,128)(2,1)S(1)}, u32[]{:S(2)}, u32[]{:S(2)}) collective-permute-start(bf16[80,1152]{1,0:T(8,128)(2,1)S(1)} %collective-permute-done.2.refs_6_), channel_id=1, source_target_pairs={{0,8},{8,12},{12,4},{4,0},{1,9},{9,13},{13,5},{5,1},{2,10},{10,14}... | collective-permute-start | bytes 552968 | tf_op jit(solution)/shard_map/ppermute | solution.py:102
  33.8 2.7 %collective-permute-done.3.refs_7_ = bf16[80,1152]{1,0:T(8,128)(2,1)S(1)} collective-permute-done((bf16[80,1152]{1,0:T(8,128)(2,1)S(1)}, bf16[80,1152]{1,0:T(8,128)(2,1)S(1)}, u32[]{:S(2)}, u32[]{:S(2)}) %collective-permute-start.3) | collective-permute-done | bytes 184352 | tf_op jit(solution)/shard_map/ppermute | solution.py:102
  36.5 0.7 %collective-permute-start.9 = (bf16[80,1152]{1,0:T(8,128)(2,1)S(1)}, bf16[80,1152]{1,0:T(8,128)(2,1)S(1)}, u32[]{:S(2)}, u32[]{:S(2)}) collective-permute-start(bf16[80,1152]{1,0:T(8,128)(2,1)S(1)} %collective-permute-done.3.refs_7_), channel_id=1, source_target_pairs={{0,8},{8,12},{12,4},{4,0},{1,9},{9,13},{13,5},{5,1},{2,10},{10,14}... | collective-permute-start | bytes 552968 | tf_op jit(solution)/shard_map/ppermute | solution.py:102
  37.2 1.6 %collective-permute-done.6.refs_13_ = bf16[80,1152]{1,0:T(8,128)(2,1)S(1)} collective-permute-done((bf16[80,1152]{1,0:T(8,128)(2,1)S(1)}, bf16[80,1152]{1,0:T(8,128)(2,1)S(1)}, u32[]{:S(2)}, u32[]{:S(2)}) %collective-permute-start.6) | collective-permute-done | bytes 184352 | tf_op jit(solution)/shard_map/ppermute | solution.py:89
  38.8 1.3 %shard_map.81 = (f32[160,512]{1,0:T(8,128)S(1)}, bf16[480,1152]{1,0:T(8,128)(2,1)S(1)}) custom-call(f32[1,640]{1,0:T(1,128)S(1)} %get-tuple-element.26.refs_0_, bf16[640,512]{1,0:T(8,128)(2,1)S(1)} %get-tuple-element.27.refs_1_, f32[480,1]{1,0:T(8,128)S(1)} %get-tuple-element.28.refs_2_, bf16[80,1152]{1,0:T(8,128)(2,1)S(1)} %get-tuple-element.29.refs_3_, ...), custom_call_target="tpu_custom_call" | custom-call | flops 1 | bytes 1 | tf_op jit(solution)/shard_map/pallas_call | solution.py:84
  40.1 0.7 %collective-permute-done.7.refs_4_ = bf16[80,1152]{1,0:T(8,128)(2,1)S(1)} collective-permute-done((bf16[80,1152]{1,0:T(8,128)(2,1)S(1)}, bf16[80,1152]{1,0:T(8,128)(2,1)S(1)}, u32[]{:S(2)}, u32[]{:S(2)}) %collective-permute-start.7) | collective-permute-done | bytes 184352 | tf_op jit(solution)/shard_map/ppermute | solution.py:89
  40.7 1.3 %collective-permute-done.9.refs_6_ = bf16[80,1152]{1,0:T(8,128)(2,1)S(1)} collective-permute-done((bf16[80,1152]{1,0:T(8,128)(2,1)S(1)}, bf16[80,1152]{1,0:T(8,128)(2,1)S(1)}, u32[]{:S(2)}, u32[]{:S(2)}) %collective-permute-start.9) | collective-permute-done | bytes 184352 | tf_op jit(solution)/shard_map/ppermute | solution.py:102
  42.0 1.0 %shard_map.82 = (f32[56,512]{1,0:T(8,128)S(1)}, f32[56,512]{1,0:T(8,128)S(1)}) custom-call(f32[1,640]{1,0:T(1,128)S(1)} %get-tuple-element.26.refs_0_, bf16[640,512]{1,0:T(8,128)(2,1)S(1)} %get-tuple-element.27.refs_1_, f32[160,512]{1,0:T(8,128)S(1)} %get-tuple-element.34.refs_2_, bf16[480,1152]{1,0:T(8,128)(2,1)S(1)} %get-tuple-element.35.refs_3_, ...), custom_call_target="tpu_custom_call" | custom-call | tf_op jit(solution)/shard_map/pallas_call | solution.py:84
  43.1 1.3 %collective-permute-done.10 = f32[56,512]{1,0:T(8,128)S(1)} collective-permute-done((f32[56,512]{1,0:T(8,128)S(1)}, f32[56,512]{1,0:T(8,128)S(1)}, u32[]{:S(2)}, u32[]{:S(2)}) %collective-permute-start.10) | collective-permute-done | bytes 114720 | tf_op jit(solution)/shard_map/ppermute | solution.py:89
  44.4 1.6 %collective-permute-start.11 = (bf16[56,512]{1,0:T(8,128)(2,1)S(1)}, bf16[56,512]{1,0:T(8,128)(2,1)S(1)}, u32[]{:S(2)}, u32[]{:S(2)}) collective-permute-start(bf16[56,512]{1,0:T(8,128)(2,1)S(1)} %add_convert_fusion.refs_4_), channel_id=1, source_target_pairs={{0,8},{4,12},{8,0},{12,4},{1,9},{5,13},{9,1},{13,5},{2,10},{6,14},... | collective-permute-start | bytes 172040 | tf_op jit(solution)/shard_map/ppermute | solution.py:112
  46.1 3.0 %collective-permute-start.12 = (bf16[56,512]{1,0:T(8,128)(2,1)S(1)}, bf16[56,512]{1,0:T(8,128)(2,1)S(1)}, u32[]{:S(2)}, u32[]{:S(2)}) collective-permute-start(bf16[56,512]{1,0:T(8,128)(2,1)S(1)} %add_convert_fusion.refs_4_), channel_id=1, source_target_pairs={{0,12},{4,8},{8,4},{12,0},{1,13},{5,9},{9,5},{13,1},{2,14},{6,10},... | collective-permute-start | bytes 172040 | tf_op jit(solution)/shard_map/ppermute | solution.py:112
  49.0 3.2 %collective-permute-done.11.refs_5_ = bf16[56,512]{1,0:T(8,128)(2,1)S(1)} collective-permute-done((bf16[56,512]{1,0:T(8,128)(2,1)S(1)}, bf16[56,512]{1,0:T(8,128)(2,1)S(1)}, u32[]{:S(2)}, u32[]{:S(2)}) %collective-permute-start.11) | collective-permute-done | bytes 57376 | tf_op jit(solution)/shard_map/ppermute | solution.py:112
  54.7 2.6 %shard_map.83 = (bf16[1,56,448]{2,1,0:T(8,128)(2,1)}, f32[1,56,128]{2,1,0:T(8,128)}) custom-call(bf16[512,640]{1,0:T(8,128)(2,1)S(1)} %get-tuple-element.23.refs_0_, bf16[512,512]{1,0:T(8,128)(2,1)S(1)} %get-tuple-element.24.refs_1_, bf16[512,448]{1,0:T(8,128)(2,1)S(1)} %get-tuple-element.25.refs_2_, s32[1,128]{1,0:T(1,128)S(1)} %copy-done.3, ...), custom_call_target="tpu_custom_call" | custom-call | tf_op jit(solution)/shard_map/pallas_call | solution.py:84
  (31 shorter events, 5.5 us)
Async XLA Ops:
  0.6 17.8 %copy-start = (bf16[512,3,1152]{2,0,1:T(8,128)(2,1)S(1)}, bf16[512,3,1152]{2,0,1:T(8,128)(2,1)}, u32[]{:S(2)}) copy-start(bf16[512,3,1152]{2,0,1:T(8,128)(2,1)} %param.11) | copy-start | bytes 10616836
  2.1 14.6 %copy-start.1 = (bf16[512,1152]{1,0:T(8,128)(2,1)S(1)}, bf16[512,1152]{1,0:T(8,128)(2,1)}, u32[]{:S(2)}) copy-start(bf16[512,1152]{1,0:T(8,128)(2,1)} %refs_1_.4) | copy-start | bytes 3538948
  17.1 7.5 %collective-permute-start = (bf16[80,1152]{1,0:T(8,128)(2,1)S(1)}, bf16[80,1152]{1,0:T(8,128)(2,1)S(1)}, u32[]{:S(2)}, u32[]{:S(2)}) collective-permute-start(bf16[80,1152]{1,0:T(8,128)(2,1)S(1)} %get-tuple-element.29.refs_3_), channel_id=1, source_target_pairs={{0,8},{2,10},{8,12},{10,14},{12,4},{14,6},{4,0},{6,2},{1,9},{3,11}... | collective-permute-start | bytes 552968 | tf_op jit(solution)/shard_map/ppermute | solution.py:105
  17.7 10.5 %collective-permute-start.1 = (bf16[80,1152]{1,0:T(8,128)(2,1)S(1)}, bf16[80,1152]{1,0:T(8,128)(2,1)S(1)}, u32[]{:S(2)}, u32[]{:S(2)}) collective-permute-start(bf16[80,1152]{1,0:T(8,128)(2,1)S(1)} %get-tuple-element.30), channel_id=1, source_target_pairs={{0,10},{2,8},{8,14},{10,12},{12,6},{14,4},{4,2},{6,0},{1,11},{3,9}... | collective-permute-start | bytes 552968 | tf_op jit(solution)/shard_map/ppermute | solution.py:105
  19.2 0.7 %copy-start.2 = (s32[1,4,4]{2,1,0:T(4,128)S(1)}, s32[1,4,4]{2,1,0:T(4,128)}, u32[]{:S(2)}) copy-start(s32[1,4,4]{2,1,0:T(4,128)} %refs_1_.5) | copy-start | bytes 196
  21.8 9.0 %collective-permute-start.4 = (bf16[80,1152]{1,0:T(8,128)(2,1)S(1)}, bf16[80,1152]{1,0:T(8,128)(2,1)S(1)}, u32[]{:S(2)}, u32[]{:S(2)}) collective-permute-start(bf16[80,1152]{1,0:T(8,128)(2,1)S(1)} %get-tuple-element.31), channel_id=1, source_target_pairs={{0,2},{2,0},{1,3},{3,1},{4,6},{6,4},{5,7},{7,5},{8,10},{10,8},{9,1... | collective-permute-start | bytes 552968 | tf_op jit(solution)/shard_map/ppermute | solution.py:89
  24.6 8.0 %collective-permute-start.2 = (bf16[80,1152]{1,0:T(8,128)(2,1)S(1)}, bf16[80,1152]{1,0:T(8,128)(2,1)S(1)}, u32[]{:S(2)}, u32[]{:S(2)}) collective-permute-start(bf16[80,1152]{1,0:T(8,128)(2,1)S(1)} %collective-permute-done.refs_4_), channel_id=1, source_target_pairs={{0,8},{8,12},{12,4},{4,0},{1,9},{9,13},{13,5},{5,1},{2,10},{10,14}... | collective-permute-start | bytes 552968 | tf_op jit(solution)/shard_map/ppermute | solution.py:102
  28.1 8.3 %collective-permute-start.3 = (bf16[80,1152]{1,0:T(8,128)(2,1)S(1)}, bf16[80,1152]{1,0:T(8,128)(2,1)S(1)}, u32[]{:S(2)}, u32[]{:S(2)}) collective-permute-start(bf16[80,1152]{1,0:T(8,128)(2,1)S(1)} %collective-permute-done.1.refs_5_), channel_id=1, source_target_pairs={{0,8},{8,12},{12,4},{4,0},{1,9},{9,13},{13,5},{5,1},{2,10},{10,14}... | collective-permute-start | bytes 552968 | tf_op jit(solution)/shard_map/ppermute | solution.py:102
  28.7 8.4 %collective-permute-start.5 = (bf16[80,1152]{1,0:T(8,128)(2,1)S(1)}, bf16[80,1152]{1,0:T(8,128)(2,1)S(1)}, u32[]{:S(2)}, u32[]{:S(2)}) collective-permute-start(bf16[80,1152]{1,0:T(8,128)(2,1)S(1)} %get-tuple-element.32), channel_id=1, source_target_pairs={{0,2},{2,0},{1,3},{3,1},{4,6},{6,4},{5,7},{7,5},{8,10},{10,8},{9,1... | collective-permute-start | bytes 552968 | tf_op jit(solution)/shard_map/ppermute | solution.py:89
  30.6 8.2 %collective-permute-start.6 = (bf16[80,1152]{1,0:T(8,128)(2,1)S(1)}, bf16[80,1152]{1,0:T(8,128)(2,1)S(1)}, u32[]{:S(2)}, u32[]{:S(2)}) collective-permute-start(bf16[80,1152]{1,0:T(8,128)(2,1)S(1)} %get-tuple-element.33), channel_id=1, source_target_pairs={{0,2},{2,0},{1,3},{3,1},{4,6},{6,4},{5,7},{7,5},{8,10},{10,8},{9,1... | collective-permute-start | bytes 552968 | tf_op jit(solution)/shard_map/ppermute | solution.py:89
  30.8 10.0 %collective-permute-start.7 = (bf16[80,1152]{1,0:T(8,128)(2,1)S(1)}, bf16[80,1152]{1,0:T(8,128)(2,1)S(1)}, u32[]{:S(2)}, u32[]{:S(2)}) collective-permute-start(bf16[80,1152]{1,0:T(8,128)(2,1)S(1)} %get-tuple-element.30), channel_id=1, source_target_pairs={{0,2},{2,0},{1,3},{3,1},{4,6},{6,4},{5,7},{7,5},{8,10},{10,8},{9,1... | collective-permute-start | bytes 552968 | tf_op jit(solution)/shard_map/ppermute | solution.py:89
  32.6 8.1 %collective-permute-start.8 = (bf16[80,1152]{1,0:T(8,128)(2,1)S(1)}, bf16[80,1152]{1,0:T(8,128)(2,1)S(1)}, u32[]{:S(2)}, u32[]{:S(2)}) collective-permute-start(bf16[80,1152]{1,0:T(8,128)(2,1)S(1)} %collective-permute-done.2.refs_6_), channel_id=1, source_target_pairs={{0,8},{8,12},{12,4},{4,0},{1,9},{9,13},{13,5},{5,1},{2,10},{10,14}... | collective-permute-start | bytes 552968 | tf_op jit(solution)/shard_map/ppermute | solution.py:102
  36.5 5.5 %collective-permute-start.9 = (bf16[80,1152]{1,0:T(8,128)(2,1)S(1)}, bf16[80,1152]{1,0:T(8,128)(2,1)S(1)}, u32[]{:S(2)}, u32[]{:S(2)}) collective-permute-start(bf16[80,1152]{1,0:T(8,128)(2,1)S(1)} %collective-permute-done.3.refs_7_), channel_id=1, source_target_pairs={{0,8},{8,12},{12,4},{4,0},{1,9},{9,13},{13,5},{5,1},{2,10},{10,14}... | collective-permute-start | bytes 552968 | tf_op jit(solution)/shard_map/ppermute | solution.py:102
  38.8 15.9 %copy-start.3 = (s32[1,128]{1,0:T(1,128)S(1)}, s32[1,128]{1,0:T(1,128)}, u32[]{:S(2)}) copy-start(s32[1,128]{1,0:T(1,128)} %refs_3_.1) | copy-start | bytes 1540
  43.0 1.4 %collective-permute-start.10 = (f32[56,512]{1,0:T(8,128)S(1)}, f32[56,512]{1,0:T(8,128)S(1)}, u32[]{:S(2)}, u32[]{:S(2)}) collective-permute-start(f32[56,512]{1,0:T(8,128)S(1)} %get-tuple-element.37), channel_id=1, source_target_pairs={{0,1},{1,0},{2,3},{3,2},{4,5},{5,4},{6,7},{7,6},{8,9},{9,8},{10,11... | collective-permute-start | bytes 344072 | tf_op jit(solution)/shard_map/ppermute | solution.py:89
  44.4 7.8 %collective-permute-start.11 = (bf16[56,512]{1,0:T(8,128)(2,1)S(1)}, bf16[56,512]{1,0:T(8,128)(2,1)S(1)}, u32[]{:S(2)}, u32[]{:S(2)}) collective-permute-start(bf16[56,512]{1,0:T(8,128)(2,1)S(1)} %add_convert_fusion.refs_4_), channel_id=1, source_target_pairs={{0,8},{4,12},{8,0},{12,4},{1,9},{5,13},{9,1},{13,5},{2,10},{6,14},... | collective-permute-start | bytes 172040 | tf_op jit(solution)/shard_map/ppermute | solution.py:112
  46.1 6.8 %collective-permute-start.12 = (bf16[56,512]{1,0:T(8,128)(2,1)S(1)}, bf16[56,512]{1,0:T(8,128)(2,1)S(1)}, u32[]{:S(2)}, u32[]{:S(2)}) collective-permute-start(bf16[56,512]{1,0:T(8,128)(2,1)S(1)} %add_convert_fusion.refs_4_), channel_id=1, source_target_pairs={{0,12},{4,8},{8,4},{12,0},{1,13},{5,9},{9,5},{13,1},{2,14},{6,10},... | collective-permute-start | bytes 172040 | tf_op jit(solution)/shard_map/ppermute | solution.py:112
  49.0 4.4 %collective-permute-start.13 = (bf16[56,512]{1,0:T(8,128)(2,1)S(1)}, bf16[56,512]{1,0:T(8,128)(2,1)S(1)}, u32[]{:S(2)}, u32[]{:S(2)}) collective-permute-start(bf16[56,512]{1,0:T(8,128)(2,1)S(1)} %add_convert_fusion.refs_4_), channel_id=1, source_target_pairs={{0,4},{4,0},{8,12},{12,8},{1,5},{5,1},{9,13},{13,9},{2,6},{6,2},{1... | collective-permute-start | bytes 172040 | tf_op jit(solution)/shard_map/ppermute | solution.py:112
  49.0 4.4 %collective-permute-start.14 = (bf16[56,512]{1,0:T(8,128)(2,1)S(1)}, bf16[56,512]{1,0:T(8,128)(2,1)S(1)}, u32[]{:S(2)}, u32[]{:S(2)}) collective-permute-start(bf16[56,512]{1,0:T(8,128)(2,1)S(1)} %add_convert_fusion.refs_4_), channel_id=1, source_target_pairs={{0,1},{1,0},{2,3},{3,2},{4,5},{5,4},{6,7},{7,6},{8,9},{9,8},{10,11... | collective-permute-start | bytes 172040 | tf_op jit(solution)/shard_map/ppermute | solution.py:89
  52.2 1.2 %collective-permute-start.15 = (bf16[56,512]{1,0:T(8,128)(2,1)S(1)}, bf16[56,512]{1,0:T(8,128)(2,1)S(1)}, u32[]{:S(2)}, u32[]{:S(2)}) collective-permute-start(bf16[56,512]{1,0:T(8,128)(2,1)S(1)} %collective-permute-done.11.refs_5_), channel_id=1, source_target_pairs={{0,1},{1,0},{2,3},{3,2},{4,5},{5,4},{6,7},{7,6},{8,9},{9,8},{10,11... | collective-permute-start | bytes 172040 | tf_op jit(solution)/shard_map/ppermute | solution.py:89
  52.9 1.2 %collective-permute-start.16 = (bf16[56,512]{1,0:T(8,128)(2,1)S(1)}, bf16[56,512]{1,0:T(8,128)(2,1)S(1)}, u32[]{:S(2)}, u32[]{:S(2)}) collective-permute-start(bf16[56,512]{1,0:T(8,128)(2,1)S(1)} %collective-permute-done.12.refs_6_), channel_id=1, source_target_pairs={{0,1},{1,0},{2,3},{3,2},{4,5},{5,4},{6,7},{7,6},{8,9},{9,8},{10,11... | collective-permute-start | bytes 172040 | tf_op jit(solution)/shard_map/ppermute | solution.py:89
  53.4 1.2 %collective-permute-start.17 = (bf16[56,512]{1,0:T(8,128)(2,1)S(1)}, bf16[56,512]{1,0:T(8,128)(2,1)S(1)}, u32[]{:S(2)}, u32[]{:S(2)}) collective-permute-start(bf16[56,512]{1,0:T(8,128)(2,1)S(1)} %collective-permute-done.13.refs_7_), channel_id=1, source_target_pairs={{0,1},{1,0},{2,3},{3,2},{4,5},{5,4},{6,7},{7,6},{8,9},{9,8},{10,11... | collective-permute-start | bytes 172040 | tf_op jit(solution)/shard_map/ppermute | solution.py:89

commit v20 on v15

--- a/solution.py
+++ b/solution.py
@@ -181,15 +181,14 @@
         return feat.astype(F32), pos.astype(F32), lax.axis_index("rep").astype(F32)
 
     def pack(ids, vals):
-        one = jnp.concatenate([ids(0).astype(F32), vals(0)], axis=0)
+        one = jnp.concatenate([ids[0].astype(F32), vals[0]], axis=0)
         one = jnp.concatenate([one, jnp.zeros((2 * positions, LANES - kslots), F32)], axis=1)
         return (jnp.broadcast_to(one, (holders,) + one.shape),)
 
     (packed,) = on_core(
         pack,
-        [],
+        [active_ids, active_vals],
         [shape(holders, 2 * positions, LANES)],
-        streams=[active_ids, active_vals],
         room=60,
     )
     lists = lax.all_to_all(packed, ("feat", "pos"), split_axis=0, concat_axis=0, tiled=True)
@@ -446,11 +445,7 @@
         current = (iota((wide, panel), 0) == targets).astype(F32)
         accum = jnp.zeros((wide, panel), F32)
         for _ in range(ITERS):
-            scaled = current * scale
-            high = part(scaled, small)
-            low = part(scaled - high.astype(F32), small)
-            both = dot(magnitude, jnp.concatenate([high, low], axis=1))
-            current = both[:, :panel] + both[:, panel:]
+            current = dot(magnitude, (current * scale).astype(BF16))
             accum = accum + current
         influence = accum[:result_rows]
         for f in range(feats):

time: 57.4 us -> 57.4 us (level)
  no operation moved by 1% of the time
where the time goes in v20:
time: 57.4 us; the launch traced here: 57.1 us
  waiting for transfers between devices  17 us (30%)
  starting transfers between devices  14.9 us (26%)
  blocking collectives  14.1 us (25%)
  Pallas kernels  8.99 us (16%)
  matrix products  0.79 us (1%)
  between operations  0.74 us (1%)
  local copies, waits for them, and re-layouts  0.69 us (1%)
    all_to_all x1, blocking collectives, per_device(): lax.all_to_all(packed, ('feat', 'pos'), split_axis=0, concat_axis=0, tile...  14.1 us
    pallas_call x7, Pallas kernels, on_core(): return list(call(*args, *streams, *through))  8.99 us
    ppermute x9, starting transfers between devices, rotate(): lax.ppermute(x, axis, [(i, (i + step) % count) for i in range(count)])  5.31 us
    ppermute x9, waiting for transfers between devices, rotate(): lax.ppermute(x, axis, [(i, (i + step) % count) for i in range(count)])  4.88 us
    ppermute x3, starting transfers between devices, spread(): found[bits] = lax.ppermute(x, axis, [(i, i ^ bits) for i in range(count)])  4.6 us
    ppermute x3, waiting for transfers between devices, spread(): found[bits] = lax.ppermute(x, axis, [(i, i ^ bits) for i in range(count)])  4.39 us
    ppermute x4, waiting for transfers between devices, ring_next(): return lax.ppermute(x, axis, steps)  3.96 us
    ppermute x2, waiting for transfers between devices, ring_next(): return lax.ppermute(x, (axis, across), pairs)  3.73 us
  transfers between devices with their start and end apart: 18, of which 12 were waited for; matrix products, arithmetic and copies ran while one was open for 2% of the time, Pallas kernels for 6%

profile of v20, /device:TPU:0, one launch (start us, length us, event | category | flops | bytes accessed | tf_op | source)
XLA Modules:
  0.0 57.1 jit_solution(2905518664517438211)
XLA Ops:
  0.6 1.5 %shard_map.77 = f32[8,8,128]{2,1,0:T(8,128)} custom-call(s32[1,4,28]{2,1,0:T(4,128)} %refs_0_.1, f32[1,4,28]{2,1,0:T(4,128)} %refs_1_.3), custom_call_target="tpu_custom_call" | custom-call | tf_op jit(solution)/shard_map/pallas_call | solution.py:84
  2.1 14.1 %all_to_all.5.refs_0_ = f32[8,8,128]{2,1,0:T(8,128)S(1)} all-to-all(f32[8,8,128]{2,1,0:T(8,128)} %shard_map.77), channel_id=1, replica_groups=mesh['grp'=2,'feat'=4,'pos'=2,'rep'=2] {'feat','pos'}, dimensions={0} | all-to-all | bytes 65536 | tf_op jit(solution)/shard_map/all_to_all | solution.py:194
  17.6 0.7 %collective-permute-start.1 = (bf16[80,1152]{1,0:T(8,128)(2,1)S(1)}, bf16[80,1152]{1,0:T(8,128)(2,1)S(1)}, u32[]{:S(2)}, u32[]{:S(2)}) collective-permute-start(bf16[80,1152]{1,0:T(8,128)(2,1)S(1)} %get-tuple-element.30), channel_id=1, source_target_pairs={{0,10},{2,8},{8,14},{10,12},{12,6},{14,4},{4,2},{6,0},{1,11},{3,9}... | collective-permute-start | bytes 552968 | tf_op jit(solution)/shard_map/ppermute | solution.py:105
  18.4 0.8 %fusion = bf16[3,160,1152]{2,1,0:T(8,128)(2,1)S(1)} fusion(bf16[512,3,1152]{2,0,1:T(8,128)(2,1)S(1)} %copy-done, bf16[160,512]{1,0:T(8,128)(2,1)S(1)} %get-tuple-element.22), kind=kOutput, calls=%fused_computation.1 | convolution fusion | flops 566784000 | bytes 4808704 | tf_op jit(solution)/shard_map/dot_general | solution.py:284
  19.9 1.9 %shard_map.80 = (bf16[448,640]{1,0:T(8,128)(2,1)S(1)}, bf16[640,512]{1,0:T(8,128)(2,1)S(1)}, f32[1,640]{1,0:T(1,128)S(1)}, f32[480,1]{1,0:T(8,128)S(1)}, bf16[51...) custom-call(f32[32,28]{1,0:T(8,128)S(1)} %get-tuple-element.20.refs_, ...), custom_call_target="tpu_custom_call", output_to_operand_aliasing={{6}: (2, {}), {7}: (3, {}), {8}: (4, {})} | custom-call | flops 1 | bytes 1 | tf_op jit(solution)/shard_map/pallas_call | solution.py:84
  21.7 1.4 %collective-permute-start.4 = (bf16[80,1152]{1,0:T(8,128)(2,1)S(1)}, bf16[80,1152]{1,0:T(8,128)(2,1)S(1)}, u32[]{:S(2)}, u32[]{:S(2)}) collective-permute-start(bf16[80,1152]{1,0:T(8,128)(2,1)S(1)} %get-tuple-element.31), channel_id=1, source_target_pairs={{0,2},{2,0},{1,3},{3,1},{4,6},{6,4},{5,7},{7,5},{8,10},{10,8},{9,1... | collective-permute-start | bytes 552968 | tf_op jit(solution)/shard_map/ppermute | solution.py:89
  23.1 1.4 %collective-permute-done.refs_4_ = bf16[80,1152]{1,0:T(8,128)(2,1)S(1)} collective-permute-done((bf16[80,1152]{1,0:T(8,128)(2,1)S(1)}, bf16[80,1152]{1,0:T(8,128)(2,1)S(1)}, u32[]{:S(2)}, u32[]{:S(2)}) %collective-permute-start) | collective-permute-done | bytes 184352 | tf_op jit(solution)/shard_map/ppermute | solution.py:105
  24.6 1.2 %collective-permute-start.2 = (bf16[80,1152]{1,0:T(8,128)(2,1)S(1)}, bf16[80,1152]{1,0:T(8,128)(2,1)S(1)}, u32[]{:S(2)}, u32[]{:S(2)}) collective-permute-start(bf16[80,1152]{1,0:T(8,128)(2,1)S(1)} %collective-permute-done.refs_4_), channel_id=1, source_target_pairs={{0,8},{8,12},{12,4},{4,0},{1,9},{9,13},{13,5},{5,1},{2,10},{10,14}... | collective-permute-start | bytes 552968 | tf_op jit(solution)/shard_map/ppermute | solution.py:102
  25.8 2.3 %collective-permute-done.1.refs_5_ = bf16[80,1152]{1,0:T(8,128)(2,1)S(1)} collective-permute-done((bf16[80,1152]{1,0:T(8,128)(2,1)S(1)}, bf16[80,1152]{1,0:T(8,128)(2,1)S(1)}, u32[]{:S(2)}, u32[]{:S(2)}) %collective-permute-start.1) | collective-permute-done | bytes 184352 | tf_op jit(solution)/shard_map/ppermute | solution.py:105
  28.7 1.8 %collective-permute-start.5 = (bf16[80,1152]{1,0:T(8,128)(2,1)S(1)}, bf16[80,1152]{1,0:T(8,128)(2,1)S(1)}, u32[]{:S(2)}, u32[]{:S(2)}) collective-permute-start(bf16[80,1152]{1,0:T(8,128)(2,1)S(1)} %get-tuple-element.32), channel_id=1, source_target_pairs={{0,2},{2,0},{1,3},{3,1},{4,6},{6,4},{5,7},{7,5},{8,10},{10,8},{9,1... | collective-permute-start | bytes 552968 | tf_op jit(solution)/shard_map/ppermute | solution.py:89
  30.7 1.8 %collective-permute-start.7 = (bf16[80,1152]{1,0:T(8,128)(2,1)S(1)}, bf16[80,1152]{1,0:T(8,128)(2,1)S(1)}, u32[]{:S(2)}, u32[]{:S(2)}) collective-permute-start(bf16[80,1152]{1,0:T(8,128)(2,1)S(1)} %get-tuple-element.30), channel_id=1, source_target_pairs={{0,2},{2,0},{1,3},{3,1},{4,6},{6,4},{5,7},{7,5},{8,10},{10,8},{9,1... | collective-permute-start | bytes 552968 | tf_op jit(solution)/shard_map/ppermute | solution.py:89
  32.5 1.2 %collective-permute-start.8 = (bf16[80,1152]{1,0:T(8,128)(2,1)S(1)}, bf16[80,1152]{1,0:T(8,128)(2,1)S(1)}, u32[]{:S(2)}, u32[]{:S(2)}) collective-permute-start(bf16[80,1152]{1,0:T(8,128)(2,1)S(1)} %collective-permute-done.2.refs_6_), channel_id=1, source_target_pairs={{0,8},{8,12},{12,4},{4,0},{1,9},{9,13},{13,5},{5,1},{2,10},{10,14}... | collective-permute-start | bytes 552968 | tf_op jit(solution)/shard_map/ppermute | solution.py:102
  33.7 2.7 %collective-permute-done.3.refs_7_ = bf16[80,1152]{1,0:T(8,128)(2,1)S(1)} collective-permute-done((bf16[80,1152]{1,0:T(8,128)(2,1)S(1)}, bf16[80,1152]{1,0:T(8,128)(2,1)S(1)}, u32[]{:S(2)}, u32[]{:S(2)}) %collective-permute-start.3) | collective-permute-done | bytes 184352 | tf_op jit(solution)/shard_map/ppermute | solution.py:102
  36.4 0.7 %collective-permute-start.9 = (bf16[80,1152]{1,0:T(8,128)(2,1)S(1)}, bf16[80,1152]{1,0:T(8,128)(2,1)S(1)}, u32[]{:S(2)}, u32[]{:S(2)}) collective-permute-start(bf16[80,1152]{1,0:T(8,128)(2,1)S(1)} %collective-permute-done.3.refs_7_), channel_id=1, source_target_pairs={{0,8},{8,12},{12,4},{4,0},{1,9},{9,13},{13,5},{5,1},{2,10},{10,14}... | collective-permute-start | bytes 552968 | tf_op jit(solution)/shard_map/ppermute | solution.py:102
  37.1 1.6 %collective-permute-done.6.refs_13_ = bf16[80,1152]{1,0:T(8,128)(2,1)S(1)} collective-permute-done((bf16[80,1152]{1,0:T(8,128)(2,1)S(1)}, bf16[80,1152]{1,0:T(8,128)(2,1)S(1)}, u32[]{:S(2)}, u32[]{:S(2)}) %collective-permute-start.6) | collective-permute-done | bytes 184352 | tf_op jit(solution)/shard_map/ppermute | solution.py:89
  38.7 1.3 %shard_map.81 = (f32[160,512]{1,0:T(8,128)S(1)}, bf16[480,1152]{1,0:T(8,128)(2,1)S(1)}) custom-call(f32[1,640]{1,0:T(1,128)S(1)} %get-tuple-element.26.refs_0_, bf16[640,512]{1,0:T(8,128)(2,1)S(1)} %get-tuple-element.27.refs_1_, f32[480,1]{1,0:T(8,128)S(1)} %get-tuple-element.28.refs_2_, bf16[80,1152]{1,0:T(8,128)(2,1)S(1)} %get-tuple-element.29.refs_3_, ...), custom_call_target="tpu_custom_call" | custom-call | flops 1 | bytes 1 | tf_op jit(solution)/shard_map/pallas_call | solution.py:84
  40.0 0.7 %collective-permute-done.7.refs_4_ = bf16[80,1152]{1,0:T(8,128)(2,1)S(1)} collective-permute-done((bf16[80,1152]{1,0:T(8,128)(2,1)S(1)}, bf16[80,1152]{1,0:T(8,128)(2,1)S(1)}, u32[]{:S(2)}, u32[]{:S(2)}) %collective-permute-start.7) | collective-permute-done | bytes 184352 | tf_op jit(solution)/shard_map/ppermute | solution.py:89
  40.7 1.2 %collective-permute-done.9.refs_6_ = bf16[80,1152]{1,0:T(8,128)(2,1)S(1)} collective-permute-done((bf16[80,1152]{1,0:T(8,128)(2,1)S(1)}, bf16[80,1152]{1,0:T(8,128)(2,1)S(1)}, u32[]{:S(2)}, u32[]{:S(2)}) %collective-permute-start.9) | collective-permute-done | bytes 184352 | tf_op jit(solution)/shard_map/ppermute | solution.py:102
  41.9 1.0 %shard_map.82 = (f32[56,512]{1,0:T(8,128)S(1)}, f32[56,512]{1,0:T(8,128)S(1)}) custom-call(f32[1,640]{1,0:T(1,128)S(1)} %get-tuple-element.26.refs_0_, bf16[640,512]{1,0:T(8,128)(2,1)S(1)} %get-tuple-element.27.refs_1_, f32[160,512]{1,0:T(8,128)S(1)} %get-tuple-element.34.refs_2_, bf16[480,1152]{1,0:T(8,128)(2,1)S(1)} %get-tuple-element.35.refs_3_, ...), custom_call_target="tpu_custom_call" | custom-call | tf_op jit(solution)/shard_map/pallas_call | solution.py:84
  43.0 1.3 %collective-permute-done.10 = f32[56,512]{1,0:T(8,128)S(1)} collective-permute-done((f32[56,512]{1,0:T(8,128)S(1)}, f32[56,512]{1,0:T(8,128)S(1)}, u32[]{:S(2)}, u32[]{:S(2)}) %collective-permute-start.10) | collective-permute-done | bytes 114720 | tf_op jit(solution)/shard_map/ppermute | solution.py:89
  44.3 1.7 %collective-permute-start.11 = (bf16[56,512]{1,0:T(8,128)(2,1)S(1)}, bf16[56,512]{1,0:T(8,128)(2,1)S(1)}, u32[]{:S(2)}, u32[]{:S(2)}) collective-permute-start(bf16[56,512]{1,0:T(8,128)(2,1)S(1)} %add_convert_fusion.refs_4_), channel_id=1, source_target_pairs={{0,8},{4,12},{8,0},{12,4},{1,9},{5,13},{9,1},{13,5},{2,10},{6,14},... | collective-permute-start | bytes 172040 | tf_op jit(solution)/shard_map/ppermute | solution.py:112
  46.0 2.9 %collective-permute-start.12 = (bf16[56,512]{1,0:T(8,128)(2,1)S(1)}, bf16[56,512]{1,0:T(8,128)(2,1)S(1)}, u32[]{:S(2)}, u32[]{:S(2)}) collective-permute-start(bf16[56,512]{1,0:T(8,128)(2,1)S(1)} %add_convert_fusion.refs_4_), channel_id=1, source_target_pairs={{0,12},{4,8},{8,4},{12,0},{1,13},{5,9},{9,5},{13,1},{2,14},{6,10},... | collective-permute-start | bytes 172040 | tf_op jit(solution)/shard_map/ppermute | solution.py:112
  48.9 3.2 %collective-permute-done.11.refs_5_ = bf16[56,512]{1,0:T(8,128)(2,1)S(1)} collective-permute-done((bf16[56,512]{1,0:T(8,128)(2,1)S(1)}, bf16[56,512]{1,0:T(8,128)(2,1)S(1)}, u32[]{:S(2)}, u32[]{:S(2)}) %collective-permute-start.11) | collective-permute-done | bytes 57376 | tf_op jit(solution)/shard_map/ppermute | solution.py:112
  54.6 2.5 %shard_map.83 = (bf16[1,56,448]{2,1,0:T(8,128)(2,1)}, f32[1,56,128]{2,1,0:T(8,128)}) custom-call(bf16[448,640]{1,0:T(8,128)(2,1)S(1)} %get-tuple-element.23.refs_0_, bf16[512,512]{1,0:T(8,128)(2,1)S(1)} %get-tuple-element.24.refs_1_, bf16[512,448]{1,0:T(8,128)(2,1)S(1)} %get-tuple-element.25.refs_2_, s32[1,128]{1,0:T(1,128)S(1)} %copy-done.3, ...), custom_call_target="tpu_custom_call" | custom-call | tf_op jit(solution)/shard_map/pallas_call | solution.py:84
  (31 shorter events, 5.5 us)
Async XLA Ops:
  0.6 17.8 %copy-start = (bf16[512,3,1152]{2,0,1:T(8,128)(2,1)S(1)}, bf16[512,3,1152]{2,0,1:T(8,128)(2,1)}, u32[]{:S(2)}) copy-start(bf16[512,3,1152]{2,0,1:T(8,128)(2,1)} %param.11) | copy-start | bytes 10616836
  2.1 14.6 %copy-start.1 = (bf16[512,1152]{1,0:T(8,128)(2,1)S(1)}, bf16[512,1152]{1,0:T(8,128)(2,1)}, u32[]{:S(2)}) copy-start(bf16[512,1152]{1,0:T(8,128)(2,1)} %refs_1_.4) | copy-start | bytes 3538948
  17.1 7.5 %collective-permute-start = (bf16[80,1152]{1,0:T(8,128)(2,1)S(1)}, bf16[80,1152]{1,0:T(8,128)(2,1)S(1)}, u32[]{:S(2)}, u32[]{:S(2)}) collective-permute-start(bf16[80,1152]{1,0:T(8,128)(2,1)S(1)} %get-tuple-element.29.refs_3_), channel_id=1, source_target_pairs={{0,8},{2,10},{8,12},{10,14},{12,4},{14,6},{4,0},{6,2},{1,9},{3,11}... | collective-permute-start | bytes 552968 | tf_op jit(solution)/shard_map/ppermute | solution.py:105
  17.6 10.4 %collective-permute-start.1 = (bf16[80,1152]{1,0:T(8,128)(2,1)S(1)}, bf16[80,1152]{1,0:T(8,128)(2,1)S(1)}, u32[]{:S(2)}, u32[]{:S(2)}) collective-permute-start(bf16[80,1152]{1,0:T(8,128)(2,1)S(1)} %get-tuple-element.30), channel_id=1, source_target_pairs={{0,10},{2,8},{8,14},{10,12},{12,6},{14,4},{4,2},{6,0},{1,11},{3,9}... | collective-permute-start | bytes 552968 | tf_op jit(solution)/shard_map/ppermute | solution.py:105
  19.2 0.7 %copy-start.2 = (s32[1,4,4]{2,1,0:T(4,128)S(1)}, s32[1,4,4]{2,1,0:T(4,128)}, u32[]{:S(2)}) copy-start(s32[1,4,4]{2,1,0:T(4,128)} %refs_1_.5) | copy-start | bytes 196
  21.7 9.0 %collective-permute-start.4 = (bf16[80,1152]{1,0:T(8,128)(2,1)S(1)}, bf16[80,1152]{1,0:T(8,128)(2,1)S(1)}, u32[]{:S(2)}, u32[]{:S(2)}) collective-permute-start(bf16[80,1152]{1,0:T(8,128)(2,1)S(1)} %get-tuple-element.31), channel_id=1, source_target_pairs={{0,2},{2,0},{1,3},{3,1},{4,6},{6,4},{5,7},{7,5},{8,10},{10,8},{9,1... | collective-permute-start | bytes 552968 | tf_op jit(solution)/shard_map/ppermute | solution.py:89
  24.6 7.9 %collective-permute-start.2 = (bf16[80,1152]{1,0:T(8,128)(2,1)S(1)}, bf16[80,1152]{1,0:T(8,128)(2,1)S(1)}, u32[]{:S(2)}, u32[]{:S(2)}) collective-permute-start(bf16[80,1152]{1,0:T(8,128)(2,1)S(1)} %collective-permute-done.refs_4_), channel_id=1, source_target_pairs={{0,8},{8,12},{12,4},{4,0},{1,9},{9,13},{13,5},{5,1},{2,10},{10,14}... | collective-permute-start | bytes 552968 | tf_op jit(solution)/shard_map/ppermute | solution.py:102
  28.1 8.3 %collective-permute-start.3 = (bf16[80,1152]{1,0:T(8,128)(2,1)S(1)}, bf16[80,1152]{1,0:T(8,128)(2,1)S(1)}, u32[]{:S(2)}, u32[]{:S(2)}) collective-permute-start(bf16[80,1152]{1,0:T(8,128)(2,1)S(1)} %collective-permute-done.1.refs_5_), channel_id=1, source_target_pairs={{0,8},{8,12},{12,4},{4,0},{1,9},{9,13},{13,5},{5,1},{2,10},{10,14}... | collective-permute-start | bytes 552968 | tf_op jit(solution)/shard_map/ppermute | solution.py:102
  28.7 8.4 %collective-permute-start.5 = (bf16[80,1152]{1,0:T(8,128)(2,1)S(1)}, bf16[80,1152]{1,0:T(8,128)(2,1)S(1)}, u32[]{:S(2)}, u32[]{:S(2)}) collective-permute-start(bf16[80,1152]{1,0:T(8,128)(2,1)S(1)} %get-tuple-element.32), channel_id=1, source_target_pairs={{0,2},{2,0},{1,3},{3,1},{4,6},{6,4},{5,7},{7,5},{8,10},{10,8},{9,1... | collective-permute-start | bytes 552968 | tf_op jit(solution)/shard_map/ppermute | solution.py:89
  30.5 8.3 %collective-permute-start.6 = (bf16[80,1152]{1,0:T(8,128)(2,1)S(1)}, bf16[80,1152]{1,0:T(8,128)(2,1)S(1)}, u32[]{:S(2)}, u32[]{:S(2)}) collective-permute-start(bf16[80,1152]{1,0:T(8,128)(2,1)S(1)} %get-tuple-element.33), channel_id=1, source_target_pairs={{0,2},{2,0},{1,3},{3,1},{4,6},{6,4},{5,7},{7,5},{8,10},{10,8},{9,1... | collective-permute-start | bytes 552968 | tf_op jit(solution)/shard_map/ppermute | solution.py:89
  30.7 10.0 %collective-permute-start.7 = (bf16[80,1152]{1,0:T(8,128)(2,1)S(1)}, bf16[80,1152]{1,0:T(8,128)(2,1)S(1)}, u32[]{:S(2)}, u32[]{:S(2)}) collective-permute-start(bf16[80,1152]{1,0:T(8,128)(2,1)S(1)} %get-tuple-element.30), channel_id=1, source_target_pairs={{0,2},{2,0},{1,3},{3,1},{4,6},{6,4},{5,7},{7,5},{8,10},{10,8},{9,1... | collective-permute-start | bytes 552968 | tf_op jit(solution)/shard_map/ppermute | solution.py:89
  32.5 8.2 %collective-permute-start.8 = (bf16[80,1152]{1,0:T(8,128)(2,1)S(1)}, bf16[80,1152]{1,0:T(8,128)(2,1)S(1)}, u32[]{:S(2)}, u32[]{:S(2)}) collective-permute-start(bf16[80,1152]{1,0:T(8,128)(2,1)S(1)} %collective-permute-done.2.refs_6_), channel_id=1, source_target_pairs={{0,8},{8,12},{12,4},{4,0},{1,9},{9,13},{13,5},{5,1},{2,10},{10,14}... | collective-permute-start | bytes 552968 | tf_op jit(solution)/shard_map/ppermute | solution.py:102
  36.4 5.5 %collective-permute-start.9 = (bf16[80,1152]{1,0:T(8,128)(2,1)S(1)}, bf16[80,1152]{1,0:T(8,128)(2,1)S(1)}, u32[]{:S(2)}, u32[]{:S(2)}) collective-permute-start(bf16[80,1152]{1,0:T(8,128)(2,1)S(1)} %collective-permute-done.3.refs_7_), channel_id=1, source_target_pairs={{0,8},{8,12},{12,4},{4,0},{1,9},{9,13},{13,5},{5,1},{2,10},{10,14}... | collective-permute-start | bytes 552968 | tf_op jit(solution)/shard_map/ppermute | solution.py:102
  38.7 15.9 %copy-start.3 = (s32[1,128]{1,0:T(1,128)S(1)}, s32[1,128]{1,0:T(1,128)}, u32[]{:S(2)}) copy-start(s32[1,128]{1,0:T(1,128)} %refs_3_.1) | copy-start | bytes 1540
  42.9 1.4 %collective-permute-start.10 = (f32[56,512]{1,0:T(8,128)S(1)}, f32[56,512]{1,0:T(8,128)S(1)}, u32[]{:S(2)}, u32[]{:S(2)}) collective-permute-start(f32[56,512]{1,0:T(8,128)S(1)} %get-tuple-element.37), channel_id=1, source_target_pairs={{0,1},{1,0},{2,3},{3,2},{4,5},{5,4},{6,7},{7,6},{8,9},{9,8},{10,11... | collective-permute-start | bytes 344072 | tf_op jit(solution)/shard_map/ppermute | solution.py:89
  44.3 7.8 %collective-permute-start.11 = (bf16[56,512]{1,0:T(8,128)(2,1)S(1)}, bf16[56,512]{1,0:T(8,128)(2,1)S(1)}, u32[]{:S(2)}, u32[]{:S(2)}) collective-permute-start(bf16[56,512]{1,0:T(8,128)(2,1)S(1)} %add_convert_fusion.refs_4_), channel_id=1, source_target_pairs={{0,8},{4,12},{8,0},{12,4},{1,9},{5,13},{9,1},{13,5},{2,10},{6,14},... | collective-permute-start | bytes 172040 | tf_op jit(solution)/shard_map/ppermute | solution.py:112
  46.0 6.8 %collective-permute-start.12 = (bf16[56,512]{1,0:T(8,128)(2,1)S(1)}, bf16[56,512]{1,0:T(8,128)(2,1)S(1)}, u32[]{:S(2)}, u32[]{:S(2)}) collective-permute-start(bf16[56,512]{1,0:T(8,128)(2,1)S(1)} %add_convert_fusion.refs_4_), channel_id=1, source_target_pairs={{0,12},{4,8},{8,4},{12,0},{1,13},{5,9},{9,5},{13,1},{2,14},{6,10},... | collective-permute-start | bytes 172040 | tf_op jit(solution)/shard_map/ppermute | solution.py:112
  48.9 4.4 %collective-permute-start.13 = (bf16[56,512]{1,0:T(8,128)(2,1)S(1)}, bf16[56,512]{1,0:T(8,128)(2,1)S(1)}, u32[]{:S(2)}, u32[]{:S(2)}) collective-permute-start(bf16[56,512]{1,0:T(8,128)(2,1)S(1)} %add_convert_fusion.refs_4_), channel_id=1, source_target_pairs={{0,4},{4,0},{8,12},{12,8},{1,5},{5,1},{9,13},{13,9},{2,6},{6,2},{1... | collective-permute-start | bytes 172040 | tf_op jit(solution)/shard_map/ppermute | solution.py:112
  48.9 4.4 %collective-permute-start.14 = (bf16[56,512]{1,0:T(8,128)(2,1)S(1)}, bf16[56,512]{1,0:T(8,128)(2,1)S(1)}, u32[]{:S(2)}, u32[]{:S(2)}) collective-permute-start(bf16[56,512]{1,0:T(8,128)(2,1)S(1)} %add_convert_fusion.refs_4_), channel_id=1, source_target_pairs={{0,1},{1,0},{2,3},{3,2},{4,5},{5,4},{6,7},{7,6},{8,9},{9,8},{10,11... | collective-permute-start | bytes 172040 | tf_op jit(solution)/shard_map/ppermute | solution.py:89
  52.1 1.2 %collective-permute-start.15 = (bf16[56,512]{1,0:T(8,128)(2,1)S(1)}, bf16[56,512]{1,0:T(8,128)(2,1)S(1)}, u32[]{:S(2)}, u32[]{:S(2)}) collective-permute-start(bf16[56,512]{1,0:T(8,128)(2,1)S(1)} %collective-permute-done.11.refs_5_), channel_id=1, source_target_pairs={{0,1},{1,0},{2,3},{3,2},{4,5},{5,4},{6,7},{7,6},{8,9},{9,8},{10,11... | collective-permute-start | bytes 172040 | tf_op jit(solution)/shard_map/ppermute | solution.py:89
  52.8 1.2 %collective-permute-start.16 = (bf16[56,512]{1,0:T(8,128)(2,1)S(1)}, bf16[56,512]{1,0:T(8,128)(2,1)S(1)}, u32[]{:S(2)}, u32[]{:S(2)}) collective-permute-start(bf16[56,512]{1,0:T(8,128)(2,1)S(1)} %collective-permute-done.12.refs_6_), channel_id=1, source_target_pairs={{0,1},{1,0},{2,3},{3,2},{4,5},{5,4},{6,7},{7,6},{8,9},{9,8},{10,11... | collective-permute-start | bytes 172040 | tf_op jit(solution)/shard_map/ppermute | solution.py:89
  53.3 1.2 %collective-permute-start.17 = (bf16[56,512]{1,0:T(8,128)(2,1)S(1)}, bf16[56,512]{1,0:T(8,128)(2,1)S(1)}, u32[]{:S(2)}, u32[]{:S(2)}) collective-permute-start(bf16[56,512]{1,0:T(8,128)(2,1)S(1)} %collective-permute-done.13.refs_7_), channel_id=1, source_target_pairs={{0,1},{1,0},{2,3},{3,2},{4,5},{5,4},{6,7},{7,6},{8,9},{9,8},{10,11... | collective-permute-start | bytes 172040 | tf_op jit(solution)/shard_map/ppermute | solution.py:89

commit v21 on v15

--- a/solution.py
+++ b/solution.py
@@ -108,7 +108,7 @@
 def spread(x, axis):
     count = lax.axis_size(axis)
     found = {0: x}
-    for bits in sorted(range(1, count), key=lambda bits: bits < count // 2):
+    for bits in range(count - 1, 0, -1):
         found[bits] = lax.ppermute(x, axis, [(i, i ^ bits) for i in range(count)])
     return list(found.items())
 

time: 57.4 us -> 57.9 us (level)
  transfers between devices with their start and end apart: 18 -> 18, of which waited for: 12 -> 11; matrix products, arithmetic and copies ran while one was open for 2% -> 2% of each run, Pallas kernels for 6% -> 5%
where the time goes in v21:
time: 57.9 us; the launch traced here: 57.6 us
  waiting for transfers between devices  17.1 us (30%)
  starting transfers between devices  15.2 us (26%)
  blocking collectives  14.1 us (24%)
  Pallas kernels  8.94 us (15%)
  matrix products  0.8 us (1%)
  between operations  0.75 us (1%)
  local copies, waits for them, and re-layouts  0.69 us (1%)
    all_to_all x1, blocking collectives, per_device(): lax.all_to_all(packed, ('feat', 'pos'), split_axis=0, concat_axis=0, tile...  14.1 us
    pallas_call x7, Pallas kernels, on_core(): return list(call(*args, *streams, *through))  8.94 us
    ppermute x9, starting transfers between devices, rotate(): lax.ppermute(x, axis, [(i, (i + step) % count) for i in range(count)])  5.83 us
    ppermute x3, waiting for transfers between devices, spread(): found[bits] = lax.ppermute(x, axis, [(i, i ^ bits) for i in range(count)])  4.89 us
    ppermute x9, waiting for transfers between devices, rotate(): lax.ppermute(x, axis, [(i, (i + step) % count) for i in range(count)])  4.53 us
    ppermute x3, starting transfers between devices, spread(): found[bits] = lax.ppermute(x, axis, [(i, i ^ bits) for i in range(count)])  4.45 us
    ppermute x4, waiting for transfers between devices, ring_next(): return lax.ppermute(x, axis, steps)  3.97 us
    ppermute x2, waiting for transfers between devices, ring_next(): return lax.ppermute(x, (axis, across), pairs)  3.73 us
  transfers between devices with their start and end apart: 18, of which 11 were waited for; matrix products, arithmetic and copies ran while one was open for 2% of the time, Pallas kernels for 5%

profile of v21, /device:TPU:0, one launch (start us, length us, event | category | flops | bytes accessed | tf_op | source)
XLA Modules:
  0.0 57.6 jit_solution(16242657372229116587)
XLA Ops:
  0.6 1.5 %shard_map.77 = f32[8,8,128]{2,1,0:T(8,128)} custom-call(s32[1,4,28]{2,1,0:T(4,128)} %refs_0_.1, f32[1,4,28]{2,1,0:T(4,128)} %refs_1_.3), custom_call_target="tpu_custom_call" | custom-call | tf_op jit(solution)/shard_map/pallas_call | solution.py:84
  2.1 14.1 %all_to_all.5.refs_0_ = f32[8,8,128]{2,1,0:T(8,128)S(1)} all-to-all(f32[8,8,128]{2,1,0:T(8,128)} %shard_map.77), channel_id=1, replica_groups=mesh['grp'=2,'feat'=4,'pos'=2,'rep'=2] {'feat','pos'}, dimensions={0} | all-to-all | bytes 65536 | tf_op jit(solution)/shard_map/all_to_all | solution.py:195
  17.7 0.7 %collective-permute-start.1 = (bf16[80,1152]{1,0:T(8,128)(2,1)S(1)}, bf16[80,1152]{1,0:T(8,128)(2,1)S(1)}, u32[]{:S(2)}, u32[]{:S(2)}) collective-permute-start(bf16[80,1152]{1,0:T(8,128)(2,1)S(1)} %get-tuple-element.30), channel_id=1, source_target_pairs={{0,10},{2,8},{8,14},{10,12},{12,6},{14,4},{4,2},{6,0},{1,11},{3,9}... | collective-permute-start | bytes 552968 | tf_op jit(solution)/shard_map/ppermute | solution.py:105
  18.4 0.8 %fusion = bf16[3,160,1152]{2,1,0:T(8,128)(2,1)S(1)} fusion(bf16[512,3,1152]{2,0,1:T(8,128)(2,1)S(1)} %copy-done, bf16[160,512]{1,0:T(8,128)(2,1)S(1)} %get-tuple-element.22), kind=kOutput, calls=%fused_computation.1 | convolution fusion | flops 566784000 | bytes 4808704 | tf_op jit(solution)/shard_map/dot_general | solution.py:285
  19.9 1.9 %shard_map.80 = (bf16[448,640]{1,0:T(8,128)(2,1)S(1)}, bf16[640,512]{1,0:T(8,128)(2,1)S(1)}, f32[1,640]{1,0:T(1,128)S(1)}, f32[480,1]{1,0:T(8,128)S(1)}, bf16[51...) custom-call(f32[32,28]{1,0:T(8,128)S(1)} %get-tuple-element.20.refs_, ...), custom_call_target="tpu_custom_call", output_to_operand_aliasing={{6}: (2, {}), {7}: (3, {}), {8}: (4, {})} | custom-call | flops 1 | bytes 1 | tf_op jit(solution)/shard_map/pallas_call | solution.py:84
  21.8 1.4 %collective-permute-start.4 = (bf16[80,1152]{1,0:T(8,128)(2,1)S(1)}, bf16[80,1152]{1,0:T(8,128)(2,1)S(1)}, u32[]{:S(2)}, u32[]{:S(2)}) collective-permute-start(bf16[80,1152]{1,0:T(8,128)(2,1)S(1)} %get-tuple-element.31), channel_id=1, source_target_pairs={{0,2},{2,0},{1,3},{3,1},{4,6},{6,4},{5,7},{7,5},{8,10},{10,8},{9,1... | collective-permute-start | bytes 552968 | tf_op jit(solution)/shard_map/ppermute | solution.py:89
  23.2 1.4 %collective-permute-done.refs_4_ = bf16[80,1152]{1,0:T(8,128)(2,1)S(1)} collective-permute-done((bf16[80,1152]{1,0:T(8,128)(2,1)S(1)}, bf16[80,1152]{1,0:T(8,128)(2,1)S(1)}, u32[]{:S(2)}, u32[]{:S(2)}) %collective-permute-start) | collective-permute-done | bytes 184352 | tf_op jit(solution)/shard_map/ppermute | solution.py:105
  24.6 1.2 %collective-permute-start.2 = (bf16[80,1152]{1,0:T(8,128)(2,1)S(1)}, bf16[80,1152]{1,0:T(8,128)(2,1)S(1)}, u32[]{:S(2)}, u32[]{:S(2)}) collective-permute-start(bf16[80,1152]{1,0:T(8,128)(2,1)S(1)} %collective-permute-done.refs_4_), channel_id=1, source_target_pairs={{0,8},{8,12},{12,4},{4,0},{1,9},{9,13},{13,5},{5,1},{2,10},{10,14}... | collective-permute-start | bytes 552968 | tf_op jit(solution)/shard_map/ppermute | solution.py:102
  25.8 2.3 %collective-permute-done.1.refs_5_ = bf16[80,1152]{1,0:T(8,128)(2,1)S(1)} collective-permute-done((bf16[80,1152]{1,0:T(8,128)(2,1)S(1)}, bf16[80,1152]{1,0:T(8,128)(2,1)S(1)}, u32[]{:S(2)}, u32[]{:S(2)}) %collective-permute-start.1) | collective-permute-done | bytes 184352 | tf_op jit(solution)/shard_map/ppermute | solution.py:105
  28.7 1.8 %collective-permute-start.5 = (bf16[80,1152]{1,0:T(8,128)(2,1)S(1)}, bf16[80,1152]{1,0:T(8,128)(2,1)S(1)}, u32[]{:S(2)}, u32[]{:S(2)}) collective-permute-start(bf16[80,1152]{1,0:T(8,128)(2,1)S(1)} %get-tuple-element.32), channel_id=1, source_target_pairs={{0,2},{2,0},{1,3},{3,1},{4,6},{6,4},{5,7},{7,5},{8,10},{10,8},{9,1... | collective-permute-start | bytes 552968 | tf_op jit(solution)/shard_map/ppermute | solution.py:89
  30.7 1.8 %collective-permute-start.7 = (bf16[80,1152]{1,0:T(8,128)(2,1)S(1)}, bf16[80,1152]{1,0:T(8,128)(2,1)S(1)}, u32[]{:S(2)}, u32[]{:S(2)}) collective-permute-start(bf16[80,1152]{1,0:T(8,128)(2,1)S(1)} %get-tuple-element.30), channel_id=1, source_target_pairs={{0,2},{2,0},{1,3},{3,1},{4,6},{6,4},{5,7},{7,5},{8,10},{10,8},{9,1... | collective-permute-start | bytes 552968 | tf_op jit(solution)/shard_map/ppermute | solution.py:89
  32.6 1.2 %collective-permute-start.8 = (bf16[80,1152]{1,0:T(8,128)(2,1)S(1)}, bf16[80,1152]{1,0:T(8,128)(2,1)S(1)}, u32[]{:S(2)}, u32[]{:S(2)}) collective-permute-start(bf16[80,1152]{1,0:T(8,128)(2,1)S(1)} %collective-permute-done.2.refs_6_), channel_id=1, source_target_pairs={{0,8},{8,12},{12,4},{4,0},{1,9},{9,13},{13,5},{5,1},{2,10},{10,14}... | collective-permute-start | bytes 552968 | tf_op jit(solution)/shard_map/ppermute | solution.py:102
  33.8 2.7 %collective-permute-done.3.refs_7_ = bf16[80,1152]{1,0:T(8,128)(2,1)S(1)} collective-permute-done((bf16[80,1152]{1,0:T(8,128)(2,1)S(1)}, bf16[80,1152]{1,0:T(8,128)(2,1)S(1)}, u32[]{:S(2)}, u32[]{:S(2)}) %collective-permute-start.3) | collective-permute-done | bytes 184352 | tf_op jit(solution)/shard_map/ppermute | solution.py:102
  37.1 1.6 %collective-permute-done.6.refs_13_ = bf16[80,1152]{1,0:T(8,128)(2,1)S(1)} collective-permute-done((bf16[80,1152]{1,0:T(8,128)(2,1)S(1)}, bf16[80,1152]{1,0:T(8,128)(2,1)S(1)}, u32[]{:S(2)}, u32[]{:S(2)}) %collective-permute-start.6) | collective-permute-done | bytes 184352 | tf_op jit(solution)/shard_map/ppermute | solution.py:89
  38.8 1.3 %shard_map.81 = (f32[160,512]{1,0:T(8,128)S(1)}, bf16[480,1152]{1,0:T(8,128)(2,1)S(1)}) custom-call(f32[1,640]{1,0:T(1,128)S(1)} %get-tuple-element.26.refs_0_, bf16[640,512]{1,0:T(8,128)(2,1)S(1)} %get-tuple-element.27.refs_1_, f32[480,1]{1,0:T(8,128)S(1)} %get-tuple-element.28.refs_2_, bf16[80,1152]{1,0:T(8,128)(2,1)S(1)} %get-tuple-element.29.refs_3_, ...), custom_call_target="tpu_custom_call" | custom-call | flops 1 | bytes 1 | tf_op jit(solution)/shard_map/pallas_call | solution.py:84
  40.8 1.3 %collective-permute-done.9.refs_6_ = bf16[80,1152]{1,0:T(8,128)(2,1)S(1)} collective-permute-done((bf16[80,1152]{1,0:T(8,128)(2,1)S(1)}, bf16[80,1152]{1,0:T(8,128)(2,1)S(1)}, u32[]{:S(2)}, u32[]{:S(2)}) %collective-permute-start.9) | collective-permute-done | bytes 184352 | tf_op jit(solution)/shard_map/ppermute | solution.py:102
  42.0 1.0 %shard_map.82 = (f32[56,512]{1,0:T(8,128)S(1)}, f32[56,512]{1,0:T(8,128)S(1)}) custom-call(f32[1,640]{1,0:T(1,128)S(1)} %get-tuple-element.26.refs_0_, bf16[640,512]{1,0:T(8,128)(2,1)S(1)} %get-tuple-element.27.refs_1_, f32[160,512]{1,0:T(8,128)S(1)} %get-tuple-element.34.refs_2_, bf16[480,1152]{1,0:T(8,128)(2,1)S(1)} %get-tuple-element.35.refs_3_, ...), custom_call_target="tpu_custom_call" | custom-call | tf_op jit(solution)/shard_map/pallas_call | solution.py:84
  43.1 1.3 %collective-permute-done.10 = f32[56,512]{1,0:T(8,128)S(1)} collective-permute-done((f32[56,512]{1,0:T(8,128)S(1)}, f32[56,512]{1,0:T(8,128)S(1)}, u32[]{:S(2)}, u32[]{:S(2)}) %collective-permute-start.10) | collective-permute-done | bytes 114720 | tf_op jit(solution)/shard_map/ppermute | solution.py:89
  44.4 1.2 %collective-permute-start.11 = (bf16[56,512]{1,0:T(8,128)(2,1)S(1)}, bf16[56,512]{1,0:T(8,128)(2,1)S(1)}, u32[]{:S(2)}, u32[]{:S(2)}) collective-permute-start(bf16[56,512]{1,0:T(8,128)(2,1)S(1)} %add_convert_fusion.refs_4_), channel_id=1, source_target_pairs={{0,12},{4,8},{8,4},{12,0},{1,13},{5,9},{9,5},{13,1},{2,14},{6,10},... | collective-permute-start | bytes 172040 | tf_op jit(solution)/shard_map/ppermute | solution.py:112
  45.6 2.5 %collective-permute-start.12 = (bf16[56,512]{1,0:T(8,128)(2,1)S(1)}, bf16[56,512]{1,0:T(8,128)(2,1)S(1)}, u32[]{:S(2)}, u32[]{:S(2)}) collective-permute-start(bf16[56,512]{1,0:T(8,128)(2,1)S(1)} %add_convert_fusion.refs_4_), channel_id=1, source_target_pairs={{0,8},{4,12},{8,0},{12,4},{1,9},{5,13},{9,1},{13,5},{2,10},{6,14},... | collective-permute-start | bytes 172040 | tf_op jit(solution)/shard_map/ppermute | solution.py:112
  48.1 0.7 %collective-permute-start.13 = (bf16[56,512]{1,0:T(8,128)(2,1)S(1)}, bf16[56,512]{1,0:T(8,128)(2,1)S(1)}, u32[]{:S(2)}, u32[]{:S(2)}) collective-permute-start(bf16[56,512]{1,0:T(8,128)(2,1)S(1)} %add_convert_fusion.refs_4_), channel_id=1, source_target_pairs={{0,4},{4,0},{8,12},{12,8},{1,5},{5,1},{9,13},{13,9},{2,6},{6,2},{1... | collective-permute-start | bytes 172040 | tf_op jit(solution)/shard_map/ppermute | solution.py:112
  48.8 2.3 %collective-permute-done.11.refs_5_ = bf16[56,512]{1,0:T(8,128)(2,1)S(1)} collective-permute-done((bf16[56,512]{1,0:T(8,128)(2,1)S(1)}, bf16[56,512]{1,0:T(8,128)(2,1)S(1)}, u32[]{:S(2)}, u32[]{:S(2)}) %collective-permute-start.11) | collective-permute-done | bytes 57376 | tf_op jit(solution)/shard_map/ppermute | solution.py:112
  51.2 2.5 %collective-permute-done.12.refs_6_ = bf16[56,512]{1,0:T(8,128)(2,1)S(1)} collective-permute-done((bf16[56,512]{1,0:T(8,128)(2,1)S(1)}, bf16[56,512]{1,0:T(8,128)(2,1)S(1)}, u32[]{:S(2)}, u32[]{:S(2)}) %collective-permute-start.12) | collective-permute-done | bytes 57376 | tf_op jit(solution)/shard_map/ppermute | solution.py:112
  55.1 2.5 %shard_map.83 = (bf16[1,56,448]{2,1,0:T(8,128)(2,1)}, f32[1,56,128]{2,1,0:T(8,128)}) custom-call(bf16[448,640]{1,0:T(8,128)(2,1)S(1)} %get-tuple-element.23.refs_0_, bf16[512,512]{1,0:T(8,128)(2,1)S(1)} %get-tuple-element.24.refs_1_, bf16[512,448]{1,0:T(8,128)(2,1)S(1)} %get-tuple-element.25.refs_2_, s32[1,128]{1,0:T(1,128)S(1)} %copy-done.3, ...), custom_call_target="tpu_custom_call" | custom-call | tf_op jit(solution)/shard_map/pallas_call | solution.py:84
  (31 shorter events, 5.8 us)
Async XLA Ops:
  0.6 17.8 %copy-start = (bf16[512,3,1152]{2,0,1:T(8,128)(2,1)S(1)}, bf16[512,3,1152]{2,0,1:T(8,128)(2,1)}, u32[]{:S(2)}) copy-start(bf16[512,3,1152]{2,0,1:T(8,128)(2,1)} %param.11) | copy-start | bytes 10616836
  2.1 14.6 %copy-start.1 = (bf16[512,1152]{1,0:T(8,128)(2,1)S(1)}, bf16[512,1152]{1,0:T(8,128)(2,1)}, u32[]{:S(2)}) copy-start(bf16[512,1152]{1,0:T(8,128)(2,1)} %refs_1_.4) | copy-start | bytes 3538948
  17.1 7.5 %collective-permute-start = (bf16[80,1152]{1,0:T(8,128)(2,1)S(1)}, bf16[80,1152]{1,0:T(8,128)(2,1)S(1)}, u32[]{:S(2)}, u32[]{:S(2)}) collective-permute-start(bf16[80,1152]{1,0:T(8,128)(2,1)S(1)} %get-tuple-element.29.refs_3_), channel_id=1, source_target_pairs={{0,8},{2,10},{8,12},{10,14},{12,4},{14,6},{4,0},{6,2},{1,9},{3,11}... | collective-permute-start | bytes 552968 | tf_op jit(solution)/shard_map/ppermute | solution.py:105
  17.7 10.4 %collective-permute-start.1 = (bf16[80,1152]{1,0:T(8,128)(2,1)S(1)}, bf16[80,1152]{1,0:T(8,128)(2,1)S(1)}, u32[]{:S(2)}, u32[]{:S(2)}) collective-permute-start(bf16[80,1152]{1,0:T(8,128)(2,1)S(1)} %get-tuple-element.30), channel_id=1, source_target_pairs={{0,10},{2,8},{8,14},{10,12},{12,6},{14,4},{4,2},{6,0},{1,11},{3,9}... | collective-permute-start | bytes 552968 | tf_op jit(solution)/shard_map/ppermute | solution.py:105
  19.2 0.7 %copy-start.2 = (s32[1,4,4]{2,1,0:T(4,128)S(1)}, s32[1,4,4]{2,1,0:T(4,128)}, u32[]{:S(2)}) copy-start(s32[1,4,4]{2,1,0:T(4,128)} %refs_1_.5) | copy-start | bytes 196
  21.8 8.9 %collective-permute-start.4 = (bf16[80,1152]{1,0:T(8,128)(2,1)S(1)}, bf16[80,1152]{1,0:T(8,128)(2,1)S(1)}, u32[]{:S(2)}, u32[]{:S(2)}) collective-permute-start(bf16[80,1152]{1,0:T(8,128)(2,1)S(1)} %get-tuple-element.31), channel_id=1, source_target_pairs={{0,2},{2,0},{1,3},{3,1},{4,6},{6,4},{5,7},{7,5},{8,10},{10,8},{9,1... | collective-permute-start | bytes 552968 | tf_op jit(solution)/shard_map/ppermute | solution.py:89
  24.6 8.0 %collective-permute-start.2 = (bf16[80,1152]{1,0:T(8,128)(2,1)S(1)}, bf16[80,1152]{1,0:T(8,128)(2,1)S(1)}, u32[]{:S(2)}, u32[]{:S(2)}) collective-permute-start(bf16[80,1152]{1,0:T(8,128)(2,1)S(1)} %collective-permute-done.refs_4_), channel_id=1, source_target_pairs={{0,8},{8,12},{12,4},{4,0},{1,9},{9,13},{13,5},{5,1},{2,10},{10,14}... | collective-permute-start | bytes 552968 | tf_op jit(solution)/shard_map/ppermute | solution.py:102
  28.1 8.3 %collective-permute-start.3 = (bf16[80,1152]{1,0:T(8,128)(2,1)S(1)}, bf16[80,1152]{1,0:T(8,128)(2,1)S(1)}, u32[]{:S(2)}, u32[]{:S(2)}) collective-permute-start(bf16[80,1152]{1,0:T(8,128)(2,1)S(1)} %collective-permute-done.1.refs_5_), channel_id=1, source_target_pairs={{0,8},{8,12},{12,4},{4,0},{1,9},{9,13},{13,5},{5,1},{2,10},{10,14}... | collective-permute-start | bytes 552968 | tf_op jit(solution)/shard_map/ppermute | solution.py:102
  28.7 8.4 %collective-permute-start.5 = (bf16[80,1152]{1,0:T(8,128)(2,1)S(1)}, bf16[80,1152]{1,0:T(8,128)(2,1)S(1)}, u32[]{:S(2)}, u32[]{:S(2)}) collective-permute-start(bf16[80,1152]{1,0:T(8,128)(2,1)S(1)} %get-tuple-element.32), channel_id=1, source_target_pairs={{0,2},{2,0},{1,3},{3,1},{4,6},{6,4},{5,7},{7,5},{8,10},{10,8},{9,1... | collective-permute-start | bytes 552968 | tf_op jit(solution)/shard_map/ppermute | solution.py:89
  30.5 8.2 %collective-permute-start.6 = (bf16[80,1152]{1,0:T(8,128)(2,1)S(1)}, bf16[80,1152]{1,0:T(8,128)(2,1)S(1)}, u32[]{:S(2)}, u32[]{:S(2)}) collective-permute-start(bf16[80,1152]{1,0:T(8,128)(2,1)S(1)} %get-tuple-element.33), channel_id=1, source_target_pairs={{0,2},{2,0},{1,3},{3,1},{4,6},{6,4},{5,7},{7,5},{8,10},{10,8},{9,1... | collective-permute-start | bytes 552968 | tf_op jit(solution)/shard_map/ppermute | solution.py:89
  30.7 10.0 %collective-permute-start.7 = (bf16[80,1152]{1,0:T(8,128)(2,1)S(1)}, bf16[80,1152]{1,0:T(8,128)(2,1)S(1)}, u32[]{:S(2)}, u32[]{:S(2)}) collective-permute-start(bf16[80,1152]{1,0:T(8,128)(2,1)S(1)} %get-tuple-element.30), channel_id=1, source_target_pairs={{0,2},{2,0},{1,3},{3,1},{4,6},{6,4},{5,7},{7,5},{8,10},{10,8},{9,1... | collective-permute-start | bytes 552968 | tf_op jit(solution)/shard_map/ppermute | solution.py:89
  32.6 8.2 %collective-permute-start.8 = (bf16[80,1152]{1,0:T(8,128)(2,1)S(1)}, bf16[80,1152]{1,0:T(8,128)(2,1)S(1)}, u32[]{:S(2)}, u32[]{:S(2)}) collective-permute-start(bf16[80,1152]{1,0:T(8,128)(2,1)S(1)} %collective-permute-done.2.refs_6_), channel_id=1, source_target_pairs={{0,8},{8,12},{12,4},{4,0},{1,9},{9,13},{13,5},{5,1},{2,10},{10,14}... | collective-permute-start | bytes 552968 | tf_op jit(solution)/shard_map/ppermute | solution.py:102
  36.5 5.5 %collective-permute-start.9 = (bf16[80,1152]{1,0:T(8,128)(2,1)S(1)}, bf16[80,1152]{1,0:T(8,128)(2,1)S(1)}, u32[]{:S(2)}, u32[]{:S(2)}) collective-permute-start(bf16[80,1152]{1,0:T(8,128)(2,1)S(1)} %collective-permute-done.3.refs_7_), channel_id=1, source_target_pairs={{0,8},{8,12},{12,4},{4,0},{1,9},{9,13},{13,5},{5,1},{2,10},{10,14}... | collective-permute-start | bytes 552968 | tf_op jit(solution)/shard_map/ppermute | solution.py:102
  38.8 16.4 %copy-start.3 = (s32[1,128]{1,0:T(1,128)S(1)}, s32[1,128]{1,0:T(1,128)}, u32[]{:S(2)}) copy-start(s32[1,128]{1,0:T(1,128)} %refs_3_.1) | copy-start | bytes 1540
  43.0 1.4 %collective-permute-start.10 = (f32[56,512]{1,0:T(8,128)S(1)}, f32[56,512]{1,0:T(8,128)S(1)}, u32[]{:S(2)}, u32[]{:S(2)}) collective-permute-start(f32[56,512]{1,0:T(8,128)S(1)} %get-tuple-element.37), channel_id=1, source_target_pairs={{0,1},{1,0},{2,3},{3,2},{4,5},{5,4},{6,7},{7,6},{8,9},{9,8},{10,11... | collective-permute-start | bytes 344072 | tf_op jit(solution)/shard_map/ppermute | solution.py:89
  44.4 6.8 %collective-permute-start.11 = (bf16[56,512]{1,0:T(8,128)(2,1)S(1)}, bf16[56,512]{1,0:T(8,128)(2,1)S(1)}, u32[]{:S(2)}, u32[]{:S(2)}) collective-permute-start(bf16[56,512]{1,0:T(8,128)(2,1)S(1)} %add_convert_fusion.refs_4_), channel_id=1, source_target_pairs={{0,12},{4,8},{8,4},{12,0},{1,13},{5,9},{9,5},{13,1},{2,14},{6,10},... | collective-permute-start | bytes 172040 | tf_op jit(solution)/shard_map/ppermute | solution.py:112
  45.6 8.1 %collective-permute-start.12 = (bf16[56,512]{1,0:T(8,128)(2,1)S(1)}, bf16[56,512]{1,0:T(8,128)(2,1)S(1)}, u32[]{:S(2)}, u32[]{:S(2)}) collective-permute-start(bf16[56,512]{1,0:T(8,128)(2,1)S(1)} %add_convert_fusion.refs_4_), channel_id=1, source_target_pairs={{0,8},{4,12},{8,0},{12,4},{1,9},{5,13},{9,1},{13,5},{2,10},{6,14},... | collective-permute-start | bytes 172040 | tf_op jit(solution)/shard_map/ppermute | solution.py:112
  48.1 5.6 %collective-permute-start.13 = (bf16[56,512]{1,0:T(8,128)(2,1)S(1)}, bf16[56,512]{1,0:T(8,128)(2,1)S(1)}, u32[]{:S(2)}, u32[]{:S(2)}) collective-permute-start(bf16[56,512]{1,0:T(8,128)(2,1)S(1)} %add_convert_fusion.refs_4_), channel_id=1, source_target_pairs={{0,4},{4,0},{8,12},{12,8},{1,5},{5,1},{9,13},{13,9},{2,6},{6,2},{1... | collective-permute-start | bytes 172040 | tf_op jit(solution)/shard_map/ppermute | solution.py:112
  48.8 5.4 %collective-permute-start.14 = (bf16[56,512]{1,0:T(8,128)(2,1)S(1)}, bf16[56,512]{1,0:T(8,128)(2,1)S(1)}, u32[]{:S(2)}, u32[]{:S(2)}) collective-permute-start(bf16[56,512]{1,0:T(8,128)(2,1)S(1)} %add_convert_fusion.refs_4_), channel_id=1, source_target_pairs={{0,1},{1,0},{2,3},{3,2},{4,5},{5,4},{6,7},{7,6},{8,9},{9,8},{10,11... | collective-permute-start | bytes 172040 | tf_op jit(solution)/shard_map/ppermute | solution.py:89
  51.2 3.1 %collective-permute-start.15 = (bf16[56,512]{1,0:T(8,128)(2,1)S(1)}, bf16[56,512]{1,0:T(8,128)(2,1)S(1)}, u32[]{:S(2)}, u32[]{:S(2)}) collective-permute-start(bf16[56,512]{1,0:T(8,128)(2,1)S(1)} %collective-permute-done.11.refs_5_), channel_id=1, source_target_pairs={{0,1},{1,0},{2,3},{3,2},{4,5},{5,4},{6,7},{7,6},{8,9},{9,8},{10,11... | collective-permute-start | bytes 172040 | tf_op jit(solution)/shard_map/ppermute | solution.py:89
  53.7 1.2 %collective-permute-start.16 = (bf16[56,512]{1,0:T(8,128)(2,1)S(1)}, bf16[56,512]{1,0:T(8,128)(2,1)S(1)}, u32[]{:S(2)}, u32[]{:S(2)}) collective-permute-start(bf16[56,512]{1,0:T(8,128)(2,1)S(1)} %collective-permute-done.12.refs_6_), channel_id=1, source_target_pairs={{0,1},{1,0},{2,3},{3,2},{4,5},{5,4},{6,7},{7,6},{8,9},{9,8},{10,11... | collective-permute-start | bytes 172040 | tf_op jit(solution)/shard_map/ppermute | solution.py:89
  53.7 1.4 %collective-permute-start.17 = (bf16[56,512]{1,0:T(8,128)(2,1)S(1)}, bf16[56,512]{1,0:T(8,128)(2,1)S(1)}, u32[]{:S(2)}, u32[]{:S(2)}) collective-permute-start(bf16[56,512]{1,0:T(8,128)(2,1)S(1)} %collective-permute-done.13.refs_7_), channel_id=1, source_target_pairs={{0,1},{1,0},{2,3},{3,2},{4,5},{5,4},{6,7},{7,6},{8,9},{9,8},{10,11... | collective-permute-start | bytes 172040 | tf_op jit(solution)/shard_map/ppermute | solution.py:89

commit v22 on v15

--- a/solution.py
+++ b/solution.py
@@ -387,8 +387,8 @@
         for l in range(depth):
             rows = every[l * column : (l + 1) * column]
             raw = raw + jnp.where(layer_row[:, lanes] == l + 1.0, rows, 0.0)
-        split = dot(jnp.concatenate(pieces(raw), axis=0), placing_t[lanes])
-        return split[:column] + (split[column : 2 * column] + split[2 * column :])
+        split = dot(jnp.concatenate(pieces(raw)[:2], axis=0), placing_t[lanes])
+        return split[:column] + split[column:]
 
     def early(layer_row, placing_t, gains, *values):
         count = depth * poses

time: 57.4 us -> 57.3 us (level)
  transfers between devices with their start and end apart: 18 -> 18, of which waited for: 12 -> 12; matrix products, arithmetic and copies ran while one was open for 2% -> 2% of each run, Pallas kernels for 6% -> 5%
where the time goes in v22:
time: 57.3 us; the launch traced here: 57 us
  waiting for transfers between devices  17 us (30%)
  starting transfers between devices  14.9 us (26%)
  blocking collectives  14.1 us (25%)
  Pallas kernels  8.78 us (15%)
  matrix products  0.8 us (1%)
  between operations  0.75 us (1%)
  local copies, waits for them, and re-layouts  0.69 us (1%)
    all_to_all x1, blocking collectives, per_device(): lax.all_to_all(packed, ('feat', 'pos'), split_axis=0, concat_axis=0, tile...  14.1 us
    pallas_call x7, Pallas kernels, on_core(): return list(call(*args, *streams, *through))  8.78 us
    ppermute x9, starting transfers between devices, rotate(): lax.ppermute(x, axis, [(i, (i + step) % count) for i in range(count)])  5.33 us
    ppermute x9, waiting for transfers between devices, rotate(): lax.ppermute(x, axis, [(i, (i + step) % count) for i in range(count)])  4.95 us
    ppermute x3, starting transfers between devices, spread(): found[bits] = lax.ppermute(x, axis, [(i, i ^ bits) for i in range(count)])  4.62 us
    ppermute x3, waiting for transfers between devices, spread(): found[bits] = lax.ppermute(x, axis, [(i, i ^ bits) for i in range(count)])  4.39 us
    ppermute x4, waiting for transfers between devices, ring_next(): return lax.ppermute(x, axis, steps)  3.97 us
    ppermute x2, waiting for transfers between devices, ring_next(): return lax.ppermute(x, (axis, across), pairs)  3.73 us
  transfers between devices with their start and end apart: 18, of which 12 were waited for; matrix products, arithmetic and copies ran while one was open for 2% of the time, Pallas kernels for 5%

profile of v22, /device:TPU:0, one launch (start us, length us, event | category | flops | bytes accessed | tf_op | source)
XLA Modules:
  0.0 57.0 jit_solution(14183508985253672565)
XLA Ops:
  0.6 1.5 %shard_map.77 = f32[8,8,128]{2,1,0:T(8,128)} custom-call(s32[1,4,28]{2,1,0:T(4,128)} %refs_0_.1, f32[1,4,28]{2,1,0:T(4,128)} %refs_1_.3), custom_call_target="tpu_custom_call" | custom-call | tf_op jit(solution)/shard_map/pallas_call | solution.py:84
  2.1 14.1 %all_to_all.5.refs_0_ = f32[8,8,128]{2,1,0:T(8,128)S(1)} all-to-all(f32[8,8,128]{2,1,0:T(8,128)} %shard_map.77), channel_id=1, replica_groups=mesh['grp'=2,'feat'=4,'pos'=2,'rep'=2] {'feat','pos'}, dimensions={0} | all-to-all | bytes 65536 | tf_op jit(solution)/shard_map/all_to_all | solution.py:195
  17.7 0.7 %collective-permute-start.1 = (bf16[80,1152]{1,0:T(8,128)(2,1)S(1)}, bf16[80,1152]{1,0:T(8,128)(2,1)S(1)}, u32[]{:S(2)}, u32[]{:S(2)}) collective-permute-start(bf16[80,1152]{1,0:T(8,128)(2,1)S(1)} %get-tuple-element.30), channel_id=1, source_target_pairs={{0,10},{2,8},{8,14},{10,12},{12,6},{14,4},{4,2},{6,0},{1,11},{3,9}... | collective-permute-start | bytes 552968 | tf_op jit(solution)/shard_map/ppermute | solution.py:105
  18.4 0.8 %fusion = bf16[3,160,1152]{2,1,0:T(8,128)(2,1)S(1)} fusion(bf16[512,3,1152]{2,0,1:T(8,128)(2,1)S(1)} %copy-done, bf16[160,512]{1,0:T(8,128)(2,1)S(1)} %get-tuple-element.22), kind=kOutput, calls=%fused_computation.1 | convolution fusion | flops 566784000 | bytes 4808704 | tf_op jit(solution)/shard_map/dot_general | solution.py:285
  19.9 1.9 %shard_map.80 = (bf16[448,640]{1,0:T(8,128)(2,1)S(1)}, bf16[640,512]{1,0:T(8,128)(2,1)S(1)}, f32[1,640]{1,0:T(1,128)S(1)}, f32[480,1]{1,0:T(8,128)S(1)}, bf16[51...) custom-call(f32[32,28]{1,0:T(8,128)S(1)} %get-tuple-element.20.refs_, ...), custom_call_target="tpu_custom_call", output_to_operand_aliasing={{6}: (2, {}), {7}: (3, {}), {8}: (4, {})} | custom-call | flops 1 | bytes 1 | tf_op jit(solution)/shard_map/pallas_call | solution.py:84
  21.8 1.4 %collective-permute-start.4 = (bf16[80,1152]{1,0:T(8,128)(2,1)S(1)}, bf16[80,1152]{1,0:T(8,128)(2,1)S(1)}, u32[]{:S(2)}, u32[]{:S(2)}) collective-permute-start(bf16[80,1152]{1,0:T(8,128)(2,1)S(1)} %get-tuple-element.31), channel_id=1, source_target_pairs={{0,2},{2,0},{1,3},{3,1},{4,6},{6,4},{5,7},{7,5},{8,10},{10,8},{9,1... | collective-permute-start | bytes 552968 | tf_op jit(solution)/shard_map/ppermute | solution.py:89
  23.2 1.4 %collective-permute-done.refs_4_ = bf16[80,1152]{1,0:T(8,128)(2,1)S(1)} collective-permute-done((bf16[80,1152]{1,0:T(8,128)(2,1)S(1)}, bf16[80,1152]{1,0:T(8,128)(2,1)S(1)}, u32[]{:S(2)}, u32[]{:S(2)}) %collective-permute-start) | collective-permute-done | bytes 184352 | tf_op jit(solution)/shard_map/ppermute | solution.py:105
  24.6 1.2 %collective-permute-start.2 = (bf16[80,1152]{1,0:T(8,128)(2,1)S(1)}, bf16[80,1152]{1,0:T(8,128)(2,1)S(1)}, u32[]{:S(2)}, u32[]{:S(2)}) collective-permute-start(bf16[80,1152]{1,0:T(8,128)(2,1)S(1)} %collective-permute-done.refs_4_), channel_id=1, source_target_pairs={{0,8},{8,12},{12,4},{4,0},{1,9},{9,13},{13,5},{5,1},{2,10},{10,14}... | collective-permute-start | bytes 552968 | tf_op jit(solution)/shard_map/ppermute | solution.py:102
  25.8 2.3 %collective-permute-done.1.refs_5_ = bf16[80,1152]{1,0:T(8,128)(2,1)S(1)} collective-permute-done((bf16[80,1152]{1,0:T(8,128)(2,1)S(1)}, bf16[80,1152]{1,0:T(8,128)(2,1)S(1)}, u32[]{:S(2)}, u32[]{:S(2)}) %collective-permute-start.1) | collective-permute-done | bytes 184352 | tf_op jit(solution)/shard_map/ppermute | solution.py:105
  28.7 1.8 %collective-permute-start.5 = (bf16[80,1152]{1,0:T(8,128)(2,1)S(1)}, bf16[80,1152]{1,0:T(8,128)(2,1)S(1)}, u32[]{:S(2)}, u32[]{:S(2)}) collective-permute-start(bf16[80,1152]{1,0:T(8,128)(2,1)S(1)} %get-tuple-element.32), channel_id=1, source_target_pairs={{0,2},{2,0},{1,3},{3,1},{4,6},{6,4},{5,7},{7,5},{8,10},{10,8},{9,1... | collective-permute-start | bytes 552968 | tf_op jit(solution)/shard_map/ppermute | solution.py:89
  30.7 1.8 %collective-permute-start.7 = (bf16[80,1152]{1,0:T(8,128)(2,1)S(1)}, bf16[80,1152]{1,0:T(8,128)(2,1)S(1)}, u32[]{:S(2)}, u32[]{:S(2)}) collective-permute-start(bf16[80,1152]{1,0:T(8,128)(2,1)S(1)} %get-tuple-element.30), channel_id=1, source_target_pairs={{0,2},{2,0},{1,3},{3,1},{4,6},{6,4},{5,7},{7,5},{8,10},{10,8},{9,1... | collective-permute-start | bytes 552968 | tf_op jit(solution)/shard_map/ppermute | solution.py:89
  32.6 1.2 %collective-permute-start.8 = (bf16[80,1152]{1,0:T(8,128)(2,1)S(1)}, bf16[80,1152]{1,0:T(8,128)(2,1)S(1)}, u32[]{:S(2)}, u32[]{:S(2)}) collective-permute-start(bf16[80,1152]{1,0:T(8,128)(2,1)S(1)} %collective-permute-done.2.refs_6_), channel_id=1, source_target_pairs={{0,8},{8,12},{12,4},{4,0},{1,9},{9,13},{13,5},{5,1},{2,10},{10,14}... | collective-permute-start | bytes 552968 | tf_op jit(solution)/shard_map/ppermute | solution.py:102
  33.8 2.7 %collective-permute-done.3.refs_7_ = bf16[80,1152]{1,0:T(8,128)(2,1)S(1)} collective-permute-done((bf16[80,1152]{1,0:T(8,128)(2,1)S(1)}, bf16[80,1152]{1,0:T(8,128)(2,1)S(1)}, u32[]{:S(2)}, u32[]{:S(2)}) %collective-permute-start.3) | collective-permute-done | bytes 184352 | tf_op jit(solution)/shard_map/ppermute | solution.py:102
  37.1 1.6 %collective-permute-done.6.refs_13_ = bf16[80,1152]{1,0:T(8,128)(2,1)S(1)} collective-permute-done((bf16[80,1152]{1,0:T(8,128)(2,1)S(1)}, bf16[80,1152]{1,0:T(8,128)(2,1)S(1)}, u32[]{:S(2)}, u32[]{:S(2)}) %collective-permute-start.6) | collective-permute-done | bytes 184352 | tf_op jit(solution)/shard_map/ppermute | solution.py:89
  38.8 1.2 %shard_map.81 = (f32[160,512]{1,0:T(8,128)S(1)}, bf16[480,1152]{1,0:T(8,128)(2,1)S(1)}) custom-call(f32[1,640]{1,0:T(1,128)S(1)} %get-tuple-element.26.refs_0_, bf16[640,512]{1,0:T(8,128)(2,1)S(1)} %get-tuple-element.27.refs_1_, f32[480,1]{1,0:T(8,128)S(1)} %get-tuple-element.28.refs_2_, bf16[80,1152]{1,0:T(8,128)(2,1)S(1)} %get-tuple-element.29.refs_3_, ...), custom_call_target="tpu_custom_call" | custom-call | flops 1 | bytes 1 | tf_op jit(solution)/shard_map/pallas_call | solution.py:84
  40.0 0.8 %collective-permute-done.7.refs_4_ = bf16[80,1152]{1,0:T(8,128)(2,1)S(1)} collective-permute-done((bf16[80,1152]{1,0:T(8,128)(2,1)S(1)}, bf16[80,1152]{1,0:T(8,128)(2,1)S(1)}, u32[]{:S(2)}, u32[]{:S(2)}) %collective-permute-start.7) | collective-permute-done | bytes 184352 | tf_op jit(solution)/shard_map/ppermute | solution.py:89
  40.8 1.3 %collective-permute-done.9.refs_6_ = bf16[80,1152]{1,0:T(8,128)(2,1)S(1)} collective-permute-done((bf16[80,1152]{1,0:T(8,128)(2,1)S(1)}, bf16[80,1152]{1,0:T(8,128)(2,1)S(1)}, u32[]{:S(2)}, u32[]{:S(2)}) %collective-permute-start.9) | collective-permute-done | bytes 184352 | tf_op jit(solution)/shard_map/ppermute | solution.py:102
  42.0 0.9 %shard_map.82 = (f32[56,512]{1,0:T(8,128)S(1)}, f32[56,512]{1,0:T(8,128)S(1)}) custom-call(f32[1,640]{1,0:T(1,128)S(1)} %get-tuple-element.26.refs_0_, bf16[640,512]{1,0:T(8,128)(2,1)S(1)} %get-tuple-element.27.refs_1_, f32[160,512]{1,0:T(8,128)S(1)} %get-tuple-element.34.refs_2_, bf16[480,1152]{1,0:T(8,128)(2,1)S(1)} %get-tuple-element.35.refs_3_, ...), custom_call_target="tpu_custom_call" | custom-call | tf_op jit(solution)/shard_map/pallas_call | solution.py:84
  43.0 1.3 %collective-permute-done.10 = f32[56,512]{1,0:T(8,128)S(1)} collective-permute-done((f32[56,512]{1,0:T(8,128)S(1)}, f32[56,512]{1,0:T(8,128)S(1)}, u32[]{:S(2)}, u32[]{:S(2)}) %collective-permute-start.10) | collective-permute-done | bytes 114720 | tf_op jit(solution)/shard_map/ppermute | solution.py:89
  44.3 1.6 %collective-permute-start.11 = (bf16[56,512]{1,0:T(8,128)(2,1)S(1)}, bf16[56,512]{1,0:T(8,128)(2,1)S(1)}, u32[]{:S(2)}, u32[]{:S(2)}) collective-permute-start(bf16[56,512]{1,0:T(8,128)(2,1)S(1)} %add_convert_fusion.refs_4_), channel_id=1, source_target_pairs={{0,8},{4,12},{8,0},{12,4},{1,9},{5,13},{9,1},{13,5},{2,10},{6,14},... | collective-permute-start | bytes 172040 | tf_op jit(solution)/shard_map/ppermute | solution.py:112
  45.9 3.0 %collective-permute-start.12 = (bf16[56,512]{1,0:T(8,128)(2,1)S(1)}, bf16[56,512]{1,0:T(8,128)(2,1)S(1)}, u32[]{:S(2)}, u32[]{:S(2)}) collective-permute-start(bf16[56,512]{1,0:T(8,128)(2,1)S(1)} %add_convert_fusion.refs_4_), channel_id=1, source_target_pairs={{0,12},{4,8},{8,4},{12,0},{1,13},{5,9},{9,5},{13,1},{2,14},{6,10},... | collective-permute-start | bytes 172040 | tf_op jit(solution)/shard_map/ppermute | solution.py:112
  48.9 3.2 %collective-permute-done.11.refs_5_ = bf16[56,512]{1,0:T(8,128)(2,1)S(1)} collective-permute-done((bf16[56,512]{1,0:T(8,128)(2,1)S(1)}, bf16[56,512]{1,0:T(8,128)(2,1)S(1)}, u32[]{:S(2)}, u32[]{:S(2)}) %collective-permute-start.11) | collective-permute-done | bytes 57376 | tf_op jit(solution)/shard_map/ppermute | solution.py:112
  53.3 0.7 %collective-permute-done.16.refs_10_ = bf16[56,512]{1,0:T(8,128)(2,1)S(1)} collective-permute-done((bf16[56,512]{1,0:T(8,128)(2,1)S(1)}, bf16[56,512]{1,0:T(8,128)(2,1)S(1)}, u32[]{:S(2)}, u32[]{:S(2)}) %collective-permute-start.16) | collective-permute-done | bytes 57376 | tf_op jit(solution)/shard_map/ppermute | solution.py:89
  54.6 2.5 %shard_map.83 = (bf16[1,56,448]{2,1,0:T(8,128)(2,1)}, f32[1,56,128]{2,1,0:T(8,128)}) custom-call(bf16[448,640]{1,0:T(8,128)(2,1)S(1)} %get-tuple-element.23.refs_0_, bf16[512,512]{1,0:T(8,128)(2,1)S(1)} %get-tuple-element.24.refs_1_, bf16[512,448]{1,0:T(8,128)(2,1)S(1)} %get-tuple-element.25.refs_2_, s32[1,128]{1,0:T(1,128)S(1)} %copy-done.3, ...), custom_call_target="tpu_custom_call" | custom-call | tf_op jit(solution)/shard_map/pallas_call | solution.py:84
  (31 shorter events, 5.5 us)
Async XLA Ops:
  0.6 17.8 %copy-start = (bf16[512,3,1152]{2,0,1:T(8,128)(2,1)S(1)}, bf16[512,3,1152]{2,0,1:T(8,128)(2,1)}, u32[]{:S(2)}) copy-start(bf16[512,3,1152]{2,0,1:T(8,128)(2,1)} %param.11) | copy-start | bytes 10616836
  2.1 14.6 %copy-start.1 = (bf16[512,1152]{1,0:T(8,128)(2,1)S(1)}, bf16[512,1152]{1,0:T(8,128)(2,1)}, u32[]{:S(2)}) copy-start(bf16[512,1152]{1,0:T(8,128)(2,1)} %refs_1_.4) | copy-start | bytes 3538948
  17.1 7.5 %collective-permute-start = (bf16[80,1152]{1,0:T(8,128)(2,1)S(1)}, bf16[80,1152]{1,0:T(8,128)(2,1)S(1)}, u32[]{:S(2)}, u32[]{:S(2)}) collective-permute-start(bf16[80,1152]{1,0:T(8,128)(2,1)S(1)} %get-tuple-element.29.refs_3_), channel_id=1, source_target_pairs={{0,8},{2,10},{8,12},{10,14},{12,4},{14,6},{4,0},{6,2},{1,9},{3,11}... | collective-permute-start | bytes 552968 | tf_op jit(solution)/shard_map/ppermute | solution.py:105
  17.7 10.4 %collective-permute-start.1 = (bf16[80,1152]{1,0:T(8,128)(2,1)S(1)}, bf16[80,1152]{1,0:T(8,128)(2,1)S(1)}, u32[]{:S(2)}, u32[]{:S(2)}) collective-permute-start(bf16[80,1152]{1,0:T(8,128)(2,1)S(1)} %get-tuple-element.30), channel_id=1, source_target_pairs={{0,10},{2,8},{8,14},{10,12},{12,6},{14,4},{4,2},{6,0},{1,11},{3,9}... | collective-permute-start | bytes 552968 | tf_op jit(solution)/shard_map/ppermute | solution.py:105
  19.2 0.7 %copy-start.2 = (s32[1,4,4]{2,1,0:T(4,128)S(1)}, s32[1,4,4]{2,1,0:T(4,128)}, u32[]{:S(2)}) copy-start(s32[1,4,4]{2,1,0:T(4,128)} %refs_1_.5) | copy-start | bytes 196
  21.8 8.9 %collective-permute-start.4 = (bf16[80,1152]{1,0:T(8,128)(2,1)S(1)}, bf16[80,1152]{1,0:T(8,128)(2,1)S(1)}, u32[]{:S(2)}, u32[]{:S(2)}) collective-permute-start(bf16[80,1152]{1,0:T(8,128)(2,1)S(1)} %get-tuple-element.31), channel_id=1, source_target_pairs={{0,2},{2,0},{1,3},{3,1},{4,6},{6,4},{5,7},{7,5},{8,10},{10,8},{9,1... | collective-permute-start | bytes 552968 | tf_op jit(solution)/shard_map/ppermute | solution.py:89
  24.6 8.0 %collective-permute-start.2 = (bf16[80,1152]{1,0:T(8,128)(2,1)S(1)}, bf16[80,1152]{1,0:T(8,128)(2,1)S(1)}, u32[]{:S(2)}, u32[]{:S(2)}) collective-permute-start(bf16[80,1152]{1,0:T(8,128)(2,1)S(1)} %collective-permute-done.refs_4_), channel_id=1, source_target_pairs={{0,8},{8,12},{12,4},{4,0},{1,9},{9,13},{13,5},{5,1},{2,10},{10,14}... | collective-permute-start | bytes 552968 | tf_op jit(solution)/shard_map/ppermute | solution.py:102
  28.1 8.3 %collective-permute-start.3 = (bf16[80,1152]{1,0:T(8,128)(2,1)S(1)}, bf16[80,1152]{1,0:T(8,128)(2,1)S(1)}, u32[]{:S(2)}, u32[]{:S(2)}) collective-permute-start(bf16[80,1152]{1,0:T(8,128)(2,1)S(1)} %collective-permute-done.1.refs_5_), channel_id=1, source_target_pairs={{0,8},{8,12},{12,4},{4,0},{1,9},{9,13},{13,5},{5,1},{2,10},{10,14}... | collective-permute-start | bytes 552968 | tf_op jit(solution)/shard_map/ppermute | solution.py:102
  28.7 8.4 %collective-permute-start.5 = (bf16[80,1152]{1,0:T(8,128)(2,1)S(1)}, bf16[80,1152]{1,0:T(8,128)(2,1)S(1)}, u32[]{:S(2)}, u32[]{:S(2)}) collective-permute-start(bf16[80,1152]{1,0:T(8,128)(2,1)S(1)} %get-tuple-element.32), channel_id=1, source_target_pairs={{0,2},{2,0},{1,3},{3,1},{4,6},{6,4},{5,7},{7,5},{8,10},{10,8},{9,1... | collective-permute-start | bytes 552968 | tf_op jit(solution)/shard_map/ppermute | solution.py:89
  30.5 8.2 %collective-permute-start.6 = (bf16[80,1152]{1,0:T(8,128)(2,1)S(1)}, bf16[80,1152]{1,0:T(8,128)(2,1)S(1)}, u32[]{:S(2)}, u32[]{:S(2)}) collective-permute-start(bf16[80,1152]{1,0:T(8,128)(2,1)S(1)} %get-tuple-element.33), channel_id=1, source_target_pairs={{0,2},{2,0},{1,3},{3,1},{4,6},{6,4},{5,7},{7,5},{8,10},{10,8},{9,1... | collective-permute-start | bytes 552968 | tf_op jit(solution)/shard_map/ppermute | solution.py:89
  30.7 10.0 %collective-permute-start.7 = (bf16[80,1152]{1,0:T(8,128)(2,1)S(1)}, bf16[80,1152]{1,0:T(8,128)(2,1)S(1)}, u32[]{:S(2)}, u32[]{:S(2)}) collective-permute-start(bf16[80,1152]{1,0:T(8,128)(2,1)S(1)} %get-tuple-element.30), channel_id=1, source_target_pairs={{0,2},{2,0},{1,3},{3,1},{4,6},{6,4},{5,7},{7,5},{8,10},{10,8},{9,1... | collective-permute-start | bytes 552968 | tf_op jit(solution)/shard_map/ppermute | solution.py:89
  32.6 8.2 %collective-permute-start.8 = (bf16[80,1152]{1,0:T(8,128)(2,1)S(1)}, bf16[80,1152]{1,0:T(8,128)(2,1)S(1)}, u32[]{:S(2)}, u32[]{:S(2)}) collective-permute-start(bf16[80,1152]{1,0:T(8,128)(2,1)S(1)} %collective-permute-done.2.refs_6_), channel_id=1, source_target_pairs={{0,8},{8,12},{12,4},{4,0},{1,9},{9,13},{13,5},{5,1},{2,10},{10,14}... | collective-permute-start | bytes 552968 | tf_op jit(solution)/shard_map/ppermute | solution.py:102
  36.5 5.5 %collective-permute-start.9 = (bf16[80,1152]{1,0:T(8,128)(2,1)S(1)}, bf16[80,1152]{1,0:T(8,128)(2,1)S(1)}, u32[]{:S(2)}, u32[]{:S(2)}) collective-permute-start(bf16[80,1152]{1,0:T(8,128)(2,1)S(1)} %collective-permute-done.3.refs_7_), channel_id=1, source_target_pairs={{0,8},{8,12},{12,4},{4,0},{1,9},{9,13},{13,5},{5,1},{2,10},{10,14}... | collective-permute-start | bytes 552968 | tf_op jit(solution)/shard_map/ppermute | solution.py:102
  38.8 15.8 %copy-start.3 = (s32[1,128]{1,0:T(1,128)S(1)}, s32[1,128]{1,0:T(1,128)}, u32[]{:S(2)}) copy-start(s32[1,128]{1,0:T(1,128)} %refs_3_.1) | copy-start | bytes 1540
  42.9 1.4 %collective-permute-start.10 = (f32[56,512]{1,0:T(8,128)S(1)}, f32[56,512]{1,0:T(8,128)S(1)}, u32[]{:S(2)}, u32[]{:S(2)}) collective-permute-start(f32[56,512]{1,0:T(8,128)S(1)} %get-tuple-element.37), channel_id=1, source_target_pairs={{0,1},{1,0},{2,3},{3,2},{4,5},{5,4},{6,7},{7,6},{8,9},{9,8},{10,11... | collective-permute-start | bytes 344072 | tf_op jit(solution)/shard_map/ppermute | solution.py:89
  44.3 7.8 %collective-permute-start.11 = (bf16[56,512]{1,0:T(8,128)(2,1)S(1)}, bf16[56,512]{1,0:T(8,128)(2,1)S(1)}, u32[]{:S(2)}, u32[]{:S(2)}) collective-permute-start(bf16[56,512]{1,0:T(8,128)(2,1)S(1)} %add_convert_fusion.refs_4_), channel_id=1, source_target_pairs={{0,8},{4,12},{8,0},{12,4},{1,9},{5,13},{9,1},{13,5},{2,10},{6,14},... | collective-permute-start | bytes 172040 | tf_op jit(solution)/shard_map/ppermute | solution.py:112
  45.9 6.8 %collective-permute-start.12 = (bf16[56,512]{1,0:T(8,128)(2,1)S(1)}, bf16[56,512]{1,0:T(8,128)(2,1)S(1)}, u32[]{:S(2)}, u32[]{:S(2)}) collective-permute-start(bf16[56,512]{1,0:T(8,128)(2,1)S(1)} %add_convert_fusion.refs_4_), channel_id=1, source_target_pairs={{0,12},{4,8},{8,4},{12,0},{1,13},{5,9},{9,5},{13,1},{2,14},{6,10},... | collective-permute-start | bytes 172040 | tf_op jit(solution)/shard_map/ppermute | solution.py:112
  48.9 4.4 %collective-permute-start.13 = (bf16[56,512]{1,0:T(8,128)(2,1)S(1)}, bf16[56,512]{1,0:T(8,128)(2,1)S(1)}, u32[]{:S(2)}, u32[]{:S(2)}) collective-permute-start(bf16[56,512]{1,0:T(8,128)(2,1)S(1)} %add_convert_fusion.refs_4_), channel_id=1, source_target_pairs={{0,4},{4,0},{8,12},{12,8},{1,5},{5,1},{9,13},{13,9},{2,6},{6,2},{1... | collective-permute-start | bytes 172040 | tf_op jit(solution)/shard_map/ppermute | solution.py:112
  48.9 4.4 %collective-permute-start.14 = (bf16[56,512]{1,0:T(8,128)(2,1)S(1)}, bf16[56,512]{1,0:T(8,128)(2,1)S(1)}, u32[]{:S(2)}, u32[]{:S(2)}) collective-permute-start(bf16[56,512]{1,0:T(8,128)(2,1)S(1)} %add_convert_fusion.refs_4_), channel_id=1, source_target_pairs={{0,1},{1,0},{2,3},{3,2},{4,5},{5,4},{6,7},{7,6},{8,9},{9,8},{10,11... | collective-permute-start | bytes 172040 | tf_op jit(solution)/shard_map/ppermute | solution.py:89
  52.1 1.2 %collective-permute-start.15 = (bf16[56,512]{1,0:T(8,128)(2,1)S(1)}, bf16[56,512]{1,0:T(8,128)(2,1)S(1)}, u32[]{:S(2)}, u32[]{:S(2)}) collective-permute-start(bf16[56,512]{1,0:T(8,128)(2,1)S(1)} %collective-permute-done.11.refs_5_), channel_id=1, source_target_pairs={{0,1},{1,0},{2,3},{3,2},{4,5},{5,4},{6,7},{7,6},{8,9},{9,8},{10,11... | collective-permute-start | bytes 172040 | tf_op jit(solution)/shard_map/ppermute | solution.py:89
  52.8 1.2 %collective-permute-start.16 = (bf16[56,512]{1,0:T(8,128)(2,1)S(1)}, bf16[56,512]{1,0:T(8,128)(2,1)S(1)}, u32[]{:S(2)}, u32[]{:S(2)}) collective-permute-start(bf16[56,512]{1,0:T(8,128)(2,1)S(1)} %collective-permute-done.12.refs_6_), channel_id=1, source_target_pairs={{0,1},{1,0},{2,3},{3,2},{4,5},{5,4},{6,7},{7,6},{8,9},{9,8},{10,11... | collective-permute-start | bytes 172040 | tf_op jit(solution)/shard_map/ppermute | solution.py:89
  53.3 1.2 %collective-permute-start.17 = (bf16[56,512]{1,0:T(8,128)(2,1)S(1)}, bf16[56,512]{1,0:T(8,128)(2,1)S(1)}, u32[]{:S(2)}, u32[]{:S(2)}) collective-permute-start(bf16[56,512]{1,0:T(8,128)(2,1)S(1)} %collective-permute-done.13.refs_7_), channel_id=1, source_target_pairs={{0,1},{1,0},{2,3},{3,2},{4,5},{5,4},{6,7},{7,6},{8,9},{9,8},{10,11... | collective-permute-start | bytes 172040 | tf_op jit(solution)/shard_map/ppermute | solution.py:89
